TPU v7x, 32 devices: a whole 2x2x4 slice. The times are simulated.
32 devices in a mesh: dom: 8 (over y, x, core), mode: 4 (over z).
Axes of the slice: x: 2, y: 2, z: 4, core: 2. Of those that a mesh axis runs over, the one named last changes fastest.
Arguments:
- iterate: float32 [256, 256, 256], P('mode', 'dom'), may hold values from -6 to 6
- source: float32 [256, 256, 256], P('mode', 'dom'), may hold values from -6 to 6
- mean_coef: float32 [256, 256], P('dom'), may hold values from 0.5 to 2
- kl_fields: float32 [20, 256, 256], P(None, 'dom'), may hold values from -1 to 1
- tri_index: int32 [5376, 3], replicated, may hold values from 0 to 255, as said below
- tri_value: float32 [5376], replicated, may hold values from 0.25 to 1.75, as said below
Outputs:
- updated: float32 [256, 256, 256], P('mode', 'dom')
- residual: float32 [256, 256, 256], P('mode', 'dom')
Inputs may be any that keep to these rules, and one draw needn't show every extreme that they name: `tri_index`: every pair of a mode i and a field l appears in exactly one entry; entries of field 0 have j = i; for fields 1 to 20 the entry (i, j, l) is listed together with (j, i, l), j differing from i; rows stand in a random order. `tri_value`: the entries (i, j, l) and (j, i, l) carry the same value.
All inputs are finite; a program needn't handle non-finite values.
Results may differ from a plain program's by a relative error of at most 0.0062.
Values may be sent and summed in bfloat16 or wider, within the bound.
No kernel may reach another device: no remote copies, remote signals or barrier semaphores. Data moves between devices by JAX's collectives and lax.ppermute only.
A program may use at most 64 MiB of HBM per device.

v0:
```python
import functools
import jax
import jax.numpy as jnp
from jax import lax
from jax.experimental import pallas as pl
from jax.experimental.pallas import tpu as pltpu
from jax.sharding import PartitionSpec as P

NZ = 16
GROUP = 7

cheb_center = 1.125
cheb_radius = 0.875
VMEM_LIMIT = 48 * 1024 * 1024


def in_vmem(count):
    return [pl.BlockSpec(memory_space=pltpu.VMEM)] * count


def in_smem():
    return pl.BlockSpec(memory_space=pltpu.SMEM)


def row_of(place, rho, slab, count, rows):
    upward = slab * place + rho
    downward = slab * place + (slab - 1 - rho)
    row = jnp.where(place < count // 2, upward, downward)
    return jnp.clip(row, 0, rows - 1)


def rim_row(place, slab, count, rows):
    row = row_of(place, -1, slab, count, rows)
    return jnp.where(place == 0, rows - 1, jnp.where(place == count - 1, 0, row))


def pack_kernel(count, slab, half, rows, z_ref, x_ref, *refs):
    z = z_ref[0]
    outs, turned = refs[:-1], refs[-1]
    turned[...] = jnp.swapaxes(x_ref[...], 0, 1).astype(jnp.bfloat16)
    for p in range(count):
        place = jnp.bitwise_xor(z, p)
        rim, early, late = outs[3 * p : 3 * p + 3]

        rim[0] = turned[rim_row(place, slab, count, rows)]
        for rho in range(slab + 1):
            row = row_of(place, rho, slab, count, rows)
            if rho <= half:
                early[rho] = turned[row]
            else:
                late[rho - half - 1] = turned[row]


def masks(cells):
    lane = lax.broadcasted_iota(jnp.int32, (1, cells), 1)
    in_z = lane % NZ
    one = jnp.float32(1.0)
    zero = jnp.float32(0.0)
    return (
        jnp.where(lane < cells - NZ, one, zero),
        jnp.where(lane >= NZ, one, zero),
        jnp.where(in_z < NZ - 1, one, zero),
        jnp.where(in_z > 0, one, zero),
    )


def beside(field, mask_set):
    cells = field.shape[-1]
    axis = field.ndim - 1
    return (
        pltpu.roll(field, cells - NZ, axis) * mask_set[0],
        pltpu.roll(field, NZ, axis) * mask_set[1],
        pltpu.roll(field, cells - 1, axis) * mask_set[2],
        pltpu.roll(field, 1, axis) * mask_set[3],
    )


def setup_kernel(
    slab, groups, modes_here, z_ref, i_ref, j_ref, l_ref, v_ref, coef_ref, dense_ref, weight_ref
):
    cells = coef_ref.shape[-1]
    size = dense_ref.shape[1]
    entries = i_ref.shape[1]
    flip = z_ref[0] * modes_here
    mode_id = jnp.bitwise_xor(lax.broadcasted_iota(jnp.int32, (size, entries), 0), flip)
    pick = jnp.where(mode_id == i_ref[...], 1.0, 0.0).astype(jnp.bfloat16)
    depth = groups * 8
    place = lax.broadcasted_iota(jnp.int32, (depth, entries), 0)
    field_of = jnp.where(place % 8 < GROUP, (place // 8) * GROUP + place % 8, -1)
    here = field_of == l_ref[...]
    partner = jnp.where(here, j_ref[...].astype(jnp.float32), 0.0).astype(jnp.bfloat16)
    value = jnp.where(here, v_ref[...], 0.0).astype(jnp.bfloat16)
    dims = (((1,), (1,)), ((), ()))
    partner_of = lax.dot_general(pick, partner, dims, preferred_element_type=jnp.float32)
    value_of = lax.dot_general(pick, value, dims, preferred_element_type=jnp.float32)
    column = jnp.bitwise_xor(lax.broadcasted_iota(jnp.int32, (size, size), 1), flip)
    column = column.astype(jnp.float32)
    for g in range(groups):
        for k in range(GROUP):
            at = g * 8 + k
            tile = jnp.where(column == partner_of[:, at : at + 1], value_of[:, at : at + 1], 0.0)
            dense_ref[g, :, k * size : (k + 1) * size] = tile.astype(jnp.bfloat16)
    mask_set = masks(cells)
    for rho in range(slab):
        centre = coef_ref[rho + 1]
        others = (coef_ref[rho + 2], coef_ref[rho]) + beside(centre, mask_set)
        for f, other in enumerate(others):
            weight_ref[rho, f] = 0.5 * (centre + other)


def mix_kernel(count, half, groups, window, *refs):
    rows_in = len(window)
    arrays = max(a for a, _ in window) + 1
    sources = refs[: arrays * count]
    dense_ref, weight_ref = refs[arrays * count : arrays * count + 2]
    outs = refs[arrays * count + 2 : arrays * count + 2 + count]
    rows_ref, diff_ref, term_ref, total_ref = refs[arrays * count + 2 + count :]
    size, cells = total_ref.shape
    here = size // count
    for k, (array, row) in enumerate(window):
        for p in range(count):
            rows_ref[k, p * here : (p + 1) * here, :] = sources[array * count + p][row]
    mask_set = masks(cells)

    def each_row(r, carry):
        centre = rows_ref[r + 1].astype(jnp.float32)
        diff_ref[0] = centre - rows_ref[r + 2].astype(jnp.float32)
        diff_ref[1] = centre - rows_ref[r].astype(jnp.float32)
        for f, other in enumerate(beside(centre, mask_set)):
            diff_ref[2 + f] = centre - other
        total_ref[...] = jnp.zeros_like(total_ref)

        def each_group(g, carry):
            for k in range(GROUP):
                term = None
                for f in range(6):
                    part = weight_ref[r, f, g, k : k + 1, :] * diff_ref[f]
                    term = part if term is None else term + part
                term_ref[k * size : (k + 1) * size, :] = term.astype(jnp.bfloat16)
            total_ref[...] += jnp.dot(
                dense_ref[g], term_ref[...], preferred_element_type=jnp.float32
            )
            return carry

        lax.fori_loop(0, groups, each_group, 0)
        for p in range(count):
            outs[p][r] = total_ref[p * here : (p + 1) * here, :].astype(jnp.bfloat16)
        return carry

    lax.fori_loop(0, half, each_row, 0)


def post_kernel(count, slab, half, rows, rho_zero, rho_one, z_ref, *refs):
    early = refs[:count]
    late = refs[count : 2 * count]
    source, iterate, low, high, faces, inverse = refs[2 * count : 2 * count + 6]
    updated, residual, image = refs[2 * count + 6 :]
    z = z_ref[0]
    modes, _, cells = source.shape
    for p in range(count):
        place = jnp.bitwise_xor(z, p)
        for rho in range(slab):
            part = early[p][rho] if rho < half else late[p][rho - half]
            image[row_of(place, rho, slab, count, rows)] = part.astype(jnp.float32)
    residual[...] = source[...] - jnp.swapaxes(image[...], 0, 1)
    place = lax.broadcasted_iota(jnp.int32, (rows, cells), 0)
    inv = inverse[...]
    for m in range(modes):
        res = residual[m]
        first = res * (inv * (1.0 / cheb_center))
        up = jnp.where(place == rows - 1, high[m : m + 1, :], pltpu.roll(first, rows - 1, 0))
        down = jnp.where(place == 0, low[m : m + 1, :], pltpu.roll(first, 1, 0))
        near = faces[0] * up + faces[1] * down
        near = near + faces[2] * pltpu.roll(first, cells - NZ, 1)
        near = near + faces[3] * pltpu.roll(first, NZ, 1)
        near = near + faces[4] * pltpu.roll(first, cells - 1, 1)
        near = near + faces[5] * pltpu.roll(first, 1, 1)
        smoothed = (1.0 - 1.0 / cheb_center) * res + near
        step = (1.0 + rho_one * rho_zero) * first + (2.0 * rho_one / cheb_radius) * smoothed * inv
        updated[m] = iterate[m] + step


def mean_faces(padded, cells):
    centre = padded[1:-1]
    lane = jnp.arange(cells)

    def shift(amount, keep):
        return jnp.where(keep, jnp.roll(centre, -amount, -1), 0.0)

    keeps = (lane < cells - NZ, lane >= NZ, lane % NZ < NZ - 1, lane % NZ > 0)
    others = [padded[2:], padded[:-2]]
    others += [shift(a, k) for a, k in zip((NZ, -NZ, 1, -1), keeps)]
    weights = [0.5 * (centre + other) for other in others]
    diag = weights[0] + weights[1] + weights[2] + weights[3] + weights[4] + weights[5]
    inner = weights[:2] + [jnp.where(k, w, 0.0) for k, w in zip(keeps, weights[2:])]
    return jnp.stack(inner), 1.0 / diag


def body(iterate, source, mean_coef, kl_fields, tri_index, tri_value):
    count = lax.axis_size("mode")
    doms = lax.axis_size("dom")
    z = lax.axis_index("mode")
    z_arg = z.astype(jnp.int32).reshape(1)
    here, rows, cells = iterate.shape
    size = here * count
    slab = rows // count
    half = slab // 2
    fields = kl_fields.shape[0] + 1
    groups = -(-fields // GROUP)
    bf16 = jnp.bfloat16
    params = pltpu.CompilerParams(vmem_limit_bytes=VMEM_LIMIT)

    shapes = []
    for _ in range(count):
        shapes += [
            jax.ShapeDtypeStruct((1, here, cells), bf16),
            jax.ShapeDtypeStruct((half + 1, here, cells), bf16),
            jax.ShapeDtypeStruct((slab - half, here, cells), bf16),
        ]
    packed = pl.pallas_call(
        functools.partial(pack_kernel, count, slab, half, rows),
        out_shape=shapes,
        in_specs=[in_smem()] + in_vmem(1),
        out_specs=in_vmem(3 * count),
        scratch_shapes=[pltpu.VMEM((rows, here, cells), bf16)],
        compiler_params=params,
        name="pack",
    )(z_arg, iterate)

    def swap(array, p):
        return lax.ppermute(array, "mode", [(i, i ^ p) for i in range(count)])

    def swap_rim(array, p):
        pairs = []
        for d in range(doms):
            for i in range(count):
                to = i ^ p
                target = d + 1 if to == 0 else d - 1 if to == count - 1 else d
                if p == 0 and target == d:
                    continue
                if 0 <= target < doms:
                    pairs.append((d * count + i, target * count + to))
        return lax.ppermute(array, ("dom", "mode"), pairs)

    rims = [swap_rim(packed[3 * p], p) for p in range(count)]
    edge = jnp.logical_or(z == 0, z == count - 1)
    rims[0] = jnp.where(edge, rims[0], packed[0])
    early = [packed[1]] + [swap(packed[3 * p + 1], p) for p in range(1, count)]
    late = [packed[2]] + [swap(packed[3 * p + 2], p) for p in range(1, count)]

    coef = jnp.concatenate([mean_coef[None], kl_fields], 0)
    upward = [(i, i + 1) for i in range(doms - 1)]
    downward = [(b, a) for a, b in upward]
    low_coef = lax.ppermute(coef[:, -1:], "dom", upward)
    high_coef = lax.ppermute(coef[:, :1], "dom", downward)
    padded = jnp.concatenate([low_coef, coef, high_coef], 1)
    slab_coef = lax.dynamic_slice_in_dim(padded, z * slab, slab + 2, 1)
    slab_coef = jnp.where(z < count // 2, slab_coef, jnp.flip(slab_coef, 1))
    slab_coef = jnp.pad(slab_coef, ((0, groups * GROUP - fields), (0, 0), (0, 0)))
    slab_coef = slab_coef.reshape(groups, GROUP, slab + 2, cells)
    slab_coef = jnp.pad(slab_coef, ((0, 0), (0, 8 - GROUP), (0, 0), (0, 0)))
    slab_coef = jnp.transpose(slab_coef, (2, 0, 1, 3))
    entries = tri_index.T
    dense, weights = pl.pallas_call(
        functools.partial(setup_kernel, slab, groups, here),
        out_shape=[
            jax.ShapeDtypeStruct((groups, size, GROUP * size), bf16),
            jax.ShapeDtypeStruct((slab, 6, groups, 8, cells), jnp.float32),
        ],
        in_specs=[in_smem()] + in_vmem(5),
        out_specs=in_vmem(2),
        compiler_params=params,
        name="setup",
    )(z_arg, entries[0:1], entries[1:2], entries[2:3], tri_value[None], slab_coef)
    faces, inverse = mean_faces(padded[0], cells)

    def mix(arrays, window, weight_rows):
        flat = [a for group in arrays for a in group]
        return pl.pallas_call(
            functools.partial(mix_kernel, count, half, groups, window),
            out_shape=[jax.ShapeDtypeStruct((half, here, cells), bf16)] * count,
            in_specs=in_vmem(len(flat) + 2),
            out_specs=in_vmem(count),
            scratch_shapes=[
                pltpu.VMEM((half + 2, size, cells), bf16),
                pltpu.VMEM((6, size, cells), jnp.float32),
                pltpu.VMEM((GROUP * size, cells), bf16),
                pltpu.VMEM((size, cells), jnp.float32),
            ],
            compiler_params=params,
            name="mix",
        )(*flat, dense, weight_rows)

    window = ((0, 0),) + tuple((1, k) for k in range(half + 1))
    mixed_early = mix([rims, early], window, weights[:half])
    back_early = [mixed_early[0]] + [swap(mixed_early[p], p) for p in range(1, count)]
    window = ((0, half - 1), (0, half)) + tuple((1, k) for k in range(slab - half))
    mixed_late = mix([early, late], window, weights[half:])
    back_late = [mixed_late[0]] + [swap(mixed_late[p], p) for p in range(1, count)]

    outer = jnp.stack([b[0] for b in back_early])
    bottom = lax.dynamic_index_in_dim(outer, z, 0, keepdims=False).astype(jnp.float32)
    top = lax.dynamic_index_in_dim(outer, z ^ (count - 1), 0, keepdims=False).astype(jnp.float32)
    first_bottom = (source[:, 0] - bottom) * (inverse[0] / cheb_center)
    first_top = (source[:, -1] - top) * (inverse[-1] / cheb_center)
    low = lax.ppermute(first_top, "dom", upward)
    high = lax.ppermute(first_bottom, "dom", downward)

    sigma = cheb_center / cheb_radius
    rho_zero = 1.0 / sigma
    rho_one = 1.0 / (2.0 * sigma - rho_zero)
    block = min(16, here)
    image_spec = pl.BlockSpec((half, block, cells), lambda i: (0, i, 0))
    flat_spec = pl.BlockSpec((block, rows, cells), lambda i: (i, 0, 0))
    row_spec = pl.BlockSpec((block, cells), lambda i: (i, 0))
    updated, residual = pl.pallas_call(
        functools.partial(post_kernel, count, slab, half, rows, rho_zero, rho_one),
        grid=(here // block,),
        out_shape=[jax.ShapeDtypeStruct((here, rows, cells), jnp.float32)] * 2,
        in_specs=[in_smem()]
        + [image_spec] * (2 * count)
        + [flat_spec, flat_spec, row_spec, row_spec]
        + [
            pl.BlockSpec((6, rows, cells), lambda i: (0, 0, 0)),
            pl.BlockSpec((rows, cells), lambda i: (0, 0)),
        ],
        out_specs=[flat_spec, flat_spec],
        scratch_shapes=[pltpu.VMEM((rows, block, cells), jnp.float32)],
        compiler_params=params,
        name="post",
    )(
        z_arg,
        *back_early,
        *back_late,
        source,
        iterate,
        low,
        high,
        faces,
        inverse,
    )
    return updated, residual


def solution(mesh):
    return jax.shard_map(
        body,
        mesh=mesh,
        in_specs=(
            P("mode", "dom", None),
            P("mode", "dom", None),
            P("dom", None),
            P(None, "dom", None),
            P(),
            P(),
        ),
        out_specs=(P("mode", "dom", None), P("mode", "dom", None)),
        check_vma=False,
    )
```

profile of v0, /device:TPU:3, one launch (start us, length us, event | category | flops | bytes accessed | tf_op | source)
XLA Modules:
  0.0 102.0 jit_solution(6115819096145070577)
XLA Ops:
  0.6 1.6 %pad_maximum_fusion.5 = (f32[21,1,256]{2,1,0:T(1,128)}, f32[21,1,256]{2,1,0:T(1,128)}) fusion(f32[20,32,256]{2,1,0:T(8,128)} %param.9, f32[1,32,256]{2,1,0:T(8,128)} %bitcast.56), kind=kLoop, calls=%fused_computation.44 | loop fusion | flops 10752 | bytes 731136 | tf_op jit(solution)/shard_map/concatenate | solution.py:251
  2.3 3.7 %collective-permute-start.7 = (f32[21,1,256]{2,1,0:T(1,128)}, f32[21,1,256]{2,1,0:T(1,128)}, u32[]{:S(2)}, u32[]{:S(2)}) collective-permute-start(f32[21,1,256]{2,1,0:T(1,128)} %get-tuple-element.55), channel_id=1, source_target_pairs={{0,4},{4,8},{8,12},{12,16},{16,20},{20,24},{24,28},{1,5},{5,9},{9,... | collective-permute-start | bytes 64520 | tf_op jit(solution)/shard_map/ppermute | solution.py:254
  6.0 1.9 %collective-permute-start.8 = (f32[21,1,256]{2,1,0:T(1,128)}, f32[21,1,256]{2,1,0:T(1,128)}, u32[]{:S(2)}, u32[]{:S(2)}) collective-permute-start(f32[21,1,256]{2,1,0:T(1,128)} %get-tuple-element.54), channel_id=1, source_target_pairs={{4,0},{8,4},{12,8},{16,12},{20,16},{24,20},{28,24},{5,1},{9,5},{13... | collective-permute-start | bytes 64520 | tf_op jit(solution)/shard_map/ppermute | solution.py:255
  7.9 1.6 %copy-done = f32[64,32,256]{2,1,0:T(8,128)S(1)} copy-done((f32[64,32,256]{2,1,0:T(8,128)S(1)}, f32[64,32,256]{2,1,0:T(8,128)}, u32[]{:S(2)}) %copy-start) | copy-done | bytes 2097176
  11.2 4.5 %collective-permute-start = (bf16[1,64,256]{2,1,0:T(8,128)(2,1)S(1)}, bf16[1,64,256]{2,1,0:T(8,128)(2,1)}, u32[]{:S(2)}, u32[]{:S(2)}) collective-permute-start(bf16[1,64,256]{2,1,0:T(8,128)(2,1)S(1)} %get-tuple-element.24), channel_id=1, source_target_pairs={{0,4},{4,8},{7,3},{8,12},{11,7},{12,16},{15,11},{16,20},{19,15},{2... | collective-permute-start | bytes 98312 | tf_op jit(solution)/shard_map/ppermute | solution.py:243
  15.9 1.6 %collective-permute-start.5 = (bf16[5,64,256]{2,1,0:T(8,128)(2,1)S(1)}, bf16[5,64,256]{2,1,0:T(8,128)(2,1)S(1)}, u32[]{:S(2)}, u32[]{:S(2)}) collective-permute-start(bf16[5,64,256]{2,1,0:T(8,128)(2,1)S(1)} %get-tuple-element.30), channel_id=1, source_target_pairs={{0,2},{1,3},{2,0},{3,1},{4,6},{5,7},{6,4},{7,5},{8,10},{9,11},{10,... | collective-permute-start | bytes 491528 | tf_op jit(solution)/shard_map/ppermute | solution.py:231
  22.9 2.0 %collective-permute-start.1 = (bf16[1,64,256]{2,1,0:T(8,128)(2,1)}, bf16[1,64,256]{2,1,0:T(8,128)(2,1)S(1)}, u32[]{:S(2)}, u32[]{:S(2)}) collective-permute-start(bf16[1,64,256]{2,1,0:T(8,128)(2,1)} %get-tuple-element.25), channel_id=1, source_target_pairs={{0,1},{1,4},{3,2},{4,5},{5,8},{6,3},{7,6},{8,9},{9,12},{10,7},{11,... | collective-permute-start | bytes 98312 | tf_op jit(solution)/shard_map/ppermute | solution.py:243
  24.9 2.7 %collective-permute-start.2 = (bf16[1,64,256]{2,1,0:T(8,128)(2,1)}, bf16[1,64,256]{2,1,0:T(8,128)(2,1)S(1)}, u32[]{:S(2)}, u32[]{:S(2)}) collective-permute-start(bf16[1,64,256]{2,1,0:T(8,128)(2,1)} %copy-done.9), channel_id=1, source_target_pairs={{0,2},{2,4},{3,1},{4,6},{5,3},{6,8},{7,5},{8,10},{9,7},{10,12},{11... | collective-permute-start | bytes 98312 | tf_op jit(solution)/shard_map/ppermute | solution.py:243
  27.6 2.0 %fusion.1 = f32[21,10,256]{2,1,0:T(8,128)} fusion(s32[]{:T(128)S(6)} %select_n.93, f32[21,1,256]{2,1,0:T(1,128)} %collective-permute-done.7, f32[1,32,256]{2,1,0:T(8,128)} %bitcast.57, f32[20,32,256]{2,1,0:T(8,128)} %param.9, f32[21,1,256]{2,1,0:T(1,128)} %collective-permute-done.8), kind=kLoop, calls=%fused_computation.5 | loop fusion | flops 161280 | bytes 946180 | tf_op jit(solution)/shard_map/concatenate | solution.py:256
  29.5 1.7 %rev.4 = f32[21,10,256]{2,1,0:T(8,128)} reverse(f32[21,10,256]{2,1,0:T(8,128)} %fusion.1), dimensions={1} | reverse | bytes 430080 | tf_op jit(solution)/shard_map/jit(_flip)/rev | solution.py:258
  31.3 1.2 %broadcast_select_fusion = f32[21,10,256]{2,1,0:T(8,128)S(1)} fusion(f32[21,10,256]{2,1,0:T(8,128)} %rev.4, pred[]{:T(512)S(6)} %lt.41, s32[]{:T(128)S(6)} %select_n.93, f32[21,1,256]{2,1,0:T(1,128)} %collective-permute-done.8, f32[20,32,256]{2,1,0:T(8,128)} %param.9, f32[1,32,256]{2,1,0:T(8,128)} %bitcast.58, f32[21,1,256]{2,1,0:T(1,128)} %collective-permute-done.7), kind=kLoop, calls=%fused_computation.8 | loop fusion | flops 215040 | bytes 1161221 | tf_op jit(solution)/shard_map/jit(_where)/select_n | solution.py:258
  32.7 2.9 %setup.1 = (bf16[3,256,1792]{2,1,0:T(8,128)(2,1)S(1)}, f32[8,6,3,8,256]{4,3,2,1,0:T(8,128)S(1)}) custom-call(s32[1]{0:T(128)} %bitcast.z_ref, s32[1,5376]{1,0:T(1,128)S(1)} %get-tuple-element.60.i_ref, s32[1,5376]{1,0:T(1,128)S(1)} %get-tuple-element.59.j_ref, s32[1,5376]{1,0:T(1,128)S(1)} %get-tuple-element.58.l_ref, f32[1,5376]{1,0:T(1,128)S(1)} %broadcast_in_dim.44.v_ref, ...), custom_call_target="tpu_custom_call" | custom-call | tf_op jit(solution)/shard_map/setup/pallas_call | solution.py:264
  37.6 5.0 %collective-permute-start.6 = (bf16[5,64,256]{2,1,0:T(8,128)(2,1)S(1)}, bf16[5,64,256]{2,1,0:T(8,128)(2,1)S(1)}, u32[]{:S(2)}, u32[]{:S(2)}) collective-permute-start(bf16[5,64,256]{2,1,0:T(8,128)(2,1)S(1)} %get-tuple-element.31), channel_id=1, source_target_pairs={{0,3},{1,2},{2,1},{3,0},{4,7},{5,6},{6,5},{7,4},{8,11},{9,10},{10,... | collective-permute-start | bytes 491528 | tf_op jit(solution)/shard_map/ppermute | solution.py:231
  42.7 1.9 %collective-permute-start.3 = (bf16[1,64,256]{2,1,0:T(8,128)(2,1)S(1)}, bf16[1,64,256]{2,1,0:T(8,128)(2,1)S(1)}, u32[]{:S(2)}, u32[]{:S(2)}) collective-permute-start(bf16[1,64,256]{2,1,0:T(8,128)(2,1)S(1)} %copy-done.8), channel_id=1, source_target_pairs={{1,2},{2,1},{3,4},{4,3},{5,6},{6,5},{7,8},{8,7},{9,10},{10,9},{11,... | collective-permute-start | bytes 98312 | tf_op jit(solution)/shard_map/ppermute | solution.py:243
  45.4 4.6 %collective-permute-done.3.refs_3_ = bf16[1,64,256]{2,1,0:T(8,128)(2,1)S(1)} collective-permute-done((bf16[1,64,256]{2,1,0:T(8,128)(2,1)S(1)}, bf16[1,64,256]{2,1,0:T(8,128)(2,1)S(1)}, u32[]{:S(2)}, u32[]{:S(2)}) %collective-permute-start.3) | collective-permute-done | bytes 32800 | tf_op jit(solution)/shard_map/ppermute | solution.py:243
  50.0 1.3 %collective-permute-start.13 = (bf16[4,64,256]{2,1,0:T(8,128)(2,1)S(1)}, bf16[4,64,256]{2,1,0:T(8,128)(2,1)S(1)}, u32[]{:S(2)}, u32[]{:S(2)}) collective-permute-start(bf16[4,64,256]{2,1,0:T(8,128)(2,1)S(1)} %copy-done.4), channel_id=1, source_target_pairs={{0,2},{1,3},{2,0},{3,1},{4,6},{5,7},{6,4},{7,5},{8,10},{9,11},{10,... | collective-permute-start | bytes 393224 | tf_op jit(solution)/shard_map/ppermute | solution.py:231
  52.0 12.4 %mix.2 = (bf16[4,64,256]{2,1,0:T(8,128)(2,1)S(1)}, bf16[4,64,256]{2,1,0:T(8,128)(2,1)S(1)}, bf16[4,64,256]{2,1,0:T(8,128)(2,1)S(1)}, bf16[4,64,256]{2,1,0:T(8,128)(2,1)S(1)}) custom-call(bf16[1,64,256]{2,1,0:T(8,128)(2,1)S(1)} %broadcast_select_fusion.1.refs_0_, bf16[1,64,256]{2,1,0:T(8,128)(2,1)S(1)} %collective-permute-done.1.refs_1_, ...), custom_call_target="tpu_custom_call" | custom-call | tf_op jit(solution)/shard_map/mix/pallas_call | solution.py:279
  65.2 2.2 %collective-permute-start.10 = (bf16[4,64,256]{2,1,0:T(8,128)(2,1)S(1)}, bf16[4,64,256]{2,1,0:T(8,128)(2,1)S(1)}, u32[]{:S(2)}, u32[]{:S(2)}) collective-permute-start(bf16[4,64,256]{2,1,0:T(8,128)(2,1)S(1)} %get-tuple-element.36), channel_id=1, source_target_pairs={{0,2},{1,3},{2,0},{3,1},{4,6},{5,7},{6,4},{7,5},{8,10},{9,11},{10,... | collective-permute-start | bytes 393224 | tf_op jit(solution)/shard_map/ppermute | solution.py:231
  68.1 12.4 %mix.3 = (bf16[4,64,256]{2,1,0:T(8,128)(2,1)S(1)}, bf16[4,64,256]{2,1,0:T(8,128)(2,1)S(1)}, bf16[4,64,256]{2,1,0:T(8,128)(2,1)S(1)}, bf16[4,64,256]{2,1,0:T(8,128)(2,1)S(1)}) custom-call(bf16[5,64,256]{2,1,0:T(8,128)(2,1)S(1)} %get-tuple-element.28.refs_4_.refs_0_, bf16[5,64,256]{2,1,0:T(8,128)(2,1)S(1)} %collective-permute-done.4.refs_5_.refs_1_, ...), custom_call_target="tpu_custom_call" | custom-call | tf_op jit(solution)/shard_map/mix/pallas_call | solution.py:279
  80.7 2.9 %collective-permute-start.16 = (bf16[4,64,256]{2,1,0:T(8,128)(2,1)S(1)}, bf16[4,64,256]{2,1,0:T(8,128)(2,1)S(1)}, u32[]{:S(2)}, u32[]{:S(2)}) collective-permute-start(bf16[4,64,256]{2,1,0:T(8,128)(2,1)S(1)} %get-tuple-element.44), channel_id=1, source_target_pairs={{0,2},{1,3},{2,0},{3,1},{4,6},{5,7},{6,4},{7,5},{8,10},{9,11},{10,... | collective-permute-start | bytes 393224 | tf_op jit(solution)/shard_map/ppermute | solution.py:231
  84.3 6.7 %collective-permute-start.18 = (f32[64,256]{1,0:T(8,128)S(1)}, f32[64,256]{1,0:T(8,128)S(1)}, u32[]{:S(2)}, u32[]{:S(2)}) collective-permute-start(f32[64,256]{1,0:T(8,128)S(1)} %get-tuple-element.57), channel_id=1, source_target_pairs={{0,4},{4,8},{8,12},{12,16},{16,20},{20,24},{24,28},{1,5},{5,9},{9,... | collective-permute-start | bytes 196616 | tf_op jit(solution)/shard_map/ppermute | solution.py:306
  91.0 1.9 %collective-permute-start.19 = (f32[64,256]{1,0:T(8,128)S(1)}, f32[64,256]{1,0:T(8,128)S(1)}, u32[]{:S(2)}, u32[]{:S(2)}) collective-permute-start(f32[64,256]{1,0:T(8,128)S(1)} %get-tuple-element.56), channel_id=1, source_target_pairs={{4,0},{8,4},{12,8},{16,12},{20,16},{24,20},{28,24},{5,1},{9,5},{13... | collective-permute-start | bytes 196616 | tf_op jit(solution)/shard_map/ppermute | solution.py:307
  93.0 4.4 %collective-permute-done.19.refs_11_ = f32[64,256]{1,0:T(8,128)S(1)} collective-permute-done((f32[64,256]{1,0:T(8,128)S(1)}, f32[64,256]{1,0:T(8,128)S(1)}, u32[]{:S(2)}, u32[]{:S(2)}) %collective-permute-start.19) | collective-permute-done | bytes 65568 | tf_op jit(solution)/shard_map/ppermute | solution.py:307
  97.5 4.5 %post.1 = (f32[64,32,256]{2,1,0:T(8,128)}, f32[64,32,256]{2,1,0:T(8,128)}) custom-call(s32[1]{0:T(128)} %bitcast.z_ref, bf16[4,64,256]{2,1,0:T(8,128)(2,1)S(1)} %get-tuple-element.34.refs_0_, bf16[4,64,256]{2,1,0:T(8,128)(2,1)S(1)} %collective-permute-done.9.refs_1_, bf16[4,64,256]{2,1,0:T(8,128)(2,1)S(1)} %collective-permute-done.10.refs_2_, ...), custom_call_target="tpu_custom_call" | custom-call | tf_op jit(solution)/shard_map/post/pallas_call | solution.py:316
  (106 shorter events, 13.0 us)
Async XLA Ops:
  0.6 16.8 %copy-start.11 = (f32[32,256]{1,0:T(8,128)S(1)}, f32[32,256]{1,0:T(8,128)}, u32[]{:S(2)}) copy-start(f32[32,256]{1,0:T(8,128)} %param.8) | copy-start | bytes 98308
  2.3 20.6 %collective-permute-start.7 = (f32[21,1,256]{2,1,0:T(1,128)}, f32[21,1,256]{2,1,0:T(1,128)}, u32[]{:S(2)}, u32[]{:S(2)}) collective-permute-start(f32[21,1,256]{2,1,0:T(1,128)} %get-tuple-element.55), channel_id=1, source_target_pairs={{0,4},{4,8},{8,12},{12,16},{16,20},{20,24},{24,28},{1,5},{5,9},{9,... | collective-permute-start | bytes 64520 | tf_op jit(solution)/shard_map/ppermute | solution.py:254
  6.0 18.9 %collective-permute-start.8 = (f32[21,1,256]{2,1,0:T(1,128)}, f32[21,1,256]{2,1,0:T(1,128)}, u32[]{:S(2)}, u32[]{:S(2)}) collective-permute-start(f32[21,1,256]{2,1,0:T(1,128)} %get-tuple-element.54), channel_id=1, source_target_pairs={{4,0},{8,4},{12,8},{16,12},{20,16},{24,20},{28,24},{5,1},{9,5},{13... | collective-permute-start | bytes 64520 | tf_op jit(solution)/shard_map/ppermute | solution.py:255
  11.2 26.4 %collective-permute-start = (bf16[1,64,256]{2,1,0:T(8,128)(2,1)S(1)}, bf16[1,64,256]{2,1,0:T(8,128)(2,1)}, u32[]{:S(2)}, u32[]{:S(2)}) collective-permute-start(bf16[1,64,256]{2,1,0:T(8,128)(2,1)S(1)} %get-tuple-element.24), channel_id=1, source_target_pairs={{0,4},{4,8},{7,3},{8,12},{11,7},{12,16},{15,11},{16,20},{19,15},{2... | collective-permute-start | bytes 98312 | tf_op jit(solution)/shard_map/ppermute | solution.py:243
  15.8 35.6 %collective-permute-start.4 = (bf16[5,64,256]{2,1,0:T(8,128)(2,1)S(1)}, bf16[5,64,256]{2,1,0:T(8,128)(2,1)S(1)}, u32[]{:S(2)}, u32[]{:S(2)}) collective-permute-start(bf16[5,64,256]{2,1,0:T(8,128)(2,1)S(1)} %get-tuple-element.29), channel_id=1, source_target_pairs={{0,1},{1,0},{2,3},{3,2},{4,5},{5,4},{6,7},{7,6},{8,9},{9,8},{10,11... | collective-permute-start | bytes 491528 | tf_op jit(solution)/shard_map/ppermute | solution.py:231
  15.9 36.2 %collective-permute-start.5 = (bf16[5,64,256]{2,1,0:T(8,128)(2,1)S(1)}, bf16[5,64,256]{2,1,0:T(8,128)(2,1)S(1)}, u32[]{:S(2)}, u32[]{:S(2)}) collective-permute-start(bf16[5,64,256]{2,1,0:T(8,128)(2,1)S(1)} %get-tuple-element.30), channel_id=1, source_target_pairs={{0,2},{1,3},{2,0},{3,1},{4,6},{5,7},{6,4},{7,5},{8,10},{9,11},{10,... | collective-permute-start | bytes 491528 | tf_op jit(solution)/shard_map/ppermute | solution.py:231
  22.9 19.7 %collective-permute-start.1 = (bf16[1,64,256]{2,1,0:T(8,128)(2,1)}, bf16[1,64,256]{2,1,0:T(8,128)(2,1)S(1)}, u32[]{:S(2)}, u32[]{:S(2)}) collective-permute-start(bf16[1,64,256]{2,1,0:T(8,128)(2,1)} %get-tuple-element.25), channel_id=1, source_target_pairs={{0,1},{1,4},{3,2},{4,5},{5,8},{6,3},{7,6},{8,9},{9,12},{10,7},{11,... | collective-permute-start | bytes 98312 | tf_op jit(solution)/shard_map/ppermute | solution.py:243
  24.9 19.7 %collective-permute-start.2 = (bf16[1,64,256]{2,1,0:T(8,128)(2,1)}, bf16[1,64,256]{2,1,0:T(8,128)(2,1)S(1)}, u32[]{:S(2)}, u32[]{:S(2)}) collective-permute-start(bf16[1,64,256]{2,1,0:T(8,128)(2,1)} %copy-done.9), channel_id=1, source_target_pairs={{0,2},{2,4},{3,1},{4,6},{5,3},{6,8},{7,5},{8,10},{9,7},{10,12},{11... | collective-permute-start | bytes 98312 | tf_op jit(solution)/shard_map/ppermute | solution.py:243
  37.6 14.4 %collective-permute-start.6 = (bf16[5,64,256]{2,1,0:T(8,128)(2,1)S(1)}, bf16[5,64,256]{2,1,0:T(8,128)(2,1)S(1)}, u32[]{:S(2)}, u32[]{:S(2)}) collective-permute-start(bf16[5,64,256]{2,1,0:T(8,128)(2,1)S(1)} %get-tuple-element.31), channel_id=1, source_target_pairs={{0,3},{1,2},{2,1},{3,0},{4,7},{5,6},{6,5},{7,4},{8,11},{9,10},{10,... | collective-permute-start | bytes 491528 | tf_op jit(solution)/shard_map/ppermute | solution.py:231
  42.7 7.4 %collective-permute-start.3 = (bf16[1,64,256]{2,1,0:T(8,128)(2,1)S(1)}, bf16[1,64,256]{2,1,0:T(8,128)(2,1)S(1)}, u32[]{:S(2)}, u32[]{:S(2)}) collective-permute-start(bf16[1,64,256]{2,1,0:T(8,128)(2,1)S(1)} %copy-done.8), channel_id=1, source_target_pairs={{1,2},{2,1},{3,4},{4,3},{5,6},{6,5},{7,8},{8,7},{9,10},{10,9},{11,... | collective-permute-start | bytes 98312 | tf_op jit(solution)/shard_map/ppermute | solution.py:243
  44.6 22.8 %collective-permute-start.12 = (bf16[4,64,256]{2,1,0:T(8,128)(2,1)S(1)}, bf16[4,64,256]{2,1,0:T(8,128)(2,1)S(1)}, u32[]{:S(2)}, u32[]{:S(2)}) collective-permute-start(bf16[4,64,256]{2,1,0:T(8,128)(2,1)S(1)} %copy-done.6), channel_id=1, source_target_pairs={{0,1},{1,0},{2,3},{3,2},{4,5},{5,4},{6,7},{7,6},{8,9},{9,8},{10,11... | collective-permute-start | bytes 393224 | tf_op jit(solution)/shard_map/ppermute | solution.py:231
  50.0 18.1 %collective-permute-start.13 = (bf16[4,64,256]{2,1,0:T(8,128)(2,1)S(1)}, bf16[4,64,256]{2,1,0:T(8,128)(2,1)S(1)}, u32[]{:S(2)}, u32[]{:S(2)}) collective-permute-start(bf16[4,64,256]{2,1,0:T(8,128)(2,1)S(1)} %copy-done.4), channel_id=1, source_target_pairs={{0,2},{1,3},{2,0},{3,1},{4,6},{5,7},{6,4},{7,5},{8,10},{9,11},{10,... | collective-permute-start | bytes 393224 | tf_op jit(solution)/shard_map/ppermute | solution.py:231
  51.4 16.7 %collective-permute-start.14 = (bf16[4,64,256]{2,1,0:T(8,128)(2,1)S(1)}, bf16[4,64,256]{2,1,0:T(8,128)(2,1)S(1)}, u32[]{:S(2)}, u32[]{:S(2)}) collective-permute-start(bf16[4,64,256]{2,1,0:T(8,128)(2,1)S(1)} %get-tuple-element.41), channel_id=1, source_target_pairs={{0,3},{1,2},{2,1},{3,0},{4,7},{5,6},{6,5},{7,4},{8,11},{9,10},{10,... | collective-permute-start | bytes 393224 | tf_op jit(solution)/shard_map/ppermute | solution.py:231
  64.5 19.1 %collective-permute-start.9 = (bf16[4,64,256]{2,1,0:T(8,128)(2,1)S(1)}, bf16[4,64,256]{2,1,0:T(8,128)(2,1)S(1)}, u32[]{:S(2)}, u32[]{:S(2)}) collective-permute-start(bf16[4,64,256]{2,1,0:T(8,128)(2,1)S(1)} %get-tuple-element.35), channel_id=1, source_target_pairs={{0,1},{1,0},{2,3},{3,2},{4,5},{5,4},{6,7},{7,6},{8,9},{9,8},{10,11... | collective-permute-start | bytes 393224 | tf_op jit(solution)/shard_map/ppermute | solution.py:231
  65.2 19.0 %collective-permute-start.10 = (bf16[4,64,256]{2,1,0:T(8,128)(2,1)S(1)}, bf16[4,64,256]{2,1,0:T(8,128)(2,1)S(1)}, u32[]{:S(2)}, u32[]{:S(2)}) collective-permute-start(bf16[4,64,256]{2,1,0:T(8,128)(2,1)S(1)} %get-tuple-element.36), channel_id=1, source_target_pairs={{0,2},{1,3},{2,0},{3,1},{4,6},{5,7},{6,4},{7,5},{8,10},{9,11},{10,... | collective-permute-start | bytes 393224 | tf_op jit(solution)/shard_map/ppermute | solution.py:231
  67.4 16.8 %collective-permute-start.11 = (bf16[4,64,256]{2,1,0:T(8,128)(2,1)S(1)}, bf16[4,64,256]{2,1,0:T(8,128)(2,1)S(1)}, u32[]{:S(2)}, u32[]{:S(2)}) collective-permute-start(bf16[4,64,256]{2,1,0:T(8,128)(2,1)S(1)} %get-tuple-element.37), channel_id=1, source_target_pairs={{0,3},{1,2},{2,1},{3,0},{4,7},{5,6},{6,5},{7,4},{8,11},{9,10},{10,... | collective-permute-start | bytes 393224 | tf_op jit(solution)/shard_map/ppermute | solution.py:231
  68.1 16.2 %copy-start.17 = (f32[64,1,256]{2,1,0:T(1,128)S(1)}, f32[64,1,256]{2,1,0:T(1,128)}, u32[]{:S(2)}) copy-start(f32[64,1,256]{2,1,0:T(1,128)} %get-tuple-element.50) | copy-start | bytes 196612
  68.1 16.2 %copy-start.18 = (f32[64,1,256]{2,1,0:T(1,128)S(1)}, f32[64,1,256]{2,1,0:T(1,128)}, u32[]{:S(2)}) copy-start(f32[64,1,256]{2,1,0:T(1,128)} %get-tuple-element.51) | copy-start | bytes 196612
  68.1 29.4 %copy-start.1 = (f32[64,32,256]{2,1,0:T(8,128)S(1)}, f32[64,32,256]{2,1,0:T(8,128)}, u32[]{:S(2)}) copy-start(f32[64,32,256]{2,1,0:T(8,128)} %refs_9_.1) | copy-start | bytes 6291460
  80.6 12.4 %collective-permute-start.15 = (bf16[4,64,256]{2,1,0:T(8,128)(2,1)S(1)}, bf16[4,64,256]{2,1,0:T(8,128)(2,1)S(1)}, u32[]{:S(2)}, u32[]{:S(2)}) collective-permute-start(bf16[4,64,256]{2,1,0:T(8,128)(2,1)S(1)} %get-tuple-element.43), channel_id=1, source_target_pairs={{0,1},{1,0},{2,3},{3,2},{4,5},{5,4},{6,7},{7,6},{8,9},{9,8},{10,11... | collective-permute-start | bytes 393224 | tf_op jit(solution)/shard_map/ppermute | solution.py:231
  80.7 12.4 %collective-permute-start.16 = (bf16[4,64,256]{2,1,0:T(8,128)(2,1)S(1)}, bf16[4,64,256]{2,1,0:T(8,128)(2,1)S(1)}, u32[]{:S(2)}, u32[]{:S(2)}) collective-permute-start(bf16[4,64,256]{2,1,0:T(8,128)(2,1)S(1)} %get-tuple-element.44), channel_id=1, source_target_pairs={{0,2},{1,3},{2,0},{3,1},{4,6},{5,7},{6,4},{7,5},{8,10},{9,11},{10,... | collective-permute-start | bytes 393224 | tf_op jit(solution)/shard_map/ppermute | solution.py:231
  83.6 9.5 %collective-permute-start.17 = (bf16[4,64,256]{2,1,0:T(8,128)(2,1)S(1)}, bf16[4,64,256]{2,1,0:T(8,128)(2,1)S(1)}, u32[]{:S(2)}, u32[]{:S(2)}) collective-permute-start(bf16[4,64,256]{2,1,0:T(8,128)(2,1)S(1)} %get-tuple-element.45), channel_id=1, source_target_pairs={{0,3},{1,2},{2,1},{3,0},{4,7},{5,6},{6,5},{7,4},{8,11},{9,10},{10,... | collective-permute-start | bytes 393224 | tf_op jit(solution)/shard_map/ppermute | solution.py:231
  84.3 8.7 %collective-permute-start.18 = (f32[64,256]{1,0:T(8,128)S(1)}, f32[64,256]{1,0:T(8,128)S(1)}, u32[]{:S(2)}, u32[]{:S(2)}) collective-permute-start(f32[64,256]{1,0:T(8,128)S(1)} %get-tuple-element.57), channel_id=1, source_target_pairs={{0,4},{4,8},{8,12},{12,16},{16,20},{20,24},{24,28},{1,5},{5,9},{9,... | collective-permute-start | bytes 196616 | tf_op jit(solution)/shard_map/ppermute | solution.py:306
  91.0 6.5 %collective-permute-start.19 = (f32[64,256]{1,0:T(8,128)S(1)}, f32[64,256]{1,0:T(8,128)S(1)}, u32[]{:S(2)}, u32[]{:S(2)}) collective-permute-start(f32[64,256]{1,0:T(8,128)S(1)} %get-tuple-element.56), channel_id=1, source_target_pairs={{4,0},{8,4},{12,8},{16,12},{20,16},{24,20},{28,24},{5,1},{9,5},{13... | collective-permute-start | bytes 196616 | tf_op jit(solution)/shard_map/ppermute | solution.py:307
  (23 other events, 117.7 us)
where the time goes:
time: 103 us; the launch traced here: 102 us
  starting transfers between devices  41.2 us (40%)
  Pallas kernels  33.4 us (32%)
  waiting for transfers between devices  9.06 us (9%)
  other arithmetic  8.63 us (8%)
  local copies, waits for them, and re-layouts  8.47 us (8%)
  between operations  1.22 us (1%)
    pallas_call x2, Pallas kernels, mix(): pl.pallas_call(functools.partial(mix_kernel, count, half, groups, window)...  24.9 us
    ppermute x12, starting transfers between devices, swap(): return lax.ppermute(array, 'mode', [(i, i ^ p) for i in range(count)])  16 us
    ppermute x4, starting transfers between devices, swap_rim(): return lax.ppermute(array, ('dom', 'mode'), pairs)  11.1 us
    ppermute x1, starting transfers between devices, body(): low = lax.ppermute(first_top, 'dom', upward)  6.67 us
    ppermute x4, waiting for transfers between devices, swap_rim(): return lax.ppermute(array, ('dom', 'mode'), pairs)  4.59 us
    pallas_call x1, Pallas kernels, body(): pl.pallas_call(functools.partial(post_kernel, count, slab, half, rows, rh...  4.55 us
    ppermute x1, waiting for transfers between devices, body(): high = lax.ppermute(first_bottom, 'dom', downward)  4.44 us
    ppermute x1, starting transfers between devices, body(): low_coef = lax.ppermute(coef[:, -1:], 'dom', upward)  3.67 us
  transfers between devices with their start and end apart: 20, of which 2 were waited for; matrix products, arithmetic and copies ran while one was open for 13% of the time, Pallas kernels for 28%

commit v1 on v0

v1 whole, which is shorter than its diff:
```python
import functools
import jax
import jax.numpy as jnp
from jax import lax
from jax.experimental import pallas as pl
from jax.experimental.pallas import tpu as pltpu
from jax.sharding import PartitionSpec as P

NZ = 16
GROUP = 5

cheb_center = 1.125
cheb_radius = 0.875
VMEM_LIMIT = 48 * 1024 * 1024


def in_vmem(count):
    return [pl.BlockSpec(memory_space=pltpu.VMEM)] * count


def in_smem():
    return pl.BlockSpec(memory_space=pltpu.SMEM)


def row_of(place, rho, slab, count, rows):
    upward = slab * place + rho
    downward = slab * place + (slab - 1 - rho)
    row = jnp.where(place < count // 2, upward, downward)
    return jnp.clip(row, 0, rows - 1)


def pack_kernel(count, slab, half, rows, z_ref, x_ref, low_ref, high_ref, *refs):
    z = z_ref[0]
    outs, turned = refs[:-1], refs[-1]
    here = turned.shape[1]
    turned[...] = jnp.swapaxes(x_ref[...], 0, 1).astype(jnp.bfloat16)
    low = low_ref[:here].astype(jnp.bfloat16)
    high = high_ref[:here].astype(jnp.bfloat16)
    for p in range(count):
        place = jnp.bitwise_xor(z, p)
        early, late = outs[2 * p : 2 * p + 2]
        for rho in range(slab + 1):
            row = row_of(place, rho, slab, count, rows)
            if rho <= half:
                early[rho + 1] = turned[row]
            else:
                late[rho - half - 1] = turned[row]
        early[0] = turned[row_of(place, -1, slab, count, rows)]

        @pl.when(place == 0)
        def _():
            early[0] = low

        @pl.when(place == count - 1)
        def _():
            early[0] = high


def masks(cells):
    lane = lax.broadcasted_iota(jnp.int32, (1, cells), 1)
    in_z = lane % NZ
    one = jnp.float32(1.0)
    zero = jnp.float32(0.0)
    return (
        jnp.where(lane < cells - NZ, one, zero),
        jnp.where(lane >= NZ, one, zero),
        jnp.where(in_z < NZ - 1, one, zero),
        jnp.where(in_z > 0, one, zero),
    )


def beside(field, mask_set):
    cells = field.shape[-1]
    axis = field.ndim - 1
    return (
        pltpu.roll(field, cells - NZ, axis) * mask_set[0],
        pltpu.roll(field, NZ, axis) * mask_set[1],
        pltpu.roll(field, cells - 1, axis) * mask_set[2],
        pltpu.roll(field, 1, axis) * mask_set[3],
    )


def setup_kernel(
    groups,
    modes_here,
    z_ref,
    entry_ref,
    value_ref,
    mean_ref,
    fields_ref,
    low_ref,
    high_ref,
    dense_ref,
    own_ref,
    weight_ref,
    faces_ref,
    inverse_ref,
):
    fields, rows, cells = fields_ref.shape
    size = dense_ref.shape[1]
    entries = entry_ref.shape[1]
    flip = z_ref[0] * modes_here
    mode_id = jnp.bitwise_xor(lax.broadcasted_iota(jnp.int32, (size, entries), 0), flip)
    pick = jnp.where(mode_id == entry_ref[0:1], 1.0, 0.0).astype(jnp.bfloat16)
    depth = -(-(fields + 1) // 16) * 16
    here = lax.broadcasted_iota(jnp.int32, (depth, entries), 0) == entry_ref[2:3]
    partner = jnp.where(here, entry_ref[1:2].astype(jnp.float32), 0.0).astype(jnp.bfloat16)
    value = jnp.where(here, value_ref[...], 0.0).astype(jnp.bfloat16)
    dims = (((1,), (1,)), ((), ()))
    partner_of = lax.dot_general(pick, partner, dims, preferred_element_type=jnp.float32)
    value_of = lax.dot_general(pick, value, dims, preferred_element_type=jnp.float32)
    column = jnp.bitwise_xor(lax.broadcasted_iota(jnp.int32, (size, size), 1), flip)
    column = column.astype(jnp.float32)
    own_ref[...] = jnp.broadcast_to(value_of[:, 0:1], own_ref.shape)
    for g in range(groups):
        for k in range(GROUP):
            at = 1 + g * GROUP + k
            if at > fields:
                tile = jnp.zeros((size, size), jnp.float32)
            else:
                tile = jnp.where(
                    column == partner_of[:, at : at + 1], value_of[:, at : at + 1], 0.0
                )
            dense_ref[g, :, k * size : (k + 1) * size] = tile.astype(jnp.bfloat16)
    mask_set = masks(cells)
    place = lax.broadcasted_iota(jnp.int32, (rows, cells), 0)
    start = low_ref.shape[0] - fields - 1
    for field in range(fields + 1):
        centre = mean_ref[...] if field == 0 else fields_ref[field - 1]
        low = low_ref[start + field : start + field + 1, :]
        high = high_ref[start + field : start + field + 1, :]
        up = jnp.where(place == rows - 1, high, pltpu.roll(centre, rows - 1, 0))
        down = jnp.where(place == 0, low, pltpu.roll(centre, 1, 0))
        diag = None
        for f, other in enumerate((up, down) + beside(centre, mask_set)):
            weight = 0.5 * (centre + other)
            weight_ref[f, field] = weight
            if field == 0:
                diag = weight if diag is None else diag + weight
                faces_ref[f] = weight if f < 2 else weight * mask_set[f - 2]
        if field == 0:
            inverse_ref[...] = 1.0 / diag


def mix_kernel(count, slab, half, groups, fields, window, begin, z_ref, *refs):
    arrays = max(a for a, _ in window) + 1
    sources = refs[: arrays * count]
    dense_ref, own_ref, weight_ref = refs[arrays * count : arrays * count + 3]
    outs = refs[arrays * count + 3 : arrays * count + 3 + count]
    rows_ref, diff_ref, term_ref, total_ref = refs[arrays * count + 3 + count :]
    size, cells = total_ref.shape
    here = size // count
    bf16 = jnp.bfloat16
    for k, (array, row) in enumerate(window):
        for p in range(count):
            rows_ref[k, p * here : (p + 1) * here, :] = sources[array * count + p][row]
    mask_set = masks(cells)
    z = z_ref[0]
    rows = weight_ref.shape[2]
    ahead = jnp.where(z < count // 2, 0, 1)
    faces = (ahead, 1 - ahead, 2, 3, 4, 5)

    def each_row(r, carry):
        row = row_of(z, begin + r, slab, count, rows)
        mean_weights = [weight_ref[f, 0, pl.ds(row, 1), :] for f in faces]
        for t in range(0, size, 16):
            at = slice(t, t + 16)
            centre = rows_ref[r + 1, at].astype(jnp.float32)
            others = (rows_ref[r + 2, at].astype(jnp.float32), rows_ref[r, at].astype(jnp.float32))
            mean = None
            for f, other in enumerate(others + beside(centre, mask_set)):
                diff = centre - other
                diff_ref[f, at] = diff.astype(bf16)
                part = mean_weights[f] * diff
                mean = part if mean is None else mean + part
            total_ref[at, :] = jnp.concatenate([own_ref[at]] * (cells // 128), 1) * mean
        for g in range(groups):
            for k in range(GROUP):
                field = min(1 + g * GROUP + k, fields - 1)
                weights = [
                    jnp.broadcast_to(weight_ref[f, field, pl.ds(row, 1), :], (16, cells))
                    for f in faces
                ]
                weights = [w.astype(bf16) for w in weights]
                for t in range(0, size, 16):
                    part = [weights[f] * diff_ref[f, t : t + 16] for f in range(6)]
                    term = ((part[0] + part[1]) + (part[2] + part[3])) + (part[4] + part[5])
                    term_ref[k * size + t : k * size + t + 16, :] = term
            total_ref[...] += jnp.dot(
                dense_ref[g], term_ref[...], preferred_element_type=jnp.float32
            )
        for p in range(count):
            outs[p][r] = total_ref[p * here : (p + 1) * here, :].astype(bf16)
        return carry

    lax.fori_loop(0, half, each_row, 0)


def post_kernel(count, slab, half, rows, rho_zero, rho_one, z_ref, *refs):
    early = refs[:count]
    late = refs[count : 2 * count]
    source, iterate, low, high, faces, inverse = refs[2 * count : 2 * count + 6]
    updated, residual, image = refs[2 * count + 6 :]
    z = z_ref[0]
    modes, _, cells = source.shape
    for p in range(count):
        place = jnp.bitwise_xor(z, p)
        for rho in range(slab):
            part = early[p][rho] if rho < half else late[p][rho - half]
            image[row_of(place, rho, slab, count, rows)] = part.astype(jnp.float32)
    residual[...] = source[...] - jnp.swapaxes(image[...], 0, 1)
    place = lax.broadcasted_iota(jnp.int32, (rows, cells), 0)
    inv = inverse[...]
    for m in range(modes):
        res = residual[m]
        first = res * (inv * (1.0 / cheb_center))
        up = jnp.where(place == rows - 1, high[m : m + 1, :], pltpu.roll(first, rows - 1, 0))
        down = jnp.where(place == 0, low[m : m + 1, :], pltpu.roll(first, 1, 0))
        near = faces[0] * up + faces[1] * down
        near = near + faces[2] * pltpu.roll(first, cells - NZ, 1)
        near = near + faces[3] * pltpu.roll(first, NZ, 1)
        near = near + faces[4] * pltpu.roll(first, cells - 1, 1)
        near = near + faces[5] * pltpu.roll(first, 1, 1)
        smoothed = (1.0 - 1.0 / cheb_center) * res + near
        step = (1.0 + rho_one * rho_zero) * first + (2.0 * rho_one / cheb_radius) * smoothed * inv
        updated[m] = iterate[m] + step


def body(iterate, source, mean_coef, kl_fields, tri_index, tri_value):
    count = lax.axis_size("mode")
    doms = lax.axis_size("dom")
    z = lax.axis_index("mode")
    z_arg = z.astype(jnp.int32).reshape(1)
    here, rows, cells = iterate.shape
    size = here * count
    slab = rows // count
    half = slab // 2
    fields = kl_fields.shape[0] + 1
    groups = -(-(fields - 1) // GROUP)
    bf16 = jnp.bfloat16
    params = pltpu.CompilerParams(vmem_limit_bytes=VMEM_LIMIT)

    upward = [(i, i + 1) for i in range(doms - 1)]
    downward = [(b, a) for a, b in upward]
    low_rim, high_rim = (
        lax.ppermute(
            jnp.concatenate([iterate[:, at], mean_coef[at][None], kl_fields[:, at]], 0), "dom", pairs
        )
        for at, pairs in ((rows - 1, upward), (0, downward))
    )

    packed = pl.pallas_call(
        functools.partial(pack_kernel, count, slab, half, rows),
        out_shape=[
            jax.ShapeDtypeStruct((half + 2, here, cells), bf16),
            jax.ShapeDtypeStruct((slab - half, here, cells), bf16),
        ]
        * count,
        in_specs=[in_smem()] + in_vmem(3),
        out_specs=in_vmem(2 * count),
        scratch_shapes=[pltpu.VMEM((rows, here, cells), bf16)],
        compiler_params=params,
        name="pack",
    )(z_arg, iterate, low_rim, high_rim)

    def swap(array, p):
        return lax.ppermute(array, "mode", [(i, i ^ p) for i in range(count)])

    early = [packed[0]] + [swap(packed[2 * p], p) for p in range(1, count)]
    late = [packed[1]] + [swap(packed[2 * p + 1], p) for p in range(1, count)]

    dense, own, weights, faces, inverse = pl.pallas_call(
        functools.partial(setup_kernel, groups, here),
        out_shape=[
            jax.ShapeDtypeStruct((groups, size, GROUP * size), bf16),
            jax.ShapeDtypeStruct((size, 128), jnp.float32),
            jax.ShapeDtypeStruct((6, fields, rows, cells), jnp.float32),
            jax.ShapeDtypeStruct((6, rows, cells), jnp.float32),
            jax.ShapeDtypeStruct((rows, cells), jnp.float32),
        ],
        in_specs=[in_smem()] + in_vmem(6),
        out_specs=in_vmem(5),
        compiler_params=params,
        name="setup",
    )(z_arg, tri_index.T, tri_value[None], mean_coef, kl_fields, low_rim, high_rim)

    def mix(arrays, window, begin):
        flat = [a for group in arrays for a in group]
        return pl.pallas_call(
            functools.partial(mix_kernel, count, slab, half, groups, fields, window, begin),
            out_shape=[jax.ShapeDtypeStruct((half, here, cells), bf16)] * count,
            in_specs=[in_smem()] + in_vmem(len(flat) + 3),
            out_specs=in_vmem(count),
            scratch_shapes=[
                pltpu.VMEM((half + 2, size, cells), bf16),
                pltpu.VMEM((6, size, cells), bf16),
                pltpu.VMEM((GROUP * size, cells), bf16),
                pltpu.VMEM((size, cells), jnp.float32),
            ],
            compiler_params=params,
            name="mix",
        )(z_arg, *flat, dense, own, weights)

    window = tuple((0, k) for k in range(half + 2))
    mixed_early = mix([early], window, 0)
    back_early = [mixed_early[0]] + [swap(mixed_early[p], p) for p in range(1, count)]
    window = ((0, half), (0, half + 1)) + tuple((1, k) for k in range(slab - half))
    mixed_late = mix([early, late], window, half)
    back_late = [mixed_late[0]] + [swap(mixed_late[p], p) for p in range(1, count)]

    outer = jnp.stack([b[0] for b in back_early])
    bottom = lax.dynamic_index_in_dim(outer, z, 0, keepdims=False).astype(jnp.float32)
    top = lax.dynamic_index_in_dim(outer, z ^ (count - 1), 0, keepdims=False).astype(jnp.float32)
    first_bottom = (source[:, 0] - bottom) * (inverse[0] / cheb_center)
    first_top = (source[:, -1] - top) * (inverse[-1] / cheb_center)
    low = lax.ppermute(first_top, "dom", upward)
    high = lax.ppermute(first_bottom, "dom", downward)

    sigma = cheb_center / cheb_radius
    rho_zero = 1.0 / sigma
    rho_one = 1.0 / (2.0 * sigma - rho_zero)
    block = min(16, here)
    image_spec = pl.BlockSpec((half, block, cells), lambda i: (0, i, 0))
    flat_spec = pl.BlockSpec((block, rows, cells), lambda i: (i, 0, 0))
    row_spec = pl.BlockSpec((block, cells), lambda i: (i, 0))
    updated, residual = pl.pallas_call(
        functools.partial(post_kernel, count, slab, half, rows, rho_zero, rho_one),
        grid=(here // block,),
        out_shape=[jax.ShapeDtypeStruct((here, rows, cells), jnp.float32)] * 2,
        in_specs=[in_smem()]
        + [image_spec] * (2 * count)
        + [flat_spec, flat_spec, row_spec, row_spec]
        + [
            pl.BlockSpec((6, rows, cells), lambda i: (0, 0, 0)),
            pl.BlockSpec((rows, cells), lambda i: (0, 0)),
        ],
        out_specs=[flat_spec, flat_spec],
        scratch_shapes=[pltpu.VMEM((rows, block, cells), jnp.float32)],
        compiler_params=params,
        name="post",
    )(
        z_arg,
        *back_early,
        *back_late,
        source,
        iterate,
        low,
        high,
        faces,
        inverse,
    )
    return updated, residual


def solution(mesh):
    return jax.shard_map(
        body,
        mesh=mesh,
        in_specs=(
            P("mode", "dom", None),
            P("mode", "dom", None),
            P("dom", None),
            P(None, "dom", None),
            P(),
            P(),
        ),
        out_specs=(P("mode", "dom", None), P("mode", "dom", None)),
        check_vma=False,
    )
```

time: 103 us -> 85.1 us (0.83)
  the two profiles are of different devices: /device:TPU:3 before, /device:TPU:11 now
where the time goes in v1:
time: 85.1 us; the launch traced here: 84.7 us
  Pallas kernels  28.6 us (34%)
  starting transfers between devices  26.3 us (31%)
  waiting for transfers between devices  23.2 us (27%)
  local copies, waits for them, and re-layouts  5.61 us (7%)
  between operations  0.9 us (1%)
    ppermute x12, waiting for transfers between devices, swap(): return lax.ppermute(array, 'mode', [(i, i ^ p) for i in range(count)])  19.2 us
    pallas_call x2, Pallas kernels, mix(): pl.pallas_call(functools.partial(mix_kernel, count, slab, half, groups, f...  18.2 us
    ppermute x12, starting transfers between devices, swap(): return lax.ppermute(array, 'mode', [(i, i ^ p) for i in range(count)])  13.8 us
    ppermute x2, starting transfers between devices, body(): lax.ppermute(jnp.concatenate([iterate[:, at], mean_coef[at][None], kl_fie...  5.6 us
    pallas_call x1, Pallas kernels, body(): pl.pallas_call(functools.partial(setup_kernel, groups, here), out_shape=[...  5.03 us
    ppermute x1, starting transfers between devices, body(): low = lax.ppermute(first_top, 'dom', upward)  4.88 us
    pallas_call x1, Pallas kernels, body(): pl.pallas_call(functools.partial(post_kernel, count, slab, half, rows, rh...  4.84 us
    ppermute x2, waiting for transfers between devices, body(): lax.ppermute(jnp.concatenate([iterate[:, at], mean_coef[at][None], kl_fie...  4.04 us
  transfers between devices with their start and end apart: 16, of which 5 were waited for; matrix products, arithmetic and copies ran while one was open for 1% of the time, Pallas kernels for 27%

profile of v1, /device:TPU:11, one launch (start us, length us, event | category | flops | bytes accessed | tf_op | source)
XLA Modules:
  0.0 84.7 jit_solution(5897914789822541882)
XLA Ops:
  0.7 0.8 fusion.7
  1.4 1.0 %fusion.6 = (f32[20,1,256]{2,1,0:T(1,128)S(1)}, f32[20,1,256]{2,1,0:T(1,128)S(1)}) fusion(f32[20,32,256]{2,1,0:T(8,128)} %fields_ref.1), kind=kLoop, calls=%fused_computation.17 | loop fusion | bytes 81920 | tf_op jit(solution)/shard_map/slice | solution.py:247
  2.5 1.3 %fusion.5 = (f32[64,1,256]{2,1,0:T(1,128)S(1)}, f32[64,1,256]{2,1,0:T(1,128)S(1)}) fusion(f32[64,32,256]{2,1,0:T(8,128)} %refs_9_.1), kind=kLoop, calls=%fused_computation.16 | loop fusion | bytes 262144 | tf_op jit(solution)/shard_map/slice | solution.py:247
  3.8 3.7 %collective-permute-start = (f32[85,256]{1,0:T(8,128)S(1)}, f32[85,256]{1,0:T(8,128)S(1)}, u32[]{:S(2)}, u32[]{:S(2)}) collective-permute-start(f32[85,256]{1,0:T(8,128)S(1)} %pad_maximum_fusion.1), channel_id=1, source_target_pairs={{0,4},{4,8},{8,12},{12,16},{16,20},{20,24},{24,28},{1,5},{5,9},{9,... | collective-permute-start | bytes 261128 | tf_op jit(solution)/shard_map/ppermute | solution.py:246
  7.6 1.9 %collective-permute-start.1 = (f32[85,256]{1,0:T(8,128)S(1)}, f32[85,256]{1,0:T(8,128)S(1)}, u32[]{:S(2)}, u32[]{:S(2)}) collective-permute-start(f32[85,256]{1,0:T(8,128)S(1)} %pad_maximum_fusion.2), channel_id=1, source_target_pairs={{4,0},{8,4},{12,8},{16,12},{20,16},{24,20},{28,24},{5,1},{9,5},{13... | collective-permute-start | bytes 261128 | tf_op jit(solution)/shard_map/ppermute | solution.py:246
  10.3 4.0 %collective-permute-done.1.high_ref = f32[85,256]{1,0:T(8,128)S(1)} collective-permute-done((f32[85,256]{1,0:T(8,128)S(1)}, f32[85,256]{1,0:T(8,128)S(1)}, u32[]{:S(2)}, u32[]{:S(2)}) %collective-permute-start.1) | collective-permute-done | bytes 87072 | tf_op jit(solution)/shard_map/ppermute | solution.py:246
  14.3 1.6 %copy-done = f32[64,32,256]{2,1,0:T(8,128)S(1)} copy-done((f32[64,32,256]{2,1,0:T(8,128)S(1)}, f32[64,32,256]{2,1,0:T(8,128)}, u32[]{:S(2)}) %copy-start) | copy-done | bytes 2097176
  16.7 1.3 %collective-permute-start.2 = (bf16[6,64,256]{2,1,0:T(8,128)(2,1)S(1)}, bf16[6,64,256]{2,1,0:T(8,128)(2,1)S(1)}, u32[]{:S(2)}, u32[]{:S(2)}) collective-permute-start(bf16[6,64,256]{2,1,0:T(8,128)(2,1)S(1)} %get-tuple-element.24), channel_id=1, source_target_pairs={{0,1},{1,0},{2,3},{3,2},{4,5},{5,4},{6,7},{7,6},{8,9},{9,8},{10,11... | collective-permute-start | bytes 589832 | tf_op jit(solution)/shard_map/ppermute | solution.py:267
  18.0 2.3 %collective-permute-start.3 = (bf16[6,64,256]{2,1,0:T(8,128)(2,1)S(1)}, bf16[6,64,256]{2,1,0:T(8,128)(2,1)S(1)}, u32[]{:S(2)}, u32[]{:S(2)}) collective-permute-start(bf16[6,64,256]{2,1,0:T(8,128)(2,1)S(1)} %get-tuple-element.25), channel_id=1, source_target_pairs={{0,2},{1,3},{2,0},{3,1},{4,6},{5,7},{6,4},{7,5},{8,10},{9,11},{10,... | collective-permute-start | bytes 589832 | tf_op jit(solution)/shard_map/ppermute | solution.py:267
  20.4 2.3 %collective-permute-start.9 = (bf16[4,64,256]{2,1,0:T(8,128)(2,1)S(1)}, bf16[4,64,256]{2,1,0:T(8,128)(2,1)S(1)}, u32[]{:S(2)}, u32[]{:S(2)}) collective-permute-start(bf16[4,64,256]{2,1,0:T(8,128)(2,1)S(1)} %get-tuple-element.36), channel_id=1, source_target_pairs={{0,2},{1,3},{2,0},{3,1},{4,6},{5,7},{6,4},{7,5},{8,10},{9,11},{10,... | collective-permute-start | bytes 393224 | tf_op jit(solution)/shard_map/ppermute | solution.py:267
  22.7 5.0 %setup.1 = (bf16[4,256,1280]{2,1,0:T(8,128)(2,1)S(1)}, f32[256,128]{1,0:T(8,128)S(1)}, f32[6,21,32,256]{3,2,1,0:T(8,128)}, f32[6,32,256]{2,1,0:T(8,128)S(1)}, f32[32,256]{1,0:T(8,128)S(1)}) custom-call(s32[1]{0:T(128)} %bitcast.z_ref, s32[3,5376]{1,0:T(4,128)S(1)} %bitcast.34, f32[1,5376]{1,0:T(1,128)S(1)} %broadcast_in_dim.2.value_ref, ...), custom_call_target="tpu_custom_call" | custom-call | tf_op jit(solution)/shard_map/setup/pallas_call | solution.py:272
  27.8 1.9 %collective-permute-start.10 = (bf16[4,64,256]{2,1,0:T(8,128)(2,1)S(1)}, bf16[4,64,256]{2,1,0:T(8,128)(2,1)S(1)}, u32[]{:S(2)}, u32[]{:S(2)}) collective-permute-start(bf16[4,64,256]{2,1,0:T(8,128)(2,1)S(1)} %get-tuple-element.37), channel_id=1, source_target_pairs={{0,3},{1,2},{2,1},{3,0},{4,7},{5,6},{6,5},{7,4},{8,11},{9,10},{10,... | collective-permute-start | bytes 393224 | tf_op jit(solution)/shard_map/ppermute | solution.py:267
  29.6 9.5 %collective-permute-done.3.refs_2_ = bf16[6,64,256]{2,1,0:T(8,128)(2,1)S(1)} collective-permute-done((bf16[6,64,256]{2,1,0:T(8,128)(2,1)S(1)}, bf16[6,64,256]{2,1,0:T(8,128)(2,1)S(1)}, u32[]{:S(2)}, u32[]{:S(2)}) %collective-permute-start.3) | collective-permute-done | bytes 196640 | tf_op jit(solution)/shard_map/ppermute | solution.py:267
  39.1 4.2 %collective-permute-done.4.refs_3_ = bf16[6,64,256]{2,1,0:T(8,128)(2,1)S(1)} collective-permute-done((bf16[6,64,256]{2,1,0:T(8,128)(2,1)S(1)}, bf16[6,64,256]{2,1,0:T(8,128)(2,1)S(1)}, u32[]{:S(2)}, u32[]{:S(2)}) %collective-permute-start.4) | collective-permute-done | bytes 196640 | tf_op jit(solution)/shard_map/ppermute | solution.py:267
  43.3 9.0 %mix.2 = (bf16[4,64,256]{2,1,0:T(8,128)(2,1)S(1)}, bf16[4,64,256]{2,1,0:T(8,128)(2,1)S(1)}, bf16[4,64,256]{2,1,0:T(8,128)(2,1)S(1)}, bf16[4,64,256]{2,1,0:T(8,128)(2,1)S(1)}) custom-call(s32[1]{0:T(128)} %bitcast.z_ref, bf16[6,64,256]{2,1,0:T(8,128)(2,1)S(1)} %get-tuple-element.23.refs_0_, bf16[6,64,256]{2,1,0:T(8,128)(2,1)S(1)} %collective-permute-done.2.refs_1_, ...), custom_call_target="tpu_custom_call" | custom-call | tf_op jit(solution)/shard_map/mix/pallas_call | solution.py:289
  52.4 3.0 %collective-permute-start.6 = (bf16[4,64,256]{2,1,0:T(8,128)(2,1)S(1)}, bf16[4,64,256]{2,1,0:T(8,128)(2,1)S(1)}, u32[]{:S(2)}, u32[]{:S(2)}) collective-permute-start(bf16[4,64,256]{2,1,0:T(8,128)(2,1)S(1)} %get-tuple-element.32), channel_id=1, source_target_pairs={{0,2},{1,3},{2,0},{3,1},{4,6},{5,7},{6,4},{7,5},{8,10},{9,11},{10,... | collective-permute-start | bytes 393224 | tf_op jit(solution)/shard_map/ppermute | solution.py:267
  55.5 9.2 %mix.3 = (bf16[4,64,256]{2,1,0:T(8,128)(2,1)S(1)}, bf16[4,64,256]{2,1,0:T(8,128)(2,1)S(1)}, bf16[4,64,256]{2,1,0:T(8,128)(2,1)S(1)}, bf16[4,64,256]{2,1,0:T(8,128)(2,1)S(1)}) custom-call(s32[1]{0:T(128)} %bitcast.z_ref, bf16[6,64,256]{2,1,0:T(8,128)(2,1)S(1)} %get-tuple-element.23.refs_0_, bf16[6,64,256]{2,1,0:T(8,128)(2,1)S(1)} %collective-permute-done.2.refs_1_, ...), custom_call_target="tpu_custom_call" | custom-call | tf_op jit(solution)/shard_map/mix/pallas_call | solution.py:289
  64.7 1.1 %collective-permute-start.11 = (bf16[4,64,256]{2,1,0:T(8,128)(2,1)S(1)}, bf16[4,64,256]{2,1,0:T(8,128)(2,1)S(1)}, u32[]{:S(2)}, u32[]{:S(2)}) collective-permute-start(bf16[4,64,256]{2,1,0:T(8,128)(2,1)S(1)} %get-tuple-element.39), channel_id=1, source_target_pairs={{0,1},{1,0},{2,3},{3,2},{4,5},{5,4},{6,7},{7,6},{8,9},{9,8},{10,11... | collective-permute-start | bytes 393224 | tf_op jit(solution)/shard_map/ppermute | solution.py:267
  65.8 1.4 %collective-permute-start.12 = (bf16[4,64,256]{2,1,0:T(8,128)(2,1)S(1)}, bf16[4,64,256]{2,1,0:T(8,128)(2,1)S(1)}, u32[]{:S(2)}, u32[]{:S(2)}) collective-permute-start(bf16[4,64,256]{2,1,0:T(8,128)(2,1)S(1)} %get-tuple-element.40), channel_id=1, source_target_pairs={{0,2},{1,3},{2,0},{3,1},{4,6},{5,7},{6,4},{7,5},{8,10},{9,11},{10,... | collective-permute-start | bytes 393224 | tf_op jit(solution)/shard_map/ppermute | solution.py:267
  67.5 2.0 %collective-permute-start.15 = (f32[64,256]{1,0:T(8,128)S(1)}, f32[64,256]{1,0:T(8,128)S(1)}, u32[]{:S(2)}, u32[]{:S(2)}) collective-permute-start(f32[64,256]{1,0:T(8,128)S(1)} %get-tuple-element.50), channel_id=1, source_target_pairs={{4,0},{8,4},{12,8},{16,12},{20,16},{24,20},{28,24},{5,1},{9,5},{13... | collective-permute-start | bytes 196616 | tf_op jit(solution)/shard_map/ppermute | solution.py:317
  69.5 4.9 %collective-permute-start.14 = (f32[64,256]{1,0:T(8,128)S(1)}, f32[64,256]{1,0:T(8,128)S(1)}, u32[]{:S(2)}, u32[]{:S(2)}) collective-permute-start(f32[64,256]{1,0:T(8,128)S(1)} %get-tuple-element.51), channel_id=1, source_target_pairs={{0,4},{4,8},{8,12},{12,16},{16,20},{20,24},{24,28},{1,5},{5,9},{9,... | collective-permute-start | bytes 196616 | tf_op jit(solution)/shard_map/ppermute | solution.py:316
  74.4 1.6 %collective-permute-done.12.refs_6_ = bf16[4,64,256]{2,1,0:T(8,128)(2,1)S(1)} collective-permute-done((bf16[4,64,256]{2,1,0:T(8,128)(2,1)S(1)}, bf16[4,64,256]{2,1,0:T(8,128)(2,1)S(1)}, u32[]{:S(2)}, u32[]{:S(2)}) %collective-permute-start.12) | collective-permute-done | bytes 131104 | tf_op jit(solution)/shard_map/ppermute | solution.py:267
  75.9 3.9 %collective-permute-done.13.refs_7_ = bf16[4,64,256]{2,1,0:T(8,128)(2,1)S(1)} collective-permute-done((bf16[4,64,256]{2,1,0:T(8,128)(2,1)S(1)}, bf16[4,64,256]{2,1,0:T(8,128)(2,1)S(1)}, u32[]{:S(2)}, u32[]{:S(2)}) %collective-permute-start.13) | collective-permute-done | bytes 131104 | tf_op jit(solution)/shard_map/ppermute | solution.py:267
  79.9 4.8 %post.1 = (f32[64,32,256]{2,1,0:T(8,128)}, f32[64,32,256]{2,1,0:T(8,128)}) custom-call(s32[1]{0:T(128)} %bitcast.z_ref, bf16[4,64,256]{2,1,0:T(8,128)(2,1)S(1)} %get-tuple-element.30.refs_0_, bf16[4,64,256]{2,1,0:T(8,128)(2,1)S(1)} %collective-permute-done.5.refs_1_, bf16[4,64,256]{2,1,0:T(8,128)(2,1)S(1)} %collective-permute-done.6.refs_2_, ...), custom_call_target="tpu_custom_call" | custom-call | tf_op jit(solution)/shard_map/post/pallas_call | solution.py:326
  (43 shorter events, 2.0 us)
Async XLA Ops:
  0.6 22.1 %copy-start.5 = (f32[32,256]{1,0:T(8,128)S(1)}, f32[32,256]{1,0:T(8,128)}, u32[]{:S(2)}) copy-start(f32[32,256]{1,0:T(8,128)} %mean_ref.1) | copy-start | bytes 98308
  0.6 22.1 %copy-start.3 = (f32[20,32,256]{2,1,0:T(8,128)S(1)}, f32[20,32,256]{2,1,0:T(8,128)}, u32[]{:S(2)}) copy-start(f32[20,32,256]{2,1,0:T(8,128)} %fields_ref.1) | copy-start | bytes 1966084
  0.7 22.1 %copy-start.4 = (s32[5376,3]{0,1:T(4,128)S(1)}, s32[5376,3]{0,1:T(4,128)}, u32[]{:S(2)}) copy-start(s32[5376,3]{0,1:T(4,128)} %param.10) | copy-start | bytes 193540
  3.8 6.4 %collective-permute-start = (f32[85,256]{1,0:T(8,128)S(1)}, f32[85,256]{1,0:T(8,128)S(1)}, u32[]{:S(2)}, u32[]{:S(2)}) collective-permute-start(f32[85,256]{1,0:T(8,128)S(1)} %pad_maximum_fusion.1), channel_id=1, source_target_pairs={{0,4},{4,8},{8,12},{12,16},{16,20},{20,24},{24,28},{1,5},{5,9},{9,... | collective-permute-start | bytes 261128 | tf_op jit(solution)/shard_map/ppermute | solution.py:246
  7.6 6.7 %collective-permute-start.1 = (f32[85,256]{1,0:T(8,128)S(1)}, f32[85,256]{1,0:T(8,128)S(1)}, u32[]{:S(2)}, u32[]{:S(2)}) collective-permute-start(f32[85,256]{1,0:T(8,128)S(1)} %pad_maximum_fusion.2), channel_id=1, source_target_pairs={{4,0},{8,4},{12,8},{16,12},{20,16},{24,20},{28,24},{5,1},{9,5},{13... | collective-permute-start | bytes 261128 | tf_op jit(solution)/shard_map/ppermute | solution.py:246
  14.3 1.6 %copy-start = (f32[64,32,256]{2,1,0:T(8,128)S(1)}, f32[64,32,256]{2,1,0:T(8,128)}, u32[]{:S(2)}) copy-start(f32[64,32,256]{2,1,0:T(8,128)} %refs_9_.1) | copy-start | bytes 6291460
  15.9 4.4 %copy-start.2 = (f32[64,32,256]{2,1,0:T(8,128)S(1)}, f32[64,32,256]{2,1,0:T(8,128)}, u32[]{:S(2)}) copy-start(f32[64,32,256]{2,1,0:T(8,128)} %refs_8_.1) | copy-start | bytes 6291460
  16.5 38.9 %collective-permute-start.8 = (bf16[4,64,256]{2,1,0:T(8,128)(2,1)S(1)}, bf16[4,64,256]{2,1,0:T(8,128)(2,1)S(1)}, u32[]{:S(2)}, u32[]{:S(2)}) collective-permute-start(bf16[4,64,256]{2,1,0:T(8,128)(2,1)S(1)} %get-tuple-element.35), channel_id=1, source_target_pairs={{0,1},{1,0},{2,3},{3,2},{4,5},{5,4},{6,7},{7,6},{8,9},{9,8},{10,11... | collective-permute-start | bytes 393224 | tf_op jit(solution)/shard_map/ppermute | solution.py:267
  16.7 11.1 %collective-permute-start.2 = (bf16[6,64,256]{2,1,0:T(8,128)(2,1)S(1)}, bf16[6,64,256]{2,1,0:T(8,128)(2,1)S(1)}, u32[]{:S(2)}, u32[]{:S(2)}) collective-permute-start(bf16[6,64,256]{2,1,0:T(8,128)(2,1)S(1)} %get-tuple-element.24), channel_id=1, source_target_pairs={{0,1},{1,0},{2,3},{3,2},{4,5},{5,4},{6,7},{7,6},{8,9},{9,8},{10,11... | collective-permute-start | bytes 589832 | tf_op jit(solution)/shard_map/ppermute | solution.py:267
  18.0 21.1 %collective-permute-start.3 = (bf16[6,64,256]{2,1,0:T(8,128)(2,1)S(1)}, bf16[6,64,256]{2,1,0:T(8,128)(2,1)S(1)}, u32[]{:S(2)}, u32[]{:S(2)}) collective-permute-start(bf16[6,64,256]{2,1,0:T(8,128)(2,1)S(1)} %get-tuple-element.25), channel_id=1, source_target_pairs={{0,2},{1,3},{2,0},{3,1},{4,6},{5,7},{6,4},{7,5},{8,10},{9,11},{10,... | collective-permute-start | bytes 589832 | tf_op jit(solution)/shard_map/ppermute | solution.py:267
  20.3 23.0 %collective-permute-start.4 = (bf16[6,64,256]{2,1,0:T(8,128)(2,1)S(1)}, bf16[6,64,256]{2,1,0:T(8,128)(2,1)S(1)}, u32[]{:S(2)}, u32[]{:S(2)}) collective-permute-start(bf16[6,64,256]{2,1,0:T(8,128)(2,1)S(1)} %get-tuple-element.26), channel_id=1, source_target_pairs={{0,3},{1,2},{2,1},{3,0},{4,7},{5,6},{6,5},{7,4},{8,11},{9,10},{10,... | collective-permute-start | bytes 589832 | tf_op jit(solution)/shard_map/ppermute | solution.py:267
  20.4 35.0 %collective-permute-start.9 = (bf16[4,64,256]{2,1,0:T(8,128)(2,1)S(1)}, bf16[4,64,256]{2,1,0:T(8,128)(2,1)S(1)}, u32[]{:S(2)}, u32[]{:S(2)}) collective-permute-start(bf16[4,64,256]{2,1,0:T(8,128)(2,1)S(1)} %get-tuple-element.36), channel_id=1, source_target_pairs={{0,2},{1,3},{2,0},{3,1},{4,6},{5,7},{6,4},{7,5},{8,10},{9,11},{10,... | collective-permute-start | bytes 393224 | tf_op jit(solution)/shard_map/ppermute | solution.py:267
  27.8 27.7 %collective-permute-start.10 = (bf16[4,64,256]{2,1,0:T(8,128)(2,1)S(1)}, bf16[4,64,256]{2,1,0:T(8,128)(2,1)S(1)}, u32[]{:S(2)}, u32[]{:S(2)}) collective-permute-start(bf16[4,64,256]{2,1,0:T(8,128)(2,1)S(1)} %get-tuple-element.37), channel_id=1, source_target_pairs={{0,3},{1,2},{2,1},{3,0},{4,7},{5,6},{6,5},{7,4},{8,11},{9,10},{10,... | collective-permute-start | bytes 393224 | tf_op jit(solution)/shard_map/ppermute | solution.py:267
  52.3 14.9 %collective-permute-start.5 = (bf16[4,64,256]{2,1,0:T(8,128)(2,1)S(1)}, bf16[4,64,256]{2,1,0:T(8,128)(2,1)S(1)}, u32[]{:S(2)}, u32[]{:S(2)}) collective-permute-start(bf16[4,64,256]{2,1,0:T(8,128)(2,1)S(1)} %get-tuple-element.31), channel_id=1, source_target_pairs={{0,1},{1,0},{2,3},{3,2},{4,5},{5,4},{6,7},{7,6},{8,9},{9,8},{10,11... | collective-permute-start | bytes 393224 | tf_op jit(solution)/shard_map/ppermute | solution.py:267
  52.4 15.0 %collective-permute-start.6 = (bf16[4,64,256]{2,1,0:T(8,128)(2,1)S(1)}, bf16[4,64,256]{2,1,0:T(8,128)(2,1)S(1)}, u32[]{:S(2)}, u32[]{:S(2)}) collective-permute-start(bf16[4,64,256]{2,1,0:T(8,128)(2,1)S(1)} %get-tuple-element.32), channel_id=1, source_target_pairs={{0,2},{1,3},{2,0},{3,1},{4,6},{5,7},{6,4},{7,5},{8,10},{9,11},{10,... | collective-permute-start | bytes 393224 | tf_op jit(solution)/shard_map/ppermute | solution.py:267
  55.4 12.0 %collective-permute-start.7 = (bf16[4,64,256]{2,1,0:T(8,128)(2,1)S(1)}, bf16[4,64,256]{2,1,0:T(8,128)(2,1)S(1)}, u32[]{:S(2)}, u32[]{:S(2)}) collective-permute-start(bf16[4,64,256]{2,1,0:T(8,128)(2,1)S(1)} %get-tuple-element.33), channel_id=1, source_target_pairs={{0,3},{1,2},{2,1},{3,0},{4,7},{5,6},{6,5},{7,4},{8,11},{9,10},{10,... | collective-permute-start | bytes 393224 | tf_op jit(solution)/shard_map/ppermute | solution.py:267
  55.4 24.4 %copy-start.1 = (f32[64,32,256]{2,1,0:T(8,128)S(1)}, f32[64,32,256]{2,1,0:T(8,128)}, u32[]{:S(2)}) copy-start(f32[64,32,256]{2,1,0:T(8,128)} %refs_9_.1) | copy-start | bytes 6291460
  64.7 9.7 %collective-permute-start.11 = (bf16[4,64,256]{2,1,0:T(8,128)(2,1)S(1)}, bf16[4,64,256]{2,1,0:T(8,128)(2,1)S(1)}, u32[]{:S(2)}, u32[]{:S(2)}) collective-permute-start(bf16[4,64,256]{2,1,0:T(8,128)(2,1)S(1)} %get-tuple-element.39), channel_id=1, source_target_pairs={{0,1},{1,0},{2,3},{3,2},{4,5},{5,4},{6,7},{7,6},{8,9},{9,8},{10,11... | collective-permute-start | bytes 393224 | tf_op jit(solution)/shard_map/ppermute | solution.py:267
  65.8 10.1 %collective-permute-start.12 = (bf16[4,64,256]{2,1,0:T(8,128)(2,1)S(1)}, bf16[4,64,256]{2,1,0:T(8,128)(2,1)S(1)}, u32[]{:S(2)}, u32[]{:S(2)}) collective-permute-start(bf16[4,64,256]{2,1,0:T(8,128)(2,1)S(1)} %get-tuple-element.40), channel_id=1, source_target_pairs={{0,2},{1,3},{2,0},{3,1},{4,6},{5,7},{6,4},{7,5},{8,10},{9,11},{10,... | collective-permute-start | bytes 393224 | tf_op jit(solution)/shard_map/ppermute | solution.py:267
  67.2 12.6 %collective-permute-start.13 = (bf16[4,64,256]{2,1,0:T(8,128)(2,1)S(1)}, bf16[4,64,256]{2,1,0:T(8,128)(2,1)S(1)}, u32[]{:S(2)}, u32[]{:S(2)}) collective-permute-start(bf16[4,64,256]{2,1,0:T(8,128)(2,1)S(1)} %get-tuple-element.41), channel_id=1, source_target_pairs={{0,3},{1,2},{2,1},{3,0},{4,7},{5,6},{6,5},{7,4},{8,11},{9,10},{10,... | collective-permute-start | bytes 393224 | tf_op jit(solution)/shard_map/ppermute | solution.py:267
  67.5 12.4 %collective-permute-start.15 = (f32[64,256]{1,0:T(8,128)S(1)}, f32[64,256]{1,0:T(8,128)S(1)}, u32[]{:S(2)}, u32[]{:S(2)}) collective-permute-start(f32[64,256]{1,0:T(8,128)S(1)} %get-tuple-element.50), channel_id=1, source_target_pairs={{4,0},{8,4},{12,8},{16,12},{20,16},{24,20},{28,24},{5,1},{9,5},{13... | collective-permute-start | bytes 196616 | tf_op jit(solution)/shard_map/ppermute | solution.py:317
  69.5 10.4 %collective-permute-start.14 = (f32[64,256]{1,0:T(8,128)S(1)}, f32[64,256]{1,0:T(8,128)S(1)}, u32[]{:S(2)}, u32[]{:S(2)}) collective-permute-start(f32[64,256]{1,0:T(8,128)S(1)} %get-tuple-element.51), channel_id=1, source_target_pairs={{0,4},{4,8},{8,12},{12,16},{16,20},{20,24},{24,28},{1,5},{5,9},{9,... | collective-permute-start | bytes 196616 | tf_op jit(solution)/shard_map/ppermute | solution.py:316

commit v2 on v1

--- a/solution.py
+++ b/solution.py
@@ -11,6 +11,7 @@
 
 cheb_center = 1.125
 cheb_radius = 0.875
+SMALL = pl.CostEstimate(flops=1, bytes_accessed=1, transcendentals=0)
 VMEM_LIMIT = 48 * 1024 * 1024
 
 
@@ -29,31 +30,33 @@
     return jnp.clip(row, 0, rows - 1)
 
 
-def pack_kernel(count, slab, half, rows, z_ref, x_ref, low_ref, high_ref, *refs):
+def turn_kernel(x_ref, turned):
+    turned[...] = jnp.swapaxes(x_ref[...], 0, 1).astype(jnp.bfloat16)
+
+
+def late_kernel(count, slab, half, rows, z_ref, turned, after, *outs):
     z = z_ref[0]
-    outs, turned = refs[:-1], refs[-1]
-    here = turned.shape[1]
-    turned[...] = jnp.swapaxes(x_ref[...], 0, 1).astype(jnp.bfloat16)
-    low = low_ref[:here].astype(jnp.bfloat16)
-    high = high_ref[:here].astype(jnp.bfloat16)
     for p in range(count):
         place = jnp.bitwise_xor(z, p)
-        early, late = outs[2 * p : 2 * p + 2]
-        for rho in range(slab + 1):
-            row = row_of(place, rho, slab, count, rows)
-            if rho <= half:
-                early[rho + 1] = turned[row]
-            else:
-                late[rho - half - 1] = turned[row]
-        early[0] = turned[row_of(place, -1, slab, count, rows)]
+        for rho in range(half + 1, slab + 1):
+            outs[p][rho - half - 1] = turned[row_of(place, rho, slab, count, rows)]
+
+
+def early_kernel(count, slab, half, rows, z_ref, turned, low_ref, high_ref, *outs):
+    z = z_ref[0]
+    here = turned.shape[1]
+    for p in range(count):
+        place = jnp.bitwise_xor(z, p)
+        for rho in range(-1, half + 1):
+            outs[p][rho + 1] = turned[row_of(place, rho, slab, count, rows)]
 
         @pl.when(place == 0)
         def _():
-            early[0] = low
+            outs[p][0] = low_ref[:here].astype(jnp.bfloat16)
 
         @pl.when(place == count - 1)
         def _():
-            early[0] = high
+            outs[p][0] = high_ref[:here].astype(jnp.bfloat16)
 
 
 def masks(cells):
@@ -80,29 +83,13 @@
     )
 
 
-def setup_kernel(
-    groups,
-    modes_here,
-    z_ref,
-    entry_ref,
-    value_ref,
-    mean_ref,
-    fields_ref,
-    low_ref,
-    high_ref,
-    dense_ref,
-    own_ref,
-    weight_ref,
-    faces_ref,
-    inverse_ref,
-):
-    fields, rows, cells = fields_ref.shape
+def dense_kernel(groups, fields, modes_here, z_ref, entry_ref, value_ref, dense_ref, own_ref):
     size = dense_ref.shape[1]
     entries = entry_ref.shape[1]
     flip = z_ref[0] * modes_here
     mode_id = jnp.bitwise_xor(lax.broadcasted_iota(jnp.int32, (size, entries), 0), flip)
     pick = jnp.where(mode_id == entry_ref[0:1], 1.0, 0.0).astype(jnp.bfloat16)
-    depth = -(-(fields + 1) // 16) * 16
+    depth = -(-fields // 16) * 16
     here = lax.broadcasted_iota(jnp.int32, (depth, entries), 0) == entry_ref[2:3]
     partner = jnp.where(here, entry_ref[1:2].astype(jnp.float32), 0.0).astype(jnp.bfloat16)
     value = jnp.where(here, value_ref[...], 0.0).astype(jnp.bfloat16)
@@ -115,31 +102,43 @@
     for g in range(groups):
         for k in range(GROUP):
             at = 1 + g * GROUP + k
-            if at > fields:
+            if at >= fields:
                 tile = jnp.zeros((size, size), jnp.float32)
             else:
                 tile = jnp.where(
                     column == partner_of[:, at : at + 1], value_of[:, at : at + 1], 0.0
                 )
             dense_ref[g, :, k * size : (k + 1) * size] = tile.astype(jnp.bfloat16)
+
+
+def weight_kernel(
+    mean_ref, fields_ref, low_ref, high_ref, weight_ref, faces_ref, inverse_ref, stack_ref, turned
+):
+    fields, rows, cells = fields_ref.shape
+    deep = stack_ref.shape[0]
     mask_set = masks(cells)
+    start = low_ref.shape[0] - deep
+    stack_ref[0] = mean_ref[...]
+    stack_ref[1 : fields + 1] = fields_ref[...]
+    stack_ref[fields + 1 :] = jnp.zeros((deep - fields - 1, rows, cells), jnp.float32)
+    turned[...] = jnp.swapaxes(stack_ref[...], 0, 1)
+    for row in range(rows):
+        centre = turned[row]
+        up = high_ref[start:, :] if row == rows - 1 else turned[row + 1]
+        down = low_ref[start:, :] if row == 0 else turned[row - 1]
+        for f, other in enumerate((up, down) + beside(centre, mask_set)):
+            weight_ref[row, f] = 0.5 * (centre + other)
     place = lax.broadcasted_iota(jnp.int32, (rows, cells), 0)
-    start = low_ref.shape[0] - fields - 1
-    for field in range(fields + 1):
-        centre = mean_ref[...] if field == 0 else fields_ref[field - 1]
-        low = low_ref[start + field : start + field + 1, :]
-        high = high_ref[start + field : start + field + 1, :]
-        up = jnp.where(place == rows - 1, high, pltpu.roll(centre, rows - 1, 0))
-        down = jnp.where(place == 0, low, pltpu.roll(centre, 1, 0))
-        diag = None
-        for f, other in enumerate((up, down) + beside(centre, mask_set)):
-            weight = 0.5 * (centre + other)
-            weight_ref[f, field] = weight
-            if field == 0:
-                diag = weight if diag is None else diag + weight
-                faces_ref[f] = weight if f < 2 else weight * mask_set[f - 2]
-        if field == 0:
-            inverse_ref[...] = 1.0 / diag
+    centre = mean_ref[...]
+    high, low = high_ref[start : start + 1, :], low_ref[start : start + 1, :]
+    up = jnp.where(place == rows - 1, high, pltpu.roll(centre, rows - 1, 0))
+    down = jnp.where(place == 0, low, pltpu.roll(centre, 1, 0))
+    diag = None
+    for f, other in enumerate((up, down) + beside(centre, mask_set)):
+        weight = 0.5 * (centre + other)
+        diag = weight if diag is None else diag + weight
+        faces_ref[f] = weight if f < 2 else weight * mask_set[f - 2]
+    inverse_ref[...] = 1.0 / diag
 
 
 def mix_kernel(count, slab, half, groups, fields, window, begin, z_ref, *refs):
@@ -156,13 +155,13 @@
             rows_ref[k, p * here : (p + 1) * here, :] = sources[array * count + p][row]
     mask_set = masks(cells)
     z = z_ref[0]
-    rows = weight_ref.shape[2]
+    rows = weight_ref.shape[0]
     ahead = jnp.where(z < count // 2, 0, 1)
     faces = (ahead, 1 - ahead, 2, 3, 4, 5)
 
     def each_row(r, carry):
         row = row_of(z, begin + r, slab, count, rows)
-        mean_weights = [weight_ref[f, 0, pl.ds(row, 1), :] for f in faces]
+        mean_weights = [weight_ref[row, f, 0:1, :] for f in faces]
         for t in range(0, size, 16):
             at = slice(t, t + 16)
             centre = rows_ref[r + 1, at].astype(jnp.float32)
@@ -178,7 +177,7 @@
             for k in range(GROUP):
                 field = min(1 + g * GROUP + k, fields - 1)
                 weights = [
-                    jnp.broadcast_to(weight_ref[f, field, pl.ds(row, 1), :], (16, cells))
+                    jnp.broadcast_to(weight_ref[row, f, field : field + 1, :], (16, cells))
                     for f in faces
                 ]
                 weights = [w.astype(bf16) for w in weights]
@@ -240,49 +239,86 @@
     bf16 = jnp.bfloat16
     params = pltpu.CompilerParams(vmem_limit_bytes=VMEM_LIMIT)
 
+    deep = -(-fields // 8) * 8
+
     upward = [(i, i + 1) for i in range(doms - 1)]
     downward = [(b, a) for a, b in upward]
+    filler = jnp.zeros((deep - fields, cells), jnp.float32)
     low_rim, high_rim = (
         lax.ppermute(
-            jnp.concatenate([iterate[:, at], mean_coef[at][None], kl_fields[:, at]], 0), "dom", pairs
+            jnp.concatenate([iterate[:, at], mean_coef[at][None], kl_fields[:, at], filler], 0),
+            "dom",
+            pairs,
         )
         for at, pairs in ((rows - 1, upward), (0, downward))
     )
-
-    packed = pl.pallas_call(
-        functools.partial(pack_kernel, count, slab, half, rows),
-        out_shape=[
-            jax.ShapeDtypeStruct((half + 2, here, cells), bf16),
-            jax.ShapeDtypeStruct((slab - half, here, cells), bf16),
-        ]
-        * count,
+    turned = pl.pallas_call(
+        turn_kernel,
+        out_shape=jax.ShapeDtypeStruct((rows, here, cells), bf16),
+        in_specs=in_vmem(1),
+        out_specs=in_vmem(1)[0],
+        compiler_params=params,
+        cost_estimate=SMALL,
+        name="turn",
+    )(iterate)
+    early = pl.pallas_call(
+        functools.partial(early_kernel, count, slab, half, rows),
+        out_shape=[jax.ShapeDtypeStruct((half + 2, here, cells), bf16)] * count,
         in_specs=[in_smem()] + in_vmem(3),
-        out_specs=in_vmem(2 * count),
-        scratch_shapes=[pltpu.VMEM((rows, here, cells), bf16)],
-        compiler_params=params,
-        name="pack",
-    )(z_arg, iterate, low_rim, high_rim)
+        out_specs=in_vmem(count),
+        compiler_params=params,
+        cost_estimate=SMALL,
+        name="early",
+    )(z_arg, turned, low_rim, high_rim)
 
     def swap(array, p):
+        if p == 0:
+            return array
         return lax.ppermute(array, "mode", [(i, i ^ p) for i in range(count)])
 
-    early = [packed[0]] + [swap(packed[2 * p], p) for p in range(1, count)]
-    late = [packed[1]] + [swap(packed[2 * p + 1], p) for p in range(1, count)]
-
-    dense, own, weights, faces, inverse = pl.pallas_call(
-        functools.partial(setup_kernel, groups, here),
+    entries, values, low_coef, high_coef, _ = lax.optimization_barrier(
+        (tri_index, tri_value, low_rim, high_rim, early[0])
+    )
+    early = [swap(e, p) for p, e in enumerate(early)]
+    dense, own = pl.pallas_call(
+        functools.partial(dense_kernel, groups, fields, here),
         out_shape=[
             jax.ShapeDtypeStruct((groups, size, GROUP * size), bf16),
             jax.ShapeDtypeStruct((size, 128), jnp.float32),
-            jax.ShapeDtypeStruct((6, fields, rows, cells), jnp.float32),
+        ],
+        in_specs=[in_smem()] + in_vmem(2),
+        out_specs=in_vmem(2),
+        compiler_params=params,
+        cost_estimate=SMALL,
+        name="dense",
+    )(z_arg, entries.T, values[None])
+    weights, faces, inverse = pl.pallas_call(
+        weight_kernel,
+        out_shape=[
+            jax.ShapeDtypeStruct((rows, 6, deep, cells), jnp.float32),
             jax.ShapeDtypeStruct((6, rows, cells), jnp.float32),
             jax.ShapeDtypeStruct((rows, cells), jnp.float32),
         ],
-        in_specs=[in_smem()] + in_vmem(6),
-        out_specs=in_vmem(5),
-        compiler_params=params,
-        name="setup",
-    )(z_arg, tri_index.T, tri_value[None], mean_coef, kl_fields, low_rim, high_rim)
+        in_specs=in_vmem(4),
+        out_specs=in_vmem(3),
+        scratch_shapes=[
+            pltpu.VMEM((deep, rows, cells), jnp.float32),
+            pltpu.VMEM((rows, deep, cells), jnp.float32),
+        ],
+        compiler_params=params,
+        cost_estimate=SMALL,
+        name="weights",
+    )(mean_coef, kl_fields, low_coef, high_coef)
+    late = pl.pallas_call(
+        functools.partial(late_kernel, count, slab, half, rows),
+        out_shape=[jax.ShapeDtypeStruct((slab - half, here, cells), bf16)] * count,
+        in_specs=[in_smem()] + in_vmem(2),
+        out_specs=in_vmem(count),
+        compiler_params=params,
+        cost_estimate=SMALL,
+        name="late",
+    )(z_arg, turned, inverse)
+    late = [swap(a, p) for p, a in enumerate(late)]
 
     def mix(arrays, window, begin):
         flat = [a for group in arrays for a in group]
@@ -302,11 +338,9 @@
         )(z_arg, *flat, dense, own, weights)
 
     window = tuple((0, k) for k in range(half + 2))
-    mixed_early = mix([early], window, 0)
-    back_early = [mixed_early[0]] + [swap(mixed_early[p], p) for p in range(1, count)]
+    back_early = [swap(a, p) for p, a in enumerate(mix([early], window, 0))]
     window = ((0, half), (0, half + 1)) + tuple((1, k) for k in range(slab - half))
-    mixed_late = mix([early, late], window, half)
-    back_late = [mixed_late[0]] + [swap(mixed_late[p], p) for p in range(1, count)]
+    back_late = [swap(a, p) for p, a in enumerate(mix([early, late], window, half))]
 
     outer = jnp.stack([b[0] for b in back_early])
     bottom = lax.dynamic_index_in_dim(outer, z, 0, keepdims=False).astype(jnp.float32)

time: 85.1 us -> 81.4 us (0.957)
  the two profiles are of different devices: /device:TPU:11 before, /device:TPU:4 now
where the time goes in v2:
time: 81.4 us; the launch traced here: 81 us
  starting transfers between devices  32.9 us (40%)
  Pallas kernels  27.6 us (34%)
  waiting for transfers between devices  10.8 us (13%)
  local copies, waits for them, and re-layouts  8.1 us (10%)
  between operations  0.88 us (1%)
    ppermute x12, starting transfers between devices, swap(): return lax.ppermute(array, 'mode', [(i, i ^ p) for i in range(count)])  23.8 us
    pallas_call x2, Pallas kernels, mix(): pl.pallas_call(functools.partial(mix_kernel, count, slab, half, groups, f...  18.4 us
    ppermute x12, waiting for transfers between devices, swap(): return lax.ppermute(array, 'mode', [(i, i ^ p) for i in range(count)])  4.91 us
    unnamed x16, local copies, waits for them, and re-layouts  4.84 us
    pallas_call x1, Pallas kernels, body(): pl.pallas_call(functools.partial(post_kernel, count, slab, half, rows, rh...  4.79 us
    ppermute x2, starting transfers between devices, body(): lax.ppermute(jnp.concatenate([iterate[:, at], mean_coef[at][None], kl_fie...  4.69 us
    ppermute x1, waiting for transfers between devices, body(): low = lax.ppermute(first_top, 'dom', upward)  3.17 us
    pallas_call x1, Pallas kernels, body(): pl.pallas_call(functools.partial(dense_kernel, groups, fields, here), out...  2.84 us
  transfers between devices with their start and end apart: 16, of which 4 were waited for; matrix products, arithmetic and copies ran while one was open for 0% of the time, Pallas kernels for 28%

profile of v2, /device:TPU:4, one launch (start us, length us, event | category | flops | bytes accessed | tf_op | source)
XLA Modules:
  0.0 81.0 jit_solution(8697010117068364843)
XLA Ops:
  1.4 1.0 %fusion.6 = (f32[20,1,256]{2,1,0:T(1,128)S(1)}, f32[20,1,256]{2,1,0:T(1,128)S(1)}) fusion(f32[20,32,256]{2,1,0:T(8,128)} %fields_ref.1), kind=kLoop, calls=%fused_computation.17 | loop fusion | bytes 81920 | tf_op jit(solution)/shard_map/slice | solution.py:249
  2.4 1.3 %fusion.5 = (f32[64,1,256]{2,1,0:T(1,128)S(1)}, f32[64,1,256]{2,1,0:T(1,128)S(1)}) fusion(f32[64,32,256]{2,1,0:T(8,128)} %refs_9_.1), kind=kLoop, calls=%fused_computation.16 | loop fusion | bytes 262144 | tf_op jit(solution)/shard_map/slice | solution.py:249
  4.5 2.8 %collective-permute-start.1 = (f32[88,256]{1,0:T(8,128)}, f32[88,256]{1,0:T(8,128)S(1)}, u32[]{:S(2)}, u32[]{:S(2)}) collective-permute-start(f32[88,256]{1,0:T(8,128)} %get-tuple-element.64), channel_id=1, source_target_pairs={{4,0},{8,4},{12,8},{16,12},{20,16},{24,20},{28,24},{5,1},{9,5},{13... | collective-permute-start | bytes 270344 | tf_op jit(solution)/shard_map/ppermute | solution.py:248
  7.3 1.9 %collective-permute-start = (f32[88,256]{1,0:T(8,128)S(1)}, f32[88,256]{1,0:T(8,128)S(1)}, u32[]{:S(2)}, u32[]{:S(2)}) collective-permute-start(f32[88,256]{1,0:T(8,128)S(1)} %get-tuple-element.65), channel_id=1, source_target_pairs={{0,4},{4,8},{8,12},{12,16},{16,20},{20,24},{24,28},{1,5},{5,9},{9,... | collective-permute-start | bytes 270344 | tf_op jit(solution)/shard_map/ppermute | solution.py:248
  9.2 1.6 %copy-done.1 = f32[64,32,256]{2,1,0:T(8,128)S(1)} copy-done((f32[64,32,256]{2,1,0:T(8,128)S(1)}, f32[64,32,256]{2,1,0:T(8,128)}, u32[]{:S(2)}) %copy-start.1) | copy-done | bytes 2097176
  11.3 2.7 %collective-permute-done.low_ref = f32[88,256]{1,0:T(8,128)S(1)} collective-permute-done((f32[88,256]{1,0:T(8,128)S(1)}, f32[88,256]{1,0:T(8,128)S(1)}, u32[]{:S(2)}, u32[]{:S(2)}) %collective-permute-start) | collective-permute-done | bytes 90144 | tf_op jit(solution)/shard_map/ppermute | solution.py:248
  14.1 1.6 %collective-permute-start.2 = (bf16[6,64,256]{2,1,0:T(8,128)(2,1)S(1)}, bf16[6,64,256]{2,1,0:T(8,128)(2,1)S(1)}, u32[]{:S(2)}, u32[]{:S(2)}) collective-permute-start(bf16[6,64,256]{2,1,0:T(8,128)(2,1)S(1)} %get-tuple-element.28), channel_id=1, source_target_pairs={{0,1},{1,0},{2,3},{3,2},{4,5},{5,4},{6,7},{7,6},{8,9},{9,8},{10,11... | collective-permute-start | bytes 589832 | tf_op jit(solution)/shard_map/ppermute | solution.py:277
  15.8 2.6 %collective-permute-start.3 = (bf16[6,64,256]{2,1,0:T(8,128)(2,1)S(1)}, bf16[6,64,256]{2,1,0:T(8,128)(2,1)S(1)}, u32[]{:S(2)}, u32[]{:S(2)}) collective-permute-start(bf16[6,64,256]{2,1,0:T(8,128)(2,1)S(1)} %get-tuple-element.29), channel_id=1, source_target_pairs={{0,2},{1,3},{2,0},{3,1},{4,6},{5,7},{6,4},{7,5},{8,10},{9,11},{10,... | collective-permute-start | bytes 589832 | tf_op jit(solution)/shard_map/ppermute | solution.py:277
  18.6 1.1 %copy-done.4 = f32[20,32,256]{2,1,0:T(8,128)S(1)} copy-done((f32[20,32,256]{2,1,0:T(8,128)S(1)}, f32[20,32,256]{2,1,0:T(8,128)}, u32[]{:S(2)}) %copy-start.4) | copy-done | bytes 655384
  20.6 2.1 %copy-done = f32[32,6,24,256]{3,2,1,0:T(8,128)} copy-done((f32[32,6,24,256]{3,2,1,0:T(8,128)}, f32[32,6,24,256]{3,2,1,0:T(8,128)S(1)}, u32[]{:S(2)}) %copy-start) | copy-done | bytes 4718616
  23.7 3.6 %collective-permute-start.9 = (bf16[4,64,256]{2,1,0:T(8,128)(2,1)S(1)}, bf16[4,64,256]{2,1,0:T(8,128)(2,1)S(1)}, u32[]{:S(2)}, u32[]{:S(2)}) collective-permute-start(bf16[4,64,256]{2,1,0:T(8,128)(2,1)S(1)} %get-tuple-element.45), channel_id=1, source_target_pairs={{0,2},{1,3},{2,0},{3,1},{4,6},{5,7},{6,4},{7,5},{8,10},{9,11},{10,... | collective-permute-start | bytes 393224 | tf_op jit(solution)/shard_map/ppermute | solution.py:277
  27.3 2.8 %dense.1 = (bf16[4,256,1280]{2,1,0:T(8,128)(2,1)S(1)}, f32[256,128]{1,0:T(8,128)S(1)}) custom-call(s32[1]{0:T(128)} %bitcast.z_ref, s32[3,5376]{1,0:T(4,128)S(1)} %bitcast.30, f32[1,5376]{1,0:T(1,128)S(1)} %broadcast_in_dim.9.value_ref), custom_call_target="tpu_custom_call" | custom-call | flops 1 | bytes 1 | tf_op jit(solution)/shard_map/dense/pallas_call | solution.py:283
  30.4 4.0 %collective-permute-done.3.refs_2_ = bf16[6,64,256]{2,1,0:T(8,128)(2,1)S(1)} collective-permute-done((bf16[6,64,256]{2,1,0:T(8,128)(2,1)S(1)}, bf16[6,64,256]{2,1,0:T(8,128)(2,1)S(1)}, u32[]{:S(2)}, u32[]{:S(2)}) %collective-permute-start.3) | collective-permute-done | bytes 196640 | tf_op jit(solution)/shard_map/ppermute | solution.py:277
  34.4 9.1 %mix.2 = (bf16[4,64,256]{2,1,0:T(8,128)(2,1)S(1)}, bf16[4,64,256]{2,1,0:T(8,128)(2,1)S(1)}, bf16[4,64,256]{2,1,0:T(8,128)(2,1)S(1)}, bf16[4,64,256]{2,1,0:T(8,128)(2,1)S(1)}) custom-call(s32[1]{0:T(128)} %bitcast.z_ref, bf16[6,64,256]{2,1,0:T(8,128)(2,1)S(1)} %get-tuple-element.27.refs_0_, bf16[6,64,256]{2,1,0:T(8,128)(2,1)S(1)} %collective-permute-done.2.refs_1_, ...), custom_call_target="tpu_custom_call" | custom-call | tf_op jit(solution)/shard_map/mix/pallas_call | solution.py:325
  43.5 7.9 %collective-permute-start.5 = (bf16[4,64,256]{2,1,0:T(8,128)(2,1)S(1)}, bf16[4,64,256]{2,1,0:T(8,128)(2,1)S(1)}, u32[]{:S(2)}, u32[]{:S(2)}) collective-permute-start(bf16[4,64,256]{2,1,0:T(8,128)(2,1)S(1)} %get-tuple-element.39), channel_id=1, source_target_pairs={{0,1},{1,0},{2,3},{3,2},{4,5},{5,4},{6,7},{7,6},{8,9},{9,8},{10,11... | collective-permute-start | bytes 393224 | tf_op jit(solution)/shard_map/ppermute | solution.py:277
  52.2 1.7 %collective-permute-start.7 = (bf16[4,64,256]{2,1,0:T(8,128)(2,1)S(1)}, bf16[4,64,256]{2,1,0:T(8,128)(2,1)S(1)}, u32[]{:S(2)}, u32[]{:S(2)}) collective-permute-start(bf16[4,64,256]{2,1,0:T(8,128)(2,1)S(1)} %get-tuple-element.41), channel_id=1, source_target_pairs={{0,3},{1,2},{2,1},{3,0},{4,7},{5,6},{6,5},{7,4},{8,11},{9,10},{10,... | collective-permute-start | bytes 393224 | tf_op jit(solution)/shard_map/ppermute | solution.py:277
  53.9 9.3 %mix.3 = (bf16[4,64,256]{2,1,0:T(8,128)(2,1)S(1)}, bf16[4,64,256]{2,1,0:T(8,128)(2,1)S(1)}, bf16[4,64,256]{2,1,0:T(8,128)(2,1)S(1)}, bf16[4,64,256]{2,1,0:T(8,128)(2,1)S(1)}) custom-call(s32[1]{0:T(128)} %bitcast.z_ref, bf16[6,64,256]{2,1,0:T(8,128)(2,1)S(1)} %get-tuple-element.27.refs_0_, bf16[6,64,256]{2,1,0:T(8,128)(2,1)S(1)} %collective-permute-done.2.refs_1_, ...), custom_call_target="tpu_custom_call" | custom-call | tf_op jit(solution)/shard_map/mix/pallas_call | solution.py:325
  63.2 1.1 %collective-permute-start.11 = (bf16[4,64,256]{2,1,0:T(8,128)(2,1)S(1)}, bf16[4,64,256]{2,1,0:T(8,128)(2,1)S(1)}, u32[]{:S(2)}, u32[]{:S(2)}) collective-permute-start(bf16[4,64,256]{2,1,0:T(8,128)(2,1)S(1)} %get-tuple-element.48), channel_id=1, source_target_pairs={{0,1},{1,0},{2,3},{3,2},{4,5},{5,4},{6,7},{7,6},{8,9},{9,8},{10,11... | collective-permute-start | bytes 393224 | tf_op jit(solution)/shard_map/ppermute | solution.py:277
  64.3 1.6 %collective-permute-start.12 = (bf16[4,64,256]{2,1,0:T(8,128)(2,1)S(1)}, bf16[4,64,256]{2,1,0:T(8,128)(2,1)S(1)}, u32[]{:S(2)}, u32[]{:S(2)}) collective-permute-start(bf16[4,64,256]{2,1,0:T(8,128)(2,1)S(1)} %get-tuple-element.49), channel_id=1, source_target_pairs={{0,2},{1,3},{2,0},{3,1},{4,6},{5,7},{6,4},{7,5},{8,10},{9,11},{10,... | collective-permute-start | bytes 393224 | tf_op jit(solution)/shard_map/ppermute | solution.py:277
  66.0 1.7 %collective-permute-start.13 = (bf16[4,64,256]{2,1,0:T(8,128)(2,1)S(1)}, bf16[4,64,256]{2,1,0:T(8,128)(2,1)S(1)}, u32[]{:S(2)}, u32[]{:S(2)}) collective-permute-start(bf16[4,64,256]{2,1,0:T(8,128)(2,1)S(1)} %get-tuple-element.50), channel_id=1, source_target_pairs={{0,3},{1,2},{2,1},{3,0},{4,7},{5,6},{6,5},{7,4},{8,11},{9,10},{10,... | collective-permute-start | bytes 393224 | tf_op jit(solution)/shard_map/ppermute | solution.py:277
  67.8 1.9 %collective-permute-start.15 = (f32[64,256]{1,0:T(8,128)S(1)}, f32[64,256]{1,0:T(8,128)S(1)}, u32[]{:S(2)}, u32[]{:S(2)}) collective-permute-start(f32[64,256]{1,0:T(8,128)S(1)} %get-tuple-element.58), channel_id=1, source_target_pairs={{4,0},{8,4},{12,8},{16,12},{20,16},{24,20},{28,24},{5,1},{9,5},{13... | collective-permute-start | bytes 196616 | tf_op jit(solution)/shard_map/ppermute | solution.py:351
  69.7 2.4 %collective-permute-start.14 = (f32[64,256]{1,0:T(8,128)S(1)}, f32[64,256]{1,0:T(8,128)S(1)}, u32[]{:S(2)}, u32[]{:S(2)}) collective-permute-start(f32[64,256]{1,0:T(8,128)S(1)} %get-tuple-element.59), channel_id=1, source_target_pairs={{0,4},{4,8},{8,12},{12,16},{16,20},{20,24},{24,28},{1,5},{5,9},{9,... | collective-permute-start | bytes 196616 | tf_op jit(solution)/shard_map/ppermute | solution.py:350
  73.0 3.2 %collective-permute-done.14.refs_10_ = f32[64,256]{1,0:T(8,128)S(1)} collective-permute-done((f32[64,256]{1,0:T(8,128)S(1)}, f32[64,256]{1,0:T(8,128)S(1)}, u32[]{:S(2)}, u32[]{:S(2)}) %collective-permute-start.14) | collective-permute-done | bytes 65568 | tf_op jit(solution)/shard_map/ppermute | solution.py:350
  76.2 4.8 %post.1 = (f32[64,32,256]{2,1,0:T(8,128)}, f32[64,32,256]{2,1,0:T(8,128)}) custom-call(s32[1]{0:T(128)} %bitcast.z_ref, bf16[4,64,256]{2,1,0:T(8,128)(2,1)S(1)} %get-tuple-element.38.refs_0_, bf16[4,64,256]{2,1,0:T(8,128)(2,1)S(1)} %collective-permute-done.5.refs_1_, bf16[4,64,256]{2,1,0:T(8,128)(2,1)S(1)} %collective-permute-done.6.refs_2_, ...), custom_call_target="tpu_custom_call" | custom-call | tf_op jit(solution)/shard_map/post/pallas_call | solution.py:360
  (49 shorter events, 6.2 us)
Async XLA Ops:
  4.5 6.8 %collective-permute-start.1 = (f32[88,256]{1,0:T(8,128)}, f32[88,256]{1,0:T(8,128)S(1)}, u32[]{:S(2)}, u32[]{:S(2)}) collective-permute-start(f32[88,256]{1,0:T(8,128)} %get-tuple-element.64), channel_id=1, source_target_pairs={{4,0},{8,4},{12,8},{16,12},{20,16},{24,20},{28,24},{5,1},{9,5},{13... | collective-permute-start | bytes 270344 | tf_op jit(solution)/shard_map/ppermute | solution.py:248
  7.3 6.7 %collective-permute-start = (f32[88,256]{1,0:T(8,128)S(1)}, f32[88,256]{1,0:T(8,128)S(1)}, u32[]{:S(2)}, u32[]{:S(2)}) collective-permute-start(f32[88,256]{1,0:T(8,128)S(1)} %get-tuple-element.65), channel_id=1, source_target_pairs={{0,4},{4,8},{8,12},{12,16},{16,20},{20,24},{24,28},{1,5},{5,9},{9,... | collective-permute-start | bytes 270344 | tf_op jit(solution)/shard_map/ppermute | solution.py:248
  9.2 1.6 %copy-start.1 = (f32[64,32,256]{2,1,0:T(8,128)S(1)}, f32[64,32,256]{2,1,0:T(8,128)}, u32[]{:S(2)}) copy-start(f32[64,32,256]{2,1,0:T(8,128)} %refs_9_.1) | copy-start | bytes 6291460
  10.8 7.8 %copy-start.6 = (f32[32,256]{1,0:T(8,128)S(1)}, f32[32,256]{1,0:T(8,128)}, u32[]{:S(2)}) copy-start(f32[32,256]{1,0:T(8,128)} %mean_ref.1) | copy-start | bytes 98308
  10.8 16.5 %copy-start.5 = (s32[5376,3]{0,1:T(4,128)S(1)}, s32[5376,3]{0,1:T(4,128)}, u32[]{:S(2)}) copy-start(s32[5376,3]{0,1:T(4,128)} %param.10) | copy-start | bytes 193540
  11.3 12.3 %copy-start.3 = (f32[64,32,256]{2,1,0:T(8,128)S(1)}, f32[64,32,256]{2,1,0:T(8,128)}, u32[]{:S(2)}) copy-start(f32[64,32,256]{2,1,0:T(8,128)} %refs_8_.1) | copy-start | bytes 6291460
  14.1 16.0 %collective-permute-start.2 = (bf16[6,64,256]{2,1,0:T(8,128)(2,1)S(1)}, bf16[6,64,256]{2,1,0:T(8,128)(2,1)S(1)}, u32[]{:S(2)}, u32[]{:S(2)}) collective-permute-start(bf16[6,64,256]{2,1,0:T(8,128)(2,1)S(1)} %get-tuple-element.28), channel_id=1, source_target_pairs={{0,1},{1,0},{2,3},{3,2},{4,5},{5,4},{6,7},{7,6},{8,9},{9,8},{10,11... | collective-permute-start | bytes 589832 | tf_op jit(solution)/shard_map/ppermute | solution.py:277
  15.8 18.6 %collective-permute-start.3 = (bf16[6,64,256]{2,1,0:T(8,128)(2,1)S(1)}, bf16[6,64,256]{2,1,0:T(8,128)(2,1)S(1)}, u32[]{:S(2)}, u32[]{:S(2)}) collective-permute-start(bf16[6,64,256]{2,1,0:T(8,128)(2,1)S(1)} %get-tuple-element.29), channel_id=1, source_target_pairs={{0,2},{1,3},{2,0},{3,1},{4,6},{5,7},{6,4},{7,5},{8,10},{9,11},{10,... | collective-permute-start | bytes 589832 | tf_op jit(solution)/shard_map/ppermute | solution.py:277
  18.4 16.0 %collective-permute-start.4 = (bf16[6,64,256]{2,1,0:T(8,128)(2,1)S(1)}, bf16[6,64,256]{2,1,0:T(8,128)(2,1)S(1)}, u32[]{:S(2)}, u32[]{:S(2)}) collective-permute-start(bf16[6,64,256]{2,1,0:T(8,128)(2,1)S(1)} %get-tuple-element.30), channel_id=1, source_target_pairs={{0,3},{1,2},{2,1},{3,0},{4,7},{5,6},{6,5},{7,4},{8,11},{9,10},{10,... | collective-permute-start | bytes 589832 | tf_op jit(solution)/shard_map/ppermute | solution.py:277
  18.6 1.1 %copy-start.4 = (f32[20,32,256]{2,1,0:T(8,128)S(1)}, f32[20,32,256]{2,1,0:T(8,128)}, u32[]{:S(2)}) copy-start(f32[20,32,256]{2,1,0:T(8,128)} %fields_ref.1) | copy-start | bytes 1966084
  19.7 4.0 %copy-start.7 = (f32[5376]{0:T(1024)S(1)}, f32[5376]{0:T(1024)}, u32[]{:S(2)}) copy-start(f32[5376]{0:T(1024)} %param.11) | copy-start | bytes 64516
  20.6 2.2 %copy-start = (f32[32,6,24,256]{3,2,1,0:T(8,128)}, f32[32,6,24,256]{3,2,1,0:T(8,128)S(1)}, u32[]{:S(2)}) copy-start(f32[32,6,24,256]{3,2,1,0:T(8,128)S(1)} %get-tuple-element.37.refs_6_.refs_10_) | copy-start | bytes 14155780
  22.8 29.4 %collective-permute-start.8 = (bf16[4,64,256]{2,1,0:T(8,128)(2,1)S(1)}, bf16[4,64,256]{2,1,0:T(8,128)(2,1)S(1)}, u32[]{:S(2)}, u32[]{:S(2)}) collective-permute-start(bf16[4,64,256]{2,1,0:T(8,128)(2,1)S(1)} %get-tuple-element.44), channel_id=1, source_target_pairs={{0,1},{1,0},{2,3},{3,2},{4,5},{5,4},{6,7},{7,6},{8,9},{9,8},{10,11... | collective-permute-start | bytes 393224 | tf_op jit(solution)/shard_map/ppermute | solution.py:277
  23.7 30.2 %collective-permute-start.9 = (bf16[4,64,256]{2,1,0:T(8,128)(2,1)S(1)}, bf16[4,64,256]{2,1,0:T(8,128)(2,1)S(1)}, u32[]{:S(2)}, u32[]{:S(2)}) collective-permute-start(bf16[4,64,256]{2,1,0:T(8,128)(2,1)S(1)} %get-tuple-element.45), channel_id=1, source_target_pairs={{0,2},{1,3},{2,0},{3,1},{4,6},{5,7},{6,4},{7,5},{8,10},{9,11},{10,... | collective-permute-start | bytes 393224 | tf_op jit(solution)/shard_map/ppermute | solution.py:277
  30.1 23.8 %collective-permute-start.10 = (bf16[4,64,256]{2,1,0:T(8,128)(2,1)S(1)}, bf16[4,64,256]{2,1,0:T(8,128)(2,1)S(1)}, u32[]{:S(2)}, u32[]{:S(2)}) collective-permute-start(bf16[4,64,256]{2,1,0:T(8,128)(2,1)S(1)} %get-tuple-element.46), channel_id=1, source_target_pairs={{0,3},{1,2},{2,1},{3,0},{4,7},{5,6},{6,5},{7,4},{8,11},{9,10},{10,... | collective-permute-start | bytes 393224 | tf_op jit(solution)/shard_map/ppermute | solution.py:277
  43.5 22.4 %collective-permute-start.5 = (bf16[4,64,256]{2,1,0:T(8,128)(2,1)S(1)}, bf16[4,64,256]{2,1,0:T(8,128)(2,1)S(1)}, u32[]{:S(2)}, u32[]{:S(2)}) collective-permute-start(bf16[4,64,256]{2,1,0:T(8,128)(2,1)S(1)} %get-tuple-element.39), channel_id=1, source_target_pairs={{0,1},{1,0},{2,3},{3,2},{4,5},{5,4},{6,7},{7,6},{8,9},{9,8},{10,11... | collective-permute-start | bytes 393224 | tf_op jit(solution)/shard_map/ppermute | solution.py:277
  51.4 16.2 %collective-permute-start.6 = (bf16[4,64,256]{2,1,0:T(8,128)(2,1)S(1)}, bf16[4,64,256]{2,1,0:T(8,128)(2,1)S(1)}, u32[]{:S(2)}, u32[]{:S(2)}) collective-permute-start(bf16[4,64,256]{2,1,0:T(8,128)(2,1)S(1)} %get-tuple-element.40), channel_id=1, source_target_pairs={{0,2},{1,3},{2,0},{3,1},{4,6},{5,7},{6,4},{7,5},{8,10},{9,11},{10,... | collective-permute-start | bytes 393224 | tf_op jit(solution)/shard_map/ppermute | solution.py:277
  52.2 15.5 %collective-permute-start.7 = (bf16[4,64,256]{2,1,0:T(8,128)(2,1)S(1)}, bf16[4,64,256]{2,1,0:T(8,128)(2,1)S(1)}, u32[]{:S(2)}, u32[]{:S(2)}) collective-permute-start(bf16[4,64,256]{2,1,0:T(8,128)(2,1)S(1)} %get-tuple-element.41), channel_id=1, source_target_pairs={{0,3},{1,2},{2,1},{3,0},{4,7},{5,6},{6,5},{7,4},{8,11},{9,10},{10,... | collective-permute-start | bytes 393224 | tf_op jit(solution)/shard_map/ppermute | solution.py:277
  53.9 22.3 %copy-start.2 = (f32[64,32,256]{2,1,0:T(8,128)S(1)}, f32[64,32,256]{2,1,0:T(8,128)}, u32[]{:S(2)}) copy-start(f32[64,32,256]{2,1,0:T(8,128)} %refs_9_.1) | copy-start | bytes 6291460
  63.2 8.9 %collective-permute-start.11 = (bf16[4,64,256]{2,1,0:T(8,128)(2,1)S(1)}, bf16[4,64,256]{2,1,0:T(8,128)(2,1)S(1)}, u32[]{:S(2)}, u32[]{:S(2)}) collective-permute-start(bf16[4,64,256]{2,1,0:T(8,128)(2,1)S(1)} %get-tuple-element.48), channel_id=1, source_target_pairs={{0,1},{1,0},{2,3},{3,2},{4,5},{5,4},{6,7},{7,6},{8,9},{9,8},{10,11... | collective-permute-start | bytes 393224 | tf_op jit(solution)/shard_map/ppermute | solution.py:277
  64.3 8.7 %collective-permute-start.12 = (bf16[4,64,256]{2,1,0:T(8,128)(2,1)S(1)}, bf16[4,64,256]{2,1,0:T(8,128)(2,1)S(1)}, u32[]{:S(2)}, u32[]{:S(2)}) collective-permute-start(bf16[4,64,256]{2,1,0:T(8,128)(2,1)S(1)} %get-tuple-element.49), channel_id=1, source_target_pairs={{0,2},{1,3},{2,0},{3,1},{4,6},{5,7},{6,4},{7,5},{8,10},{9,11},{10,... | collective-permute-start | bytes 393224 | tf_op jit(solution)/shard_map/ppermute | solution.py:277
  66.0 7.0 %collective-permute-start.13 = (bf16[4,64,256]{2,1,0:T(8,128)(2,1)S(1)}, bf16[4,64,256]{2,1,0:T(8,128)(2,1)S(1)}, u32[]{:S(2)}, u32[]{:S(2)}) collective-permute-start(bf16[4,64,256]{2,1,0:T(8,128)(2,1)S(1)} %get-tuple-element.50), channel_id=1, source_target_pairs={{0,3},{1,2},{2,1},{3,0},{4,7},{5,6},{6,5},{7,4},{8,11},{9,10},{10,... | collective-permute-start | bytes 393224 | tf_op jit(solution)/shard_map/ppermute | solution.py:277
  67.8 5.2 %collective-permute-start.15 = (f32[64,256]{1,0:T(8,128)S(1)}, f32[64,256]{1,0:T(8,128)S(1)}, u32[]{:S(2)}, u32[]{:S(2)}) collective-permute-start(f32[64,256]{1,0:T(8,128)S(1)} %get-tuple-element.58), channel_id=1, source_target_pairs={{4,0},{8,4},{12,8},{16,12},{20,16},{24,20},{28,24},{5,1},{9,5},{13... | collective-permute-start | bytes 196616 | tf_op jit(solution)/shard_map/ppermute | solution.py:351
  69.7 6.5 %collective-permute-start.14 = (f32[64,256]{1,0:T(8,128)S(1)}, f32[64,256]{1,0:T(8,128)S(1)}, u32[]{:S(2)}, u32[]{:S(2)}) collective-permute-start(f32[64,256]{1,0:T(8,128)S(1)} %get-tuple-element.59), channel_id=1, source_target_pairs={{0,4},{4,8},{8,12},{12,16},{16,20},{20,24},{24,28},{1,5},{5,9},{9,... | collective-permute-start | bytes 196616 | tf_op jit(solution)/shard_map/ppermute | solution.py:350

commit v3 on v2

--- a/solution.py
+++ b/solution.py
@@ -30,8 +30,25 @@
     return jnp.clip(row, 0, rows - 1)
 
 
-def turn_kernel(x_ref, turned):
-    turned[...] = jnp.swapaxes(x_ref[...], 0, 1).astype(jnp.bfloat16)
+def turn_kernel(x_ref, mean_ref, fields_ref, turned, last, first):
+    step = pl.program_id(0)
+    modes, rows, _ = x_ref.shape
+    block = jnp.swapaxes(x_ref[...], 0, 1)
+    turned[...] = block.astype(jnp.bfloat16)
+    at = pl.ds(pl.multiple_of(step * modes, modes), modes)
+    first[at, :] = block[0]
+    last[at, :] = block[rows - 1]
+
+    @pl.when(step == pl.num_programs(0) - 1)
+    def _():
+        fields = fields_ref.shape[0]
+        here = modes * pl.num_programs(0)
+        for out, row in ((first, 0), (last, rows - 1)):
+            out[here : here + 1, :] = mean_ref[row : row + 1, :]
+            for field in range(fields):
+                out[here + 1 + field : here + 2 + field, :] = fields_ref[field, row : row + 1, :]
+            rest = out.shape[0] - here - 1 - fields
+            out[here + 1 + fields :, :] = jnp.zeros((rest, out.shape[1]), jnp.float32)
 
 
 def late_kernel(count, slab, half, rows, z_ref, turned, after, *outs):
@@ -152,7 +169,8 @@
     bf16 = jnp.bfloat16
     for k, (array, row) in enumerate(window):
         for p in range(count):
-            rows_ref[k, p * here : (p + 1) * here, :] = sources[array * count + p][row]
+            part = sources[array * count + (count - p) % count]
+            rows_ref[k, p * here : (p + 1) * here, :] = part[row]
     mask_set = masks(cells)
     z = z_ref[0]
     rows = weight_ref.shape[0]
@@ -202,10 +220,10 @@
     updated, residual, image = refs[2 * count + 6 :]
     z = z_ref[0]
     modes, _, cells = source.shape
-    for p in range(count):
-        place = jnp.bitwise_xor(z, p)
+    for k in range(count):
+        place = jnp.bitwise_xor(z, (count - k) % count)
         for rho in range(slab):
-            part = early[p][rho] if rho < half else late[p][rho - half]
+            part = early[k][rho] if rho < half else late[k][rho - half]
             image[row_of(place, rho, slab, count, rows)] = part.astype(jnp.float32)
     residual[...] = source[...] - jnp.swapaxes(image[...], 0, 1)
     place = lax.broadcasted_iota(jnp.int32, (rows, cells), 0)
@@ -243,24 +261,25 @@
 
     upward = [(i, i + 1) for i in range(doms - 1)]
     downward = [(b, a) for a, b in upward]
-    filler = jnp.zeros((deep - fields, cells), jnp.float32)
-    low_rim, high_rim = (
-        lax.ppermute(
-            jnp.concatenate([iterate[:, at], mean_coef[at][None], kl_fields[:, at], filler], 0),
-            "dom",
-            pairs,
-        )
-        for at, pairs in ((rows - 1, upward), (0, downward))
-    )
-    turned = pl.pallas_call(
+    block = min(16, here)
+    rim_shape = jax.ShapeDtypeStruct((here + deep, cells), jnp.float32)
+    rim_spec = pl.BlockSpec((here + deep, cells), lambda i: (0, 0))
+    turned, last_rim, first_rim = pl.pallas_call(
         turn_kernel,
-        out_shape=jax.ShapeDtypeStruct((rows, here, cells), bf16),
-        in_specs=in_vmem(1),
-        out_specs=in_vmem(1)[0],
+        grid=(here // block,),
+        out_shape=[jax.ShapeDtypeStruct((rows, here, cells), bf16), rim_shape, rim_shape],
+        in_specs=[
+            pl.BlockSpec((block, rows, cells), lambda i: (i, 0, 0)),
+            pl.BlockSpec((rows, cells), lambda i: (0, 0)),
+            pl.BlockSpec((fields - 1, rows, cells), lambda i: (0, 0, 0)),
+        ],
+        out_specs=[pl.BlockSpec((rows, block, cells), lambda i: (0, i, 0)), rim_spec, rim_spec],
         compiler_params=params,
         cost_estimate=SMALL,
         name="turn",
-    )(iterate)
+    )(iterate, mean_coef, kl_fields)
+    low_rim = lax.ppermute(last_rim, "dom", upward)
+    high_rim = lax.ppermute(first_rim, "dom", downward)
     early = pl.pallas_call(
         functools.partial(early_kernel, count, slab, half, rows),
         out_shape=[jax.ShapeDtypeStruct((half + 2, here, cells), bf16)] * count,
@@ -271,15 +290,16 @@
         name="early",
     )(z_arg, turned, low_rim, high_rim)
 
-    def swap(array, p):
-        if p == 0:
-            return array
-        return lax.ppermute(array, "mode", [(i, i ^ p) for i in range(count)])
+    def swap(arrays):
+        taken = [arrays[0]]
+        for p in reversed(range(1, count)):
+            taken.append(lax.ppermute(arrays[p], "mode", [(i, i ^ p) for i in range(count)]))
+        return taken
 
     entries, values, low_coef, high_coef, _ = lax.optimization_barrier(
         (tri_index, tri_value, low_rim, high_rim, early[0])
     )
-    early = [swap(e, p) for p, e in enumerate(early)]
+    early = swap(early)
     dense, own = pl.pallas_call(
         functools.partial(dense_kernel, groups, fields, here),
         out_shape=[
@@ -317,8 +337,8 @@
         compiler_params=params,
         cost_estimate=SMALL,
         name="late",
-    )(z_arg, turned, inverse)
-    late = [swap(a, p) for p, a in enumerate(late)]
+    )(z_arg, turned, own)
+    late = swap(late)
 
     def mix(arrays, window, begin):
         flat = [a for group in arrays for a in group]
@@ -338,13 +358,15 @@
         )(z_arg, *flat, dense, own, weights)
 
     window = tuple((0, k) for k in range(half + 2))
-    back_early = [swap(a, p) for p, a in enumerate(mix([early], window, 0))]
+    back_early = swap(mix([early], window, 0))
     window = ((0, half), (0, half + 1)) + tuple((1, k) for k in range(slab - half))
-    back_late = [swap(a, p) for p, a in enumerate(mix([early, late], window, half))]
+    back_late = swap(mix([early, late], window, half))
 
     outer = jnp.stack([b[0] for b in back_early])
-    bottom = lax.dynamic_index_in_dim(outer, z, 0, keepdims=False).astype(jnp.float32)
-    top = lax.dynamic_index_in_dim(outer, z ^ (count - 1), 0, keepdims=False).astype(jnp.float32)
+    place_of = lambda p: (count - p) % count
+    bottom = lax.dynamic_index_in_dim(outer, place_of(z), 0, keepdims=False).astype(jnp.float32)
+    top = lax.dynamic_index_in_dim(outer, place_of(z ^ (count - 1)), 0, keepdims=False)
+    top = top.astype(jnp.float32)
     first_bottom = (source[:, 0] - bottom) * (inverse[0] / cheb_center)
     first_top = (source[:, -1] - top) * (inverse[-1] / cheb_center)
     low = lax.ppermute(first_top, "dom", upward)
@@ -353,7 +375,6 @@
     sigma = cheb_center / cheb_radius
     rho_zero = 1.0 / sigma
     rho_one = 1.0 / (2.0 * sigma - rho_zero)
-    block = min(16, here)
     image_spec = pl.BlockSpec((half, block, cells), lambda i: (0, i, 0))
     flat_spec = pl.BlockSpec((block, rows, cells), lambda i: (i, 0, 0))
     row_spec = pl.BlockSpec((block, cells), lambda i: (i, 0))

time: 81.4 us -> 81.5 us (level)
  the two profiles are of different devices: /device:TPU:4 before, /device:TPU:3 now
where the time goes in v3:
time: 81.5 us; the launch traced here: 80.6 us
  starting transfers between devices  32.8 us (40%)
  Pallas kernels  27.4 us (34%)
  waiting for transfers between devices  12.5 us (15%)
  local copies, waits for them, and re-layouts  6.92 us (8%)
  between operations  0.95 us (1%)
    ppermute x12, starting transfers between devices, swap(): lax.ppermute(arrays[p], 'mode', [(i, i ^ p) for i in range(count)])  19.8 us
    pallas_call x2, Pallas kernels, mix(): pl.pallas_call(functools.partial(mix_kernel, count, slab, half, groups, f...  18.1 us
    ppermute x12, waiting for transfers between devices, swap(): lax.ppermute(arrays[p], 'mode', [(i, i ^ p) for i in range(count)])  7.73 us
    unnamed x20, local copies, waits for them, and re-layouts  5.59 us
    ppermute x1, starting transfers between devices, body(): low = lax.ppermute(first_top, 'dom', upward)  4.85 us
    ppermute x1, waiting for transfers between devices, body(): high_rim = lax.ppermute(first_rim, 'dom', downward)  4.77 us
    pallas_call x1, Pallas kernels, body(): pl.pallas_call(functools.partial(post_kernel, count, slab, half, rows, rh...  4.74 us
    ppermute x1, starting transfers between devices, body(): low_rim = lax.ppermute(last_rim, 'dom', upward)  3.81 us
  transfers between devices with their start and end apart: 16, of which 3 were waited for; matrix products, arithmetic and copies ran while one was open for 2% of the time, Pallas kernels for 27%

profile of v3, /device:TPU:3, one launch (start us, length us, event | category | flops | bytes accessed | tf_op | source)
XLA Modules:
  0.0 80.6 jit_solution(6123117468329635235)
XLA Ops:
  0.6 1.6 %copy-done.1 = f32[64,32,256]{2,1,0:T(8,128)S(1)} copy-done((f32[64,32,256]{2,1,0:T(8,128)S(1)}, f32[64,32,256]{2,1,0:T(8,128)}, u32[]{:S(2)}) %copy-start.1) | copy-done | bytes 2097176
  2.2 1.1 %copy-done.3 = f32[20,32,256]{2,1,0:T(8,128)S(1)} copy-done((f32[20,32,256]{2,1,0:T(8,128)S(1)}, f32[20,32,256]{2,1,0:T(8,128)}, u32[]{:S(2)}) %copy-start.3) | copy-done | bytes 655384
  3.3 0.8 copy-done.6
  4.1 0.5 turn.1
  4.7 3.8 %collective-permute-start = (f32[88,256]{1,0:T(8,128)S(1)}, f32[88,256]{1,0:T(8,128)S(1)}, u32[]{:S(2)}, u32[]{:S(2)}) collective-permute-start(f32[88,256]{1,0:T(8,128)S(1)} %get-tuple-element.31), channel_id=1, source_target_pairs={{0,4},{4,8},{8,12},{12,16},{16,20},{20,24},{24,28},{1,5},{5,9},{9,... | collective-permute-start | bytes 270344 | tf_op jit(solution)/shard_map/ppermute | solution.py:281
  8.5 1.9 %collective-permute-start.1 = (f32[88,256]{1,0:T(8,128)S(1)}, f32[88,256]{1,0:T(8,128)S(1)}, u32[]{:S(2)}, u32[]{:S(2)}) collective-permute-start(f32[88,256]{1,0:T(8,128)S(1)} %get-tuple-element.32), channel_id=1, source_target_pairs={{4,0},{8,4},{12,8},{16,12},{20,16},{24,20},{28,24},{5,1},{9,5},{13... | collective-permute-start | bytes 270344 | tf_op jit(solution)/shard_map/ppermute | solution.py:282
  10.5 4.8 %collective-permute-done.1.high_ref = f32[88,256]{1,0:T(8,128)S(1)} collective-permute-done((f32[88,256]{1,0:T(8,128)S(1)}, f32[88,256]{1,0:T(8,128)S(1)}, u32[]{:S(2)}, u32[]{:S(2)}) %collective-permute-start.1) | collective-permute-done | bytes 90144 | tf_op jit(solution)/shard_map/ppermute | solution.py:282
  15.4 3.4 %collective-permute-start.2 = (bf16[6,64,256]{2,1,0:T(8,128)(2,1)S(1)}, bf16[6,64,256]{2,1,0:T(8,128)(2,1)S(1)}, u32[]{:S(2)}, u32[]{:S(2)}) collective-permute-start(bf16[6,64,256]{2,1,0:T(8,128)(2,1)S(1)} %get-tuple-element.34), channel_id=1, source_target_pairs={{0,3},{1,2},{2,1},{3,0},{4,7},{5,6},{6,5},{7,4},{8,11},{9,10},{10,... | collective-permute-start | bytes 589832 | tf_op jit(solution)/shard_map/ppermute | solution.py:296
  19.1 2.8 %dense.1 = (bf16[4,256,1280]{2,1,0:T(8,128)(2,1)S(1)}, f32[256,128]{1,0:T(8,128)S(1)}) custom-call(s32[1]{0:T(128)} %bitcast.z_ref, s32[3,5376]{1,0:T(4,128)S(1)} %bitcast.22, f32[1,5376]{1,0:T(1,128)S(1)} %broadcast_in_dim.2.value_ref), custom_call_target="tpu_custom_call" | custom-call | flops 1 | bytes 1 | tf_op jit(solution)/shard_map/dense/pallas_call | solution.py:303
  22.0 3.3 %collective-permute-start.8 = (bf16[4,64,256]{2,1,0:T(8,128)(2,1)S(1)}, bf16[4,64,256]{2,1,0:T(8,128)(2,1)S(1)}, u32[]{:S(2)}, u32[]{:S(2)}) collective-permute-start(bf16[4,64,256]{2,1,0:T(8,128)(2,1)S(1)} %get-tuple-element.49), channel_id=1, source_target_pairs={{0,3},{1,2},{2,1},{3,0},{4,7},{5,6},{6,5},{7,4},{8,11},{9,10},{10,... | collective-permute-start | bytes 393224 | tf_op jit(solution)/shard_map/ppermute | solution.py:296
  25.3 1.3 %fusion.4 = (f32[64,1,256]{2,1,0:T(1,128)S(1)}, f32[64,1,256]{2,1,0:T(1,128)S(1)}) fusion(f32[64,32,256]{2,1,0:T(8,128)} %refs_8_.1), kind=kLoop, calls=%fused_computation.9 | loop fusion | bytes 262144 | tf_op jit(solution)/shard_map/slice | solution.py:370
  26.7 0.9 %weights.1 = (f32[32,6,24,256]{3,2,1,0:T(8,128)S(1)}, f32[6,32,256]{2,1,0:T(8,128)S(1)}, f32[32,256]{1,0:T(8,128)S(1)}) custom-call(f32[32,256]{1,0:T(8,128)S(1)} %copy-done.7, f32[20,32,256]{2,1,0:T(8,128)S(1)} %copy-done.4, f32[88,256]{1,0:T(8,128)S(1)} %collective-permute-done.low_ref, f32[88,256]{1,0:T(8,128)S(1)} %collective-permute-done.1.high_ref), custom_call_target="tpu_custom_call" | custom-call | flops 1 | bytes 1 | tf_op jit(solution)/shard_map/weights/pallas_call | solution.py:315
  27.6 2.1 %copy-done = f32[32,6,24,256]{3,2,1,0:T(8,128)} copy-done((f32[32,6,24,256]{3,2,1,0:T(8,128)}, f32[32,6,24,256]{3,2,1,0:T(8,128)S(1)}, u32[]{:S(2)}) %copy-start) | copy-done | bytes 4718616
  29.8 5.5 %collective-permute-start.10 = (bf16[4,64,256]{2,1,0:T(8,128)(2,1)S(1)}, bf16[4,64,256]{2,1,0:T(8,128)(2,1)S(1)}, u32[]{:S(2)}, u32[]{:S(2)}) collective-permute-start(bf16[4,64,256]{2,1,0:T(8,128)(2,1)S(1)} %get-tuple-element.51), channel_id=1, source_target_pairs={{0,1},{1,0},{2,3},{3,2},{4,5},{5,4},{6,7},{7,6},{8,9},{9,8},{10,11... | collective-permute-start | bytes 393224 | tf_op jit(solution)/shard_map/ppermute | solution.py:296
  35.3 5.4 %collective-permute-done.3.refs_2_ = bf16[6,64,256]{2,1,0:T(8,128)(2,1)S(1)} collective-permute-done((bf16[6,64,256]{2,1,0:T(8,128)(2,1)S(1)}, bf16[6,64,256]{2,1,0:T(8,128)(2,1)S(1)}, u32[]{:S(2)}, u32[]{:S(2)}) %collective-permute-start.3) | collective-permute-done | bytes 196640 | tf_op jit(solution)/shard_map/ppermute | solution.py:296
  40.7 9.0 %mix.2 = (bf16[4,64,256]{2,1,0:T(8,128)(2,1)S(1)}, bf16[4,64,256]{2,1,0:T(8,128)(2,1)S(1)}, bf16[4,64,256]{2,1,0:T(8,128)(2,1)S(1)}, bf16[4,64,256]{2,1,0:T(8,128)(2,1)S(1)}) custom-call(s32[1]{0:T(128)} %bitcast.z_ref, bf16[6,64,256]{2,1,0:T(8,128)(2,1)S(1)} %get-tuple-element.33.refs_0_, bf16[6,64,256]{2,1,0:T(8,128)(2,1)S(1)} %collective-permute-done.2.refs_1_, ...), custom_call_target="tpu_custom_call" | custom-call | tf_op jit(solution)/shard_map/mix/pallas_call | solution.py:345
  49.7 3.3 %collective-permute-start.5 = (bf16[4,64,256]{2,1,0:T(8,128)(2,1)S(1)}, bf16[4,64,256]{2,1,0:T(8,128)(2,1)S(1)}, u32[]{:S(2)}, u32[]{:S(2)}) collective-permute-start(bf16[4,64,256]{2,1,0:T(8,128)(2,1)S(1)} %get-tuple-element.45), channel_id=1, source_target_pairs={{0,3},{1,2},{2,1},{3,0},{4,7},{5,6},{6,5},{7,4},{8,11},{9,10},{10,... | collective-permute-start | bytes 393224 | tf_op jit(solution)/shard_map/ppermute | solution.py:296
  52.9 0.4 collective-permute-start.7
  53.4 9.2 %mix.3 = (bf16[4,64,256]{2,1,0:T(8,128)(2,1)S(1)}, bf16[4,64,256]{2,1,0:T(8,128)(2,1)S(1)}, bf16[4,64,256]{2,1,0:T(8,128)(2,1)S(1)}, bf16[4,64,256]{2,1,0:T(8,128)(2,1)S(1)}) custom-call(s32[1]{0:T(128)} %bitcast.z_ref, bf16[6,64,256]{2,1,0:T(8,128)(2,1)S(1)} %get-tuple-element.33.refs_0_, bf16[6,64,256]{2,1,0:T(8,128)(2,1)S(1)} %collective-permute-done.2.refs_1_, ...), custom_call_target="tpu_custom_call" | custom-call | tf_op jit(solution)/shard_map/mix/pallas_call | solution.py:345
  62.5 3.3 %collective-permute-start.11 = (bf16[4,64,256]{2,1,0:T(8,128)(2,1)S(1)}, bf16[4,64,256]{2,1,0:T(8,128)(2,1)S(1)}, u32[]{:S(2)}, u32[]{:S(2)}) collective-permute-start(bf16[4,64,256]{2,1,0:T(8,128)(2,1)S(1)} %get-tuple-element.53), channel_id=1, source_target_pairs={{0,3},{1,2},{2,1},{3,0},{4,7},{5,6},{6,5},{7,4},{8,11},{9,10},{10,... | collective-permute-start | bytes 393224 | tf_op jit(solution)/shard_map/ppermute | solution.py:296
  66.3 2.4 %collective-permute-start.15 = (f32[64,256]{1,0:T(8,128)S(1)}, f32[64,256]{1,0:T(8,128)S(1)}, u32[]{:S(2)}, u32[]{:S(2)}) collective-permute-start(f32[64,256]{1,0:T(8,128)S(1)} %get-tuple-element.60), channel_id=1, source_target_pairs={{4,0},{8,4},{12,8},{16,12},{20,16},{24,20},{28,24},{5,1},{9,5},{13... | collective-permute-start | bytes 196616 | tf_op jit(solution)/shard_map/ppermute | solution.py:373
  68.7 4.8 %collective-permute-start.14 = (f32[64,256]{1,0:T(8,128)S(1)}, f32[64,256]{1,0:T(8,128)S(1)}, u32[]{:S(2)}, u32[]{:S(2)}) collective-permute-start(f32[64,256]{1,0:T(8,128)S(1)} %get-tuple-element.61), channel_id=1, source_target_pairs={{0,4},{4,8},{8,12},{12,16},{16,20},{20,24},{24,28},{1,5},{5,9},{9,... | collective-permute-start | bytes 196616 | tf_op jit(solution)/shard_map/ppermute | solution.py:372
  73.5 2.3 %collective-permute-done.12.refs_6_ = bf16[4,64,256]{2,1,0:T(8,128)(2,1)S(1)} collective-permute-done((bf16[4,64,256]{2,1,0:T(8,128)(2,1)S(1)}, bf16[4,64,256]{2,1,0:T(8,128)(2,1)S(1)}, u32[]{:S(2)}, u32[]{:S(2)}) %collective-permute-start.12) | collective-permute-done | bytes 131104 | tf_op jit(solution)/shard_map/ppermute | solution.py:296
  75.9 4.7 %post.1 = (f32[64,32,256]{2,1,0:T(8,128)}, f32[64,32,256]{2,1,0:T(8,128)}) custom-call(s32[1]{0:T(128)} %bitcast.z_ref, bf16[4,64,256]{2,1,0:T(8,128)(2,1)S(1)} %get-tuple-element.44.refs_0_, bf16[4,64,256]{2,1,0:T(8,128)(2,1)S(1)} %collective-permute-done.5.refs_1_, bf16[4,64,256]{2,1,0:T(8,128)(2,1)S(1)} %collective-permute-done.6.refs_2_, ...), custom_call_target="tpu_custom_call" | custom-call | tf_op jit(solution)/shard_map/post/pallas_call | solution.py:381
  (45 shorter events, 1.1 us)
Async XLA Ops:
  0.6 1.6 %copy-start.1 = (f32[64,32,256]{2,1,0:T(8,128)S(1)}, f32[64,32,256]{2,1,0:T(8,128)}, u32[]{:S(2)}) copy-start(f32[64,32,256]{2,1,0:T(8,128)} %refs_9_.1) | copy-start | bytes 6291460
  4.1 11.3 %copy-start.9 = (f32[5376]{0:T(1024)S(1)}, f32[5376]{0:T(1024)}, u32[]{:S(2)}) copy-start(f32[5376]{0:T(1024)} %param.11) | copy-start | bytes 64516
  4.1 15.0 %copy-start.8 = (s32[5376,3]{0,1:T(4,128)S(1)}, s32[5376,3]{0,1:T(4,128)}, u32[]{:S(2)}) copy-start(s32[5376,3]{0,1:T(4,128)} %param.10) | copy-start | bytes 193540
  4.6 22.0 %copy-start.4 = (f32[20,32,256]{2,1,0:T(8,128)S(1)}, f32[20,32,256]{2,1,0:T(8,128)}, u32[]{:S(2)}) copy-start(f32[20,32,256]{2,1,0:T(8,128)} %fields_ref.3) | copy-start | bytes 1966084
  4.6 22.0 %copy-start.7 = (f32[32,256]{1,0:T(8,128)S(1)}, f32[32,256]{1,0:T(8,128)}, u32[]{:S(2)}) copy-start(f32[32,256]{1,0:T(8,128)} %mean_ref.3) | copy-start | bytes 98308
  4.7 5.8 %collective-permute-start = (f32[88,256]{1,0:T(8,128)S(1)}, f32[88,256]{1,0:T(8,128)S(1)}, u32[]{:S(2)}, u32[]{:S(2)}) collective-permute-start(f32[88,256]{1,0:T(8,128)S(1)} %get-tuple-element.31), channel_id=1, source_target_pairs={{0,4},{4,8},{8,12},{12,16},{16,20},{20,24},{24,28},{1,5},{5,9},{9,... | collective-permute-start | bytes 270344 | tf_op jit(solution)/shard_map/ppermute | solution.py:281
  8.5 6.7 %collective-permute-start.1 = (f32[88,256]{1,0:T(8,128)S(1)}, f32[88,256]{1,0:T(8,128)S(1)}, u32[]{:S(2)}, u32[]{:S(2)}) collective-permute-start(f32[88,256]{1,0:T(8,128)S(1)} %get-tuple-element.32), channel_id=1, source_target_pairs={{4,0},{8,4},{12,8},{16,12},{20,16},{24,20},{28,24},{5,1},{9,5},{13... | collective-permute-start | bytes 270344 | tf_op jit(solution)/shard_map/ppermute | solution.py:282
  15.4 14.4 %collective-permute-start.2 = (bf16[6,64,256]{2,1,0:T(8,128)(2,1)S(1)}, bf16[6,64,256]{2,1,0:T(8,128)(2,1)S(1)}, u32[]{:S(2)}, u32[]{:S(2)}) collective-permute-start(bf16[6,64,256]{2,1,0:T(8,128)(2,1)S(1)} %get-tuple-element.34), channel_id=1, source_target_pairs={{0,3},{1,2},{2,1},{3,0},{4,7},{5,6},{6,5},{7,4},{8,11},{9,10},{10,... | collective-permute-start | bytes 589832 | tf_op jit(solution)/shard_map/ppermute | solution.py:296
  18.8 21.9 %collective-permute-start.3 = (bf16[6,64,256]{2,1,0:T(8,128)(2,1)S(1)}, bf16[6,64,256]{2,1,0:T(8,128)(2,1)S(1)}, u32[]{:S(2)}, u32[]{:S(2)}) collective-permute-start(bf16[6,64,256]{2,1,0:T(8,128)(2,1)S(1)} %get-tuple-element.35), channel_id=1, source_target_pairs={{0,2},{1,3},{2,0},{3,1},{4,6},{5,7},{6,4},{7,5},{8,10},{9,11},{10,... | collective-permute-start | bytes 589832 | tf_op jit(solution)/shard_map/ppermute | solution.py:296
  18.8 21.9 %collective-permute-start.4 = (bf16[6,64,256]{2,1,0:T(8,128)(2,1)S(1)}, bf16[6,64,256]{2,1,0:T(8,128)(2,1)S(1)}, u32[]{:S(2)}, u32[]{:S(2)}) collective-permute-start(bf16[6,64,256]{2,1,0:T(8,128)(2,1)S(1)} %get-tuple-element.36), channel_id=1, source_target_pairs={{0,1},{1,0},{2,3},{3,2},{4,5},{5,4},{6,7},{7,6},{8,9},{9,8},{10,11... | collective-permute-start | bytes 589832 | tf_op jit(solution)/shard_map/ppermute | solution.py:296
  22.0 30.9 %collective-permute-start.8 = (bf16[4,64,256]{2,1,0:T(8,128)(2,1)S(1)}, bf16[4,64,256]{2,1,0:T(8,128)(2,1)S(1)}, u32[]{:S(2)}, u32[]{:S(2)}) collective-permute-start(bf16[4,64,256]{2,1,0:T(8,128)(2,1)S(1)} %get-tuple-element.49), channel_id=1, source_target_pairs={{0,3},{1,2},{2,1},{3,0},{4,7},{5,6},{6,5},{7,4},{8,11},{9,10},{10,... | collective-permute-start | bytes 393224 | tf_op jit(solution)/shard_map/ppermute | solution.py:296
  26.6 26.8 %collective-permute-start.9 = (bf16[4,64,256]{2,1,0:T(8,128)(2,1)S(1)}, bf16[4,64,256]{2,1,0:T(8,128)(2,1)S(1)}, u32[]{:S(2)}, u32[]{:S(2)}) collective-permute-start(bf16[4,64,256]{2,1,0:T(8,128)(2,1)S(1)} %get-tuple-element.50), channel_id=1, source_target_pairs={{0,2},{1,3},{2,0},{3,1},{4,6},{5,7},{6,4},{7,5},{8,10},{9,11},{10,... | collective-permute-start | bytes 393224 | tf_op jit(solution)/shard_map/ppermute | solution.py:296
  27.6 2.1 %copy-start = (f32[32,6,24,256]{3,2,1,0:T(8,128)}, f32[32,6,24,256]{3,2,1,0:T(8,128)S(1)}, u32[]{:S(2)}) copy-start(f32[32,6,24,256]{3,2,1,0:T(8,128)S(1)} %get-tuple-element.43.refs_6_.refs_10_) | copy-start | bytes 14155780
  29.8 23.6 %collective-permute-start.10 = (bf16[4,64,256]{2,1,0:T(8,128)(2,1)S(1)}, bf16[4,64,256]{2,1,0:T(8,128)(2,1)S(1)}, u32[]{:S(2)}, u32[]{:S(2)}) collective-permute-start(bf16[4,64,256]{2,1,0:T(8,128)(2,1)S(1)} %get-tuple-element.51), channel_id=1, source_target_pairs={{0,1},{1,0},{2,3},{3,2},{4,5},{5,4},{6,7},{7,6},{8,9},{9,8},{10,11... | collective-permute-start | bytes 393224 | tf_op jit(solution)/shard_map/ppermute | solution.py:296
  49.7 16.1 %collective-permute-start.5 = (bf16[4,64,256]{2,1,0:T(8,128)(2,1)S(1)}, bf16[4,64,256]{2,1,0:T(8,128)(2,1)S(1)}, u32[]{:S(2)}, u32[]{:S(2)}) collective-permute-start(bf16[4,64,256]{2,1,0:T(8,128)(2,1)S(1)} %get-tuple-element.45), channel_id=1, source_target_pairs={{0,3},{1,2},{2,1},{3,0},{4,7},{5,6},{6,5},{7,4},{8,11},{9,10},{10,... | collective-permute-start | bytes 393224 | tf_op jit(solution)/shard_map/ppermute | solution.py:296
  52.9 13.2 %collective-permute-start.6 = (bf16[4,64,256]{2,1,0:T(8,128)(2,1)S(1)}, bf16[4,64,256]{2,1,0:T(8,128)(2,1)S(1)}, u32[]{:S(2)}, u32[]{:S(2)}) collective-permute-start(bf16[4,64,256]{2,1,0:T(8,128)(2,1)S(1)} %get-tuple-element.46), channel_id=1, source_target_pairs={{0,2},{1,3},{2,0},{3,1},{4,6},{5,7},{6,4},{7,5},{8,10},{9,11},{10,... | collective-permute-start | bytes 393224 | tf_op jit(solution)/shard_map/ppermute | solution.py:296
  52.9 13.2 %collective-permute-start.7 = (bf16[4,64,256]{2,1,0:T(8,128)(2,1)S(1)}, bf16[4,64,256]{2,1,0:T(8,128)(2,1)S(1)}, u32[]{:S(2)}, u32[]{:S(2)}) collective-permute-start(bf16[4,64,256]{2,1,0:T(8,128)(2,1)S(1)} %get-tuple-element.47), channel_id=1, source_target_pairs={{0,1},{1,0},{2,3},{3,2},{4,5},{5,4},{6,7},{7,6},{8,9},{9,8},{10,11... | collective-permute-start | bytes 393224 | tf_op jit(solution)/shard_map/ppermute | solution.py:296
  53.3 22.5 %copy-start.2 = (f32[64,32,256]{2,1,0:T(8,128)S(1)}, f32[64,32,256]{2,1,0:T(8,128)}, u32[]{:S(2)}) copy-start(f32[64,32,256]{2,1,0:T(8,128)} %refs_9_.1) | copy-start | bytes 6291460
  53.4 22.5 %copy-start.5 = (f32[64,32,256]{2,1,0:T(8,128)S(1)}, f32[64,32,256]{2,1,0:T(8,128)}, u32[]{:S(2)}) copy-start(f32[64,32,256]{2,1,0:T(8,128)} %refs_8_.1) | copy-start | bytes 6291460
  62.5 11.0 %collective-permute-start.11 = (bf16[4,64,256]{2,1,0:T(8,128)(2,1)S(1)}, bf16[4,64,256]{2,1,0:T(8,128)(2,1)S(1)}, u32[]{:S(2)}, u32[]{:S(2)}) collective-permute-start(bf16[4,64,256]{2,1,0:T(8,128)(2,1)S(1)} %get-tuple-element.53), channel_id=1, source_target_pairs={{0,3},{1,2},{2,1},{3,0},{4,7},{5,6},{6,5},{7,4},{8,11},{9,10},{10,... | collective-permute-start | bytes 393224 | tf_op jit(solution)/shard_map/ppermute | solution.py:296
  65.8 10.0 %collective-permute-start.12 = (bf16[4,64,256]{2,1,0:T(8,128)(2,1)S(1)}, bf16[4,64,256]{2,1,0:T(8,128)(2,1)S(1)}, u32[]{:S(2)}, u32[]{:S(2)}) collective-permute-start(bf16[4,64,256]{2,1,0:T(8,128)(2,1)S(1)} %get-tuple-element.54), channel_id=1, source_target_pairs={{0,2},{1,3},{2,0},{3,1},{4,6},{5,7},{6,4},{7,5},{8,10},{9,11},{10,... | collective-permute-start | bytes 393224 | tf_op jit(solution)/shard_map/ppermute | solution.py:296
  65.8 10.0 %collective-permute-start.13 = (bf16[4,64,256]{2,1,0:T(8,128)(2,1)S(1)}, bf16[4,64,256]{2,1,0:T(8,128)(2,1)S(1)}, u32[]{:S(2)}, u32[]{:S(2)}) collective-permute-start(bf16[4,64,256]{2,1,0:T(8,128)(2,1)S(1)} %get-tuple-element.55), channel_id=1, source_target_pairs={{0,1},{1,0},{2,3},{3,2},{4,5},{5,4},{6,7},{7,6},{8,9},{9,8},{10,11... | collective-permute-start | bytes 393224 | tf_op jit(solution)/shard_map/ppermute | solution.py:296
  66.3 9.6 %collective-permute-start.15 = (f32[64,256]{1,0:T(8,128)S(1)}, f32[64,256]{1,0:T(8,128)S(1)}, u32[]{:S(2)}, u32[]{:S(2)}) collective-permute-start(f32[64,256]{1,0:T(8,128)S(1)} %get-tuple-element.60), channel_id=1, source_target_pairs={{4,0},{8,4},{12,8},{16,12},{20,16},{24,20},{28,24},{5,1},{9,5},{13... | collective-permute-start | bytes 196616 | tf_op jit(solution)/shard_map/ppermute | solution.py:373
  68.7 7.2 %collective-permute-start.14 = (f32[64,256]{1,0:T(8,128)S(1)}, f32[64,256]{1,0:T(8,128)S(1)}, u32[]{:S(2)}, u32[]{:S(2)}) collective-permute-start(f32[64,256]{1,0:T(8,128)S(1)} %get-tuple-element.61), channel_id=1, source_target_pairs={{0,4},{4,8},{8,12},{12,16},{16,20},{20,24},{24,28},{1,5},{5,9},{9,... | collective-permute-start | bytes 196616 | tf_op jit(solution)/shard_map/ppermute | solution.py:372
  (2 other events, 1.8 us)

commit v4 on v3

--- a/solution.py
+++ b/solution.py
@@ -12,6 +12,7 @@
 cheb_center = 1.125
 cheb_radius = 0.875
 SMALL = pl.CostEstimate(flops=1, bytes_accessed=1, transcendentals=0)
+LARGE = pl.CostEstimate(flops=10**10, bytes_accessed=2**24, transcendentals=0)
 VMEM_LIMIT = 48 * 1024 * 1024
 
 
@@ -30,42 +31,37 @@
     return jnp.clip(row, 0, rows - 1)
 
 
-def turn_kernel(x_ref, mean_ref, fields_ref, turned, last, first):
-    step = pl.program_id(0)
-    modes, rows, _ = x_ref.shape
-    block = jnp.swapaxes(x_ref[...], 0, 1)
-    turned[...] = block.astype(jnp.bfloat16)
-    at = pl.ds(pl.multiple_of(step * modes, modes), modes)
-    first[at, :] = block[0]
-    last[at, :] = block[rows - 1]
-
-    @pl.when(step == pl.num_programs(0) - 1)
-    def _():
-        fields = fields_ref.shape[0]
-        here = modes * pl.num_programs(0)
-        for out, row in ((first, 0), (last, rows - 1)):
-            out[here : here + 1, :] = mean_ref[row : row + 1, :]
-            for field in range(fields):
-                out[here + 1 + field : here + 2 + field, :] = fields_ref[field, row : row + 1, :]
-            rest = out.shape[0] - here - 1 - fields
-            out[here + 1 + fields :, :] = jnp.zeros((rest, out.shape[1]), jnp.float32)
-
-
-def late_kernel(count, slab, half, rows, z_ref, turned, after, *outs):
+def turn_kernel(count, slab, rows, z_ref, x_ref, turned, *refs):
+    outs, block_ref, sems = refs[:count], refs[count], refs[count + 1]
     z = z_ref[0]
+    parts, modes = block_ref.shape[:2]
+    copies = [
+        pltpu.make_async_copy(
+            x_ref.at[k * modes : (k + 1) * modes], block_ref.at[k], sems.at[k]
+        )
+        for k in range(parts)
+    ]
+    for copy in copies:
+        copy.start()
+    for k, copy in enumerate(copies):
+        copy.wait()
+        block = jnp.swapaxes(block_ref[k], 0, 1).astype(jnp.bfloat16)
+        turned[:, k * modes : (k + 1) * modes, :] = block
     for p in range(count):
         place = jnp.bitwise_xor(z, p)
-        for rho in range(half + 1, slab + 1):
-            outs[p][rho - half - 1] = turned[row_of(place, rho, slab, count, rows)]
-
-
-def early_kernel(count, slab, half, rows, z_ref, turned, low_ref, high_ref, *outs):
+        for rho in range(outs[p].shape[0]):
+            outs[p][rho] = turned[row_of(place, rho, slab, count, rows)]
+
+
+def late_kernel(count, slab, rows, z_ref, turned, low_ref, high_ref, after, *outs):
     z = z_ref[0]
     here = turned.shape[1]
     for p in range(count):
         place = jnp.bitwise_xor(z, p)
-        for rho in range(-1, half + 1):
-            outs[p][rho + 1] = turned[row_of(place, rho, slab, count, rows)]
+        for k in range(1, outs[p].shape[0]):
+            rho = slab - outs[p].shape[0] + 1 + k
+            outs[p][k] = turned[row_of(place, rho, slab, count, rows)]
+        outs[p][0] = turned[row_of(place, -1, slab, count, rows)]
 
         @pl.when(place == 0)
         def _():
@@ -158,12 +154,12 @@
     inverse_ref[...] = 1.0 / diag
 
 
-def mix_kernel(count, slab, half, groups, fields, window, begin, z_ref, *refs):
+def mix_kernel(count, slab, groups, fields, window, skip, begin, extra, z_ref, *refs):
     arrays = max(a for a, _ in window) + 1
     sources = refs[: arrays * count]
     dense_ref, own_ref, weight_ref = refs[arrays * count : arrays * count + 3]
-    outs = refs[arrays * count + 3 : arrays * count + 3 + count]
-    rows_ref, diff_ref, term_ref, total_ref = refs[arrays * count + 3 + count :]
+    outs = refs[arrays * count + 3 + extra : -4]
+    rows_ref, diff_ref, term_ref, total_ref = refs[-4:]
     size, cells = total_ref.shape
     here = size // count
     bf16 = jnp.bfloat16
@@ -178,12 +174,16 @@
     faces = (ahead, 1 - ahead, 2, 3, 4, 5)
 
     def each_row(r, carry):
-        row = row_of(z, begin + r, slab, count, rows)
+        row = row_of(z, jnp.where(r == 0, begin[0], begin[1] + r), slab, count, rows)
+        r_in = r + jnp.where(r == 0, 0, skip)
         mean_weights = [weight_ref[row, f, 0:1, :] for f in faces]
         for t in range(0, size, 16):
             at = slice(t, t + 16)
-            centre = rows_ref[r + 1, at].astype(jnp.float32)
-            others = (rows_ref[r + 2, at].astype(jnp.float32), rows_ref[r, at].astype(jnp.float32))
+            centre = rows_ref[r_in + 1, at].astype(jnp.float32)
+            others = (
+                rows_ref[r_in + 2, at].astype(jnp.float32),
+                rows_ref[r_in, at].astype(jnp.float32),
+            )
             mean = None
             for f, other in enumerate(others + beside(centre, mask_set)):
                 diff = centre - other
@@ -210,30 +210,54 @@
             outs[p][r] = total_ref[p * here : (p + 1) * here, :].astype(bf16)
         return carry
 
-    lax.fori_loop(0, half, each_row, 0)
+    lax.fori_loop(0, outs[0].shape[0], each_row, 0)
+
+
+def edge_kernel(count, z_ref, *refs):
+    parts = refs[:count]
+    bottom_source, top_source, inverse = refs[count : count + 3]
+    bottom, top = refs[-2:]
+    z = z_ref[0]
+    rows = inverse.shape[0]
+    for k in range(count):
+        place = jnp.bitwise_xor(z, (count - k) % count)
+        image = parts[k][0].astype(jnp.float32)
+
+        @pl.when(place == 0)
+        def _():
+            scale = inverse[0:1] * (1.0 / cheb_center)
+            bottom[...] = (bottom_source[...] - image) * scale
+
+        @pl.when(place == count - 1)
+        def _():
+            scale = inverse[rows - 1 : rows] * (1.0 / cheb_center)
+            top[...] = (top_source[...] - image) * scale
 
 
 def post_kernel(count, slab, half, rows, rho_zero, rho_one, z_ref, *refs):
     early = refs[:count]
     late = refs[count : 2 * count]
-    source, iterate, low, high, faces, inverse = refs[2 * count : 2 * count + 6]
-    updated, residual, image = refs[2 * count + 6 :]
+    source, iterate, faces, inverse = refs[2 * count : 2 * count + 4]
+    updated, residual, image = refs[2 * count + 4 :]
     z = z_ref[0]
     modes, _, cells = source.shape
     for k in range(count):
         place = jnp.bitwise_xor(z, (count - k) % count)
         for rho in range(slab):
-            part = early[k][rho] if rho < half else late[k][rho - half]
+            if 1 <= rho <= half:
+                part = early[k][rho - 1]
+            else:
+                part = late[k][max(rho - half, 0)]
             image[row_of(place, rho, slab, count, rows)] = part.astype(jnp.float32)
     residual[...] = source[...] - jnp.swapaxes(image[...], 0, 1)
     place = lax.broadcasted_iota(jnp.int32, (rows, cells), 0)
     inv = inverse[...]
+    up_face = jnp.where(place == rows - 1, 0.0, faces[0])
+    down_face = jnp.where(place == 0, 0.0, faces[1])
     for m in range(modes):
         res = residual[m]
         first = res * (inv * (1.0 / cheb_center))
-        up = jnp.where(place == rows - 1, high[m : m + 1, :], pltpu.roll(first, rows - 1, 0))
-        down = jnp.where(place == 0, low[m : m + 1, :], pltpu.roll(first, 1, 0))
-        near = faces[0] * up + faces[1] * down
+        near = up_face * pltpu.roll(first, rows - 1, 0) + down_face * pltpu.roll(first, 1, 0)
         near = near + faces[2] * pltpu.roll(first, cells - NZ, 1)
         near = near + faces[3] * pltpu.roll(first, NZ, 1)
         near = near + faces[4] * pltpu.roll(first, cells - 1, 1)
@@ -241,6 +265,21 @@
         smoothed = (1.0 - 1.0 / cheb_center) * res + near
         step = (1.0 + rho_one * rho_zero) * first + (2.0 * rho_one / cheb_radius) * smoothed * inv
         updated[m] = iterate[m] + step
+
+
+def close_kernel(rho_one, low, high, faces, inverse, partial, updated):
+    modes, deep, cells = partial.shape
+    bottom = pl.program_id(0) == 0
+    rows = inverse.shape[0]
+    scale = 2.0 * rho_one / cheb_radius
+    weight = jnp.where(
+        bottom, faces[1, 0:1] * inverse[0:1], faces[0, rows - 1 : rows] * inverse[rows - 1 : rows]
+    )
+    share = jnp.where(bottom, low[...], high[...]) * (weight * scale)
+    place = lax.broadcasted_iota(jnp.int32, (deep, cells), 0)
+    here = place == jnp.where(bottom, 0, deep - 1)
+    for m in range(modes):
+        updated[m] = partial[m] + jnp.where(here, share[m : m + 1], 0.0)
 
 
 def body(iterate, source, mean_coef, kl_fields, tri_index, tri_value):
@@ -259,36 +298,21 @@
 
     deep = -(-fields // 8) * 8
 
-    upward = [(i, i + 1) for i in range(doms - 1)]
-    downward = [(b, a) for a, b in upward]
-    block = min(16, here)
-    rim_shape = jax.ShapeDtypeStruct((here + deep, cells), jnp.float32)
-    rim_spec = pl.BlockSpec((here + deep, cells), lambda i: (0, 0))
-    turned, last_rim, first_rim = pl.pallas_call(
-        turn_kernel,
-        grid=(here // block,),
-        out_shape=[jax.ShapeDtypeStruct((rows, here, cells), bf16), rim_shape, rim_shape],
-        in_specs=[
-            pl.BlockSpec((block, rows, cells), lambda i: (i, 0, 0)),
-            pl.BlockSpec((rows, cells), lambda i: (0, 0)),
-            pl.BlockSpec((fields - 1, rows, cells), lambda i: (0, 0, 0)),
-        ],
-        out_specs=[pl.BlockSpec((rows, block, cells), lambda i: (0, i, 0)), rim_spec, rim_spec],
+    parts = max(1, here // 16)
+    turned, *early = pl.pallas_call(
+        functools.partial(turn_kernel, count, slab, rows),
+        out_shape=[jax.ShapeDtypeStruct((rows, here, cells), bf16)]
+        + [jax.ShapeDtypeStruct((half + 2, here, cells), bf16)] * count,
+        in_specs=[in_smem(), pl.BlockSpec(memory_space=pltpu.HBM)],
+        out_specs=in_vmem(count + 1),
+        scratch_shapes=[
+            pltpu.VMEM((parts, here // parts, rows, cells), jnp.float32),
+            pltpu.SemaphoreType.DMA((parts,)),
+        ],
         compiler_params=params,
         cost_estimate=SMALL,
         name="turn",
-    )(iterate, mean_coef, kl_fields)
-    low_rim = lax.ppermute(last_rim, "dom", upward)
-    high_rim = lax.ppermute(first_rim, "dom", downward)
-    early = pl.pallas_call(
-        functools.partial(early_kernel, count, slab, half, rows),
-        out_shape=[jax.ShapeDtypeStruct((half + 2, here, cells), bf16)] * count,
-        in_specs=[in_smem()] + in_vmem(3),
-        out_specs=in_vmem(count),
-        compiler_params=params,
-        cost_estimate=SMALL,
-        name="early",
-    )(z_arg, turned, low_rim, high_rim)
+    )(z_arg, iterate)
 
     def swap(arrays):
         taken = [arrays[0]]
@@ -296,10 +320,8 @@
             taken.append(lax.ppermute(arrays[p], "mode", [(i, i ^ p) for i in range(count)]))
         return taken
 
-    entries, values, low_coef, high_coef, _ = lax.optimization_barrier(
-        (tri_index, tri_value, low_rim, high_rim, early[0])
-    )
     early = swap(early)
+    entries, values, _ = lax.optimization_barrier((tri_index, tri_value, turned))
     dense, own = pl.pallas_call(
         functools.partial(dense_kernel, groups, fields, here),
         out_shape=[
@@ -312,6 +334,22 @@
         cost_estimate=SMALL,
         name="dense",
     )(z_arg, entries.T, values[None])
+    upward = [(i, i + 1) for i in range(doms - 1)]
+    downward = [(b, a) for a, b in upward]
+    iterate_here, mean_here, fields_here, _ = lax.optimization_barrier(
+        (iterate, mean_coef, kl_fields, own)
+    )
+    filler = jnp.zeros((deep - fields, cells), jnp.float32)
+    low_rim, high_rim = (
+        lax.ppermute(
+            jnp.concatenate(
+                [iterate_here[:, at], mean_here[at][None], fields_here[:, at], filler], 0
+            ),
+            "dom",
+            pairs,
+        )
+        for at, pairs in ((rows - 1, upward), (0, downward))
+    )
     weights, faces, inverse = pl.pallas_call(
         weight_kernel,
         out_shape=[
@@ -328,63 +366,76 @@
         compiler_params=params,
         cost_estimate=SMALL,
         name="weights",
-    )(mean_coef, kl_fields, low_coef, high_coef)
+    )(mean_coef, kl_fields, low_rim, high_rim)
     late = pl.pallas_call(
-        functools.partial(late_kernel, count, slab, half, rows),
+        functools.partial(late_kernel, count, slab, rows),
         out_shape=[jax.ShapeDtypeStruct((slab - half, here, cells), bf16)] * count,
-        in_specs=[in_smem()] + in_vmem(2),
+        in_specs=[in_smem()] + in_vmem(3) + [pl.BlockSpec(memory_space=pl.ANY)],
         out_specs=in_vmem(count),
         compiler_params=params,
         cost_estimate=SMALL,
         name="late",
-    )(z_arg, turned, own)
+    )(z_arg, turned, low_rim, high_rim, early[-2])
     late = swap(late)
 
-    def mix(arrays, window, begin):
+    def mix(arrays, window, skip, begin, rows_out, after=()):
         flat = [a for group in arrays for a in group]
         return pl.pallas_call(
-            functools.partial(mix_kernel, count, slab, half, groups, fields, window, begin),
-            out_shape=[jax.ShapeDtypeStruct((half, here, cells), bf16)] * count,
-            in_specs=[in_smem()] + in_vmem(len(flat) + 3),
+            functools.partial(
+                mix_kernel, count, slab, groups, fields, window, skip, begin, len(after)
+            ),
+            out_shape=[jax.ShapeDtypeStruct((rows_out, here, cells), bf16)] * count,
+            in_specs=[in_smem()]
+            + in_vmem(len(flat) + 3)
+            + [pl.BlockSpec(memory_space=pl.ANY)] * len(after),
             out_specs=in_vmem(count),
             scratch_shapes=[
-                pltpu.VMEM((half + 2, size, cells), bf16),
+                pltpu.VMEM((len(window), size, cells), bf16),
                 pltpu.VMEM((6, size, cells), bf16),
                 pltpu.VMEM((GROUP * size, cells), bf16),
                 pltpu.VMEM((size, cells), jnp.float32),
             ],
             compiler_params=params,
+            cost_estimate=LARGE,
             name="mix",
-        )(z_arg, *flat, dense, own, weights)
+        )(z_arg, *flat, dense, own, weights, *after)
 
     window = tuple((0, k) for k in range(half + 2))
-    back_early = swap(mix([early], window, 0))
-    window = ((0, half), (0, half + 1)) + tuple((1, k) for k in range(slab - half))
-    back_late = swap(mix([early, late], window, half))
-
-    outer = jnp.stack([b[0] for b in back_early])
-    place_of = lambda p: (count - p) % count
-    bottom = lax.dynamic_index_in_dim(outer, place_of(z), 0, keepdims=False).astype(jnp.float32)
-    top = lax.dynamic_index_in_dim(outer, place_of(z ^ (count - 1)), 0, keepdims=False)
-    top = top.astype(jnp.float32)
-    first_bottom = (source[:, 0] - bottom) * (inverse[0] / cheb_center)
-    first_top = (source[:, -1] - top) * (inverse[-1] / cheb_center)
-    low = lax.ppermute(first_top, "dom", upward)
-    high = lax.ppermute(first_bottom, "dom", downward)
+    mixed = mix([early], window, 0, (1, 1), half)
+    back_early = swap(mixed)
+    window = ((1, 0), (0, 0), (0, 1), (0, half), (0, half + 1))
+    window += tuple((1, k) for k in range(1, slab - half))
+    back_late = swap(mix([early, late], window, 2, (0, half), slab - half, mixed[-1:]))
+
+    bottom, top = pl.pallas_call(
+        functools.partial(edge_kernel, count),
+        out_shape=[jax.ShapeDtypeStruct((here, cells), jnp.float32)] * 2,
+        in_specs=[in_smem()]
+        + in_vmem(count + 3)
+        + [pl.BlockSpec(memory_space=pl.ANY)] * (count - 1),
+        out_specs=in_vmem(2),
+        compiler_params=params,
+        cost_estimate=SMALL,
+        name="edge",
+    )(z_arg, *back_late, source[:, 0], source[:, rows - 1], inverse, *back_early[1:])
+    low = lax.ppermute(top, "dom", upward)
+    high = lax.ppermute(bottom, "dom", downward)
 
     sigma = cheb_center / cheb_radius
     rho_zero = 1.0 / sigma
     rho_one = 1.0 / (2.0 * sigma - rho_zero)
-    image_spec = pl.BlockSpec((half, block, cells), lambda i: (0, i, 0))
+    block = min(16, here)
+    early_spec = pl.BlockSpec((half, block, cells), lambda i: (0, i, 0))
+    late_spec = pl.BlockSpec((slab - half, block, cells), lambda i: (0, i, 0))
     flat_spec = pl.BlockSpec((block, rows, cells), lambda i: (i, 0, 0))
-    row_spec = pl.BlockSpec((block, cells), lambda i: (i, 0))
     updated, residual = pl.pallas_call(
         functools.partial(post_kernel, count, slab, half, rows, rho_zero, rho_one),
         grid=(here // block,),
         out_shape=[jax.ShapeDtypeStruct((here, rows, cells), jnp.float32)] * 2,
         in_specs=[in_smem()]
-        + [image_spec] * (2 * count)
-        + [flat_spec, flat_spec, row_spec, row_spec]
+        + [early_spec] * count
+        + [late_spec] * count
+        + [flat_spec, flat_spec]
         + [
             pl.BlockSpec((6, rows, cells), lambda i: (0, 0, 0)),
             pl.BlockSpec((rows, cells), lambda i: (0, 0)),
@@ -399,11 +450,28 @@
         *back_late,
         source,
         iterate,
-        low,
-        high,
         faces,
         inverse,
     )
+    tile = 8 if rows % 8 == 0 else rows
+    last = rows // tile - 1
+    tile_spec = pl.BlockSpec((here, tile, cells), lambda i: (0, i * last, 0))
+    updated = pl.pallas_call(
+        functools.partial(close_kernel, rho_one),
+        grid=(2 if last else 1,),
+        out_shape=jax.ShapeDtypeStruct((here, rows, cells), jnp.float32),
+        in_specs=[
+            pl.BlockSpec((here, cells), lambda i: (0, 0)),
+            pl.BlockSpec((here, cells), lambda i: (0, 0)),
+            pl.BlockSpec((6, rows, cells), lambda i: (0, 0, 0)),
+            pl.BlockSpec((rows, cells), lambda i: (0, 0)),
+            tile_spec,
+        ],
+        out_specs=tile_spec,
+        input_output_aliases={4: 0},
+        compiler_params=params,
+        name="close",
+    )(low, high, faces, inverse, updated)
     return updated, residual
 
 

time: 81.5 us -> 81.5 us (level)
  the two profiles are of different devices: /device:TPU:3 before, /device:TPU:1 now
where the time goes in v4:
time: 81.5 us; the launch traced here: 81 us
  Pallas kernels  29.1 us (36%)
  starting transfers between devices  28.8 us (35%)
  waiting for transfers between devices  13.9 us (17%)
  local copies, waits for them, and re-layouts  8.27 us (10%)
  between operations  0.87 us (1%)
    pallas_call x2, Pallas kernels, mix(): pl.pallas_call(functools.partial(mix_kernel, count, slab, groups, fields,...  18 us
    ppermute x12, starting transfers between devices, swap(): lax.ppermute(arrays[p], 'mode', [(i, i ^ p) for i in range(count)])  15.6 us
    ppermute x12, waiting for transfers between devices, swap(): lax.ppermute(arrays[p], 'mode', [(i, i ^ p) for i in range(count)])  10.1 us
    ppermute x2, starting transfers between devices, body(): lax.ppermute(jnp.concatenate([iterate_here[:, at], mean_here[at][None], f...  6.3 us
    ppermute x1, starting transfers between devices, body(): low = lax.ppermute(top, 'dom', upward)  4.97 us
    unnamed x14, local copies, waits for them, and re-layouts  4.62 us
    pallas_call x1, Pallas kernels, body(): pl.pallas_call(functools.partial(post_kernel, count, slab, half, rows, rh...  4.52 us
    ppermute x2, waiting for transfers between devices, body(): lax.ppermute(jnp.concatenate([iterate_here[:, at], mean_here[at][None], f...  3.8 us
  transfers between devices with their start and end apart: 16, of which 3 were waited for; matrix products, arithmetic and copies ran while one was open for 5% of the time, Pallas kernels for 33%

profile of v4, /device:TPU:1, one launch (start us, length us, event | category | flops | bytes accessed | tf_op | source)
XLA Modules:
  0.0 81.0 jit_solution(3404797744454989310)
XLA Ops:
  0.6 1.6 %copy-done = f32[64,32,256]{2,1,0:T(8,128)S(1)} copy-done((f32[64,32,256]{2,1,0:T(8,128)S(1)}, f32[64,32,256]{2,1,0:T(8,128)}, u32[]{:S(2)}) %copy-start) | copy-done | bytes 2097176
  2.2 0.6 turn.1
  2.9 4.2 %collective-permute-start = (bf16[6,64,256]{2,1,0:T(8,128)(2,1)S(1)}, bf16[6,64,256]{2,1,0:T(8,128)(2,1)S(1)}, u32[]{:S(2)}, u32[]{:S(2)}) collective-permute-start(bf16[6,64,256]{2,1,0:T(8,128)(2,1)S(1)} %get-tuple-element.34), channel_id=1, source_target_pairs={{0,3},{1,2},{2,1},{3,0},{4,7},{5,6},{6,5},{7,4},{8,11},{9,10},{10,... | collective-permute-start | bytes 589832 | tf_op jit(solution)/shard_map/ppermute | solution.py:320
  7.5 0.8 broadcast_in_dim.6.value_ref
  8.2 0.9 %copy-done.4 = s32[5376,3]{0,1:T(4,128)S(1)} copy-done((s32[5376,3]{0,1:T(4,128)S(1)}, s32[5376,3]{0,1:T(4,128)}, u32[]{:S(2)}) %copy-start.4) | copy-done | bytes 64536
  9.1 2.8 %dense.1 = (bf16[4,256,1280]{2,1,0:T(8,128)(2,1)S(1)}, f32[256,128]{1,0:T(8,128)S(1)}) custom-call(s32[1]{0:T(128)} %bitcast.z_ref, s32[3,5376]{1,0:T(4,128)S(1)} %bitcast.14, f32[1,5376]{1,0:T(1,128)S(1)} %broadcast_in_dim.6.value_ref), custom_call_target="tpu_custom_call" | custom-call | flops 1 | bytes 1 | tf_op jit(solution)/shard_map/dense/pallas_call | solution.py:325
  12.0 1.5 %copy.10 = f32[20,32,256]{2,0,1:T(8,128)S(1)} copy(f32[20,32,256]{2,1,0:T(8,128)} %fields_ref.1) | data formatting | bytes 1310720 | tf_op jit(solution)/shard_map/optimization_barrier | solution.py:339
  13.5 1.2 %copy.9 = f32[64,32,256]{2,0,1:T(8,128)S(1)} copy(f32[64,32,256]{2,1,0:T(8,128)S(1)} %copy-done.1) | data formatting | bytes 4194304 | tf_op jit(solution)/shard_map/optimization_barrier | solution.py:339
  14.9 4.4 %collective-permute-start.3 = (f32[88,256]{1,0:T(8,128)S(1)}, f32[88,256]{1,0:T(8,128)S(1)}, u32[]{:S(2)}, u32[]{:S(2)}) collective-permute-start(f32[88,256]{1,0:T(8,128)S(1)} %get-tuple-element.73), channel_id=1, source_target_pairs={{0,4},{4,8},{8,12},{12,16},{16,20},{20,24},{24,28},{1,5},{5,9},{9,... | collective-permute-start | bytes 270344 | tf_op jit(solution)/shard_map/ppermute | solution.py:344
  19.3 1.9 %collective-permute-start.4 = (f32[88,256]{1,0:T(8,128)S(1)}, f32[88,256]{1,0:T(8,128)S(1)}, u32[]{:S(2)}, u32[]{:S(2)}) collective-permute-start(f32[88,256]{1,0:T(8,128)S(1)} %get-tuple-element.72), channel_id=1, source_target_pairs={{4,0},{8,4},{12,8},{16,12},{20,16},{24,20},{28,24},{5,1},{9,5},{13... | collective-permute-start | bytes 270344 | tf_op jit(solution)/shard_map/ppermute | solution.py:344
  21.4 3.8 %collective-permute-done.4.high_ref = f32[88,256]{1,0:T(8,128)S(1)} collective-permute-done((f32[88,256]{1,0:T(8,128)S(1)}, f32[88,256]{1,0:T(8,128)S(1)}, u32[]{:S(2)}, u32[]{:S(2)}) %collective-permute-start.4) | collective-permute-done | bytes 90144 | tf_op jit(solution)/shard_map/ppermute | solution.py:344
  25.2 0.9 %weights.1 = (f32[32,6,24,256]{3,2,1,0:T(8,128)S(1)}, f32[6,32,256]{2,1,0:T(8,128)S(1)}, f32[32,256]{1,0:T(8,128)S(1)}) custom-call(f32[32,256]{1,0:T(8,128)S(1)} %copy-done.5, f32[20,32,256]{2,1,0:T(8,128)S(1)} %copy-done.2, f32[88,256]{1,0:T(8,128)S(1)} %collective-permute-done.3.low_ref, f32[88,256]{1,0:T(8,128)S(1)} %collective-permute-done.4.high_ref), custom_call_target="tpu_custom_call" | custom-call | flops 1 | bytes 1 | tf_op jit(solution)/shard_map/weights/pallas_call | solution.py:353
  26.1 2.1 %copy-done.6 = f32[32,6,24,256]{3,2,1,0:T(8,128)} copy-done((f32[32,6,24,256]{3,2,1,0:T(8,128)}, f32[32,6,24,256]{3,2,1,0:T(8,128)S(1)}, u32[]{:S(2)}) %copy-start.6) | copy-done | bytes 4718616
  28.3 3.4 %collective-permute-start.5 = (bf16[4,64,256]{2,1,0:T(8,128)(2,1)S(1)}, bf16[4,64,256]{2,1,0:T(8,128)(2,1)S(1)}, u32[]{:S(2)}, u32[]{:S(2)}) collective-permute-start(bf16[4,64,256]{2,1,0:T(8,128)(2,1)S(1)} %get-tuple-element.45), channel_id=1, source_target_pairs={{0,3},{1,2},{2,1},{3,0},{4,7},{5,6},{6,5},{7,4},{8,11},{9,10},{10,... | collective-permute-start | bytes 393224 | tf_op jit(solution)/shard_map/ppermute | solution.py:320
  32.1 9.0 %mix.2 = (bf16[4,64,256]{2,1,0:T(8,128)(2,1)S(1)}, bf16[4,64,256]{2,1,0:T(8,128)(2,1)S(1)}, bf16[4,64,256]{2,1,0:T(8,128)(2,1)S(1)}, bf16[4,64,256]{2,1,0:T(8,128)(2,1)S(1)}) custom-call(s32[1]{0:T(128)} %bitcast.z_ref, bf16[6,64,256]{2,1,0:T(8,128)(2,1)S(1)} %get-tuple-element.33.refs_0_, bf16[6,64,256]{2,1,0:T(8,128)(2,1)S(1)} %collective-permute-done.refs_1_, ...), custom_call_target="tpu_custom_call" | custom-call | flops 10000000000 | bytes 16777216 | tf_op jit(solution)/shard_map/mix/pallas_call | solution.py:383
  41.1 3.3 %collective-permute-start.11 = (bf16[4,64,256]{2,1,0:T(8,128)(2,1)S(1)}, bf16[4,64,256]{2,1,0:T(8,128)(2,1)S(1)}, u32[]{:S(2)}, u32[]{:S(2)}) collective-permute-start(bf16[4,64,256]{2,1,0:T(8,128)(2,1)S(1)} %get-tuple-element.50.refs_11_), channel_id=1, source_target_pairs={{0,3},{1,2},{2,1},{3,0},{4,7},{5,6},{6,5},{7,4},{8,11},{9,10},{10,... | collective-permute-start | bytes 393224 | tf_op jit(solution)/shard_map/ppermute | solution.py:320
  44.7 9.0 %mix.3 = (bf16[4,64,256]{2,1,0:T(8,128)(2,1)S(1)}, bf16[4,64,256]{2,1,0:T(8,128)(2,1)S(1)}, bf16[4,64,256]{2,1,0:T(8,128)(2,1)S(1)}, bf16[4,64,256]{2,1,0:T(8,128)(2,1)S(1)}) custom-call(s32[1]{0:T(128)} %bitcast.z_ref, bf16[6,64,256]{2,1,0:T(8,128)(2,1)S(1)} %get-tuple-element.33.refs_0_, bf16[6,64,256]{2,1,0:T(8,128)(2,1)S(1)} %collective-permute-done.refs_1_, ...), custom_call_target="tpu_custom_call" | custom-call | flops 10000000000 | bytes 16777216 | tf_op jit(solution)/shard_map/mix/pallas_call | solution.py:383
  53.7 3.3 %collective-permute-start.8 = (bf16[4,64,256]{2,1,0:T(8,128)(2,1)S(1)}, bf16[4,64,256]{2,1,0:T(8,128)(2,1)S(1)}, u32[]{:S(2)}, u32[]{:S(2)}) collective-permute-start(bf16[4,64,256]{2,1,0:T(8,128)(2,1)S(1)} %get-tuple-element.52), channel_id=1, source_target_pairs={{0,3},{1,2},{2,1},{3,0},{4,7},{5,6},{6,5},{7,4},{8,11},{9,10},{10,... | collective-permute-start | bytes 393224 | tf_op jit(solution)/shard_map/ppermute | solution.py:320
  57.4 3.5 %collective-permute-done.8.refs_1_.refs_5_ = bf16[4,64,256]{2,1,0:T(8,128)(2,1)S(1)} collective-permute-done((bf16[4,64,256]{2,1,0:T(8,128)(2,1)S(1)}, bf16[4,64,256]{2,1,0:T(8,128)(2,1)S(1)}, u32[]{:S(2)}, u32[]{:S(2)}) %collective-permute-start.8) | collective-permute-done | bytes 131104 | tf_op jit(solution)/shard_map/ppermute | solution.py:320
  60.8 6.6 %collective-permute-done.9.refs_2_.refs_6_ = bf16[4,64,256]{2,1,0:T(8,128)(2,1)S(1)} collective-permute-done((bf16[4,64,256]{2,1,0:T(8,128)(2,1)S(1)}, bf16[4,64,256]{2,1,0:T(8,128)(2,1)S(1)}, u32[]{:S(2)}, u32[]{:S(2)}) %collective-permute-start.9) | collective-permute-done | bytes 131104 | tf_op jit(solution)/shard_map/ppermute | solution.py:320
  67.5 5.0 %collective-permute-start.14 = (f32[64,256]{1,0:T(8,128)S(1)}, f32[64,256]{1,0:T(8,128)S(1)}, u32[]{:S(2)}, u32[]{:S(2)}) collective-permute-start(f32[64,256]{1,0:T(8,128)S(1)} %get-tuple-element.58), channel_id=1, source_target_pairs={{0,4},{4,8},{8,12},{12,16},{16,20},{20,24},{24,28},{1,5},{5,9},{9,... | collective-permute-start | bytes 196616 | tf_op jit(solution)/shard_map/ppermute | solution.py:421
  72.5 1.9 %collective-permute-start.15 = (f32[64,256]{1,0:T(8,128)S(1)}, f32[64,256]{1,0:T(8,128)S(1)}, u32[]{:S(2)}, u32[]{:S(2)}) collective-permute-start(f32[64,256]{1,0:T(8,128)S(1)} %get-tuple-element.59), channel_id=1, source_target_pairs={{4,0},{8,4},{12,8},{16,12},{20,16},{24,20},{28,24},{5,1},{9,5},{13... | collective-permute-start | bytes 196616 | tf_op jit(solution)/shard_map/ppermute | solution.py:422
  74.4 4.5 %post.1 = (f32[64,32,256]{2,1,0:T(8,128)}, f32[64,32,256]{2,1,0:T(8,128)}) custom-call(s32[1]{0:T(128)} %bitcast.z_ref, bf16[4,64,256]{2,1,0:T(8,128)(2,1)S(1)} %get-tuple-element.61.refs_0_, bf16[4,64,256]{2,1,0:T(8,128)(2,1)S(1)} %collective-permute-done.11.refs_7_.refs_1_, bf16[4,64,256]{2,1,0:T(8,128)(2,1)S(1)} %collective-permute-done.12.refs_8_.refs_2_, ...), custom_call_target="tpu_custom_call" | custom-call | tf_op jit(solution)/shard_map/post/pallas_call | solution.py:431
  79.0 2.1 %close.1 = f32[64,32,256]{2,1,0:T(8,128)} custom-call(f32[64,256]{1,0:T(8,128)S(1)} %collective-permute-done.14.low, f32[64,256]{1,0:T(8,128)S(1)} %collective-permute-done.15.high, f32[6,32,256]{2,1,0:T(8,128)S(1)} %get-tuple-element.60.refs_10_.faces, f32[32,256]{1,0:T(8,128)S(1)} %get-tuple-element.55.refs_6_.refs_11_.inverse, ...), custom_call_target="tpu_custom_call", output_to_operand_aliasing={{}: (4, {})} | custom-call | tf_op jit(solution)/shard_map/close/pallas_call | solution.py:459
  (42 shorter events, 1.9 us)
Async XLA Ops:
  0.6 1.6 %copy-start = (f32[64,32,256]{2,1,0:T(8,128)S(1)}, f32[64,32,256]{2,1,0:T(8,128)}, u32[]{:S(2)}) copy-start(f32[64,32,256]{2,1,0:T(8,128)} %refs_9_.1) | copy-start | bytes 6291460
  2.2 11.2 %copy-start.5 = (f32[32,256]{1,0:T(8,128)S(1)}, f32[32,256]{1,0:T(8,128)}, u32[]{:S(2)}) copy-start(f32[32,256]{1,0:T(8,128)} %mean_ref.1) | copy-start | bytes 98308
  2.2 11.2 %copy-start.1 = (f32[64,32,256]{2,1,0:T(8,128)S(1)}, f32[64,32,256]{2,1,0:T(8,128)}, u32[]{:S(2)}) copy-start(f32[64,32,256]{2,1,0:T(8,128)} %refs_9_.1) | copy-start | bytes 6291460
  2.9 29.2 %collective-permute-start = (bf16[6,64,256]{2,1,0:T(8,128)(2,1)S(1)}, bf16[6,64,256]{2,1,0:T(8,128)(2,1)S(1)}, u32[]{:S(2)}, u32[]{:S(2)}) collective-permute-start(bf16[6,64,256]{2,1,0:T(8,128)(2,1)S(1)} %get-tuple-element.34), channel_id=1, source_target_pairs={{0,3},{1,2},{2,1},{3,0},{4,7},{5,6},{6,5},{7,4},{8,11},{9,10},{10,... | collective-permute-start | bytes 589832 | tf_op jit(solution)/shard_map/ppermute | solution.py:320
  7.1 21.2 %collective-permute-start.1 = (bf16[6,64,256]{2,1,0:T(8,128)(2,1)S(1)}, bf16[6,64,256]{2,1,0:T(8,128)(2,1)S(1)}, u32[]{:S(2)}, u32[]{:S(2)}) collective-permute-start(bf16[6,64,256]{2,1,0:T(8,128)(2,1)S(1)} %get-tuple-element.35), channel_id=1, source_target_pairs={{0,2},{1,3},{2,0},{3,1},{4,6},{5,7},{6,4},{7,5},{8,10},{9,11},{10,... | collective-permute-start | bytes 589832 | tf_op jit(solution)/shard_map/ppermute | solution.py:320
  7.1 25.0 %collective-permute-start.2 = (bf16[6,64,256]{2,1,0:T(8,128)(2,1)S(1)}, bf16[6,64,256]{2,1,0:T(8,128)(2,1)S(1)}, u32[]{:S(2)}, u32[]{:S(2)}) collective-permute-start(bf16[6,64,256]{2,1,0:T(8,128)(2,1)S(1)} %get-tuple-element.36), channel_id=1, source_target_pairs={{0,1},{1,0},{2,3},{3,2},{4,5},{5,4},{6,7},{7,6},{8,9},{9,8},{10,11... | collective-permute-start | bytes 589832 | tf_op jit(solution)/shard_map/ppermute | solution.py:320
  8.2 0.9 %copy-start.4 = (s32[5376,3]{0,1:T(4,128)S(1)}, s32[5376,3]{0,1:T(4,128)}, u32[]{:S(2)}) copy-start(s32[5376,3]{0,1:T(4,128)} %param.10) | copy-start | bytes 193540
  13.5 7.8 %copy-start.3 = (f32[64,32,256]{2,1,0:T(8,128)S(1)}, f32[64,32,256]{2,1,0:T(8,128)}, u32[]{:S(2)}) copy-start(f32[64,32,256]{2,1,0:T(8,128)} %refs_8_.1) | copy-start | bytes 6291460
  13.5 11.7 %copy-start.2 = (f32[20,32,256]{2,1,0:T(8,128)S(1)}, f32[20,32,256]{2,1,0:T(8,128)}, u32[]{:S(2)}) copy-start(f32[20,32,256]{2,1,0:T(8,128)} %fields_ref.1) | copy-start | bytes 1966084
  14.9 6.4 %collective-permute-start.3 = (f32[88,256]{1,0:T(8,128)S(1)}, f32[88,256]{1,0:T(8,128)S(1)}, u32[]{:S(2)}, u32[]{:S(2)}) collective-permute-start(f32[88,256]{1,0:T(8,128)S(1)} %get-tuple-element.73), channel_id=1, source_target_pairs={{0,4},{4,8},{8,12},{12,16},{16,20},{20,24},{24,28},{1,5},{5,9},{9,... | collective-permute-start | bytes 270344 | tf_op jit(solution)/shard_map/ppermute | solution.py:344
  19.3 5.8 %collective-permute-start.4 = (f32[88,256]{1,0:T(8,128)S(1)}, f32[88,256]{1,0:T(8,128)S(1)}, u32[]{:S(2)}, u32[]{:S(2)}) collective-permute-start(f32[88,256]{1,0:T(8,128)S(1)} %get-tuple-element.72), channel_id=1, source_target_pairs={{4,0},{8,4},{12,8},{16,12},{20,16},{24,20},{28,24},{5,1},{9,5},{13... | collective-permute-start | bytes 270344 | tf_op jit(solution)/shard_map/ppermute | solution.py:344
  26.1 2.1 %copy-start.6 = (f32[32,6,24,256]{3,2,1,0:T(8,128)}, f32[32,6,24,256]{3,2,1,0:T(8,128)S(1)}, u32[]{:S(2)}) copy-start(f32[32,6,24,256]{3,2,1,0:T(8,128)S(1)} %get-tuple-element.49.refs_6_.refs_10_) | copy-start | bytes 14155780
  28.3 16.0 %collective-permute-start.5 = (bf16[4,64,256]{2,1,0:T(8,128)(2,1)S(1)}, bf16[4,64,256]{2,1,0:T(8,128)(2,1)S(1)}, u32[]{:S(2)}, u32[]{:S(2)}) collective-permute-start(bf16[4,64,256]{2,1,0:T(8,128)(2,1)S(1)} %get-tuple-element.45), channel_id=1, source_target_pairs={{0,3},{1,2},{2,1},{3,0},{4,7},{5,6},{6,5},{7,4},{8,11},{9,10},{10,... | collective-permute-start | bytes 393224 | tf_op jit(solution)/shard_map/ppermute | solution.py:320
  31.7 13.0 %collective-permute-start.6 = (bf16[4,64,256]{2,1,0:T(8,128)(2,1)S(1)}, bf16[4,64,256]{2,1,0:T(8,128)(2,1)S(1)}, u32[]{:S(2)}, u32[]{:S(2)}) collective-permute-start(bf16[4,64,256]{2,1,0:T(8,128)(2,1)S(1)} %get-tuple-element.46), channel_id=1, source_target_pairs={{0,2},{1,3},{2,0},{3,1},{4,6},{5,7},{6,4},{7,5},{8,10},{9,11},{10,... | collective-permute-start | bytes 393224 | tf_op jit(solution)/shard_map/ppermute | solution.py:320
  31.7 13.0 %collective-permute-start.7 = (bf16[4,64,256]{2,1,0:T(8,128)(2,1)S(1)}, bf16[4,64,256]{2,1,0:T(8,128)(2,1)S(1)}, u32[]{:S(2)}, u32[]{:S(2)}) collective-permute-start(bf16[4,64,256]{2,1,0:T(8,128)(2,1)S(1)} %get-tuple-element.47), channel_id=1, source_target_pairs={{0,1},{1,0},{2,3},{3,2},{4,5},{5,4},{6,7},{7,6},{8,9},{9,8},{10,11... | collective-permute-start | bytes 393224 | tf_op jit(solution)/shard_map/ppermute | solution.py:320
  41.1 15.9 %collective-permute-start.11 = (bf16[4,64,256]{2,1,0:T(8,128)(2,1)S(1)}, bf16[4,64,256]{2,1,0:T(8,128)(2,1)S(1)}, u32[]{:S(2)}, u32[]{:S(2)}) collective-permute-start(bf16[4,64,256]{2,1,0:T(8,128)(2,1)S(1)} %get-tuple-element.50.refs_11_), channel_id=1, source_target_pairs={{0,3},{1,2},{2,1},{3,0},{4,7},{5,6},{6,5},{7,4},{8,11},{9,10},{10,... | collective-permute-start | bytes 393224 | tf_op jit(solution)/shard_map/ppermute | solution.py:320
  44.3 13.0 %collective-permute-start.12 = (bf16[4,64,256]{2,1,0:T(8,128)(2,1)S(1)}, bf16[4,64,256]{2,1,0:T(8,128)(2,1)S(1)}, u32[]{:S(2)}, u32[]{:S(2)}) collective-permute-start(bf16[4,64,256]{2,1,0:T(8,128)(2,1)S(1)} %get-tuple-element.56), channel_id=1, source_target_pairs={{0,2},{1,3},{2,0},{3,1},{4,6},{5,7},{6,4},{7,5},{8,10},{9,11},{10,... | collective-permute-start | bytes 393224 | tf_op jit(solution)/shard_map/ppermute | solution.py:320
  44.4 13.0 %collective-permute-start.13 = (bf16[4,64,256]{2,1,0:T(8,128)(2,1)S(1)}, bf16[4,64,256]{2,1,0:T(8,128)(2,1)S(1)}, u32[]{:S(2)}, u32[]{:S(2)}) collective-permute-start(bf16[4,64,256]{2,1,0:T(8,128)(2,1)S(1)} %get-tuple-element.57), channel_id=1, source_target_pairs={{0,1},{1,0},{2,3},{3,2},{4,5},{5,4},{6,7},{7,6},{8,9},{9,8},{10,11... | collective-permute-start | bytes 393224 | tf_op jit(solution)/shard_map/ppermute | solution.py:320
  53.7 7.1 %collective-permute-start.8 = (bf16[4,64,256]{2,1,0:T(8,128)(2,1)S(1)}, bf16[4,64,256]{2,1,0:T(8,128)(2,1)S(1)}, u32[]{:S(2)}, u32[]{:S(2)}) collective-permute-start(bf16[4,64,256]{2,1,0:T(8,128)(2,1)S(1)} %get-tuple-element.52), channel_id=1, source_target_pairs={{0,3},{1,2},{2,1},{3,0},{4,7},{5,6},{6,5},{7,4},{8,11},{9,10},{10,... | collective-permute-start | bytes 393224 | tf_op jit(solution)/shard_map/ppermute | solution.py:320
  57.0 10.5 %collective-permute-start.9 = (bf16[4,64,256]{2,1,0:T(8,128)(2,1)S(1)}, bf16[4,64,256]{2,1,0:T(8,128)(2,1)S(1)}, u32[]{:S(2)}, u32[]{:S(2)}) collective-permute-start(bf16[4,64,256]{2,1,0:T(8,128)(2,1)S(1)} %get-tuple-element.53), channel_id=1, source_target_pairs={{0,2},{1,3},{2,0},{3,1},{4,6},{5,7},{6,4},{7,5},{8,10},{9,11},{10,... | collective-permute-start | bytes 393224 | tf_op jit(solution)/shard_map/ppermute | solution.py:320
  57.0 10.5 %collective-permute-start.10 = (bf16[4,64,256]{2,1,0:T(8,128)(2,1)S(1)}, bf16[4,64,256]{2,1,0:T(8,128)(2,1)S(1)}, u32[]{:S(2)}, u32[]{:S(2)}) collective-permute-start(bf16[4,64,256]{2,1,0:T(8,128)(2,1)S(1)} %get-tuple-element.54), channel_id=1, source_target_pairs={{0,1},{1,0},{2,3},{3,2},{4,5},{5,4},{6,7},{7,6},{8,9},{9,8},{10,11... | collective-permute-start | bytes 393224 | tf_op jit(solution)/shard_map/ppermute | solution.py:320
  67.5 11.4 %collective-permute-start.14 = (f32[64,256]{1,0:T(8,128)S(1)}, f32[64,256]{1,0:T(8,128)S(1)}, u32[]{:S(2)}, u32[]{:S(2)}) collective-permute-start(f32[64,256]{1,0:T(8,128)S(1)} %get-tuple-element.58), channel_id=1, source_target_pairs={{0,4},{4,8},{8,12},{12,16},{16,20},{20,24},{24,28},{1,5},{5,9},{9,... | collective-permute-start | bytes 196616 | tf_op jit(solution)/shard_map/ppermute | solution.py:421
  72.5 6.5 %collective-permute-start.15 = (f32[64,256]{1,0:T(8,128)S(1)}, f32[64,256]{1,0:T(8,128)S(1)}, u32[]{:S(2)}, u32[]{:S(2)}) collective-permute-start(f32[64,256]{1,0:T(8,128)S(1)} %get-tuple-element.59), channel_id=1, source_target_pairs={{4,0},{8,4},{12,8},{16,12},{20,16},{24,20},{28,24},{5,1},{9,5},{13... | collective-permute-start | bytes 196616 | tf_op jit(solution)/shard_map/ppermute | solution.py:422

commit v5 on v4

--- a/solution.py
+++ b/solution.py
@@ -13,7 +13,8 @@
 cheb_radius = 0.875
 SMALL = pl.CostEstimate(flops=1, bytes_accessed=1, transcendentals=0)
 LARGE = pl.CostEstimate(flops=10**10, bytes_accessed=2**24, transcendentals=0)
-VMEM_LIMIT = 48 * 1024 * 1024
+VMEM_LIMIT = 16 * 1024 * 1024
+VMEM_MOST = 115 * 512 * 1024
 
 
 def in_vmem(count):
@@ -51,6 +52,18 @@
         place = jnp.bitwise_xor(z, p)
         for rho in range(outs[p].shape[0]):
             outs[p][rho] = turned[row_of(place, rho, slab, count, rows)]
+
+
+def rim_kernel(turned, mean_ref, fields_ref, after, last, first):
+    rows, here, cells = turned.shape
+    fields = fields_ref.shape[0]
+    for out, row in ((first, 0), (last, rows - 1)):
+        out[:here] = turned[row].astype(jnp.float32)
+        out[here : here + 1, :] = mean_ref[row : row + 1, :]
+        for field in range(fields):
+            out[here + 1 + field : here + 2 + field, :] = fields_ref[field, row : row + 1, :]
+        rest = out.shape[0] - here - 1 - fields
+        out[here + 1 + fields :, :] = jnp.zeros((rest, cells), jnp.float32)
 
 
 def late_kernel(count, slab, rows, z_ref, turned, low_ref, high_ref, after, *outs):
@@ -125,7 +138,17 @@
 
 
 def weight_kernel(
-    mean_ref, fields_ref, low_ref, high_ref, weight_ref, faces_ref, inverse_ref, stack_ref, turned
+    count,
+    z_ref,
+    mean_ref,
+    fields_ref,
+    low_ref,
+    high_ref,
+    weight_ref,
+    faces_ref,
+    inverse_ref,
+    stack_ref,
+    turned,
 ):
     fields, rows, cells = fields_ref.shape
     deep = stack_ref.shape[0]
@@ -134,13 +157,18 @@
     stack_ref[0] = mean_ref[...]
     stack_ref[1 : fields + 1] = fields_ref[...]
     stack_ref[fields + 1 :] = jnp.zeros((deep - fields - 1, rows, cells), jnp.float32)
-    turned[...] = jnp.swapaxes(stack_ref[...], 0, 1)
-    for row in range(rows):
+    turned[1 : rows + 1] = jnp.swapaxes(stack_ref[...], 0, 1)
+    turned[0] = low_ref[start:, :]
+    turned[rows + 1] = high_ref[start:, :]
+    z = z_ref[0]
+    slab = weight_ref.shape[0]
+    ahead = jnp.where(z < count // 2, 1, -1)
+    for rho in range(slab):
+        row = 1 + row_of(z, rho, slab, count, rows)
         centre = turned[row]
-        up = high_ref[start:, :] if row == rows - 1 else turned[row + 1]
-        down = low_ref[start:, :] if row == 0 else turned[row - 1]
-        for f, other in enumerate((up, down) + beside(centre, mask_set)):
-            weight_ref[row, f] = 0.5 * (centre + other)
+        others = (turned[row + ahead], turned[row - ahead]) + beside(centre, mask_set)
+        for f, other in enumerate(others):
+            weight_ref[rho, f] = 0.5 * (centre + other)
     place = lax.broadcasted_iota(jnp.int32, (rows, cells), 0)
     centre = mean_ref[...]
     high, low = high_ref[start : start + 1, :], low_ref[start : start + 1, :]
@@ -154,7 +182,7 @@
     inverse_ref[...] = 1.0 / diag
 
 
-def mix_kernel(count, slab, groups, fields, window, skip, begin, extra, z_ref, *refs):
+def mix_kernel(count, groups, fields, window, skip, begin, extra, *refs):
     arrays = max(a for a, _ in window) + 1
     sources = refs[: arrays * count]
     dense_ref, own_ref, weight_ref = refs[arrays * count : arrays * count + 3]
@@ -168,15 +196,10 @@
             part = sources[array * count + (count - p) % count]
             rows_ref[k, p * here : (p + 1) * here, :] = part[row]
     mask_set = masks(cells)
-    z = z_ref[0]
-    rows = weight_ref.shape[0]
-    ahead = jnp.where(z < count // 2, 0, 1)
-    faces = (ahead, 1 - ahead, 2, 3, 4, 5)
-
     def each_row(r, carry):
-        row = row_of(z, jnp.where(r == 0, begin[0], begin[1] + r), slab, count, rows)
+        row = jnp.where(r == 0, begin[0], begin[1] + r)
         r_in = r + jnp.where(r == 0, 0, skip)
-        mean_weights = [weight_ref[row, f, 0:1, :] for f in faces]
+        mean_weights = [weight_ref[row, f, 0:1, :] for f in range(6)]
         for t in range(0, size, 16):
             at = slice(t, t + 16)
             centre = rows_ref[r_in + 1, at].astype(jnp.float32)
@@ -196,7 +219,7 @@
                 field = min(1 + g * GROUP + k, fields - 1)
                 weights = [
                     jnp.broadcast_to(weight_ref[row, f, field : field + 1, :], (16, cells))
-                    for f in faces
+                    for f in range(6)
                 ]
                 weights = [w.astype(bf16) for w in weights]
                 for t in range(0, size, 16):
@@ -309,7 +332,7 @@
             pltpu.VMEM((parts, here // parts, rows, cells), jnp.float32),
             pltpu.SemaphoreType.DMA((parts,)),
         ],
-        compiler_params=params,
+        compiler_params=pltpu.CompilerParams(vmem_limit_bytes=VMEM_MOST),
         cost_estimate=SMALL,
         name="turn",
     )(z_arg, iterate)
@@ -336,37 +359,34 @@
     )(z_arg, entries.T, values[None])
     upward = [(i, i + 1) for i in range(doms - 1)]
     downward = [(b, a) for a, b in upward]
-    iterate_here, mean_here, fields_here, _ = lax.optimization_barrier(
-        (iterate, mean_coef, kl_fields, own)
-    )
-    filler = jnp.zeros((deep - fields, cells), jnp.float32)
-    low_rim, high_rim = (
-        lax.ppermute(
-            jnp.concatenate(
-                [iterate_here[:, at], mean_here[at][None], fields_here[:, at], filler], 0
-            ),
-            "dom",
-            pairs,
-        )
-        for at, pairs in ((rows - 1, upward), (0, downward))
-    )
+    last_rim, first_rim = pl.pallas_call(
+        rim_kernel,
+        out_shape=[jax.ShapeDtypeStruct((here + deep, cells), jnp.float32)] * 2,
+        in_specs=in_vmem(3) + [pl.BlockSpec(memory_space=pl.ANY)],
+        out_specs=in_vmem(2),
+        compiler_params=params,
+        cost_estimate=SMALL,
+        name="rim",
+    )(turned, mean_coef, kl_fields, own)
+    low_rim = lax.ppermute(last_rim, "dom", upward)
+    high_rim = lax.ppermute(first_rim, "dom", downward)
     weights, faces, inverse = pl.pallas_call(
-        weight_kernel,
+        functools.partial(weight_kernel, count),
         out_shape=[
-            jax.ShapeDtypeStruct((rows, 6, deep, cells), jnp.float32),
+            jax.ShapeDtypeStruct((slab, 6, deep, cells), jnp.float32),
             jax.ShapeDtypeStruct((6, rows, cells), jnp.float32),
             jax.ShapeDtypeStruct((rows, cells), jnp.float32),
         ],
-        in_specs=in_vmem(4),
+        in_specs=[in_smem()] + in_vmem(4),
         out_specs=in_vmem(3),
         scratch_shapes=[
             pltpu.VMEM((deep, rows, cells), jnp.float32),
-            pltpu.VMEM((rows, deep, cells), jnp.float32),
+            pltpu.VMEM((rows + 2, deep, cells), jnp.float32),
         ],
         compiler_params=params,
         cost_estimate=SMALL,
         name="weights",
-    )(mean_coef, kl_fields, low_rim, high_rim)
+    )(z_arg, mean_coef, kl_fields, low_rim, high_rim)
     late = pl.pallas_call(
         functools.partial(late_kernel, count, slab, rows),
         out_shape=[jax.ShapeDtypeStruct((slab - half, here, cells), bf16)] * count,
@@ -382,11 +402,10 @@
         flat = [a for group in arrays for a in group]
         return pl.pallas_call(
             functools.partial(
-                mix_kernel, count, slab, groups, fields, window, skip, begin, len(after)
+                mix_kernel, count, groups, fields, window, skip, begin, len(after)
             ),
             out_shape=[jax.ShapeDtypeStruct((rows_out, here, cells), bf16)] * count,
-            in_specs=[in_smem()]
-            + in_vmem(len(flat) + 3)
+            in_specs=in_vmem(len(flat) + 3)
             + [pl.BlockSpec(memory_space=pl.ANY)] * len(after),
             out_specs=in_vmem(count),
             scratch_shapes=[
@@ -398,7 +417,7 @@
             compiler_params=params,
             cost_estimate=LARGE,
             name="mix",
-        )(z_arg, *flat, dense, own, weights, *after)
+        )(*flat, dense, own, weights, *after)
 
     window = tuple((0, k) for k in range(half + 2))
     mixed = mix([early], window, 0, (1, 1), half)

time: 81.5 us -> 73.8 us (0.906)
  local copies, waits for them, and re-layouts: 8.27 us -> 2.58 us
  Pallas kernels: 29.1 us -> 26.1 us
    pallas_call x3 -> x4, Pallas kernels: 18.9 us -> 13.6 us  [the longest x2 13.1 us: mix(): pl.pallas_call(functools.partial(mix_kernel, count, groups, fields, windo...]
    unnamed x14 -> x18, local copies, waits for them, and re-layouts: 4.62 us -> 1.25 us
    optimization_barrier x2 -> x0, local copies, waits for them, and re-layouts: 2.7 us -> none  [body(): lax.optimization_barrier((iterate, mean_coef, kl_fields, own))]
    pallas_call x1, Pallas kernels: 0.64 us -> 2.95 us  [body(): pl.pallas_call(functools.partial(turn_kernel, count, slab, rows), out_sha...]
    ppermute x12, waiting for transfers between devices: 10.1 us -> 11.7 us  [swap(): lax.ppermute(arrays[p], 'mode', [(i, i ^ p) for i in range(count)])]
    slice x1, local copies, waits for them, and re-layouts: 0.09 us -> 1.3 us  [body(): source[:, rows - 1]]
    ppermute x2, waiting for transfers between devices: 3.8 us -> 2.9 us  [the longest x1 2.9 us: body(): high_rim = lax.ppermute(first_rim, 'dom', downward)]
  transfers between devices with their start and end apart: 16 -> 16, of which waited for: 3 -> 4; matrix products, arithmetic and copies ran while one was open for 5% -> 2% of each run, Pallas kernels for 33% -> 29%
where the time goes in v5:
time: 73.8 us; the launch traced here: 73.4 us
  starting transfers between devices  29.3 us (40%)
  Pallas kernels  26.1 us (35%)
  waiting for transfers between devices  14.6 us (20%)
  local copies, waits for them, and re-layouts  2.58 us (3%)
  between operations  0.86 us (1%)
    ppermute x12, starting transfers between devices, swap(): lax.ppermute(arrays[p], 'mode', [(i, i ^ p) for i in range(count)])  15.4 us
    pallas_call x2, Pallas kernels, mix(): pl.pallas_call(functools.partial(mix_kernel, count, groups, fields, windo...  13.1 us
    ppermute x12, waiting for transfers between devices, swap(): lax.ppermute(arrays[p], 'mode', [(i, i ^ p) for i in range(count)])  11.7 us
    ppermute x1, starting transfers between devices, body(): low = lax.ppermute(top, 'dom', upward)  5.54 us
    pallas_call x1, Pallas kernels, body(): pl.pallas_call(functools.partial(post_kernel, count, slab, half, rows, rh...  4.52 us
    ppermute x1, starting transfers between devices, body(): low_rim = lax.ppermute(last_rim, 'dom', upward)  4.51 us
    pallas_call x1, Pallas kernels, body(): pl.pallas_call(functools.partial(turn_kernel, count, slab, rows), out_sha...  2.95 us
    ppermute x1, waiting for transfers between devices, body(): high_rim = lax.ppermute(first_rim, 'dom', downward)  2.9 us
  transfers between devices with their start and end apart: 16, of which 4 were waited for; matrix products, arithmetic and copies ran while one was open for 2% of the time, Pallas kernels for 29%

profile of v5, /device:TPU:1, one launch (start us, length us, event | category | flops | bytes accessed | tf_op | source)
XLA Modules:
  0.0 73.4 jit_solution(16808124663569658929)
XLA Ops:
  0.7 2.9 %turn.1 = (bf16[32,64,256]{2,1,0:T(8,128)(2,1)}, bf16[6,64,256]{2,1,0:T(8,128)(2,1)}, bf16[6,64,256]{2,1,0:T(8,128)(2,1)}, bf16[6,64,256]{2,1,0:T(8,128)(2,1)}, bf16[6,64,256]{2,1,0:T(8,128)(2,1)}) custom-call(s32[1]{0:T(128)} %bitcast.z_ref, f32[64,32,256]{2,1,0:T(8,128)} %refs_9_.1), custom_call_target="tpu_custom_call" | custom-call | flops 1 | bytes 1 | tf_op jit(solution)/shard_map/turn/pallas_call | solution.py:325
  3.6 4.2 %collective-permute-start = (bf16[6,64,256]{2,1,0:T(8,128)(2,1)}, bf16[6,64,256]{2,1,0:T(8,128)(2,1)S(1)}, u32[]{:S(2)}, u32[]{:S(2)}) collective-permute-start(bf16[6,64,256]{2,1,0:T(8,128)(2,1)} %get-tuple-element.33), channel_id=1, source_target_pairs={{0,3},{1,2},{2,1},{3,0},{4,7},{5,6},{6,5},{7,4},{8,11},{9,10},{10,... | collective-permute-start | bytes 589832 | tf_op jit(solution)/shard_map/ppermute | solution.py:343
  8.2 2.8 %dense.1 = (bf16[4,256,1280]{2,1,0:T(8,128)(2,1)S(1)}, f32[256,128]{1,0:T(8,128)S(1)}) custom-call(s32[1]{0:T(128)} %bitcast.z_ref, s32[3,5376]{1,0:T(4,128)S(1)} %bitcast.6, f32[1,5376]{1,0:T(1,128)S(1)} %broadcast_in_dim.3.value_ref), custom_call_target="tpu_custom_call" | custom-call | flops 1 | bytes 1 | tf_op jit(solution)/shard_map/dense/pallas_call | solution.py:348
  11.1 1.2 %copy-done.1 = bf16[32,64,256]{2,1,0:T(8,128)(2,1)S(1)} copy-done((bf16[32,64,256]{2,1,0:T(8,128)(2,1)S(1)}, bf16[32,64,256]{2,1,0:T(8,128)(2,1)}, u32[]{:S(2)}) %copy-start.1) | copy-done | bytes 1048600
  12.4 4.5 %collective-permute-start.3 = (f32[88,256]{1,0:T(8,128)S(1)}, f32[88,256]{1,0:T(8,128)S(1)}, u32[]{:S(2)}, u32[]{:S(2)}) collective-permute-start(f32[88,256]{1,0:T(8,128)S(1)} %get-tuple-element.40), channel_id=1, source_target_pairs={{0,4},{4,8},{8,12},{12,16},{16,20},{20,24},{24,28},{1,5},{5,9},{9,... | collective-permute-start | bytes 270344 | tf_op jit(solution)/shard_map/ppermute | solution.py:371
  16.9 1.9 %collective-permute-start.4 = (f32[88,256]{1,0:T(8,128)S(1)}, f32[88,256]{1,0:T(8,128)S(1)}, u32[]{:S(2)}, u32[]{:S(2)}) collective-permute-start(f32[88,256]{1,0:T(8,128)S(1)} %get-tuple-element.41), channel_id=1, source_target_pairs={{4,0},{8,4},{12,8},{16,12},{20,16},{24,20},{28,24},{5,1},{9,5},{13... | collective-permute-start | bytes 270344 | tf_op jit(solution)/shard_map/ppermute | solution.py:372
  18.8 1.3 %fusion = (f32[64,1,256]{2,1,0:T(1,128)S(1)}, f32[64,1,256]{2,1,0:T(1,128)S(1)}) fusion(f32[64,32,256]{2,1,0:T(8,128)} %refs_8_.1), kind=kLoop, calls=%fused_computation.2 | loop fusion | bytes 262144 | tf_op jit(solution)/shard_map/slice | solution.py:439
  20.1 2.9 %collective-permute-done.4.high_ref = f32[88,256]{1,0:T(8,128)S(1)} collective-permute-done((f32[88,256]{1,0:T(8,128)S(1)}, f32[88,256]{1,0:T(8,128)S(1)}, u32[]{:S(2)}, u32[]{:S(2)}) %collective-permute-start.4) | collective-permute-done | bytes 90144 | tf_op jit(solution)/shard_map/ppermute | solution.py:372
  23.0 0.5 weights.1
  23.5 0.8 %collective-permute-done.1.after.refs_2_ = bf16[6,64,256]{2,1,0:T(8,128)(2,1)S(1)} collective-permute-done((bf16[6,64,256]{2,1,0:T(8,128)(2,1)}, bf16[6,64,256]{2,1,0:T(8,128)(2,1)S(1)}, u32[]{:S(2)}, u32[]{:S(2)}) %collective-permute-start.1) | collective-permute-done | bytes 196640 | tf_op jit(solution)/shard_map/ppermute | solution.py:343
  24.4 2.6 %collective-permute-start.5 = (bf16[4,64,256]{2,1,0:T(8,128)(2,1)S(1)}, bf16[4,64,256]{2,1,0:T(8,128)(2,1)S(1)}, u32[]{:S(2)}, u32[]{:S(2)}) collective-permute-start(bf16[4,64,256]{2,1,0:T(8,128)(2,1)S(1)} %get-tuple-element.43), channel_id=1, source_target_pairs={{0,3},{1,2},{2,1},{3,0},{4,7},{5,6},{6,5},{7,4},{8,11},{9,10},{10,... | collective-permute-start | bytes 393224 | tf_op jit(solution)/shard_map/ppermute | solution.py:343
  27.0 1.0 %collective-permute-start.7 = (bf16[4,64,256]{2,1,0:T(8,128)(2,1)S(1)}, bf16[4,64,256]{2,1,0:T(8,128)(2,1)S(1)}, u32[]{:S(2)}, u32[]{:S(2)}) collective-permute-start(bf16[4,64,256]{2,1,0:T(8,128)(2,1)S(1)} %get-tuple-element.45), channel_id=1, source_target_pairs={{0,1},{1,0},{2,3},{3,2},{4,5},{5,4},{6,7},{7,6},{8,9},{9,8},{10,11... | collective-permute-start | bytes 393224 | tf_op jit(solution)/shard_map/ppermute | solution.py:343
  28.1 6.5 %mix.2 = (bf16[4,64,256]{2,1,0:T(8,128)(2,1)S(1)}, bf16[4,64,256]{2,1,0:T(8,128)(2,1)S(1)}, bf16[4,64,256]{2,1,0:T(8,128)(2,1)S(1)}, bf16[4,64,256]{2,1,0:T(8,128)(2,1)S(1)}) custom-call(bf16[6,64,256]{2,1,0:T(8,128)(2,1)S(1)} %copy-done.7, bf16[6,64,256]{2,1,0:T(8,128)(2,1)S(1)} %collective-permute-done.refs_1_, ...), custom_call_target="tpu_custom_call" | custom-call | flops 10000000000 | bytes 16777216 | tf_op jit(solution)/shard_map/mix/pallas_call | solution.py:403
  34.6 2.6 %collective-permute-start.11 = (bf16[4,64,256]{2,1,0:T(8,128)(2,1)S(1)}, bf16[4,64,256]{2,1,0:T(8,128)(2,1)S(1)}, u32[]{:S(2)}, u32[]{:S(2)}) collective-permute-start(bf16[4,64,256]{2,1,0:T(8,128)(2,1)S(1)} %get-tuple-element.48.refs_11_), channel_id=1, source_target_pairs={{0,3},{1,2},{2,1},{3,0},{4,7},{5,6},{6,5},{7,4},{8,11},{9,10},{10,... | collective-permute-start | bytes 393224 | tf_op jit(solution)/shard_map/ppermute | solution.py:343
  37.2 1.0 %collective-permute-start.13 = (bf16[4,64,256]{2,1,0:T(8,128)(2,1)S(1)}, bf16[4,64,256]{2,1,0:T(8,128)(2,1)S(1)}, u32[]{:S(2)}, u32[]{:S(2)}) collective-permute-start(bf16[4,64,256]{2,1,0:T(8,128)(2,1)S(1)} %get-tuple-element.55), channel_id=1, source_target_pairs={{0,1},{1,0},{2,3},{3,2},{4,5},{5,4},{6,7},{7,6},{8,9},{9,8},{10,11... | collective-permute-start | bytes 393224 | tf_op jit(solution)/shard_map/ppermute | solution.py:343
  38.2 6.5 %mix.3 = (bf16[4,64,256]{2,1,0:T(8,128)(2,1)S(1)}, bf16[4,64,256]{2,1,0:T(8,128)(2,1)S(1)}, bf16[4,64,256]{2,1,0:T(8,128)(2,1)S(1)}, bf16[4,64,256]{2,1,0:T(8,128)(2,1)S(1)}) custom-call(bf16[6,64,256]{2,1,0:T(8,128)(2,1)S(1)} %copy-done.7, bf16[6,64,256]{2,1,0:T(8,128)(2,1)S(1)} %collective-permute-done.refs_1_, ...), custom_call_target="tpu_custom_call" | custom-call | flops 10000000000 | bytes 16777216 | tf_op jit(solution)/shard_map/mix/pallas_call | solution.py:403
  44.8 2.6 %collective-permute-start.8 = (bf16[4,64,256]{2,1,0:T(8,128)(2,1)S(1)}, bf16[4,64,256]{2,1,0:T(8,128)(2,1)S(1)}, u32[]{:S(2)}, u32[]{:S(2)}) collective-permute-start(bf16[4,64,256]{2,1,0:T(8,128)(2,1)S(1)} %get-tuple-element.50), channel_id=1, source_target_pairs={{0,3},{1,2},{2,1},{3,0},{4,7},{5,6},{6,5},{7,4},{8,11},{9,10},{10,... | collective-permute-start | bytes 393224 | tf_op jit(solution)/shard_map/ppermute | solution.py:343
  47.4 1.0 %collective-permute-start.10 = (bf16[4,64,256]{2,1,0:T(8,128)(2,1)S(1)}, bf16[4,64,256]{2,1,0:T(8,128)(2,1)S(1)}, u32[]{:S(2)}, u32[]{:S(2)}) collective-permute-start(bf16[4,64,256]{2,1,0:T(8,128)(2,1)S(1)} %get-tuple-element.52), channel_id=1, source_target_pairs={{0,1},{1,0},{2,3},{3,2},{4,5},{5,4},{6,7},{7,6},{8,9},{9,8},{10,11... | collective-permute-start | bytes 393224 | tf_op jit(solution)/shard_map/ppermute | solution.py:343
  48.4 2.2 %collective-permute-done.8.refs_1_.refs_5_ = bf16[4,64,256]{2,1,0:T(8,128)(2,1)S(1)} collective-permute-done((bf16[4,64,256]{2,1,0:T(8,128)(2,1)S(1)}, bf16[4,64,256]{2,1,0:T(8,128)(2,1)S(1)}, u32[]{:S(2)}, u32[]{:S(2)}) %collective-permute-start.8) | collective-permute-done | bytes 131104 | tf_op jit(solution)/shard_map/ppermute | solution.py:343
  50.6 8.6 %collective-permute-done.9.refs_2_.refs_6_ = bf16[4,64,256]{2,1,0:T(8,128)(2,1)S(1)} collective-permute-done((bf16[4,64,256]{2,1,0:T(8,128)(2,1)S(1)}, bf16[4,64,256]{2,1,0:T(8,128)(2,1)S(1)}, u32[]{:S(2)}, u32[]{:S(2)}) %collective-permute-start.9) | collective-permute-done | bytes 131104 | tf_op jit(solution)/shard_map/ppermute | solution.py:343
  59.3 5.5 %collective-permute-start.14 = (f32[64,256]{1,0:T(8,128)S(1)}, f32[64,256]{1,0:T(8,128)S(1)}, u32[]{:S(2)}, u32[]{:S(2)}) collective-permute-start(f32[64,256]{1,0:T(8,128)S(1)} %get-tuple-element.56), channel_id=1, source_target_pairs={{0,4},{4,8},{8,12},{12,16},{16,20},{20,24},{24,28},{1,5},{5,9},{9,... | collective-permute-start | bytes 196616 | tf_op jit(solution)/shard_map/ppermute | solution.py:440
  64.9 1.9 %collective-permute-start.15 = (f32[64,256]{1,0:T(8,128)S(1)}, f32[64,256]{1,0:T(8,128)S(1)}, u32[]{:S(2)}, u32[]{:S(2)}) collective-permute-start(f32[64,256]{1,0:T(8,128)S(1)} %get-tuple-element.57), channel_id=1, source_target_pairs={{4,0},{8,4},{12,8},{16,12},{20,16},{24,20},{28,24},{5,1},{9,5},{13... | collective-permute-start | bytes 196616 | tf_op jit(solution)/shard_map/ppermute | solution.py:441
  66.8 4.5 %post.1 = (f32[64,32,256]{2,1,0:T(8,128)}, f32[64,32,256]{2,1,0:T(8,128)}) custom-call(s32[1]{0:T(128)} %bitcast.z_ref, bf16[4,64,256]{2,1,0:T(8,128)(2,1)S(1)} %get-tuple-element.59.refs_0_, bf16[4,64,256]{2,1,0:T(8,128)(2,1)S(1)} %collective-permute-done.11.refs_7_.refs_1_, bf16[4,64,256]{2,1,0:T(8,128)(2,1)S(1)} %collective-permute-done.12.refs_8_.refs_2_, ...), custom_call_target="tpu_custom_call" | custom-call | tf_op jit(solution)/shard_map/post/pallas_call | solution.py:450
  71.3 2.1 %close.1 = f32[64,32,256]{2,1,0:T(8,128)} custom-call(f32[64,256]{1,0:T(8,128)S(1)} %collective-permute-done.14.low, f32[64,256]{1,0:T(8,128)S(1)} %collective-permute-done.15.high, f32[6,32,256]{2,1,0:T(8,128)S(1)} %get-tuple-element.58.refs_10_.faces, f32[32,256]{1,0:T(8,128)S(1)} %get-tuple-element.53.refs_6_.refs_11_.inverse, ...), custom_call_target="tpu_custom_call", output_to_operand_aliasing={{}: (4, {})} | custom-call | tf_op jit(solution)/shard_map/close/pallas_call | solution.py:478
  (39 shorter events, 0.6 us)
Async XLA Ops:
  0.6 7.6 %copy-start.6 = (s32[5376,3]{0,1:T(4,128)S(1)}, s32[5376,3]{0,1:T(4,128)}, u32[]{:S(2)}) copy-start(s32[5376,3]{0,1:T(4,128)} %param.10) | copy-start | bytes 193540
  0.6 7.6 %copy-start.8 = (f32[5376]{0:T(1024)S(1)}, f32[5376]{0:T(1024)}, u32[]{:S(2)}) copy-start(f32[5376]{0:T(1024)} %param.11) | copy-start | bytes 64516
  0.7 10.4 %copy-start.5 = (f32[32,256]{1,0:T(8,128)S(1)}, f32[32,256]{1,0:T(8,128)}, u32[]{:S(2)}) copy-start(f32[32,256]{1,0:T(8,128)} %mean_ref.3) | copy-start | bytes 98308
  0.7 10.4 %copy-start.3 = (f32[20,32,256]{2,1,0:T(8,128)S(1)}, f32[20,32,256]{2,1,0:T(8,128)}, u32[]{:S(2)}) copy-start(f32[20,32,256]{2,1,0:T(8,128)} %fields_ref.3) | copy-start | bytes 1966084
  3.6 24.4 %collective-permute-start = (bf16[6,64,256]{2,1,0:T(8,128)(2,1)}, bf16[6,64,256]{2,1,0:T(8,128)(2,1)S(1)}, u32[]{:S(2)}, u32[]{:S(2)}) collective-permute-start(bf16[6,64,256]{2,1,0:T(8,128)(2,1)} %get-tuple-element.33), channel_id=1, source_target_pairs={{0,3},{1,2},{2,1},{3,0},{4,7},{5,6},{6,5},{7,4},{8,11},{9,10},{10,... | collective-permute-start | bytes 589832 | tf_op jit(solution)/shard_map/ppermute | solution.py:343
  7.8 16.5 %collective-permute-start.1 = (bf16[6,64,256]{2,1,0:T(8,128)(2,1)}, bf16[6,64,256]{2,1,0:T(8,128)(2,1)S(1)}, u32[]{:S(2)}, u32[]{:S(2)}) collective-permute-start(bf16[6,64,256]{2,1,0:T(8,128)(2,1)} %get-tuple-element.34), channel_id=1, source_target_pairs={{0,2},{1,3},{2,0},{3,1},{4,6},{5,7},{6,4},{7,5},{8,10},{9,11},{10,... | collective-permute-start | bytes 589832 | tf_op jit(solution)/shard_map/ppermute | solution.py:343
  7.9 20.2 %collective-permute-start.2 = (bf16[6,64,256]{2,1,0:T(8,128)(2,1)}, bf16[6,64,256]{2,1,0:T(8,128)(2,1)S(1)}, u32[]{:S(2)}, u32[]{:S(2)}) collective-permute-start(bf16[6,64,256]{2,1,0:T(8,128)(2,1)} %get-tuple-element.35), channel_id=1, source_target_pairs={{0,1},{1,0},{2,3},{3,2},{4,5},{5,4},{6,7},{7,6},{8,9},{9,8},{10,11... | collective-permute-start | bytes 589832 | tf_op jit(solution)/shard_map/ppermute | solution.py:343
  12.3 12.0 %copy-start.2 = (bf16[32,64,256]{2,1,0:T(8,128)(2,1)S(1)}, bf16[32,64,256]{2,1,0:T(8,128)(2,1)}, u32[]{:S(2)}) copy-start(bf16[32,64,256]{2,1,0:T(8,128)(2,1)} %get-tuple-element.36.turned) | copy-start | bytes 3145732
  12.3 15.7 %copy-start.7 = (bf16[6,64,256]{2,1,0:T(8,128)(2,1)S(1)}, bf16[6,64,256]{2,1,0:T(8,128)(2,1)}, u32[]{:S(2)}) copy-start(bf16[6,64,256]{2,1,0:T(8,128)(2,1)} %get-tuple-element.32.refs_0_) | copy-start | bytes 589828
  12.4 7.8 %collective-permute-start.3 = (f32[88,256]{1,0:T(8,128)S(1)}, f32[88,256]{1,0:T(8,128)S(1)}, u32[]{:S(2)}, u32[]{:S(2)}) collective-permute-start(f32[88,256]{1,0:T(8,128)S(1)} %get-tuple-element.40), channel_id=1, source_target_pairs={{0,4},{4,8},{8,12},{12,16},{16,20},{20,24},{24,28},{1,5},{5,9},{9,... | collective-permute-start | bytes 270344 | tf_op jit(solution)/shard_map/ppermute | solution.py:371
  16.9 6.1 %collective-permute-start.4 = (f32[88,256]{1,0:T(8,128)S(1)}, f32[88,256]{1,0:T(8,128)S(1)}, u32[]{:S(2)}, u32[]{:S(2)}) collective-permute-start(f32[88,256]{1,0:T(8,128)S(1)} %get-tuple-element.41), channel_id=1, source_target_pairs={{4,0},{8,4},{12,8},{16,12},{20,16},{24,20},{28,24},{5,1},{9,5},{13... | collective-permute-start | bytes 270344 | tf_op jit(solution)/shard_map/ppermute | solution.py:372
  24.4 12.8 %collective-permute-start.5 = (bf16[4,64,256]{2,1,0:T(8,128)(2,1)S(1)}, bf16[4,64,256]{2,1,0:T(8,128)(2,1)S(1)}, u32[]{:S(2)}, u32[]{:S(2)}) collective-permute-start(bf16[4,64,256]{2,1,0:T(8,128)(2,1)S(1)} %get-tuple-element.43), channel_id=1, source_target_pairs={{0,3},{1,2},{2,1},{3,0},{4,7},{5,6},{6,5},{7,4},{8,11},{9,10},{10,... | collective-permute-start | bytes 393224 | tf_op jit(solution)/shard_map/ppermute | solution.py:343
  27.0 11.2 %collective-permute-start.6 = (bf16[4,64,256]{2,1,0:T(8,128)(2,1)S(1)}, bf16[4,64,256]{2,1,0:T(8,128)(2,1)S(1)}, u32[]{:S(2)}, u32[]{:S(2)}) collective-permute-start(bf16[4,64,256]{2,1,0:T(8,128)(2,1)S(1)} %get-tuple-element.44), channel_id=1, source_target_pairs={{0,2},{1,3},{2,0},{3,1},{4,6},{5,7},{6,4},{7,5},{8,10},{9,11},{10,... | collective-permute-start | bytes 393224 | tf_op jit(solution)/shard_map/ppermute | solution.py:343
  27.0 11.2 %collective-permute-start.7 = (bf16[4,64,256]{2,1,0:T(8,128)(2,1)S(1)}, bf16[4,64,256]{2,1,0:T(8,128)(2,1)S(1)}, u32[]{:S(2)}, u32[]{:S(2)}) collective-permute-start(bf16[4,64,256]{2,1,0:T(8,128)(2,1)S(1)} %get-tuple-element.45), channel_id=1, source_target_pairs={{0,1},{1,0},{2,3},{3,2},{4,5},{5,4},{6,7},{7,6},{8,9},{9,8},{10,11... | collective-permute-start | bytes 393224 | tf_op jit(solution)/shard_map/ppermute | solution.py:343
  34.6 12.8 %collective-permute-start.11 = (bf16[4,64,256]{2,1,0:T(8,128)(2,1)S(1)}, bf16[4,64,256]{2,1,0:T(8,128)(2,1)S(1)}, u32[]{:S(2)}, u32[]{:S(2)}) collective-permute-start(bf16[4,64,256]{2,1,0:T(8,128)(2,1)S(1)} %get-tuple-element.48.refs_11_), channel_id=1, source_target_pairs={{0,3},{1,2},{2,1},{3,0},{4,7},{5,6},{6,5},{7,4},{8,11},{9,10},{10,... | collective-permute-start | bytes 393224 | tf_op jit(solution)/shard_map/ppermute | solution.py:343
  37.2 11.2 %collective-permute-start.12 = (bf16[4,64,256]{2,1,0:T(8,128)(2,1)S(1)}, bf16[4,64,256]{2,1,0:T(8,128)(2,1)S(1)}, u32[]{:S(2)}, u32[]{:S(2)}) collective-permute-start(bf16[4,64,256]{2,1,0:T(8,128)(2,1)S(1)} %get-tuple-element.54), channel_id=1, source_target_pairs={{0,2},{1,3},{2,0},{3,1},{4,6},{5,7},{6,4},{7,5},{8,10},{9,11},{10,... | collective-permute-start | bytes 393224 | tf_op jit(solution)/shard_map/ppermute | solution.py:343
  37.2 11.2 %collective-permute-start.13 = (bf16[4,64,256]{2,1,0:T(8,128)(2,1)S(1)}, bf16[4,64,256]{2,1,0:T(8,128)(2,1)S(1)}, u32[]{:S(2)}, u32[]{:S(2)}) collective-permute-start(bf16[4,64,256]{2,1,0:T(8,128)(2,1)S(1)} %get-tuple-element.55), channel_id=1, source_target_pairs={{0,1},{1,0},{2,3},{3,2},{4,5},{5,4},{6,7},{7,6},{8,9},{9,8},{10,11... | collective-permute-start | bytes 393224 | tf_op jit(solution)/shard_map/ppermute | solution.py:343
  38.2 28.6 %copy-start = (f32[64,32,256]{2,1,0:T(8,128)S(1)}, f32[64,32,256]{2,1,0:T(8,128)}, u32[]{:S(2)}) copy-start(f32[64,32,256]{2,1,0:T(8,128)} %refs_9_.1) | copy-start | bytes 6291460
  38.2 28.6 %copy-start.4 = (f32[64,32,256]{2,1,0:T(8,128)S(1)}, f32[64,32,256]{2,1,0:T(8,128)}, u32[]{:S(2)}) copy-start(f32[64,32,256]{2,1,0:T(8,128)} %refs_8_.1) | copy-start | bytes 6291460
  44.8 5.9 %collective-permute-start.8 = (bf16[4,64,256]{2,1,0:T(8,128)(2,1)S(1)}, bf16[4,64,256]{2,1,0:T(8,128)(2,1)S(1)}, u32[]{:S(2)}, u32[]{:S(2)}) collective-permute-start(bf16[4,64,256]{2,1,0:T(8,128)(2,1)S(1)} %get-tuple-element.50), channel_id=1, source_target_pairs={{0,3},{1,2},{2,1},{3,0},{4,7},{5,6},{6,5},{7,4},{8,11},{9,10},{10,... | collective-permute-start | bytes 393224 | tf_op jit(solution)/shard_map/ppermute | solution.py:343
  47.4 11.9 %collective-permute-start.9 = (bf16[4,64,256]{2,1,0:T(8,128)(2,1)S(1)}, bf16[4,64,256]{2,1,0:T(8,128)(2,1)S(1)}, u32[]{:S(2)}, u32[]{:S(2)}) collective-permute-start(bf16[4,64,256]{2,1,0:T(8,128)(2,1)S(1)} %get-tuple-element.51), channel_id=1, source_target_pairs={{0,2},{1,3},{2,0},{3,1},{4,6},{5,7},{6,4},{7,5},{8,10},{9,11},{10,... | collective-permute-start | bytes 393224 | tf_op jit(solution)/shard_map/ppermute | solution.py:343
  47.4 11.9 %collective-permute-start.10 = (bf16[4,64,256]{2,1,0:T(8,128)(2,1)S(1)}, bf16[4,64,256]{2,1,0:T(8,128)(2,1)S(1)}, u32[]{:S(2)}, u32[]{:S(2)}) collective-permute-start(bf16[4,64,256]{2,1,0:T(8,128)(2,1)S(1)} %get-tuple-element.52), channel_id=1, source_target_pairs={{0,1},{1,0},{2,3},{3,2},{4,5},{5,4},{6,7},{7,6},{8,9},{9,8},{10,11... | collective-permute-start | bytes 393224 | tf_op jit(solution)/shard_map/ppermute | solution.py:343
  59.3 12.0 %collective-permute-start.14 = (f32[64,256]{1,0:T(8,128)S(1)}, f32[64,256]{1,0:T(8,128)S(1)}, u32[]{:S(2)}, u32[]{:S(2)}) collective-permute-start(f32[64,256]{1,0:T(8,128)S(1)} %get-tuple-element.56), channel_id=1, source_target_pairs={{0,4},{4,8},{8,12},{12,16},{16,20},{20,24},{24,28},{1,5},{5,9},{9,... | collective-permute-start | bytes 196616 | tf_op jit(solution)/shard_map/ppermute | solution.py:440
  64.9 6.5 %collective-permute-start.15 = (f32[64,256]{1,0:T(8,128)S(1)}, f32[64,256]{1,0:T(8,128)S(1)}, u32[]{:S(2)}, u32[]{:S(2)}) collective-permute-start(f32[64,256]{1,0:T(8,128)S(1)} %get-tuple-element.57), channel_id=1, source_target_pairs={{4,0},{8,4},{12,8},{16,12},{20,16},{24,20},{28,24},{5,1},{9,5},{13... | collective-permute-start | bytes 196616 | tf_op jit(solution)/shard_map/ppermute | solution.py:441
  (1 other events, 1.2 us)

commit v6 on v5

--- a/solution.py
+++ b/solution.py
@@ -14,7 +14,6 @@
 SMALL = pl.CostEstimate(flops=1, bytes_accessed=1, transcendentals=0)
 LARGE = pl.CostEstimate(flops=10**10, bytes_accessed=2**24, transcendentals=0)
 VMEM_LIMIT = 16 * 1024 * 1024
-VMEM_MOST = 115 * 512 * 1024
 
 
 def in_vmem(count):
@@ -32,41 +31,34 @@
     return jnp.clip(row, 0, rows - 1)
 
 
-def turn_kernel(count, slab, rows, z_ref, x_ref, turned, *refs):
-    outs, block_ref, sems = refs[:count], refs[count], refs[count + 1]
+def turn_kernel(count, slab, rows, z_ref, x_ref, turned, *outs):
     z = z_ref[0]
-    parts, modes = block_ref.shape[:2]
-    copies = [
-        pltpu.make_async_copy(
-            x_ref.at[k * modes : (k + 1) * modes], block_ref.at[k], sems.at[k]
-        )
-        for k in range(parts)
-    ]
-    for copy in copies:
-        copy.start()
-    for k, copy in enumerate(copies):
-        copy.wait()
-        block = jnp.swapaxes(block_ref[k], 0, 1).astype(jnp.bfloat16)
-        turned[:, k * modes : (k + 1) * modes, :] = block
+    turned[...] = jnp.swapaxes(x_ref[...], 0, 1).astype(jnp.bfloat16)
     for p in range(count):
         place = jnp.bitwise_xor(z, p)
         for rho in range(outs[p].shape[0]):
             outs[p][rho] = turned[row_of(place, rho, slab, count, rows)]
 
 
-def rim_kernel(turned, mean_ref, fields_ref, after, last, first):
+def rim_kernel(turned, mean_ref, fields_ref, source_ref, after, last, first):
     rows, here, cells = turned.shape
     fields = fields_ref.shape[0]
-    for out, row in ((first, 0), (last, rows - 1)):
+    deep = last.shape[0] - 2 * here
+    for out, row, inner in ((first, 0, 1), (last, rows - 1, rows - 2)):
         out[:here] = turned[row].astype(jnp.float32)
         out[here : here + 1, :] = mean_ref[row : row + 1, :]
         for field in range(fields):
             out[here + 1 + field : here + 2 + field, :] = fields_ref[field, row : row + 1, :]
-        rest = out.shape[0] - here - 1 - fields
-        out[here + 1 + fields :, :] = jnp.zeros((rest, cells), jnp.float32)
-
-
-def late_kernel(count, slab, rows, z_ref, turned, low_ref, high_ref, after, *outs):
+        at = here + 1 + fields
+        out[at : at + 1, :] = mean_ref[inner : inner + 1, :]
+        rest = deep - fields - 2
+        if rest:
+            out[at + 1 : at + 1 + rest, :] = jnp.zeros((rest, cells), jnp.float32)
+        out[here + deep :] = source_ref[0 if row == 0 else 1]
+
+
+def late_kernel(count, slab, rows, z_ref, turned, low_ref, high_ref, *refs):
+    outs = refs[2:]
     z = z_ref[0]
     here = turned.shape[1]
     for p in range(count):
@@ -147,19 +139,20 @@
     weight_ref,
     faces_ref,
     inverse_ref,
+    beyond_ref,
     stack_ref,
     turned,
 ):
     fields, rows, cells = fields_ref.shape
     deep = stack_ref.shape[0]
     mask_set = masks(cells)
-    start = low_ref.shape[0] - deep
+    start = (low_ref.shape[0] - deep) // 2
     stack_ref[0] = mean_ref[...]
     stack_ref[1 : fields + 1] = fields_ref[...]
     stack_ref[fields + 1 :] = jnp.zeros((deep - fields - 1, rows, cells), jnp.float32)
     turned[1 : rows + 1] = jnp.swapaxes(stack_ref[...], 0, 1)
-    turned[0] = low_ref[start:, :]
-    turned[rows + 1] = high_ref[start:, :]
+    turned[0] = low_ref[start : start + deep, :]
+    turned[rows + 1] = high_ref[start : start + deep, :]
     z = z_ref[0]
     slab = weight_ref.shape[0]
     ahead = jnp.where(z < count // 2, 1, -1)
@@ -180,6 +173,16 @@
         diag = weight if diag is None else diag + weight
         faces_ref[f] = weight if f < 2 else weight * mask_set[f - 2]
     inverse_ref[...] = 1.0 / diag
+    second = start + fields + 1
+    edges = (
+        (low, low_ref[second : second + 1, :], centre[0:1], z_ref[1] > 0),
+        (high, high_ref[second : second + 1, :], centre[rows - 1 : rows], z_ref[1] < z_ref[2] - 1),
+    )
+    for k, (own, outer, inner, there) in enumerate(edges):
+        diag = 0.5 * (own + outer) + 0.5 * (own + inner)
+        for other in beside(own, mask_set):
+            diag = diag + 0.5 * (own + other)
+        beyond_ref[k : k + 1, :] = jnp.where(there, 1.0 / jnp.where(there, diag, 1.0), 0.0)
 
 
 def mix_kernel(count, groups, fields, window, skip, begin, extra, *refs):
@@ -236,32 +239,30 @@
     lax.fori_loop(0, outs[0].shape[0], each_row, 0)
 
 
-def edge_kernel(count, z_ref, *refs):
+def edge_kernel(count, z_ref, low_rim, high_rim, beyond, *refs):
     parts = refs[:count]
-    bottom_source, top_source, inverse = refs[count : count + 3]
-    bottom, top = refs[-2:]
+    low, high = refs[-2:]
+    here = low.shape[0]
     z = z_ref[0]
-    rows = inverse.shape[0]
+    start = low_rim.shape[0] - here
+    scale = beyond[...] * (1.0 / cheb_center)
     for k in range(count):
-        place = jnp.bitwise_xor(z, (count - k) % count)
         image = parts[k][0].astype(jnp.float32)
 
-        @pl.when(place == 0)
+        @pl.when(z == k)
         def _():
-            scale = inverse[0:1] * (1.0 / cheb_center)
-            bottom[...] = (bottom_source[...] - image) * scale
-
-        @pl.when(place == count - 1)
+            high[...] = (high_rim[start:] - image) * scale[1:2]
+
+        @pl.when(jnp.bitwise_xor(z, count - 1) == k)
         def _():
-            scale = inverse[rows - 1 : rows] * (1.0 / cheb_center)
-            top[...] = (top_source[...] - image) * scale
+            low[...] = (low_rim[start:] - image) * scale[0:1]
 
 
 def post_kernel(count, slab, half, rows, rho_zero, rho_one, z_ref, *refs):
     early = refs[:count]
     late = refs[count : 2 * count]
-    source, iterate, faces, inverse = refs[2 * count : 2 * count + 4]
-    updated, residual, image = refs[2 * count + 4 :]
+    source, iterate, low, high, faces, inverse = refs[2 * count : 2 * count + 6]
+    updated, residual, image = refs[2 * count + 6 :]
     z = z_ref[0]
     modes, _, cells = source.shape
     for k in range(count):
@@ -275,12 +276,12 @@
     residual[...] = source[...] - jnp.swapaxes(image[...], 0, 1)
     place = lax.broadcasted_iota(jnp.int32, (rows, cells), 0)
     inv = inverse[...]
-    up_face = jnp.where(place == rows - 1, 0.0, faces[0])
-    down_face = jnp.where(place == 0, 0.0, faces[1])
     for m in range(modes):
         res = residual[m]
         first = res * (inv * (1.0 / cheb_center))
-        near = up_face * pltpu.roll(first, rows - 1, 0) + down_face * pltpu.roll(first, 1, 0)
+        up = jnp.where(place == rows - 1, high[m : m + 1, :], pltpu.roll(first, rows - 1, 0))
+        down = jnp.where(place == 0, low[m : m + 1, :], pltpu.roll(first, 1, 0))
+        near = faces[0] * up + faces[1] * down
         near = near + faces[2] * pltpu.roll(first, cells - NZ, 1)
         near = near + faces[3] * pltpu.roll(first, NZ, 1)
         near = near + faces[4] * pltpu.roll(first, cells - 1, 1)
@@ -290,26 +291,12 @@
         updated[m] = iterate[m] + step
 
 
-def close_kernel(rho_one, low, high, faces, inverse, partial, updated):
-    modes, deep, cells = partial.shape
-    bottom = pl.program_id(0) == 0
-    rows = inverse.shape[0]
-    scale = 2.0 * rho_one / cheb_radius
-    weight = jnp.where(
-        bottom, faces[1, 0:1] * inverse[0:1], faces[0, rows - 1 : rows] * inverse[rows - 1 : rows]
-    )
-    share = jnp.where(bottom, low[...], high[...]) * (weight * scale)
-    place = lax.broadcasted_iota(jnp.int32, (deep, cells), 0)
-    here = place == jnp.where(bottom, 0, deep - 1)
-    for m in range(modes):
-        updated[m] = partial[m] + jnp.where(here, share[m : m + 1], 0.0)
-
-
 def body(iterate, source, mean_coef, kl_fields, tri_index, tri_value):
     count = lax.axis_size("mode")
     doms = lax.axis_size("dom")
     z = lax.axis_index("mode")
-    z_arg = z.astype(jnp.int32).reshape(1)
+    places = [z, lax.axis_index("dom"), doms]
+    z_arg = jnp.stack([jnp.asarray(a, jnp.int32) for a in places])
     here, rows, cells = iterate.shape
     size = here * count
     slab = rows // count
@@ -319,20 +306,15 @@
     bf16 = jnp.bfloat16
     params = pltpu.CompilerParams(vmem_limit_bytes=VMEM_LIMIT)
 
-    deep = -(-fields // 8) * 8
-
-    parts = max(1, here // 16)
+    deep = -(-(fields + 1) // 8) * 8
+
     turned, *early = pl.pallas_call(
         functools.partial(turn_kernel, count, slab, rows),
         out_shape=[jax.ShapeDtypeStruct((rows, here, cells), bf16)]
         + [jax.ShapeDtypeStruct((half + 2, here, cells), bf16)] * count,
-        in_specs=[in_smem(), pl.BlockSpec(memory_space=pltpu.HBM)],
+        in_specs=[in_smem()] + in_vmem(1),
         out_specs=in_vmem(count + 1),
-        scratch_shapes=[
-            pltpu.VMEM((parts, here // parts, rows, cells), jnp.float32),
-            pltpu.SemaphoreType.DMA((parts,)),
-        ],
-        compiler_params=pltpu.CompilerParams(vmem_limit_bytes=VMEM_MOST),
+        compiler_params=params,
         cost_estimate=SMALL,
         name="turn",
     )(z_arg, iterate)
@@ -359,26 +341,28 @@
     )(z_arg, entries.T, values[None])
     upward = [(i, i + 1) for i in range(doms - 1)]
     downward = [(b, a) for a, b in upward]
+    source_rows = jnp.stack([source[:, 0], source[:, rows - 1]])
     last_rim, first_rim = pl.pallas_call(
         rim_kernel,
-        out_shape=[jax.ShapeDtypeStruct((here + deep, cells), jnp.float32)] * 2,
-        in_specs=in_vmem(3) + [pl.BlockSpec(memory_space=pl.ANY)],
+        out_shape=[jax.ShapeDtypeStruct((2 * here + deep, cells), jnp.float32)] * 2,
+        in_specs=in_vmem(4) + [pl.BlockSpec(memory_space=pl.ANY)],
         out_specs=in_vmem(2),
         compiler_params=params,
         cost_estimate=SMALL,
         name="rim",
-    )(turned, mean_coef, kl_fields, own)
+    )(turned, mean_coef, kl_fields, source_rows, own)
     low_rim = lax.ppermute(last_rim, "dom", upward)
     high_rim = lax.ppermute(first_rim, "dom", downward)
-    weights, faces, inverse = pl.pallas_call(
+    weights, faces, inverse, beyond = pl.pallas_call(
         functools.partial(weight_kernel, count),
         out_shape=[
             jax.ShapeDtypeStruct((slab, 6, deep, cells), jnp.float32),
             jax.ShapeDtypeStruct((6, rows, cells), jnp.float32),
             jax.ShapeDtypeStruct((rows, cells), jnp.float32),
+            jax.ShapeDtypeStruct((2, cells), jnp.float32),
         ],
         in_specs=[in_smem()] + in_vmem(4),
-        out_specs=in_vmem(3),
+        out_specs=in_vmem(4),
         scratch_shapes=[
             pltpu.VMEM((deep, rows, cells), jnp.float32),
             pltpu.VMEM((rows + 2, deep, cells), jnp.float32),
@@ -390,12 +374,12 @@
     late = pl.pallas_call(
         functools.partial(late_kernel, count, slab, rows),
         out_shape=[jax.ShapeDtypeStruct((slab - half, here, cells), bf16)] * count,
-        in_specs=[in_smem()] + in_vmem(3) + [pl.BlockSpec(memory_space=pl.ANY)],
+        in_specs=[in_smem()] + in_vmem(3) + [pl.BlockSpec(memory_space=pl.ANY)] * 2,
         out_specs=in_vmem(count),
         compiler_params=params,
         cost_estimate=SMALL,
         name="late",
-    )(z_arg, turned, low_rim, high_rim, early[-2])
+    )(z_arg, turned, low_rim, high_rim, early[1], inverse)
     late = swap(late)
 
     def mix(arrays, window, skip, begin, rows_out, after=()):
@@ -424,9 +408,19 @@
     back_early = swap(mixed)
     window = ((1, 0), (0, 0), (0, 1), (0, half), (0, half + 1))
     window += tuple((1, k) for k in range(1, slab - half))
-    back_late = swap(mix([early, late], window, 2, (0, half), slab - half, mixed[-1:]))
-
-    bottom, top = pl.pallas_call(
+    mixed_late = mix([early, late], window, 2, (0, half), slab - half, mixed[-1:])
+    back_late = swap(mixed_late)
+
+    def swap_edge(array, p):
+        pairs = []
+        for d in range(doms):
+            for place, target in ((0, d - 1), (count - 1, d + 1)):
+                if 0 <= target < doms:
+                    pairs.append((d * count + place, target * count + (place ^ p)))
+        return lax.ppermute(array[:1], ("dom", "mode"), pairs)
+
+    edges = [swap_edge(a, p) for p, a in enumerate(mixed_late)]
+    low, high = pl.pallas_call(
         functools.partial(edge_kernel, count),
         out_shape=[jax.ShapeDtypeStruct((here, cells), jnp.float32)] * 2,
         in_specs=[in_smem()]
@@ -436,14 +430,13 @@
         compiler_params=params,
         cost_estimate=SMALL,
         name="edge",
-    )(z_arg, *back_late, source[:, 0], source[:, rows - 1], inverse, *back_early[1:])
-    low = lax.ppermute(top, "dom", upward)
-    high = lax.ppermute(bottom, "dom", downward)
+    )(z_arg, low_rim, high_rim, beyond, *edges, *back_early[1:])
 
     sigma = cheb_center / cheb_radius
     rho_zero = 1.0 / sigma
     rho_one = 1.0 / (2.0 * sigma - rho_zero)
     block = min(16, here)
+    row_spec = pl.BlockSpec((block, cells), lambda i: (i, 0))
     early_spec = pl.BlockSpec((half, block, cells), lambda i: (0, i, 0))
     late_spec = pl.BlockSpec((slab - half, block, cells), lambda i: (0, i, 0))
     flat_spec = pl.BlockSpec((block, rows, cells), lambda i: (i, 0, 0))
@@ -454,7 +447,7 @@
         in_specs=[in_smem()]
         + [early_spec] * count
         + [late_spec] * count
-        + [flat_spec, flat_spec]
+        + [flat_spec, flat_spec, row_spec, row_spec]
         + [
             pl.BlockSpec((6, rows, cells), lambda i: (0, 0, 0)),
             pl.BlockSpec((rows, cells), lambda i: (0, 0)),
@@ -469,28 +462,11 @@
         *back_late,
         source,
         iterate,
+        low,
+        high,
         faces,
         inverse,
     )
-    tile = 8 if rows % 8 == 0 else rows
-    last = rows // tile - 1
-    tile_spec = pl.BlockSpec((here, tile, cells), lambda i: (0, i * last, 0))
-    updated = pl.pallas_call(
-        functools.partial(close_kernel, rho_one),
-        grid=(2 if last else 1,),
-        out_shape=jax.ShapeDtypeStruct((here, rows, cells), jnp.float32),
-        in_specs=[
-            pl.BlockSpec((here, cells), lambda i: (0, 0)),
-            pl.BlockSpec((here, cells), lambda i: (0, 0)),
-            pl.BlockSpec((6, rows, cells), lambda i: (0, 0, 0)),
-            pl.BlockSpec((rows, cells), lambda i: (0, 0)),
-            tile_spec,
-        ],
-        out_specs=tile_spec,
-        input_output_aliases={4: 0},
-        compiler_params=params,
-        name="close",
-    )(low, high, faces, inverse, updated)
     return updated, residual
 
 

time: 73.8 us -> 74.8 us (1.014)
  the two profiles are of different devices: /device:TPU:1 before, /device:TPU:3 now
where the time goes in v6:
time: 74.8 us; the launch traced here: 74.5 us
  starting transfers between devices  30.2 us (40%)
  Pallas kernels  24.8 us (33%)
  waiting for transfers between devices  15.6 us (21%)
  local copies, waits for them, and re-layouts  2.96 us (4%)
  between operations  0.9 us (1%)
    ppermute x12, starting transfers between devices, swap(): lax.ppermute(arrays[p], 'mode', [(i, i ^ p) for i in range(count)])  14.6 us
    pallas_call x2, Pallas kernels, mix(): pl.pallas_call(functools.partial(mix_kernel, count, groups, fields, windo...  13.1 us
    ppermute x4, waiting for transfers between devices, swap_edge(): return lax.ppermute(array[:1], ('dom', 'mode'), pairs)  9.84 us
    ppermute x4, starting transfers between devices, swap_edge(): return lax.ppermute(array[:1], ('dom', 'mode'), pairs)  9.28 us
    ppermute x1, waiting for transfers between devices, body(): high_rim = lax.ppermute(first_rim, 'dom', downward)  5.51 us
    pallas_call x1, Pallas kernels, body(): pl.pallas_call(functools.partial(post_kernel, count, slab, half, rows, rh...  5.07 us
    ppermute x1, starting transfers between devices, body(): low_rim = lax.ppermute(last_rim, 'dom', upward)  4.37 us
    pallas_call x1, Pallas kernels, body(): pl.pallas_call(functools.partial(dense_kernel, groups, fields, here), out...  3.39 us
  transfers between devices with their start and end apart: 18, of which 5 were waited for; matrix products, arithmetic and copies ran while one was open for 2% of the time, Pallas kernels for 25%

profile of v6, /device:TPU:3, one launch (start us, length us, event | category | flops | bytes accessed | tf_op | source)
XLA Modules:
  0.0 74.5 jit_solution(18206474478850622803)
XLA Ops:
  0.7 1.6 %copy-done = f32[64,32,256]{2,1,0:T(8,128)S(1)} copy-done((f32[64,32,256]{2,1,0:T(8,128)S(1)}, f32[64,32,256]{2,1,0:T(8,128)}, u32[]{:S(2)}) %copy-start) | copy-done | bytes 2097176
  2.3 1.0 %turn.1 = (bf16[32,64,256]{2,1,0:T(8,128)(2,1)S(1)}, bf16[6,64,256]{2,1,0:T(8,128)(2,1)S(1)}, bf16[6,64,256]{2,1,0:T(8,128)(2,1)S(1)}, bf16[6,64,256]{2,1,0:T(8,128)(2,1)S(1)}, bf16[6,64,256]{2,1,0:T(8,128)(2,1)S(1)}) custom-call(s32[3]{0:T(128)S(1)} %pad_add_fusion.z_ref, f32[64,32,256]{2,1,0:T(8,128)S(1)} %copy-done), custom_call_target="tpu_custom_call" | custom-call | flops 1 | bytes 1 | tf_op jit(solution)/shard_map/turn/pallas_call | solution.py:311
  3.3 3.4 %collective-permute-start = (bf16[6,64,256]{2,1,0:T(8,128)(2,1)S(1)}, bf16[6,64,256]{2,1,0:T(8,128)(2,1)S(1)}, u32[]{:S(2)}, u32[]{:S(2)}) collective-permute-start(bf16[6,64,256]{2,1,0:T(8,128)(2,1)S(1)} %get-tuple-element.32), channel_id=1, source_target_pairs={{0,3},{1,2},{2,1},{3,0},{4,7},{5,6},{6,5},{7,4},{8,11},{9,10},{10,... | collective-permute-start | bytes 589832 | tf_op jit(solution)/shard_map/ppermute | solution.py:325
  7.1 1.3 %fusion = (f32[64,1,256]{2,1,0:T(1,128)S(1)}, f32[64,1,256]{2,1,0:T(1,128)S(1)}) fusion(f32[64,32,256]{2,1,0:T(8,128)} %refs_8_.1), kind=kLoop, calls=%fused_computation.4 | loop fusion | bytes 262144 | tf_op jit(solution)/shard_map/slice | solution.py:344
  8.5 3.4 %dense.1 = (bf16[4,256,1280]{2,1,0:T(8,128)(2,1)S(1)}, f32[256,128]{1,0:T(8,128)S(1)}) custom-call(s32[3]{0:T(128)S(1)} %pad_add_fusion.z_ref, s32[3,5376]{1,0:T(4,128)S(1)} %bitcast.7, f32[1,5376]{1,0:T(1,128)S(1)} %broadcast_in_dim.3.value_ref), custom_call_target="tpu_custom_call" | custom-call | flops 1 | bytes 1 | tf_op jit(solution)/shard_map/dense/pallas_call | solution.py:330
  11.9 4.4 %collective-permute-start.3 = (f32[152,256]{1,0:T(8,128)S(1)}, f32[152,256]{1,0:T(8,128)S(1)}, u32[]{:S(2)}, u32[]{:S(2)}) collective-permute-start(f32[152,256]{1,0:T(8,128)S(1)} %get-tuple-element.40), channel_id=1, source_target_pairs={{0,4},{4,8},{8,12},{12,16},{16,20},{20,24},{24,28},{1,5},{5,9},{9,... | collective-permute-start | bytes 466952 | tf_op jit(solution)/shard_map/ppermute | solution.py:354
  16.3 1.9 %collective-permute-start.4 = (f32[152,256]{1,0:T(8,128)S(1)}, f32[152,256]{1,0:T(8,128)S(1)}, u32[]{:S(2)}, u32[]{:S(2)}) collective-permute-start(f32[152,256]{1,0:T(8,128)S(1)} %get-tuple-element.41), channel_id=1, source_target_pairs={{4,0},{8,4},{12,8},{16,12},{20,16},{24,20},{28,24},{5,1},{9,5},{13... | collective-permute-start | bytes 466952 | tf_op jit(solution)/shard_map/ppermute | solution.py:355
  18.5 5.5 %collective-permute-done.4.high_ref.high_rim = f32[152,256]{1,0:T(8,128)S(1)} collective-permute-done((f32[152,256]{1,0:T(8,128)S(1)}, f32[152,256]{1,0:T(8,128)S(1)}, u32[]{:S(2)}, u32[]{:S(2)}) %collective-permute-start.4) | collective-permute-done | bytes 155680 | tf_op jit(solution)/shard_map/ppermute | solution.py:355
  24.0 1.0 %weights.1 = (f32[8,6,24,256]{3,2,1,0:T(8,128)S(1)}, f32[6,32,256]{2,1,0:T(8,128)S(1)}, f32[32,256]{1,0:T(8,128)S(1)}, f32[2,256]{1,0:T(2,128)S(1)}) custom-call(s32[3]{0:T(128)S(1)} %pad_add_fusion.z_ref, f32[32,256]{1,0:T(8,128)S(1)} %copy-done.4, f32[20,32,256]{2,1,0:T(8,128)S(1)} %copy-done.2, f32[152,256]{1,0:T(8,128)S(1)} %collective-permute-done.3.low_ref.low_rim, ...), custom_call_target="tpu_custom_call" | custom-call | flops 1 | bytes 1 | tf_op jit(solution)/shard_map/weights/pallas_call | solution.py:356
  25.0 0.6 late.1
  25.7 3.2 %collective-permute-start.8 = (bf16[4,64,256]{2,1,0:T(8,128)(2,1)S(1)}, bf16[4,64,256]{2,1,0:T(8,128)(2,1)S(1)}, u32[]{:S(2)}, u32[]{:S(2)}) collective-permute-start(bf16[4,64,256]{2,1,0:T(8,128)(2,1)S(1)} %get-tuple-element.49), channel_id=1, source_target_pairs={{0,3},{1,2},{2,1},{3,0},{4,7},{5,6},{6,5},{7,4},{8,11},{9,10},{10,... | collective-permute-start | bytes 393224 | tf_op jit(solution)/shard_map/ppermute | solution.py:325
  29.3 6.5 %mix.2 = (bf16[4,64,256]{2,1,0:T(8,128)(2,1)S(1)}, bf16[4,64,256]{2,1,0:T(8,128)(2,1)S(1)}, bf16[4,64,256]{2,1,0:T(8,128)(2,1)S(1)}, bf16[4,64,256]{2,1,0:T(8,128)(2,1)S(1)}) custom-call(bf16[6,64,256]{2,1,0:T(8,128)(2,1)S(1)} %get-tuple-element.31.refs_0_, bf16[6,64,256]{2,1,0:T(8,128)(2,1)S(1)} %collective-permute-done.refs_1_.refs_0_, ...), custom_call_target="tpu_custom_call" | custom-call | flops 10000000000 | bytes 16777216 | tf_op jit(solution)/shard_map/mix/pallas_call | solution.py:387
  35.8 2.0 %collective-permute-start.6 = (bf16[4,64,256]{2,1,0:T(8,128)(2,1)S(1)}, bf16[4,64,256]{2,1,0:T(8,128)(2,1)S(1)}, u32[]{:S(2)}, u32[]{:S(2)}) collective-permute-start(bf16[4,64,256]{2,1,0:T(8,128)(2,1)S(1)} %get-tuple-element.45), channel_id=1, source_target_pairs={{0,2},{1,3},{2,0},{3,1},{4,6},{5,7},{6,4},{7,5},{8,10},{9,11},{10,... | collective-permute-start | bytes 393224 | tf_op jit(solution)/shard_map/ppermute | solution.py:325
  37.8 1.5 %collective-permute-start.7 = (bf16[4,64,256]{2,1,0:T(8,128)(2,1)S(1)}, bf16[4,64,256]{2,1,0:T(8,128)(2,1)S(1)}, u32[]{:S(2)}, u32[]{:S(2)}) collective-permute-start(bf16[4,64,256]{2,1,0:T(8,128)(2,1)S(1)} %get-tuple-element.46), channel_id=1, source_target_pairs={{0,1},{1,0},{2,3},{3,2},{4,5},{5,4},{6,7},{7,6},{8,9},{9,8},{10,11... | collective-permute-start | bytes 393224 | tf_op jit(solution)/shard_map/ppermute | solution.py:325
  39.4 6.5 %mix.3 = (bf16[4,64,256]{2,1,0:T(8,128)(2,1)S(1)}, bf16[4,64,256]{2,1,0:T(8,128)(2,1)S(1)}, bf16[4,64,256]{2,1,0:T(8,128)(2,1)S(1)}, bf16[4,64,256]{2,1,0:T(8,128)(2,1)S(1)}) custom-call(bf16[6,64,256]{2,1,0:T(8,128)(2,1)S(1)} %get-tuple-element.31.refs_0_, bf16[6,64,256]{2,1,0:T(8,128)(2,1)S(1)} %collective-permute-done.refs_1_.refs_0_, ...), custom_call_target="tpu_custom_call" | custom-call | flops 10000000000 | bytes 16777216 | tf_op jit(solution)/shard_map/mix/pallas_call | solution.py:387
  46.0 3.2 %collective-permute-start.11 = (bf16[4,64,256]{2,1,0:T(8,128)(2,1)S(1)}, bf16[4,64,256]{2,1,0:T(8,128)(2,1)S(1)}, u32[]{:S(2)}, u32[]{:S(2)}) collective-permute-start(bf16[4,64,256]{2,1,0:T(8,128)(2,1)S(1)} %get-tuple-element.53), channel_id=1, source_target_pairs={{0,3},{1,2},{2,1},{3,0},{4,7},{5,6},{6,5},{7,4},{8,11},{9,10},{10,... | collective-permute-start | bytes 393224 | tf_op jit(solution)/shard_map/ppermute | solution.py:325
  49.6 2.9 %collective-permute-start.15 = (bf16[1,64,256]{2,1,0:T(8,128)(2,1)S(1)}, bf16[1,64,256]{2,1,0:T(8,128)(2,1)S(1)}, u32[]{:S(2)}, u32[]{:S(2)}) collective-permute-start(bf16[1,64,256]{2,1,0:T(8,128)(2,1)S(1)} %slice.21), channel_id=1, source_target_pairs={{3,6},{4,1},{7,10},{8,5},{11,14},{12,9},{15,18},{16,13},{19,22},{2... | collective-permute-start | bytes 98312 | tf_op jit(solution)/shard_map/ppermute | solution.py:420
  52.5 2.2 %collective-permute-start.16 = (bf16[1,64,256]{2,1,0:T(8,128)(2,1)S(1)}, bf16[1,64,256]{2,1,0:T(8,128)(2,1)S(1)}, u32[]{:S(2)}, u32[]{:S(2)}) collective-permute-start(bf16[1,64,256]{2,1,0:T(8,128)(2,1)S(1)} %slice.22), channel_id=1, source_target_pairs={{3,5},{4,2},{7,9},{8,6},{11,13},{12,10},{15,17},{16,14},{19,21},{2... | collective-permute-start | bytes 98312 | tf_op jit(solution)/shard_map/ppermute | solution.py:420
  54.8 4.1 %collective-permute-done.15.refs_1_ = bf16[1,64,256]{2,1,0:T(8,128)(2,1)S(1)} collective-permute-done((bf16[1,64,256]{2,1,0:T(8,128)(2,1)S(1)}, bf16[1,64,256]{2,1,0:T(8,128)(2,1)S(1)}, u32[]{:S(2)}, u32[]{:S(2)}) %collective-permute-start.15) | collective-permute-done | bytes 32800 | tf_op jit(solution)/shard_map/ppermute | solution.py:420
  58.9 1.9 %collective-permute-start.17 = (bf16[1,64,256]{2,1,0:T(8,128)(2,1)S(1)}, bf16[1,64,256]{2,1,0:T(8,128)(2,1)S(1)}, u32[]{:S(2)}, u32[]{:S(2)}) collective-permute-start(bf16[1,64,256]{2,1,0:T(8,128)(2,1)S(1)} %slice.23), channel_id=1, source_target_pairs={{3,4},{4,3},{7,8},{8,7},{11,12},{12,11},{15,16},{16,15},{19,20},{2... | collective-permute-start | bytes 98312 | tf_op jit(solution)/shard_map/ppermute | solution.py:420
  60.8 2.3 %collective-permute-start.14 = (bf16[1,64,256]{2,1,0:T(8,128)(2,1)S(1)}, bf16[1,64,256]{2,1,0:T(8,128)(2,1)S(1)}, u32[]{:S(2)}, u32[]{:S(2)}) collective-permute-start(bf16[1,64,256]{2,1,0:T(8,128)(2,1)S(1)} %slice.20), channel_id=1, source_target_pairs={{3,7},{4,0},{7,11},{8,4},{11,15},{12,8},{15,19},{16,12},{19,23},{2... | collective-permute-start | bytes 98312 | tf_op jit(solution)/shard_map/ppermute | solution.py:420
  63.1 3.4 %collective-permute-done.17.refs_3_ = bf16[1,64,256]{2,1,0:T(8,128)(2,1)S(1)} collective-permute-done((bf16[1,64,256]{2,1,0:T(8,128)(2,1)S(1)}, bf16[1,64,256]{2,1,0:T(8,128)(2,1)S(1)}, u32[]{:S(2)}, u32[]{:S(2)}) %collective-permute-start.17) | collective-permute-done | bytes 32800 | tf_op jit(solution)/shard_map/ppermute | solution.py:420
  66.5 2.3 %collective-permute-done.14.refs_0_ = bf16[1,64,256]{2,1,0:T(8,128)(2,1)S(1)} collective-permute-done((bf16[1,64,256]{2,1,0:T(8,128)(2,1)S(1)}, bf16[1,64,256]{2,1,0:T(8,128)(2,1)S(1)}, u32[]{:S(2)}, u32[]{:S(2)}) %collective-permute-start.14) | collective-permute-done | bytes 32800 | tf_op jit(solution)/shard_map/ppermute | solution.py:420
  69.5 5.1 %post.1 = (f32[64,32,256]{2,1,0:T(8,128)}, f32[64,32,256]{2,1,0:T(8,128)}) custom-call(s32[3]{0:T(128)S(1)} %pad_add_fusion.z_ref, bf16[4,64,256]{2,1,0:T(8,128)(2,1)S(1)} %get-tuple-element.43.refs_0_, bf16[4,64,256]{2,1,0:T(8,128)(2,1)S(1)} %collective-permute-done.5.refs_4_.refs_1_, bf16[4,64,256]{2,1,0:T(8,128)(2,1)S(1)} %collective-permute-done.6.refs_5_.refs_2_, ...), custom_call_target="tpu_custom_call" | custom-call | tf_op jit(solution)/shard_map/post/pallas_call | solution.py:443
  (44 shorter events, 2.4 us)
Async XLA Ops:
  2.3 6.1 %copy-start.6 = (f32[5376]{0:T(1024)S(1)}, f32[5376]{0:T(1024)}, u32[]{:S(2)}) copy-start(f32[5376]{0:T(1024)} %param.11) | copy-start | bytes 64516
  2.3 6.2 %copy-start.5 = (s32[5376,3]{0,1:T(4,128)S(1)}, s32[5376,3]{0,1:T(4,128)}, u32[]{:S(2)}) copy-start(s32[5376,3]{0,1:T(4,128)} %param.10) | copy-start | bytes 193540
  2.3 9.6 %copy-start.2 = (f32[20,32,256]{2,1,0:T(8,128)S(1)}, f32[20,32,256]{2,1,0:T(8,128)}, u32[]{:S(2)}) copy-start(f32[20,32,256]{2,1,0:T(8,128)} %fields_ref.3) | copy-start | bytes 1966084
  2.3 9.6 %copy-start.4 = (f32[32,256]{1,0:T(8,128)S(1)}, f32[32,256]{1,0:T(8,128)}, u32[]{:S(2)}) copy-start(f32[32,256]{1,0:T(8,128)} %mean_ref.3) | copy-start | bytes 98308
  3.3 21.7 %collective-permute-start = (bf16[6,64,256]{2,1,0:T(8,128)(2,1)S(1)}, bf16[6,64,256]{2,1,0:T(8,128)(2,1)S(1)}, u32[]{:S(2)}, u32[]{:S(2)}) collective-permute-start(bf16[6,64,256]{2,1,0:T(8,128)(2,1)S(1)} %get-tuple-element.32), channel_id=1, source_target_pairs={{0,3},{1,2},{2,1},{3,0},{4,7},{5,6},{6,5},{7,4},{8,11},{9,10},{10,... | collective-permute-start | bytes 589832 | tf_op jit(solution)/shard_map/ppermute | solution.py:325
  6.7 22.5 %collective-permute-start.1 = (bf16[6,64,256]{2,1,0:T(8,128)(2,1)S(1)}, bf16[6,64,256]{2,1,0:T(8,128)(2,1)S(1)}, u32[]{:S(2)}, u32[]{:S(2)}) collective-permute-start(bf16[6,64,256]{2,1,0:T(8,128)(2,1)S(1)} %get-tuple-element.33), channel_id=1, source_target_pairs={{0,2},{1,3},{2,0},{3,1},{4,6},{5,7},{6,4},{7,5},{8,10},{9,11},{10,... | collective-permute-start | bytes 589832 | tf_op jit(solution)/shard_map/ppermute | solution.py:325
  6.7 22.5 %collective-permute-start.2 = (bf16[6,64,256]{2,1,0:T(8,128)(2,1)S(1)}, bf16[6,64,256]{2,1,0:T(8,128)(2,1)S(1)}, u32[]{:S(2)}, u32[]{:S(2)}) collective-permute-start(bf16[6,64,256]{2,1,0:T(8,128)(2,1)S(1)} %get-tuple-element.34), channel_id=1, source_target_pairs={{0,1},{1,0},{2,3},{3,2},{4,5},{5,4},{6,7},{7,6},{8,9},{9,8},{10,11... | collective-permute-start | bytes 589832 | tf_op jit(solution)/shard_map/ppermute | solution.py:325
  11.9 6.5 %collective-permute-start.3 = (f32[152,256]{1,0:T(8,128)S(1)}, f32[152,256]{1,0:T(8,128)S(1)}, u32[]{:S(2)}, u32[]{:S(2)}) collective-permute-start(f32[152,256]{1,0:T(8,128)S(1)} %get-tuple-element.40), channel_id=1, source_target_pairs={{0,4},{4,8},{8,12},{12,16},{16,20},{20,24},{24,28},{1,5},{5,9},{9,... | collective-permute-start | bytes 466952 | tf_op jit(solution)/shard_map/ppermute | solution.py:354
  16.3 7.7 %collective-permute-start.4 = (f32[152,256]{1,0:T(8,128)S(1)}, f32[152,256]{1,0:T(8,128)S(1)}, u32[]{:S(2)}, u32[]{:S(2)}) collective-permute-start(f32[152,256]{1,0:T(8,128)S(1)} %get-tuple-element.41), channel_id=1, source_target_pairs={{4,0},{8,4},{12,8},{16,12},{20,16},{24,20},{28,24},{5,1},{9,5},{13... | collective-permute-start | bytes 466952 | tf_op jit(solution)/shard_map/ppermute | solution.py:355
  25.7 13.6 %collective-permute-start.8 = (bf16[4,64,256]{2,1,0:T(8,128)(2,1)S(1)}, bf16[4,64,256]{2,1,0:T(8,128)(2,1)S(1)}, u32[]{:S(2)}, u32[]{:S(2)}) collective-permute-start(bf16[4,64,256]{2,1,0:T(8,128)(2,1)S(1)} %get-tuple-element.49), channel_id=1, source_target_pairs={{0,3},{1,2},{2,1},{3,0},{4,7},{5,6},{6,5},{7,4},{8,11},{9,10},{10,... | collective-permute-start | bytes 393224 | tf_op jit(solution)/shard_map/ppermute | solution.py:325
  28.8 10.6 %collective-permute-start.9 = (bf16[4,64,256]{2,1,0:T(8,128)(2,1)S(1)}, bf16[4,64,256]{2,1,0:T(8,128)(2,1)S(1)}, u32[]{:S(2)}, u32[]{:S(2)}) collective-permute-start(bf16[4,64,256]{2,1,0:T(8,128)(2,1)S(1)} %get-tuple-element.50), channel_id=1, source_target_pairs={{0,2},{1,3},{2,0},{3,1},{4,6},{5,7},{6,4},{7,5},{8,10},{9,11},{10,... | collective-permute-start | bytes 393224 | tf_op jit(solution)/shard_map/ppermute | solution.py:325
  28.8 10.6 %collective-permute-start.10 = (bf16[4,64,256]{2,1,0:T(8,128)(2,1)S(1)}, bf16[4,64,256]{2,1,0:T(8,128)(2,1)S(1)}, u32[]{:S(2)}, u32[]{:S(2)}) collective-permute-start(bf16[4,64,256]{2,1,0:T(8,128)(2,1)S(1)} %get-tuple-element.51), channel_id=1, source_target_pairs={{0,1},{1,0},{2,3},{3,2},{4,5},{5,4},{6,7},{7,6},{8,9},{9,8},{10,11... | collective-permute-start | bytes 393224 | tf_op jit(solution)/shard_map/ppermute | solution.py:325
  35.8 13.4 %collective-permute-start.6 = (bf16[4,64,256]{2,1,0:T(8,128)(2,1)S(1)}, bf16[4,64,256]{2,1,0:T(8,128)(2,1)S(1)}, u32[]{:S(2)}, u32[]{:S(2)}) collective-permute-start(bf16[4,64,256]{2,1,0:T(8,128)(2,1)S(1)} %get-tuple-element.45), channel_id=1, source_target_pairs={{0,2},{1,3},{2,0},{3,1},{4,6},{5,7},{6,4},{7,5},{8,10},{9,11},{10,... | collective-permute-start | bytes 393224 | tf_op jit(solution)/shard_map/ppermute | solution.py:325
  37.8 11.8 %collective-permute-start.7 = (bf16[4,64,256]{2,1,0:T(8,128)(2,1)S(1)}, bf16[4,64,256]{2,1,0:T(8,128)(2,1)S(1)}, u32[]{:S(2)}, u32[]{:S(2)}) collective-permute-start(bf16[4,64,256]{2,1,0:T(8,128)(2,1)S(1)} %get-tuple-element.46), channel_id=1, source_target_pairs={{0,1},{1,0},{2,3},{3,2},{4,5},{5,4},{6,7},{7,6},{8,9},{9,8},{10,11... | collective-permute-start | bytes 393224 | tf_op jit(solution)/shard_map/ppermute | solution.py:325
  39.3 13.3 %collective-permute-start.5 = (bf16[4,64,256]{2,1,0:T(8,128)(2,1)S(1)}, bf16[4,64,256]{2,1,0:T(8,128)(2,1)S(1)}, u32[]{:S(2)}, u32[]{:S(2)}) collective-permute-start(bf16[4,64,256]{2,1,0:T(8,128)(2,1)S(1)} %get-tuple-element.44.refs_11_), channel_id=1, source_target_pairs={{0,3},{1,2},{2,1},{3,0},{4,7},{5,6},{6,5},{7,4},{8,11},{9,10},{10,... | collective-permute-start | bytes 393224 | tf_op jit(solution)/shard_map/ppermute | solution.py:325
  39.4 30.0 %copy-start.1 = (f32[64,32,256]{2,1,0:T(8,128)S(1)}, f32[64,32,256]{2,1,0:T(8,128)}, u32[]{:S(2)}) copy-start(f32[64,32,256]{2,1,0:T(8,128)} %refs_9_.1) | copy-start | bytes 6291460
  39.4 30.0 %copy-start.3 = (f32[64,32,256]{2,1,0:T(8,128)S(1)}, f32[64,32,256]{2,1,0:T(8,128)}, u32[]{:S(2)}) copy-start(f32[64,32,256]{2,1,0:T(8,128)} %refs_8_.1) | copy-start | bytes 6291460
  46.0 23.4 %collective-permute-start.11 = (bf16[4,64,256]{2,1,0:T(8,128)(2,1)S(1)}, bf16[4,64,256]{2,1,0:T(8,128)(2,1)S(1)}, u32[]{:S(2)}, u32[]{:S(2)}) collective-permute-start(bf16[4,64,256]{2,1,0:T(8,128)(2,1)S(1)} %get-tuple-element.53), channel_id=1, source_target_pairs={{0,3},{1,2},{2,1},{3,0},{4,7},{5,6},{6,5},{7,4},{8,11},{9,10},{10,... | collective-permute-start | bytes 393224 | tf_op jit(solution)/shard_map/ppermute | solution.py:325
  49.2 20.3 %collective-permute-start.12 = (bf16[4,64,256]{2,1,0:T(8,128)(2,1)S(1)}, bf16[4,64,256]{2,1,0:T(8,128)(2,1)S(1)}, u32[]{:S(2)}, u32[]{:S(2)}) collective-permute-start(bf16[4,64,256]{2,1,0:T(8,128)(2,1)S(1)} %get-tuple-element.54), channel_id=1, source_target_pairs={{0,2},{1,3},{2,0},{3,1},{4,6},{5,7},{6,4},{7,5},{8,10},{9,11},{10,... | collective-permute-start | bytes 393224 | tf_op jit(solution)/shard_map/ppermute | solution.py:325
  49.2 20.3 %collective-permute-start.13 = (bf16[4,64,256]{2,1,0:T(8,128)(2,1)S(1)}, bf16[4,64,256]{2,1,0:T(8,128)(2,1)S(1)}, u32[]{:S(2)}, u32[]{:S(2)}) collective-permute-start(bf16[4,64,256]{2,1,0:T(8,128)(2,1)S(1)} %get-tuple-element.55), channel_id=1, source_target_pairs={{0,1},{1,0},{2,3},{3,2},{4,5},{5,4},{6,7},{7,6},{8,9},{9,8},{10,11... | collective-permute-start | bytes 393224 | tf_op jit(solution)/shard_map/ppermute | solution.py:325
  49.6 9.3 %collective-permute-start.15 = (bf16[1,64,256]{2,1,0:T(8,128)(2,1)S(1)}, bf16[1,64,256]{2,1,0:T(8,128)(2,1)S(1)}, u32[]{:S(2)}, u32[]{:S(2)}) collective-permute-start(bf16[1,64,256]{2,1,0:T(8,128)(2,1)S(1)} %slice.21), channel_id=1, source_target_pairs={{3,6},{4,1},{7,10},{8,5},{11,14},{12,9},{15,18},{16,13},{19,22},{2... | collective-permute-start | bytes 98312 | tf_op jit(solution)/shard_map/ppermute | solution.py:420
  52.5 8.3 %collective-permute-start.16 = (bf16[1,64,256]{2,1,0:T(8,128)(2,1)S(1)}, bf16[1,64,256]{2,1,0:T(8,128)(2,1)S(1)}, u32[]{:S(2)}, u32[]{:S(2)}) collective-permute-start(bf16[1,64,256]{2,1,0:T(8,128)(2,1)S(1)} %slice.22), channel_id=1, source_target_pairs={{3,5},{4,2},{7,9},{8,6},{11,13},{12,10},{15,17},{16,14},{19,21},{2... | collective-permute-start | bytes 98312 | tf_op jit(solution)/shard_map/ppermute | solution.py:420
  58.9 7.6 %collective-permute-start.17 = (bf16[1,64,256]{2,1,0:T(8,128)(2,1)S(1)}, bf16[1,64,256]{2,1,0:T(8,128)(2,1)S(1)}, u32[]{:S(2)}, u32[]{:S(2)}) collective-permute-start(bf16[1,64,256]{2,1,0:T(8,128)(2,1)S(1)} %slice.23), channel_id=1, source_target_pairs={{3,4},{4,3},{7,8},{8,7},{11,12},{12,11},{15,16},{16,15},{19,20},{2... | collective-permute-start | bytes 98312 | tf_op jit(solution)/shard_map/ppermute | solution.py:420
  60.8 8.0 %collective-permute-start.14 = (bf16[1,64,256]{2,1,0:T(8,128)(2,1)S(1)}, bf16[1,64,256]{2,1,0:T(8,128)(2,1)S(1)}, u32[]{:S(2)}, u32[]{:S(2)}) collective-permute-start(bf16[1,64,256]{2,1,0:T(8,128)(2,1)S(1)} %slice.20), channel_id=1, source_target_pairs={{3,7},{4,0},{7,11},{8,4},{11,15},{12,8},{15,19},{16,12},{19,23},{2... | collective-permute-start | bytes 98312 | tf_op jit(solution)/shard_map/ppermute | solution.py:420
  (1 other events, 1.6 us)

commit v7 on v6

--- a/solution.py
+++ b/solution.py
@@ -417,9 +417,12 @@
             for place, target in ((0, d - 1), (count - 1, d + 1)):
                 if 0 <= target < doms:
                     pairs.append((d * count + place, target * count + (place ^ p)))
-        return lax.ppermute(array[:1], ("dom", "mode"), pairs)
-
-    edges = [swap_edge(a, p) for p, a in enumerate(mixed_late)]
+        return lax.ppermute(array, ("dom", "mode"), pairs)
+
+    near_edges, *_ = lax.optimization_barrier(
+        (tuple(a[:1] for a in mixed_late), back_late[-1], *back_early[1:])
+    )
+    edges = [swap_edge(a, p) for p, a in enumerate(near_edges)]
     low, high = pl.pallas_call(
         functools.partial(edge_kernel, count),
         out_shape=[jax.ShapeDtypeStruct((here, cells), jnp.float32)] * 2,

time: 74.8 us -> 74.9 us (level)
  the two profiles are of different devices: /device:TPU:3 before, /device:TPU:4 now
where the time goes in v7:
time: 74.9 us; the launch traced here: 74.6 us
  starting transfers between devices  37.3 us (50%)
  Pallas kernels  24.8 us (33%)
  waiting for transfers between devices  8.51 us (11%)
  local copies, waits for them, and re-layouts  2.95 us (4%)
  between operations  0.9 us (1%)
    ppermute x12, starting transfers between devices, swap(): lax.ppermute(arrays[p], 'mode', [(i, i ^ p) for i in range(count)])  17.5 us
    ppermute x4, starting transfers between devices, swap_edge(): return lax.ppermute(array, ('dom', 'mode'), pairs)  13.4 us
    pallas_call x2, Pallas kernels, mix(): pl.pallas_call(functools.partial(mix_kernel, count, groups, fields, windo...  13.1 us
    pallas_call x1, Pallas kernels, body(): pl.pallas_call(functools.partial(post_kernel, count, slab, half, rows, rh...  5.07 us
    ppermute x1, starting transfers between devices, body(): high_rim = lax.ppermute(first_rim, 'dom', downward)  4.54 us
    ppermute x4, waiting for transfers between devices, swap_edge(): return lax.ppermute(array, ('dom', 'mode'), pairs)  3.98 us
    pallas_call x1, Pallas kernels, body(): pl.pallas_call(functools.partial(dense_kernel, groups, fields, here), out...  3.38 us
    ppermute x1, starting transfers between devices, body(): low_rim = lax.ppermute(last_rim, 'dom', upward)  1.92 us
  transfers between devices with their start and end apart: 18, of which 5 were waited for; matrix products, arithmetic and copies ran while one was open for 2% of the time, Pallas kernels for 25%

profile of v7, /device:TPU:4, one launch (start us, length us, event | category | flops | bytes accessed | tf_op | source)
XLA Modules:
  0.0 74.6 jit_solution(9246550396925789559)
XLA Ops:
  0.7 1.6 %copy-done = f32[64,32,256]{2,1,0:T(8,128)S(1)} copy-done((f32[64,32,256]{2,1,0:T(8,128)S(1)}, f32[64,32,256]{2,1,0:T(8,128)}, u32[]{:S(2)}) %copy-start) | copy-done | bytes 2097176
  2.3 1.0 %turn.1 = (bf16[32,64,256]{2,1,0:T(8,128)(2,1)S(1)}, bf16[6,64,256]{2,1,0:T(8,128)(2,1)S(1)}, bf16[6,64,256]{2,1,0:T(8,128)(2,1)S(1)}, bf16[6,64,256]{2,1,0:T(8,128)(2,1)S(1)}, bf16[6,64,256]{2,1,0:T(8,128)(2,1)S(1)}) custom-call(s32[3]{0:T(128)S(1)} %pad_add_fusion.z_ref, f32[64,32,256]{2,1,0:T(8,128)S(1)} %copy-done), custom_call_target="tpu_custom_call" | custom-call | flops 1 | bytes 1 | tf_op jit(solution)/shard_map/turn/pallas_call | solution.py:311
  3.3 3.7 %collective-permute-start = (bf16[6,64,256]{2,1,0:T(8,128)(2,1)S(1)}, bf16[6,64,256]{2,1,0:T(8,128)(2,1)S(1)}, u32[]{:S(2)}, u32[]{:S(2)}) collective-permute-start(bf16[6,64,256]{2,1,0:T(8,128)(2,1)S(1)} %get-tuple-element.36), channel_id=1, source_target_pairs={{0,3},{1,2},{2,1},{3,0},{4,7},{5,6},{6,5},{7,4},{8,11},{9,10},{10,... | collective-permute-start | bytes 589832 | tf_op jit(solution)/shard_map/ppermute | solution.py:325
  7.0 0.8 %collective-permute-start.2 = (bf16[6,64,256]{2,1,0:T(8,128)(2,1)S(1)}, bf16[6,64,256]{2,1,0:T(8,128)(2,1)S(1)}, u32[]{:S(2)}, u32[]{:S(2)}) collective-permute-start(bf16[6,64,256]{2,1,0:T(8,128)(2,1)S(1)} %get-tuple-element.38), channel_id=1, source_target_pairs={{0,1},{1,0},{2,3},{3,2},{4,5},{5,4},{6,7},{7,6},{8,9},{9,8},{10,11... | collective-permute-start | bytes 589832 | tf_op jit(solution)/shard_map/ppermute | solution.py:325
  7.8 1.3 %fusion = (f32[64,1,256]{2,1,0:T(1,128)S(1)}, f32[64,1,256]{2,1,0:T(1,128)S(1)}) fusion(f32[64,32,256]{2,1,0:T(8,128)} %refs_8_.1), kind=kLoop, calls=%fused_computation.4 | loop fusion | bytes 262144 | tf_op jit(solution)/shard_map/slice | solution.py:344
  9.2 3.4 %dense.1 = (bf16[4,256,1280]{2,1,0:T(8,128)(2,1)S(1)}, f32[256,128]{1,0:T(8,128)S(1)}) custom-call(s32[3]{0:T(128)S(1)} %pad_add_fusion.z_ref, s32[3,5376]{1,0:T(4,128)S(1)} %bitcast.7, f32[1,5376]{1,0:T(1,128)S(1)} %broadcast_in_dim.3.value_ref), custom_call_target="tpu_custom_call" | custom-call | flops 1 | bytes 1 | tf_op jit(solution)/shard_map/dense/pallas_call | solution.py:330
  12.6 1.9 %collective-permute-start.3 = (f32[152,256]{1,0:T(8,128)S(1)}, f32[152,256]{1,0:T(8,128)S(1)}, u32[]{:S(2)}, u32[]{:S(2)}) collective-permute-start(f32[152,256]{1,0:T(8,128)S(1)} %get-tuple-element.44), channel_id=1, source_target_pairs={{0,4},{4,8},{8,12},{12,16},{16,20},{20,24},{24,28},{1,5},{5,9},{9,... | collective-permute-start | bytes 466952 | tf_op jit(solution)/shard_map/ppermute | solution.py:354
  14.5 4.5 %collective-permute-start.4 = (f32[152,256]{1,0:T(8,128)S(1)}, f32[152,256]{1,0:T(8,128)S(1)}, u32[]{:S(2)}, u32[]{:S(2)}) collective-permute-start(f32[152,256]{1,0:T(8,128)S(1)} %get-tuple-element.45), channel_id=1, source_target_pairs={{4,0},{8,4},{12,8},{16,12},{20,16},{24,20},{28,24},{5,1},{9,5},{13... | collective-permute-start | bytes 466952 | tf_op jit(solution)/shard_map/ppermute | solution.py:355
  19.1 1.0 %collective-permute-done.3.low_ref.low_rim = f32[152,256]{1,0:T(8,128)S(1)} collective-permute-done((f32[152,256]{1,0:T(8,128)S(1)}, f32[152,256]{1,0:T(8,128)S(1)}, u32[]{:S(2)}, u32[]{:S(2)}) %collective-permute-start.3) | collective-permute-done | bytes 155680 | tf_op jit(solution)/shard_map/ppermute | solution.py:354
  20.1 1.8 %collective-permute-done.4.high_ref.high_rim = f32[152,256]{1,0:T(8,128)S(1)} collective-permute-done((f32[152,256]{1,0:T(8,128)S(1)}, f32[152,256]{1,0:T(8,128)S(1)}, u32[]{:S(2)}, u32[]{:S(2)}) %collective-permute-start.4) | collective-permute-done | bytes 155680 | tf_op jit(solution)/shard_map/ppermute | solution.py:355
  21.8 1.0 %weights.1 = (f32[8,6,24,256]{3,2,1,0:T(8,128)S(1)}, f32[6,32,256]{2,1,0:T(8,128)S(1)}, f32[32,256]{1,0:T(8,128)S(1)}, f32[2,256]{1,0:T(2,128)S(1)}) custom-call(s32[3]{0:T(128)S(1)} %pad_add_fusion.z_ref, f32[32,256]{1,0:T(8,128)S(1)} %copy-done.4, f32[20,32,256]{2,1,0:T(8,128)S(1)} %copy-done.2, f32[152,256]{1,0:T(8,128)S(1)} %collective-permute-done.3.low_ref.low_rim, ...), custom_call_target="tpu_custom_call" | custom-call | flops 1 | bytes 1 | tf_op jit(solution)/shard_map/weights/pallas_call | solution.py:356
  23.5 3.7 %collective-permute-start.8 = (bf16[4,64,256]{2,1,0:T(8,128)(2,1)S(1)}, bf16[4,64,256]{2,1,0:T(8,128)(2,1)S(1)}, u32[]{:S(2)}, u32[]{:S(2)}) collective-permute-start(bf16[4,64,256]{2,1,0:T(8,128)(2,1)S(1)} %get-tuple-element.53), channel_id=1, source_target_pairs={{0,3},{1,2},{2,1},{3,0},{4,7},{5,6},{6,5},{7,4},{8,11},{9,10},{10,... | collective-permute-start | bytes 393224 | tf_op jit(solution)/shard_map/ppermute | solution.py:325
  28.0 6.5 %mix.2 = (bf16[4,64,256]{2,1,0:T(8,128)(2,1)S(1)}, bf16[4,64,256]{2,1,0:T(8,128)(2,1)S(1)}, bf16[4,64,256]{2,1,0:T(8,128)(2,1)S(1)}, bf16[4,64,256]{2,1,0:T(8,128)(2,1)S(1)}) custom-call(bf16[6,64,256]{2,1,0:T(8,128)(2,1)S(1)} %get-tuple-element.35.refs_0_, bf16[6,64,256]{2,1,0:T(8,128)(2,1)S(1)} %collective-permute-done.refs_1_.refs_0_, ...), custom_call_target="tpu_custom_call" | custom-call | flops 10000000000 | bytes 16777216 | tf_op jit(solution)/shard_map/mix/pallas_call | solution.py:387
  34.5 2.2 %collective-permute-start.6 = (bf16[4,64,256]{2,1,0:T(8,128)(2,1)S(1)}, bf16[4,64,256]{2,1,0:T(8,128)(2,1)S(1)}, u32[]{:S(2)}, u32[]{:S(2)}) collective-permute-start(bf16[4,64,256]{2,1,0:T(8,128)(2,1)S(1)} %get-tuple-element.49), channel_id=1, source_target_pairs={{0,2},{1,3},{2,0},{3,1},{4,6},{5,7},{6,4},{7,5},{8,10},{9,11},{10,... | collective-permute-start | bytes 393224 | tf_op jit(solution)/shard_map/ppermute | solution.py:325
  36.7 2.0 %collective-permute-start.7 = (bf16[4,64,256]{2,1,0:T(8,128)(2,1)S(1)}, bf16[4,64,256]{2,1,0:T(8,128)(2,1)S(1)}, u32[]{:S(2)}, u32[]{:S(2)}) collective-permute-start(bf16[4,64,256]{2,1,0:T(8,128)(2,1)S(1)} %get-tuple-element.50), channel_id=1, source_target_pairs={{0,1},{1,0},{2,3},{3,2},{4,5},{5,4},{6,7},{7,6},{8,9},{9,8},{10,11... | collective-permute-start | bytes 393224 | tf_op jit(solution)/shard_map/ppermute | solution.py:325
  39.1 6.5 %mix.3 = (bf16[4,64,256]{2,1,0:T(8,128)(2,1)S(1)}, bf16[4,64,256]{2,1,0:T(8,128)(2,1)S(1)}, bf16[4,64,256]{2,1,0:T(8,128)(2,1)S(1)}, bf16[4,64,256]{2,1,0:T(8,128)(2,1)S(1)}) custom-call(bf16[6,64,256]{2,1,0:T(8,128)(2,1)S(1)} %get-tuple-element.35.refs_0_, bf16[6,64,256]{2,1,0:T(8,128)(2,1)S(1)} %collective-permute-done.refs_1_.refs_0_, ...), custom_call_target="tpu_custom_call" | custom-call | flops 10000000000 | bytes 16777216 | tf_op jit(solution)/shard_map/mix/pallas_call | solution.py:387
  46.0 3.3 %collective-permute-start.11 = (bf16[4,64,256]{2,1,0:T(8,128)(2,1)S(1)}, bf16[4,64,256]{2,1,0:T(8,128)(2,1)S(1)}, u32[]{:S(2)}, u32[]{:S(2)}) collective-permute-start(bf16[4,64,256]{2,1,0:T(8,128)(2,1)S(1)} %get-tuple-element.57), channel_id=1, source_target_pairs={{0,3},{1,2},{2,1},{3,0},{4,7},{5,6},{6,5},{7,4},{8,11},{9,10},{10,... | collective-permute-start | bytes 393224 | tf_op jit(solution)/shard_map/ppermute | solution.py:325
  49.8 1.7 %collective-permute-done.13.refs_7_ = bf16[4,64,256]{2,1,0:T(8,128)(2,1)S(1)} collective-permute-done((bf16[4,64,256]{2,1,0:T(8,128)(2,1)S(1)}, bf16[4,64,256]{2,1,0:T(8,128)(2,1)S(1)}, u32[]{:S(2)}, u32[]{:S(2)}) %collective-permute-start.13) | collective-permute-done | bytes 131104 | tf_op jit(solution)/shard_map/ppermute | solution.py:325
  51.5 2.4 %collective-permute-start.14 = (bf16[1,64,256]{2,1,0:T(8,128)(2,1)S(1)}, bf16[1,64,256]{2,1,0:T(8,128)(2,1)S(1)}, u32[]{:S(2)}, u32[]{:S(2)}) collective-permute-start(bf16[1,64,256]{2,1,0:T(8,128)(2,1)S(1)} %slice.20), channel_id=1, source_target_pairs={{3,7},{4,0},{7,11},{8,4},{11,15},{12,8},{15,19},{16,12},{19,23},{2... | collective-permute-start | bytes 98312 | tf_op jit(solution)/shard_map/ppermute | solution.py:420
  53.9 1.3 %collective-permute-start.15 = (bf16[1,64,256]{2,1,0:T(8,128)(2,1)S(1)}, bf16[1,64,256]{2,1,0:T(8,128)(2,1)S(1)}, u32[]{:S(2)}, u32[]{:S(2)}) collective-permute-start(bf16[1,64,256]{2,1,0:T(8,128)(2,1)S(1)} %slice.21), channel_id=1, source_target_pairs={{3,6},{4,1},{7,10},{8,5},{11,14},{12,9},{15,18},{16,13},{19,22},{2... | collective-permute-start | bytes 98312 | tf_op jit(solution)/shard_map/ppermute | solution.py:420
  55.2 4.8 %collective-permute-start.16 = (bf16[1,64,256]{2,1,0:T(8,128)(2,1)S(1)}, bf16[1,64,256]{2,1,0:T(8,128)(2,1)S(1)}, u32[]{:S(2)}, u32[]{:S(2)}) collective-permute-start(bf16[1,64,256]{2,1,0:T(8,128)(2,1)S(1)} %slice.22), channel_id=1, source_target_pairs={{3,5},{4,2},{7,9},{8,6},{11,13},{12,10},{15,17},{16,14},{19,21},{2... | collective-permute-start | bytes 98312 | tf_op jit(solution)/shard_map/ppermute | solution.py:420
  60.0 4.8 %collective-permute-start.17 = (bf16[1,64,256]{2,1,0:T(8,128)(2,1)S(1)}, bf16[1,64,256]{2,1,0:T(8,128)(2,1)S(1)}, u32[]{:S(2)}, u32[]{:S(2)}) collective-permute-start(bf16[1,64,256]{2,1,0:T(8,128)(2,1)S(1)} %slice.23), channel_id=1, source_target_pairs={{3,4},{4,3},{7,8},{8,7},{11,12},{12,11},{15,16},{16,15},{19,20},{2... | collective-permute-start | bytes 98312 | tf_op jit(solution)/shard_map/ppermute | solution.py:420
  64.9 4.0 %collective-permute-done.17.refs_3_ = bf16[1,64,256]{2,1,0:T(8,128)(2,1)S(1)} collective-permute-done((bf16[1,64,256]{2,1,0:T(8,128)(2,1)S(1)}, bf16[1,64,256]{2,1,0:T(8,128)(2,1)S(1)}, u32[]{:S(2)}, u32[]{:S(2)}) %collective-permute-start.17) | collective-permute-done | bytes 32800 | tf_op jit(solution)/shard_map/ppermute | solution.py:420
  69.5 5.1 %post.1 = (f32[64,32,256]{2,1,0:T(8,128)}, f32[64,32,256]{2,1,0:T(8,128)}) custom-call(s32[3]{0:T(128)S(1)} %pad_add_fusion.z_ref, bf16[4,64,256]{2,1,0:T(8,128)(2,1)S(1)} %get-tuple-element.47.refs_0_, bf16[4,64,256]{2,1,0:T(8,128)(2,1)S(1)} %collective-permute-done.5.refs_4_.refs_1_, bf16[4,64,256]{2,1,0:T(8,128)(2,1)S(1)} %collective-permute-done.6.refs_5_.refs_2_, ...), custom_call_target="tpu_custom_call" | custom-call | tf_op jit(solution)/shard_map/post/pallas_call | solution.py:446
  (44 shorter events, 3.4 us)
Async XLA Ops:
  2.3 6.8 %copy-start.6 = (f32[5376]{0:T(1024)S(1)}, f32[5376]{0:T(1024)}, u32[]{:S(2)}) copy-start(f32[5376]{0:T(1024)} %param.11) | copy-start | bytes 64516
  2.3 6.9 %copy-start.5 = (s32[5376,3]{0,1:T(4,128)S(1)}, s32[5376,3]{0,1:T(4,128)}, u32[]{:S(2)}) copy-start(s32[5376,3]{0,1:T(4,128)} %param.10) | copy-start | bytes 193540
  2.3 10.2 %copy-start.2 = (f32[20,32,256]{2,1,0:T(8,128)S(1)}, f32[20,32,256]{2,1,0:T(8,128)}, u32[]{:S(2)}) copy-start(f32[20,32,256]{2,1,0:T(8,128)} %fields_ref.3) | copy-start | bytes 1966084
  2.3 10.3 %copy-start.4 = (f32[32,256]{1,0:T(8,128)S(1)}, f32[32,256]{1,0:T(8,128)}, u32[]{:S(2)}) copy-start(f32[32,256]{1,0:T(8,128)} %mean_ref.3) | copy-start | bytes 98308
  3.3 19.5 %collective-permute-start = (bf16[6,64,256]{2,1,0:T(8,128)(2,1)S(1)}, bf16[6,64,256]{2,1,0:T(8,128)(2,1)S(1)}, u32[]{:S(2)}, u32[]{:S(2)}) collective-permute-start(bf16[6,64,256]{2,1,0:T(8,128)(2,1)S(1)} %get-tuple-element.36), channel_id=1, source_target_pairs={{0,3},{1,2},{2,1},{3,0},{4,7},{5,6},{6,5},{7,4},{8,11},{9,10},{10,... | collective-permute-start | bytes 589832 | tf_op jit(solution)/shard_map/ppermute | solution.py:325
  7.0 21.0 %collective-permute-start.1 = (bf16[6,64,256]{2,1,0:T(8,128)(2,1)S(1)}, bf16[6,64,256]{2,1,0:T(8,128)(2,1)S(1)}, u32[]{:S(2)}, u32[]{:S(2)}) collective-permute-start(bf16[6,64,256]{2,1,0:T(8,128)(2,1)S(1)} %get-tuple-element.37), channel_id=1, source_target_pairs={{0,2},{1,3},{2,0},{3,1},{4,6},{5,7},{6,4},{7,5},{8,10},{9,11},{10,... | collective-permute-start | bytes 589832 | tf_op jit(solution)/shard_map/ppermute | solution.py:325
  7.0 21.0 %collective-permute-start.2 = (bf16[6,64,256]{2,1,0:T(8,128)(2,1)S(1)}, bf16[6,64,256]{2,1,0:T(8,128)(2,1)S(1)}, u32[]{:S(2)}, u32[]{:S(2)}) collective-permute-start(bf16[6,64,256]{2,1,0:T(8,128)(2,1)S(1)} %get-tuple-element.38), channel_id=1, source_target_pairs={{0,1},{1,0},{2,3},{3,2},{4,5},{5,4},{6,7},{7,6},{8,9},{9,8},{10,11... | collective-permute-start | bytes 589832 | tf_op jit(solution)/shard_map/ppermute | solution.py:325
  12.6 7.4 %collective-permute-start.3 = (f32[152,256]{1,0:T(8,128)S(1)}, f32[152,256]{1,0:T(8,128)S(1)}, u32[]{:S(2)}, u32[]{:S(2)}) collective-permute-start(f32[152,256]{1,0:T(8,128)S(1)} %get-tuple-element.44), channel_id=1, source_target_pairs={{0,4},{4,8},{8,12},{12,16},{16,20},{20,24},{24,28},{1,5},{5,9},{9,... | collective-permute-start | bytes 466952 | tf_op jit(solution)/shard_map/ppermute | solution.py:354
  14.5 7.3 %collective-permute-start.4 = (f32[152,256]{1,0:T(8,128)S(1)}, f32[152,256]{1,0:T(8,128)S(1)}, u32[]{:S(2)}, u32[]{:S(2)}) collective-permute-start(f32[152,256]{1,0:T(8,128)S(1)} %get-tuple-element.45), channel_id=1, source_target_pairs={{4,0},{8,4},{12,8},{16,12},{20,16},{24,20},{28,24},{5,1},{9,5},{13... | collective-permute-start | bytes 466952 | tf_op jit(solution)/shard_map/ppermute | solution.py:355
  23.5 15.2 %collective-permute-start.8 = (bf16[4,64,256]{2,1,0:T(8,128)(2,1)S(1)}, bf16[4,64,256]{2,1,0:T(8,128)(2,1)S(1)}, u32[]{:S(2)}, u32[]{:S(2)}) collective-permute-start(bf16[4,64,256]{2,1,0:T(8,128)(2,1)S(1)} %get-tuple-element.53), channel_id=1, source_target_pairs={{0,3},{1,2},{2,1},{3,0},{4,7},{5,6},{6,5},{7,4},{8,11},{9,10},{10,... | collective-permute-start | bytes 393224 | tf_op jit(solution)/shard_map/ppermute | solution.py:325
  27.2 11.9 %collective-permute-start.9 = (bf16[4,64,256]{2,1,0:T(8,128)(2,1)S(1)}, bf16[4,64,256]{2,1,0:T(8,128)(2,1)S(1)}, u32[]{:S(2)}, u32[]{:S(2)}) collective-permute-start(bf16[4,64,256]{2,1,0:T(8,128)(2,1)S(1)} %get-tuple-element.54), channel_id=1, source_target_pairs={{0,2},{1,3},{2,0},{3,1},{4,6},{5,7},{6,4},{7,5},{8,10},{9,11},{10,... | collective-permute-start | bytes 393224 | tf_op jit(solution)/shard_map/ppermute | solution.py:325
  27.2 11.9 %collective-permute-start.10 = (bf16[4,64,256]{2,1,0:T(8,128)(2,1)S(1)}, bf16[4,64,256]{2,1,0:T(8,128)(2,1)S(1)}, u32[]{:S(2)}, u32[]{:S(2)}) collective-permute-start(bf16[4,64,256]{2,1,0:T(8,128)(2,1)S(1)} %get-tuple-element.55), channel_id=1, source_target_pairs={{0,1},{1,0},{2,3},{3,2},{4,5},{5,4},{6,7},{7,6},{8,9},{9,8},{10,11... | collective-permute-start | bytes 393224 | tf_op jit(solution)/shard_map/ppermute | solution.py:325
  34.5 14.8 %collective-permute-start.6 = (bf16[4,64,256]{2,1,0:T(8,128)(2,1)S(1)}, bf16[4,64,256]{2,1,0:T(8,128)(2,1)S(1)}, u32[]{:S(2)}, u32[]{:S(2)}) collective-permute-start(bf16[4,64,256]{2,1,0:T(8,128)(2,1)S(1)} %get-tuple-element.49), channel_id=1, source_target_pairs={{0,2},{1,3},{2,0},{3,1},{4,6},{5,7},{6,4},{7,5},{8,10},{9,11},{10,... | collective-permute-start | bytes 393224 | tf_op jit(solution)/shard_map/ppermute | solution.py:325
  36.7 13.1 %collective-permute-start.7 = (bf16[4,64,256]{2,1,0:T(8,128)(2,1)S(1)}, bf16[4,64,256]{2,1,0:T(8,128)(2,1)S(1)}, u32[]{:S(2)}, u32[]{:S(2)}) collective-permute-start(bf16[4,64,256]{2,1,0:T(8,128)(2,1)S(1)} %get-tuple-element.50), channel_id=1, source_target_pairs={{0,1},{1,0},{2,3},{3,2},{4,5},{5,4},{6,7},{7,6},{8,9},{9,8},{10,11... | collective-permute-start | bytes 393224 | tf_op jit(solution)/shard_map/ppermute | solution.py:325
  38.7 11.1 %collective-permute-start.5 = (bf16[4,64,256]{2,1,0:T(8,128)(2,1)S(1)}, bf16[4,64,256]{2,1,0:T(8,128)(2,1)S(1)}, u32[]{:S(2)}, u32[]{:S(2)}) collective-permute-start(bf16[4,64,256]{2,1,0:T(8,128)(2,1)S(1)} %get-tuple-element.48.refs_11_), channel_id=1, source_target_pairs={{0,3},{1,2},{2,1},{3,0},{4,7},{5,6},{6,5},{7,4},{8,11},{9,10},{10,... | collective-permute-start | bytes 393224 | tf_op jit(solution)/shard_map/ppermute | solution.py:325
  39.1 30.4 %copy-start.1 = (f32[64,32,256]{2,1,0:T(8,128)S(1)}, f32[64,32,256]{2,1,0:T(8,128)}, u32[]{:S(2)}) copy-start(f32[64,32,256]{2,1,0:T(8,128)} %refs_9_.1) | copy-start | bytes 6291460
  39.1 30.4 %copy-start.3 = (f32[64,32,256]{2,1,0:T(8,128)S(1)}, f32[64,32,256]{2,1,0:T(8,128)}, u32[]{:S(2)}) copy-start(f32[64,32,256]{2,1,0:T(8,128)} %refs_8_.1) | copy-start | bytes 6291460
  45.6 5.9 %collective-permute-start.13 = (bf16[4,64,256]{2,1,0:T(8,128)(2,1)S(1)}, bf16[4,64,256]{2,1,0:T(8,128)(2,1)S(1)}, u32[]{:S(2)}, u32[]{:S(2)}) collective-permute-start(bf16[4,64,256]{2,1,0:T(8,128)(2,1)S(1)} %get-tuple-element.59), channel_id=1, source_target_pairs={{0,1},{1,0},{2,3},{3,2},{4,5},{5,4},{6,7},{7,6},{8,9},{9,8},{10,11... | collective-permute-start | bytes 393224 | tf_op jit(solution)/shard_map/ppermute | solution.py:325
  46.0 23.5 %collective-permute-start.11 = (bf16[4,64,256]{2,1,0:T(8,128)(2,1)S(1)}, bf16[4,64,256]{2,1,0:T(8,128)(2,1)S(1)}, u32[]{:S(2)}, u32[]{:S(2)}) collective-permute-start(bf16[4,64,256]{2,1,0:T(8,128)(2,1)S(1)} %get-tuple-element.57), channel_id=1, source_target_pairs={{0,3},{1,2},{2,1},{3,0},{4,7},{5,6},{6,5},{7,4},{8,11},{9,10},{10,... | collective-permute-start | bytes 393224 | tf_op jit(solution)/shard_map/ppermute | solution.py:325
  49.3 20.2 %collective-permute-start.12 = (bf16[4,64,256]{2,1,0:T(8,128)(2,1)S(1)}, bf16[4,64,256]{2,1,0:T(8,128)(2,1)S(1)}, u32[]{:S(2)}, u32[]{:S(2)}) collective-permute-start(bf16[4,64,256]{2,1,0:T(8,128)(2,1)S(1)} %get-tuple-element.58), channel_id=1, source_target_pairs={{0,2},{1,3},{2,0},{3,1},{4,6},{5,7},{6,4},{7,5},{8,10},{9,11},{10,... | collective-permute-start | bytes 393224 | tf_op jit(solution)/shard_map/ppermute | solution.py:325
  51.5 8.6 %collective-permute-start.14 = (bf16[1,64,256]{2,1,0:T(8,128)(2,1)S(1)}, bf16[1,64,256]{2,1,0:T(8,128)(2,1)S(1)}, u32[]{:S(2)}, u32[]{:S(2)}) collective-permute-start(bf16[1,64,256]{2,1,0:T(8,128)(2,1)S(1)} %slice.20), channel_id=1, source_target_pairs={{3,7},{4,0},{7,11},{8,4},{11,15},{12,8},{15,19},{16,12},{19,23},{2... | collective-permute-start | bytes 98312 | tf_op jit(solution)/shard_map/ppermute | solution.py:420
  53.9 11.0 %collective-permute-start.15 = (bf16[1,64,256]{2,1,0:T(8,128)(2,1)S(1)}, bf16[1,64,256]{2,1,0:T(8,128)(2,1)S(1)}, u32[]{:S(2)}, u32[]{:S(2)}) collective-permute-start(bf16[1,64,256]{2,1,0:T(8,128)(2,1)S(1)} %slice.21), channel_id=1, source_target_pairs={{3,6},{4,1},{7,10},{8,5},{11,14},{12,9},{15,18},{16,13},{19,22},{2... | collective-permute-start | bytes 98312 | tf_op jit(solution)/shard_map/ppermute | solution.py:420
  55.2 9.7 %collective-permute-start.16 = (bf16[1,64,256]{2,1,0:T(8,128)(2,1)S(1)}, bf16[1,64,256]{2,1,0:T(8,128)(2,1)S(1)}, u32[]{:S(2)}, u32[]{:S(2)}) collective-permute-start(bf16[1,64,256]{2,1,0:T(8,128)(2,1)S(1)} %slice.22), channel_id=1, source_target_pairs={{3,5},{4,2},{7,9},{8,6},{11,13},{12,10},{15,17},{16,14},{19,21},{2... | collective-permute-start | bytes 98312 | tf_op jit(solution)/shard_map/ppermute | solution.py:420
  60.0 8.8 %collective-permute-start.17 = (bf16[1,64,256]{2,1,0:T(8,128)(2,1)S(1)}, bf16[1,64,256]{2,1,0:T(8,128)(2,1)S(1)}, u32[]{:S(2)}, u32[]{:S(2)}) collective-permute-start(bf16[1,64,256]{2,1,0:T(8,128)(2,1)S(1)} %slice.23), channel_id=1, source_target_pairs={{3,4},{4,3},{7,8},{8,7},{11,12},{12,11},{15,16},{16,15},{19,20},{2... | collective-permute-start | bytes 98312 | tf_op jit(solution)/shard_map/ppermute | solution.py:420
  (1 other events, 1.6 us)

commit v8 on v5

--- a/solution.py
+++ b/solution.py
@@ -14,7 +14,6 @@
 SMALL = pl.CostEstimate(flops=1, bytes_accessed=1, transcendentals=0)
 LARGE = pl.CostEstimate(flops=10**10, bytes_accessed=2**24, transcendentals=0)
 VMEM_LIMIT = 16 * 1024 * 1024
-VMEM_MOST = 115 * 512 * 1024
 
 
 def in_vmem(count):
@@ -32,22 +31,9 @@
     return jnp.clip(row, 0, rows - 1)
 
 
-def turn_kernel(count, slab, rows, z_ref, x_ref, turned, *refs):
-    outs, block_ref, sems = refs[:count], refs[count], refs[count + 1]
-    z = z_ref[0]
-    parts, modes = block_ref.shape[:2]
-    copies = [
-        pltpu.make_async_copy(
-            x_ref.at[k * modes : (k + 1) * modes], block_ref.at[k], sems.at[k]
-        )
-        for k in range(parts)
-    ]
-    for copy in copies:
-        copy.start()
-    for k, copy in enumerate(copies):
-        copy.wait()
-        block = jnp.swapaxes(block_ref[k], 0, 1).astype(jnp.bfloat16)
-        turned[:, k * modes : (k + 1) * modes, :] = block
+def turn_kernel(count, slab, rows, z_ref, x_ref, turned, *outs):
+    z = z_ref[0]
+    turned[...] = jnp.swapaxes(x_ref[...], 0, 1).astype(jnp.bfloat16)
     for p in range(count):
         place = jnp.bitwise_xor(z, p)
         for rho in range(outs[p].shape[0]):
@@ -66,14 +52,21 @@
         out[here + 1 + fields :, :] = jnp.zeros((rest, cells), jnp.float32)
 
 
-def late_kernel(count, slab, rows, z_ref, turned, low_ref, high_ref, after, *outs):
+def late_kernel(count, slab, rows, z_ref, turned, *refs):
+    outs = refs[2:]
+    z = z_ref[0]
+    for p in range(count):
+        place = jnp.bitwise_xor(z, p)
+        for k in range(outs[p].shape[0]):
+            rho = slab + 1 - outs[p].shape[0] + k
+            outs[p][k] = turned[row_of(place, rho, slab, count, rows)]
+
+
+def beyond_kernel(count, slab, rows, z_ref, turned, low_ref, high_ref, *outs):
     z = z_ref[0]
     here = turned.shape[1]
     for p in range(count):
         place = jnp.bitwise_xor(z, p)
-        for k in range(1, outs[p].shape[0]):
-            rho = slab - outs[p].shape[0] + 1 + k
-            outs[p][k] = turned[row_of(place, rho, slab, count, rows)]
         outs[p][0] = turned[row_of(place, -1, slab, count, rows)]
 
         @pl.when(place == 0)
@@ -260,27 +253,24 @@
 def post_kernel(count, slab, half, rows, rho_zero, rho_one, z_ref, *refs):
     early = refs[:count]
     late = refs[count : 2 * count]
-    source, iterate, faces, inverse = refs[2 * count : 2 * count + 4]
-    updated, residual, image = refs[2 * count + 4 :]
+    source, iterate, low, high, faces, inverse = refs[2 * count : 2 * count + 6]
+    updated, residual, image = refs[2 * count + 6 :]
     z = z_ref[0]
     modes, _, cells = source.shape
     for k in range(count):
         place = jnp.bitwise_xor(z, (count - k) % count)
         for rho in range(slab):
-            if 1 <= rho <= half:
-                part = early[k][rho - 1]
-            else:
-                part = late[k][max(rho - half, 0)]
+            part = early[k][rho] if rho < half else late[k][rho - half]
             image[row_of(place, rho, slab, count, rows)] = part.astype(jnp.float32)
     residual[...] = source[...] - jnp.swapaxes(image[...], 0, 1)
     place = lax.broadcasted_iota(jnp.int32, (rows, cells), 0)
     inv = inverse[...]
-    up_face = jnp.where(place == rows - 1, 0.0, faces[0])
-    down_face = jnp.where(place == 0, 0.0, faces[1])
     for m in range(modes):
         res = residual[m]
         first = res * (inv * (1.0 / cheb_center))
-        near = up_face * pltpu.roll(first, rows - 1, 0) + down_face * pltpu.roll(first, 1, 0)
+        up = jnp.where(place == rows - 1, high[m : m + 1, :], pltpu.roll(first, rows - 1, 0))
+        down = jnp.where(place == 0, low[m : m + 1, :], pltpu.roll(first, 1, 0))
+        near = faces[0] * up + faces[1] * down
         near = near + faces[2] * pltpu.roll(first, cells - NZ, 1)
         near = near + faces[3] * pltpu.roll(first, NZ, 1)
         near = near + faces[4] * pltpu.roll(first, cells - 1, 1)
@@ -288,21 +278,6 @@
         smoothed = (1.0 - 1.0 / cheb_center) * res + near
         step = (1.0 + rho_one * rho_zero) * first + (2.0 * rho_one / cheb_radius) * smoothed * inv
         updated[m] = iterate[m] + step
-
-
-def close_kernel(rho_one, low, high, faces, inverse, partial, updated):
-    modes, deep, cells = partial.shape
-    bottom = pl.program_id(0) == 0
-    rows = inverse.shape[0]
-    scale = 2.0 * rho_one / cheb_radius
-    weight = jnp.where(
-        bottom, faces[1, 0:1] * inverse[0:1], faces[0, rows - 1 : rows] * inverse[rows - 1 : rows]
-    )
-    share = jnp.where(bottom, low[...], high[...]) * (weight * scale)
-    place = lax.broadcasted_iota(jnp.int32, (deep, cells), 0)
-    here = place == jnp.where(bottom, 0, deep - 1)
-    for m in range(modes):
-        updated[m] = partial[m] + jnp.where(here, share[m : m + 1], 0.0)
 
 
 def body(iterate, source, mean_coef, kl_fields, tri_index, tri_value):
@@ -321,18 +296,13 @@
 
     deep = -(-fields // 8) * 8
 
-    parts = max(1, here // 16)
     turned, *early = pl.pallas_call(
         functools.partial(turn_kernel, count, slab, rows),
         out_shape=[jax.ShapeDtypeStruct((rows, here, cells), bf16)]
-        + [jax.ShapeDtypeStruct((half + 2, here, cells), bf16)] * count,
-        in_specs=[in_smem(), pl.BlockSpec(memory_space=pltpu.HBM)],
+        + [jax.ShapeDtypeStruct((half + 1, here, cells), bf16)] * count,
+        in_specs=[in_smem()] + in_vmem(1),
         out_specs=in_vmem(count + 1),
-        scratch_shapes=[
-            pltpu.VMEM((parts, here // parts, rows, cells), jnp.float32),
-            pltpu.SemaphoreType.DMA((parts,)),
-        ],
-        compiler_params=pltpu.CompilerParams(vmem_limit_bytes=VMEM_MOST),
+        compiler_params=params,
         cost_estimate=SMALL,
         name="turn",
     )(z_arg, iterate)
@@ -387,15 +357,25 @@
         cost_estimate=SMALL,
         name="weights",
     )(z_arg, mean_coef, kl_fields, low_rim, high_rim)
+    rims = pl.pallas_call(
+        functools.partial(beyond_kernel, count, slab, rows),
+        out_shape=[jax.ShapeDtypeStruct((1, here, cells), bf16)] * count,
+        in_specs=[in_smem()] + in_vmem(3),
+        out_specs=in_vmem(count),
+        compiler_params=params,
+        cost_estimate=SMALL,
+        name="beyond",
+    )(z_arg, turned, low_rim, high_rim)
+    rims = swap(rims)
     late = pl.pallas_call(
         functools.partial(late_kernel, count, slab, rows),
         out_shape=[jax.ShapeDtypeStruct((slab - half, here, cells), bf16)] * count,
-        in_specs=[in_smem()] + in_vmem(3) + [pl.BlockSpec(memory_space=pl.ANY)],
+        in_specs=[in_smem()] + in_vmem(1) + [pl.BlockSpec(memory_space=pl.ANY)] * 2,
         out_specs=in_vmem(count),
         compiler_params=params,
         cost_estimate=SMALL,
         name="late",
-    )(z_arg, turned, low_rim, high_rim, early[-2])
+    )(z_arg, turned, early[-2], inverse)
     late = swap(late)
 
     def mix(arrays, window, skip, begin, rows_out, after=()):
@@ -419,24 +399,21 @@
             name="mix",
         )(*flat, dense, own, weights, *after)
 
-    window = tuple((0, k) for k in range(half + 2))
-    mixed = mix([early], window, 0, (1, 1), half)
+    window = ((0, 0),) + tuple((1, k) for k in range(half + 1))
+    mixed = mix([rims, early], window, 0, (0, 0), half)
     back_early = swap(mixed)
-    window = ((1, 0), (0, 0), (0, 1), (0, half), (0, half + 1))
-    window += tuple((1, k) for k in range(1, slab - half))
-    back_late = swap(mix([early, late], window, 2, (0, half), slab - half, mixed[-1:]))
+    window = ((0, half - 1), (0, half)) + tuple((1, k) for k in range(slab - half))
+    back_late = swap(mix([early, late], window, 0, (half, half), slab - half, mixed[-1:]))
 
     bottom, top = pl.pallas_call(
         functools.partial(edge_kernel, count),
         out_shape=[jax.ShapeDtypeStruct((here, cells), jnp.float32)] * 2,
-        in_specs=[in_smem()]
-        + in_vmem(count + 3)
-        + [pl.BlockSpec(memory_space=pl.ANY)] * (count - 1),
+        in_specs=[in_smem()] + in_vmem(count + 3),
         out_specs=in_vmem(2),
         compiler_params=params,
         cost_estimate=SMALL,
         name="edge",
-    )(z_arg, *back_late, source[:, 0], source[:, rows - 1], inverse, *back_early[1:])
+    )(z_arg, *back_early, source[:, 0], source[:, rows - 1], inverse)
     low = lax.ppermute(top, "dom", upward)
     high = lax.ppermute(bottom, "dom", downward)
 
@@ -444,6 +421,7 @@
     rho_zero = 1.0 / sigma
     rho_one = 1.0 / (2.0 * sigma - rho_zero)
     block = min(16, here)
+    row_spec = pl.BlockSpec((block, cells), lambda i: (i, 0))
     early_spec = pl.BlockSpec((half, block, cells), lambda i: (0, i, 0))
     late_spec = pl.BlockSpec((slab - half, block, cells), lambda i: (0, i, 0))
     flat_spec = pl.BlockSpec((block, rows, cells), lambda i: (i, 0, 0))
@@ -454,7 +432,7 @@
         in_specs=[in_smem()]
         + [early_spec] * count
         + [late_spec] * count
-        + [flat_spec, flat_spec]
+        + [flat_spec, flat_spec, row_spec, row_spec]
         + [
             pl.BlockSpec((6, rows, cells), lambda i: (0, 0, 0)),
             pl.BlockSpec((rows, cells), lambda i: (0, 0)),
@@ -469,28 +447,11 @@
         *back_late,
         source,
         iterate,
+        low,
+        high,
         faces,
         inverse,
     )
-    tile = 8 if rows % 8 == 0 else rows
-    last = rows // tile - 1
-    tile_spec = pl.BlockSpec((here, tile, cells), lambda i: (0, i * last, 0))
-    updated = pl.pallas_call(
-        functools.partial(close_kernel, rho_one),
-        grid=(2 if last else 1,),
-        out_shape=jax.ShapeDtypeStruct((here, rows, cells), jnp.float32),
-        in_specs=[
-            pl.BlockSpec((here, cells), lambda i: (0, 0)),
-            pl.BlockSpec((here, cells), lambda i: (0, 0)),
-            pl.BlockSpec((6, rows, cells), lambda i: (0, 0, 0)),
-            pl.BlockSpec((rows, cells), lambda i: (0, 0)),
-            tile_spec,
-        ],
-        out_specs=tile_spec,
-        input_output_aliases={4: 0},
-        compiler_params=params,
-        name="close",
-    )(low, high, faces, inverse, updated)
     return updated, residual
 
 

time: 73.8 us -> 70 us (0.949)
  the two profiles are of different devices: /device:TPU:1 before, /device:TPU:3 now
where the time goes in v8:
time: 70 us; the launch traced here: 69.8 us
  starting transfers between devices  35.8 us (51%)
  Pallas kernels  21.6 us (31%)
  waiting for transfers between devices  9.82 us (14%)
  local copies, waits for them, and re-layouts  1.73 us (2%)
  between operations  0.84 us (1%)
    ppermute x15, starting transfers between devices, swap(): lax.ppermute(arrays[p], 'mode', [(i, i ^ p) for i in range(count)])  18.2 us
    pallas_call x2, Pallas kernels, mix(): pl.pallas_call(functools.partial(mix_kernel, count, groups, fields, windo...  13 us
    ppermute x1, starting transfers between devices, body(): low = lax.ppermute(top, 'dom', upward)  9.8 us
    pallas_call x1, Pallas kernels, body(): pl.pallas_call(functools.partial(post_kernel, count, slab, half, rows, rh...  4.57 us
    ppermute x1, waiting for transfers between devices, body(): high = lax.ppermute(bottom, 'dom', downward)  4.54 us
    ppermute x1, starting transfers between devices, body(): low_rim = lax.ppermute(last_rim, 'dom', upward)  3.96 us
    ppermute x1, waiting for transfers between devices, body(): high_rim = lax.ppermute(first_rim, 'dom', downward)  3.37 us
    pallas_call x1, Pallas kernels, body(): pl.pallas_call(functools.partial(dense_kernel, groups, fields, here), out...  2.84 us
  transfers between devices with their start and end apart: 19, of which 3 were waited for; matrix products, arithmetic and copies ran while one was open for 0% of the time, Pallas kernels for 24%

profile of v8, /device:TPU:3, one launch (start us, length us, event | category | flops | bytes accessed | tf_op | source)
XLA Modules:
  0.0 69.8 jit_solution(1155496960864099690)
XLA Ops:
  0.6 1.6 %copy-done = f32[64,32,256]{2,1,0:T(8,128)S(1)} copy-done((f32[64,32,256]{2,1,0:T(8,128)S(1)}, f32[64,32,256]{2,1,0:T(8,128)}, u32[]{:S(2)}) %copy-start) | copy-done | bytes 2097176
  2.7 2.4 %collective-permute-start.6 = (bf16[5,64,256]{2,1,0:T(8,128)(2,1)S(1)}, bf16[5,64,256]{2,1,0:T(8,128)(2,1)S(1)}, u32[]{:S(2)}, u32[]{:S(2)}) collective-permute-start(bf16[5,64,256]{2,1,0:T(8,128)(2,1)S(1)} %get-tuple-element.46), channel_id=1, source_target_pairs={{0,2},{1,3},{2,0},{3,1},{4,6},{5,7},{6,4},{7,5},{8,10},{9,11},{10,... | collective-permute-start | bytes 491528 | tf_op jit(solution)/shard_map/ppermute | solution.py:313
  5.1 2.8 %dense.1 = (bf16[4,256,1280]{2,1,0:T(8,128)(2,1)S(1)}, f32[256,128]{1,0:T(8,128)S(1)}) custom-call(s32[1]{0:T(128)} %bitcast.z_ref, s32[3,5376]{1,0:T(4,128)S(1)} %bitcast.6, f32[1,5376]{1,0:T(1,128)S(1)} %broadcast_in_dim.3.value_ref), custom_call_target="tpu_custom_call" | custom-call | flops 1 | bytes 1 | tf_op jit(solution)/shard_map/dense/pallas_call | solution.py:318
  8.0 4.0 %collective-permute-start = (f32[88,256]{1,0:T(8,128)S(1)}, f32[88,256]{1,0:T(8,128)S(1)}, u32[]{:S(2)}, u32[]{:S(2)}) collective-permute-start(f32[88,256]{1,0:T(8,128)S(1)} %get-tuple-element.38), channel_id=1, source_target_pairs={{0,4},{4,8},{8,12},{12,16},{16,20},{20,24},{24,28},{1,5},{5,9},{9,... | collective-permute-start | bytes 270344 | tf_op jit(solution)/shard_map/ppermute | solution.py:341
  12.0 1.9 %collective-permute-start.1 = (f32[88,256]{1,0:T(8,128)S(1)}, f32[88,256]{1,0:T(8,128)S(1)}, u32[]{:S(2)}, u32[]{:S(2)}) collective-permute-start(f32[88,256]{1,0:T(8,128)S(1)} %get-tuple-element.39), channel_id=1, source_target_pairs={{4,0},{8,4},{12,8},{16,12},{20,16},{24,20},{28,24},{5,1},{9,5},{13... | collective-permute-start | bytes 270344 | tf_op jit(solution)/shard_map/ppermute | solution.py:342
  13.9 1.1 %collective-permute-start.5 = (bf16[5,64,256]{2,1,0:T(8,128)(2,1)S(1)}, bf16[5,64,256]{2,1,0:T(8,128)(2,1)S(1)}, u32[]{:S(2)}, u32[]{:S(2)}) collective-permute-start(bf16[5,64,256]{2,1,0:T(8,128)(2,1)S(1)} %get-tuple-element.45), channel_id=1, source_target_pairs={{0,3},{1,2},{2,1},{3,0},{4,7},{5,6},{6,5},{7,4},{8,11},{9,10},{10,... | collective-permute-start | bytes 491528 | tf_op jit(solution)/shard_map/ppermute | solution.py:313
  15.4 3.4 %collective-permute-done.1.high_ref = f32[88,256]{1,0:T(8,128)S(1)} collective-permute-done((f32[88,256]{1,0:T(8,128)S(1)}, f32[88,256]{1,0:T(8,128)S(1)}, u32[]{:S(2)}, u32[]{:S(2)}) %collective-permute-start.1) | collective-permute-done | bytes 90144 | tf_op jit(solution)/shard_map/ppermute | solution.py:342
  18.8 1.1 %collective-permute-start.2 = (bf16[1,64,256]{2,1,0:T(8,128)(2,1)S(1)}, bf16[1,64,256]{2,1,0:T(8,128)(2,1)S(1)}, u32[]{:S(2)}, u32[]{:S(2)}) collective-permute-start(bf16[1,64,256]{2,1,0:T(8,128)(2,1)S(1)} %get-tuple-element.41), channel_id=1, source_target_pairs={{0,3},{1,2},{2,1},{3,0},{4,7},{5,6},{6,5},{7,4},{8,11},{9,10},{10,... | collective-permute-start | bytes 98312 | tf_op jit(solution)/shard_map/ppermute | solution.py:313
  19.9 1.4 %collective-permute-start.3 = (bf16[1,64,256]{2,1,0:T(8,128)(2,1)S(1)}, bf16[1,64,256]{2,1,0:T(8,128)(2,1)S(1)}, u32[]{:S(2)}, u32[]{:S(2)}) collective-permute-start(bf16[1,64,256]{2,1,0:T(8,128)(2,1)S(1)} %get-tuple-element.42), channel_id=1, source_target_pairs={{0,2},{1,3},{2,0},{3,1},{4,6},{5,7},{6,4},{7,5},{8,10},{9,11},{10,... | collective-permute-start | bytes 98312 | tf_op jit(solution)/shard_map/ppermute | solution.py:313
  21.3 1.1 %collective-permute-start.4 = (bf16[1,64,256]{2,1,0:T(8,128)(2,1)S(1)}, bf16[1,64,256]{2,1,0:T(8,128)(2,1)S(1)}, u32[]{:S(2)}, u32[]{:S(2)}) collective-permute-start(bf16[1,64,256]{2,1,0:T(8,128)(2,1)S(1)} %get-tuple-element.43), channel_id=1, source_target_pairs={{0,1},{1,0},{2,3},{3,2},{4,5},{5,4},{6,7},{7,6},{8,9},{9,8},{10,11... | collective-permute-start | bytes 98312 | tf_op jit(solution)/shard_map/ppermute | solution.py:313
  23.1 1.9 %collective-permute-done.2.refs_1_ = bf16[1,64,256]{2,1,0:T(8,128)(2,1)S(1)} collective-permute-done((bf16[1,64,256]{2,1,0:T(8,128)(2,1)S(1)}, bf16[1,64,256]{2,1,0:T(8,128)(2,1)S(1)}, u32[]{:S(2)}, u32[]{:S(2)}) %collective-permute-start.2) | collective-permute-done | bytes 32800 | tf_op jit(solution)/shard_map/ppermute | solution.py:313
  24.9 1.1 %collective-permute-start.11 = (bf16[4,64,256]{2,1,0:T(8,128)(2,1)S(1)}, bf16[4,64,256]{2,1,0:T(8,128)(2,1)S(1)}, u32[]{:S(2)}, u32[]{:S(2)}) collective-permute-start(bf16[4,64,256]{2,1,0:T(8,128)(2,1)S(1)} %get-tuple-element.56), channel_id=1, source_target_pairs={{0,3},{1,2},{2,1},{3,0},{4,7},{5,6},{6,5},{7,4},{8,11},{9,10},{10,... | collective-permute-start | bytes 393224 | tf_op jit(solution)/shard_map/ppermute | solution.py:313
  26.1 2.4 %collective-permute-start.13 = (bf16[4,64,256]{2,1,0:T(8,128)(2,1)S(1)}, bf16[4,64,256]{2,1,0:T(8,128)(2,1)S(1)}, u32[]{:S(2)}, u32[]{:S(2)}) collective-permute-start(bf16[4,64,256]{2,1,0:T(8,128)(2,1)S(1)} %get-tuple-element.58), channel_id=1, source_target_pairs={{0,1},{1,0},{2,3},{3,2},{4,5},{5,4},{6,7},{7,6},{8,9},{9,8},{10,11... | collective-permute-start | bytes 393224 | tf_op jit(solution)/shard_map/ppermute | solution.py:313
  28.5 6.5 %mix.2 = (bf16[4,64,256]{2,1,0:T(8,128)(2,1)S(1)}, bf16[4,64,256]{2,1,0:T(8,128)(2,1)S(1)}, bf16[4,64,256]{2,1,0:T(8,128)(2,1)S(1)}, bf16[4,64,256]{2,1,0:T(8,128)(2,1)S(1)}) custom-call(bf16[1,64,256]{2,1,0:T(8,128)(2,1)S(1)} %get-tuple-element.40.refs_0_, bf16[1,64,256]{2,1,0:T(8,128)(2,1)S(1)} %collective-permute-done.2.refs_1_, ...), custom_call_target="tpu_custom_call" | custom-call | flops 10000000000 | bytes 16777216 | tf_op jit(solution)/shard_map/mix/pallas_call | solution.py:383
  35.0 0.6 collective-permute-start.9
  35.6 0.9 %collective-permute-start.10 = (bf16[4,64,256]{2,1,0:T(8,128)(2,1)S(1)}, bf16[4,64,256]{2,1,0:T(8,128)(2,1)S(1)}, u32[]{:S(2)}, u32[]{:S(2)}) collective-permute-start(bf16[4,64,256]{2,1,0:T(8,128)(2,1)S(1)} %get-tuple-element.53), channel_id=1, source_target_pairs={{0,1},{1,0},{2,3},{3,2},{4,5},{5,4},{6,7},{7,6},{8,9},{9,8},{10,11... | collective-permute-start | bytes 393224 | tf_op jit(solution)/shard_map/ppermute | solution.py:313
  36.4 2.2 %collective-permute-start.8 = (bf16[4,64,256]{2,1,0:T(8,128)(2,1)S(1)}, bf16[4,64,256]{2,1,0:T(8,128)(2,1)S(1)}, u32[]{:S(2)}, u32[]{:S(2)}) collective-permute-start(bf16[4,64,256]{2,1,0:T(8,128)(2,1)S(1)} %get-tuple-element.51.refs_11_), channel_id=1, source_target_pairs={{0,3},{1,2},{2,1},{3,0},{4,7},{5,6},{6,5},{7,4},{8,11},{9,10},{10,... | collective-permute-start | bytes 393224 | tf_op jit(solution)/shard_map/ppermute | solution.py:313
  38.6 6.5 %mix.3 = (bf16[4,64,256]{2,1,0:T(8,128)(2,1)S(1)}, bf16[4,64,256]{2,1,0:T(8,128)(2,1)S(1)}, bf16[4,64,256]{2,1,0:T(8,128)(2,1)S(1)}, bf16[4,64,256]{2,1,0:T(8,128)(2,1)S(1)}) custom-call(bf16[5,64,256]{2,1,0:T(8,128)(2,1)S(1)} %get-tuple-element.44.refs_4_.refs_0_, bf16[5,64,256]{2,1,0:T(8,128)(2,1)S(1)} %collective-permute-done.5.refs_5_.refs_1_, ...), custom_call_target="tpu_custom_call" | custom-call | flops 10000000000 | bytes 16777216 | tf_op jit(solution)/shard_map/mix/pallas_call | solution.py:383
  45.2 1.1 %collective-permute-start.14 = (bf16[4,64,256]{2,1,0:T(8,128)(2,1)S(1)}, bf16[4,64,256]{2,1,0:T(8,128)(2,1)S(1)}, u32[]{:S(2)}, u32[]{:S(2)}) collective-permute-start(bf16[4,64,256]{2,1,0:T(8,128)(2,1)S(1)} %get-tuple-element.60), channel_id=1, source_target_pairs={{0,3},{1,2},{2,1},{3,0},{4,7},{5,6},{6,5},{7,4},{8,11},{9,10},{10,... | collective-permute-start | bytes 393224 | tf_op jit(solution)/shard_map/ppermute | solution.py:313
  46.3 2.5 %collective-permute-start.16 = (bf16[4,64,256]{2,1,0:T(8,128)(2,1)S(1)}, bf16[4,64,256]{2,1,0:T(8,128)(2,1)S(1)}, u32[]{:S(2)}, u32[]{:S(2)}) collective-permute-start(bf16[4,64,256]{2,1,0:T(8,128)(2,1)S(1)} %get-tuple-element.62), channel_id=1, source_target_pairs={{0,1},{1,0},{2,3},{3,2},{4,5},{5,4},{6,7},{7,6},{8,9},{9,8},{10,11... | collective-permute-start | bytes 393224 | tf_op jit(solution)/shard_map/ppermute | solution.py:313
  48.9 9.8 %collective-permute-start.17 = (f32[64,256]{1,0:T(8,128)S(1)}, f32[64,256]{1,0:T(8,128)S(1)}, u32[]{:S(2)}, u32[]{:S(2)}) collective-permute-start(f32[64,256]{1,0:T(8,128)S(1)} %get-tuple-element.63), channel_id=1, source_target_pairs={{0,4},{4,8},{8,12},{12,16},{16,20},{20,24},{24,28},{1,5},{5,9},{9,... | collective-permute-start | bytes 196616 | tf_op jit(solution)/shard_map/ppermute | solution.py:417
  58.7 1.9 %collective-permute-start.18 = (f32[64,256]{1,0:T(8,128)S(1)}, f32[64,256]{1,0:T(8,128)S(1)}, u32[]{:S(2)}, u32[]{:S(2)}) collective-permute-start(f32[64,256]{1,0:T(8,128)S(1)} %get-tuple-element.64), channel_id=1, source_target_pairs={{4,0},{8,4},{12,8},{16,12},{20,16},{24,20},{28,24},{5,1},{9,5},{13... | collective-permute-start | bytes 196616 | tf_op jit(solution)/shard_map/ppermute | solution.py:418
  60.6 4.5 %collective-permute-done.18.refs_11_ = f32[64,256]{1,0:T(8,128)S(1)} collective-permute-done((f32[64,256]{1,0:T(8,128)S(1)}, f32[64,256]{1,0:T(8,128)S(1)}, u32[]{:S(2)}, u32[]{:S(2)}) %collective-permute-start.18) | collective-permute-done | bytes 65568 | tf_op jit(solution)/shard_map/ppermute | solution.py:418
  65.2 4.6 %post.1 = (f32[64,32,256]{2,1,0:T(8,128)}, f32[64,32,256]{2,1,0:T(8,128)}) custom-call(s32[1]{0:T(128)} %bitcast.z_ref, bf16[4,64,256]{2,1,0:T(8,128)(2,1)S(1)} %get-tuple-element.50.refs_0_, bf16[4,64,256]{2,1,0:T(8,128)(2,1)S(1)} %collective-permute-done.8.refs_1_, bf16[4,64,256]{2,1,0:T(8,128)(2,1)S(1)} %collective-permute-done.9.refs_2_, ...), custom_call_target="tpu_custom_call" | custom-call | tf_op jit(solution)/shard_map/post/pallas_call | solution.py:428
  (41 shorter events, 1.7 us)
Async XLA Ops:
  2.2 2.9 %copy-start.5 = (s32[5376,3]{0,1:T(4,128)S(1)}, s32[5376,3]{0,1:T(4,128)}, u32[]{:S(2)}) copy-start(s32[5376,3]{0,1:T(4,128)} %param.10) | copy-start | bytes 193540
  2.2 5.7 %copy-start.2 = (f32[20,32,256]{2,1,0:T(8,128)S(1)}, f32[20,32,256]{2,1,0:T(8,128)}, u32[]{:S(2)}) copy-start(f32[20,32,256]{2,1,0:T(8,128)} %fields_ref.3) | copy-start | bytes 1966084
  2.2 5.8 %copy-start.4 = (f32[32,256]{1,0:T(8,128)S(1)}, f32[32,256]{1,0:T(8,128)}, u32[]{:S(2)}) copy-start(f32[32,256]{1,0:T(8,128)} %mean_ref.3) | copy-start | bytes 98308
  2.7 19.7 %copy-start.3 = (f32[64,32,256]{2,1,0:T(8,128)S(1)}, f32[64,32,256]{2,1,0:T(8,128)}, u32[]{:S(2)}) copy-start(f32[64,32,256]{2,1,0:T(8,128)} %refs_8_.1) | copy-start | bytes 6291460
  2.7 18.6 %collective-permute-start.6 = (bf16[5,64,256]{2,1,0:T(8,128)(2,1)S(1)}, bf16[5,64,256]{2,1,0:T(8,128)(2,1)S(1)}, u32[]{:S(2)}, u32[]{:S(2)}) collective-permute-start(bf16[5,64,256]{2,1,0:T(8,128)(2,1)S(1)} %get-tuple-element.46), channel_id=1, source_target_pairs={{0,2},{1,3},{2,0},{3,1},{4,6},{5,7},{6,4},{7,5},{8,10},{9,11},{10,... | collective-permute-start | bytes 491528 | tf_op jit(solution)/shard_map/ppermute | solution.py:313
  8.0 7.3 %collective-permute-start = (f32[88,256]{1,0:T(8,128)S(1)}, f32[88,256]{1,0:T(8,128)S(1)}, u32[]{:S(2)}, u32[]{:S(2)}) collective-permute-start(f32[88,256]{1,0:T(8,128)S(1)} %get-tuple-element.38), channel_id=1, source_target_pairs={{0,4},{4,8},{8,12},{12,16},{16,20},{20,24},{24,28},{1,5},{5,9},{9,... | collective-permute-start | bytes 270344 | tf_op jit(solution)/shard_map/ppermute | solution.py:341
  12.0 6.7 %collective-permute-start.1 = (f32[88,256]{1,0:T(8,128)S(1)}, f32[88,256]{1,0:T(8,128)S(1)}, u32[]{:S(2)}, u32[]{:S(2)}) collective-permute-start(f32[88,256]{1,0:T(8,128)S(1)} %get-tuple-element.39), channel_id=1, source_target_pairs={{4,0},{8,4},{12,8},{16,12},{20,16},{24,20},{28,24},{5,1},{9,5},{13... | collective-permute-start | bytes 270344 | tf_op jit(solution)/shard_map/ppermute | solution.py:342
  13.9 14.5 %collective-permute-start.5 = (bf16[5,64,256]{2,1,0:T(8,128)(2,1)S(1)}, bf16[5,64,256]{2,1,0:T(8,128)(2,1)S(1)}, u32[]{:S(2)}, u32[]{:S(2)}) collective-permute-start(bf16[5,64,256]{2,1,0:T(8,128)(2,1)S(1)} %get-tuple-element.45), channel_id=1, source_target_pairs={{0,3},{1,2},{2,1},{3,0},{4,7},{5,6},{6,5},{7,4},{8,11},{9,10},{10,... | collective-permute-start | bytes 491528 | tf_op jit(solution)/shard_map/ppermute | solution.py:313
  15.1 13.4 %collective-permute-start.7 = (bf16[5,64,256]{2,1,0:T(8,128)(2,1)S(1)}, bf16[5,64,256]{2,1,0:T(8,128)(2,1)S(1)}, u32[]{:S(2)}, u32[]{:S(2)}) collective-permute-start(bf16[5,64,256]{2,1,0:T(8,128)(2,1)S(1)} %get-tuple-element.47), channel_id=1, source_target_pairs={{0,1},{1,0},{2,3},{3,2},{4,5},{5,4},{6,7},{7,6},{8,9},{9,8},{10,11... | collective-permute-start | bytes 491528 | tf_op jit(solution)/shard_map/ppermute | solution.py:313
  18.8 6.1 %collective-permute-start.2 = (bf16[1,64,256]{2,1,0:T(8,128)(2,1)S(1)}, bf16[1,64,256]{2,1,0:T(8,128)(2,1)S(1)}, u32[]{:S(2)}, u32[]{:S(2)}) collective-permute-start(bf16[1,64,256]{2,1,0:T(8,128)(2,1)S(1)} %get-tuple-element.41), channel_id=1, source_target_pairs={{0,3},{1,2},{2,1},{3,0},{4,7},{5,6},{6,5},{7,4},{8,11},{9,10},{10,... | collective-permute-start | bytes 98312 | tf_op jit(solution)/shard_map/ppermute | solution.py:313
  19.9 6.1 %collective-permute-start.3 = (bf16[1,64,256]{2,1,0:T(8,128)(2,1)S(1)}, bf16[1,64,256]{2,1,0:T(8,128)(2,1)S(1)}, u32[]{:S(2)}, u32[]{:S(2)}) collective-permute-start(bf16[1,64,256]{2,1,0:T(8,128)(2,1)S(1)} %get-tuple-element.42), channel_id=1, source_target_pairs={{0,2},{1,3},{2,0},{3,1},{4,6},{5,7},{6,4},{7,5},{8,10},{9,11},{10,... | collective-permute-start | bytes 98312 | tf_op jit(solution)/shard_map/ppermute | solution.py:313
  21.3 4.7 %collective-permute-start.4 = (bf16[1,64,256]{2,1,0:T(8,128)(2,1)S(1)}, bf16[1,64,256]{2,1,0:T(8,128)(2,1)S(1)}, u32[]{:S(2)}, u32[]{:S(2)}) collective-permute-start(bf16[1,64,256]{2,1,0:T(8,128)(2,1)S(1)} %get-tuple-element.43), channel_id=1, source_target_pairs={{0,1},{1,0},{2,3},{3,2},{4,5},{5,4},{6,7},{7,6},{8,9},{9,8},{10,11... | collective-permute-start | bytes 98312 | tf_op jit(solution)/shard_map/ppermute | solution.py:313
  24.9 11.5 %collective-permute-start.11 = (bf16[4,64,256]{2,1,0:T(8,128)(2,1)S(1)}, bf16[4,64,256]{2,1,0:T(8,128)(2,1)S(1)}, u32[]{:S(2)}, u32[]{:S(2)}) collective-permute-start(bf16[4,64,256]{2,1,0:T(8,128)(2,1)S(1)} %get-tuple-element.56), channel_id=1, source_target_pairs={{0,3},{1,2},{2,1},{3,0},{4,7},{5,6},{6,5},{7,4},{8,11},{9,10},{10,... | collective-permute-start | bytes 393224 | tf_op jit(solution)/shard_map/ppermute | solution.py:313
  26.0 12.6 %collective-permute-start.12 = (bf16[4,64,256]{2,1,0:T(8,128)(2,1)S(1)}, bf16[4,64,256]{2,1,0:T(8,128)(2,1)S(1)}, u32[]{:S(2)}, u32[]{:S(2)}) collective-permute-start(bf16[4,64,256]{2,1,0:T(8,128)(2,1)S(1)} %get-tuple-element.57), channel_id=1, source_target_pairs={{0,2},{1,3},{2,0},{3,1},{4,6},{5,7},{6,4},{7,5},{8,10},{9,11},{10,... | collective-permute-start | bytes 393224 | tf_op jit(solution)/shard_map/ppermute | solution.py:313
  26.1 12.6 %collective-permute-start.13 = (bf16[4,64,256]{2,1,0:T(8,128)(2,1)S(1)}, bf16[4,64,256]{2,1,0:T(8,128)(2,1)S(1)}, u32[]{:S(2)}, u32[]{:S(2)}) collective-permute-start(bf16[4,64,256]{2,1,0:T(8,128)(2,1)S(1)} %get-tuple-element.58), channel_id=1, source_target_pairs={{0,1},{1,0},{2,3},{3,2},{4,5},{5,4},{6,7},{7,6},{8,9},{9,8},{10,11... | collective-permute-start | bytes 393224 | tf_op jit(solution)/shard_map/ppermute | solution.py:313
  35.0 11.3 %collective-permute-start.9 = (bf16[4,64,256]{2,1,0:T(8,128)(2,1)S(1)}, bf16[4,64,256]{2,1,0:T(8,128)(2,1)S(1)}, u32[]{:S(2)}, u32[]{:S(2)}) collective-permute-start(bf16[4,64,256]{2,1,0:T(8,128)(2,1)S(1)} %get-tuple-element.52), channel_id=1, source_target_pairs={{0,2},{1,3},{2,0},{3,1},{4,6},{5,7},{6,4},{7,5},{8,10},{9,11},{10,... | collective-permute-start | bytes 393224 | tf_op jit(solution)/shard_map/ppermute | solution.py:313
  35.6 13.2 %collective-permute-start.10 = (bf16[4,64,256]{2,1,0:T(8,128)(2,1)S(1)}, bf16[4,64,256]{2,1,0:T(8,128)(2,1)S(1)}, u32[]{:S(2)}, u32[]{:S(2)}) collective-permute-start(bf16[4,64,256]{2,1,0:T(8,128)(2,1)S(1)} %get-tuple-element.53), channel_id=1, source_target_pairs={{0,1},{1,0},{2,3},{3,2},{4,5},{5,4},{6,7},{7,6},{8,9},{9,8},{10,11... | collective-permute-start | bytes 393224 | tf_op jit(solution)/shard_map/ppermute | solution.py:313
  36.4 12.4 %collective-permute-start.8 = (bf16[4,64,256]{2,1,0:T(8,128)(2,1)S(1)}, bf16[4,64,256]{2,1,0:T(8,128)(2,1)S(1)}, u32[]{:S(2)}, u32[]{:S(2)}) collective-permute-start(bf16[4,64,256]{2,1,0:T(8,128)(2,1)S(1)} %get-tuple-element.51.refs_11_), channel_id=1, source_target_pairs={{0,3},{1,2},{2,1},{3,0},{4,7},{5,6},{6,5},{7,4},{8,11},{9,10},{10,... | collective-permute-start | bytes 393224 | tf_op jit(solution)/shard_map/ppermute | solution.py:313
  38.6 26.6 %copy-start.1 = (f32[64,32,256]{2,1,0:T(8,128)S(1)}, f32[64,32,256]{2,1,0:T(8,128)}, u32[]{:S(2)}) copy-start(f32[64,32,256]{2,1,0:T(8,128)} %refs_9_.1) | copy-start | bytes 6291460
  45.2 20.0 %collective-permute-start.14 = (bf16[4,64,256]{2,1,0:T(8,128)(2,1)S(1)}, bf16[4,64,256]{2,1,0:T(8,128)(2,1)S(1)}, u32[]{:S(2)}, u32[]{:S(2)}) collective-permute-start(bf16[4,64,256]{2,1,0:T(8,128)(2,1)S(1)} %get-tuple-element.60), channel_id=1, source_target_pairs={{0,3},{1,2},{2,1},{3,0},{4,7},{5,6},{6,5},{7,4},{8,11},{9,10},{10,... | collective-permute-start | bytes 393224 | tf_op jit(solution)/shard_map/ppermute | solution.py:313
  46.3 18.9 %collective-permute-start.15 = (bf16[4,64,256]{2,1,0:T(8,128)(2,1)S(1)}, bf16[4,64,256]{2,1,0:T(8,128)(2,1)S(1)}, u32[]{:S(2)}, u32[]{:S(2)}) collective-permute-start(bf16[4,64,256]{2,1,0:T(8,128)(2,1)S(1)} %get-tuple-element.61), channel_id=1, source_target_pairs={{0,2},{1,3},{2,0},{3,1},{4,6},{5,7},{6,4},{7,5},{8,10},{9,11},{10,... | collective-permute-start | bytes 393224 | tf_op jit(solution)/shard_map/ppermute | solution.py:313
  46.3 18.9 %collective-permute-start.16 = (bf16[4,64,256]{2,1,0:T(8,128)(2,1)S(1)}, bf16[4,64,256]{2,1,0:T(8,128)(2,1)S(1)}, u32[]{:S(2)}, u32[]{:S(2)}) collective-permute-start(bf16[4,64,256]{2,1,0:T(8,128)(2,1)S(1)} %get-tuple-element.62), channel_id=1, source_target_pairs={{0,1},{1,0},{2,3},{3,2},{4,5},{5,4},{6,7},{7,6},{8,9},{9,8},{10,11... | collective-permute-start | bytes 393224 | tf_op jit(solution)/shard_map/ppermute | solution.py:313
  48.9 11.7 %collective-permute-start.17 = (f32[64,256]{1,0:T(8,128)S(1)}, f32[64,256]{1,0:T(8,128)S(1)}, u32[]{:S(2)}, u32[]{:S(2)}) collective-permute-start(f32[64,256]{1,0:T(8,128)S(1)} %get-tuple-element.63), channel_id=1, source_target_pairs={{0,4},{4,8},{8,12},{12,16},{16,20},{20,24},{24,28},{1,5},{5,9},{9,... | collective-permute-start | bytes 196616 | tf_op jit(solution)/shard_map/ppermute | solution.py:417
  58.7 6.5 %collective-permute-start.18 = (f32[64,256]{1,0:T(8,128)S(1)}, f32[64,256]{1,0:T(8,128)S(1)}, u32[]{:S(2)}, u32[]{:S(2)}) collective-permute-start(f32[64,256]{1,0:T(8,128)S(1)} %get-tuple-element.64), channel_id=1, source_target_pairs={{4,0},{8,4},{12,8},{16,12},{20,16},{24,20},{28,24},{5,1},{9,5},{13... | collective-permute-start | bytes 196616 | tf_op jit(solution)/shard_map/ppermute | solution.py:418
  (2 other events, 4.5 us)

commit v9 on v8

--- a/solution.py
+++ b/solution.py
@@ -40,7 +40,8 @@
             outs[p][rho] = turned[row_of(place, rho, slab, count, rows)]
 
 
-def rim_kernel(turned, mean_ref, fields_ref, after, last, first):
+def rim_kernel(turned, mean_ref, fields_ref, *refs):
+    last, first = refs[-2:]
     rows, here, cells = turned.shape
     fields = fields_ref.shape[0]
     for out, row in ((first, 0), (last, rows - 1)):
@@ -62,7 +63,8 @@
             outs[p][k] = turned[row_of(place, rho, slab, count, rows)]
 
 
-def beyond_kernel(count, slab, rows, z_ref, turned, low_ref, high_ref, *outs):
+def beyond_kernel(count, slab, rows, z_ref, turned, low_ref, high_ref, *refs):
+    outs = refs[-count:]
     z = z_ref[0]
     here = turned.shape[1]
     for p in range(count):
@@ -329,15 +331,16 @@
     )(z_arg, entries.T, values[None])
     upward = [(i, i + 1) for i in range(doms - 1)]
     downward = [(b, a) for a, b in upward]
+    before = []
     last_rim, first_rim = pl.pallas_call(
         rim_kernel,
         out_shape=[jax.ShapeDtypeStruct((here + deep, cells), jnp.float32)] * 2,
-        in_specs=in_vmem(3) + [pl.BlockSpec(memory_space=pl.ANY)],
+        in_specs=in_vmem(3) + [pl.BlockSpec(memory_space=pl.ANY)] * len(before),
         out_specs=in_vmem(2),
         compiler_params=params,
         cost_estimate=SMALL,
         name="rim",
-    )(turned, mean_coef, kl_fields, own)
+    )(turned, mean_coef, kl_fields, *before)
     low_rim = lax.ppermute(last_rim, "dom", upward)
     high_rim = lax.ppermute(first_rim, "dom", downward)
     weights, faces, inverse = pl.pallas_call(
@@ -357,15 +360,16 @@
         cost_estimate=SMALL,
         name="weights",
     )(z_arg, mean_coef, kl_fields, low_rim, high_rim)
+    before = [own]
     rims = pl.pallas_call(
         functools.partial(beyond_kernel, count, slab, rows),
         out_shape=[jax.ShapeDtypeStruct((1, here, cells), bf16)] * count,
-        in_specs=[in_smem()] + in_vmem(3),
+        in_specs=[in_smem()] + in_vmem(3) + [pl.BlockSpec(memory_space=pl.ANY)] * len(before),
         out_specs=in_vmem(count),
         compiler_params=params,
         cost_estimate=SMALL,
         name="beyond",
-    )(z_arg, turned, low_rim, high_rim)
+    )(z_arg, turned, low_rim, high_rim, *before)
     rims = swap(rims)
     late = pl.pallas_call(
         functools.partial(late_kernel, count, slab, rows),

time: 70 us -> 66 us (0.943); the launches traced: 69.8 us -> 65 us
  waiting for transfers between devices: 9.82 us -> 6.93 us
  starting transfers between devices: 35.8 us -> 34 us
    ppermute x1, starting transfers between devices: 9.8 us -> 6.83 us  [body(): low = lax.ppermute(top, 'dom', upward)]
    ppermute x1, waiting for transfers between devices: 3.37 us -> 0.49 us  [body(): high_rim = lax.ppermute(first_rim, 'dom', downward)]
    ppermute x15, starting transfers between devices: 18.2 us -> 19.4 us  [swap(): lax.ppermute(arrays[p], 'mode', [(i, i ^ p) for i in range(count)])]
  transfers between devices with their start and end apart: 19 -> 19, of which waited for: 3 -> 3; matrix products, arithmetic and copies ran while one was open for 0% -> 0% of each run, Pallas kernels for 24% -> 25%
where the time goes in v9:
time: 66 us; the launch traced here: 65 us
  starting transfers between devices  34 us (52%)
  Pallas kernels  21.6 us (33%)
  waiting for transfers between devices  6.93 us (10%)
  local copies, waits for them, and re-layouts  1.73 us (3%)
  between operations  0.82 us (1%)
    ppermute x15, starting transfers between devices, swap(): lax.ppermute(arrays[p], 'mode', [(i, i ^ p) for i in range(count)])  19.4 us
    pallas_call x2, Pallas kernels, mix(): pl.pallas_call(functools.partial(mix_kernel, count, groups, fields, windo...  13 us
    ppermute x1, starting transfers between devices, body(): low = lax.ppermute(top, 'dom', upward)  6.83 us
    pallas_call x1, Pallas kernels, body(): pl.pallas_call(functools.partial(post_kernel, count, slab, half, rows, rh...  4.57 us
    ppermute x1, waiting for transfers between devices, body(): high = lax.ppermute(bottom, 'dom', downward)  4.54 us
    ppermute x1, starting transfers between devices, body(): low_rim = lax.ppermute(last_rim, 'dom', upward)  3.96 us
    pallas_call x1, Pallas kernels, body(): pl.pallas_call(functools.partial(dense_kernel, groups, fields, here), out...  2.84 us
    ppermute x1, starting transfers between devices, body(): high_rim = lax.ppermute(first_rim, 'dom', downward)  1.92 us
  transfers between devices with their start and end apart: 19, of which 3 were waited for; matrix products, arithmetic and copies ran while one was open for 0% of the time, Pallas kernels for 25%

profile of v9, /device:TPU:3, one launch (start us, length us, event | category | flops | bytes accessed | tf_op | source)
XLA Modules:
  0.0 65.0 jit_solution(8730337724029226674)
XLA Ops:
  0.6 1.6 %copy-done = f32[64,32,256]{2,1,0:T(8,128)S(1)} copy-done((f32[64,32,256]{2,1,0:T(8,128)S(1)}, f32[64,32,256]{2,1,0:T(8,128)}, u32[]{:S(2)}) %copy-start) | copy-done | bytes 2097176
  2.2 0.5 turn.1
  2.7 2.4 %collective-permute-start.6 = (bf16[5,64,256]{2,1,0:T(8,128)(2,1)S(1)}, bf16[5,64,256]{2,1,0:T(8,128)(2,1)S(1)}, u32[]{:S(2)}, u32[]{:S(2)}) collective-permute-start(bf16[5,64,256]{2,1,0:T(8,128)(2,1)S(1)} %get-tuple-element.46), channel_id=1, source_target_pairs={{0,2},{1,3},{2,0},{3,1},{4,6},{5,7},{6,4},{7,5},{8,10},{9,11},{10,... | collective-permute-start | bytes 491528 | tf_op jit(solution)/shard_map/ppermute | solution.py:315
  5.1 4.0 %collective-permute-start = (f32[88,256]{1,0:T(8,128)S(1)}, f32[88,256]{1,0:T(8,128)S(1)}, u32[]{:S(2)}, u32[]{:S(2)}) collective-permute-start(f32[88,256]{1,0:T(8,128)S(1)} %get-tuple-element.35), channel_id=1, source_target_pairs={{0,4},{4,8},{8,12},{12,16},{16,20},{20,24},{24,28},{1,5},{5,9},{9,... | collective-permute-start | bytes 270344 | tf_op jit(solution)/shard_map/ppermute | solution.py:344
  9.1 1.9 %collective-permute-start.1 = (f32[88,256]{1,0:T(8,128)S(1)}, f32[88,256]{1,0:T(8,128)S(1)}, u32[]{:S(2)}, u32[]{:S(2)}) collective-permute-start(f32[88,256]{1,0:T(8,128)S(1)} %get-tuple-element.36), channel_id=1, source_target_pairs={{4,0},{8,4},{12,8},{16,12},{20,16},{24,20},{28,24},{5,1},{9,5},{13... | collective-permute-start | bytes 270344 | tf_op jit(solution)/shard_map/ppermute | solution.py:345
  11.0 1.3 %collective-permute-start.5 = (bf16[5,64,256]{2,1,0:T(8,128)(2,1)S(1)}, bf16[5,64,256]{2,1,0:T(8,128)(2,1)S(1)}, u32[]{:S(2)}, u32[]{:S(2)}) collective-permute-start(bf16[5,64,256]{2,1,0:T(8,128)(2,1)S(1)} %get-tuple-element.45), channel_id=1, source_target_pairs={{0,3},{1,2},{2,1},{3,0},{4,7},{5,6},{6,5},{7,4},{8,11},{9,10},{10,... | collective-permute-start | bytes 491528 | tf_op jit(solution)/shard_map/ppermute | solution.py:315
  12.5 2.8 %dense.1 = (bf16[4,256,1280]{2,1,0:T(8,128)(2,1)S(1)}, f32[256,128]{1,0:T(8,128)S(1)}) custom-call(s32[1]{0:T(128)} %bitcast.z_ref, s32[3,5376]{1,0:T(4,128)S(1)} %bitcast.6, f32[1,5376]{1,0:T(1,128)S(1)} %broadcast_in_dim.3.value_ref), custom_call_target="tpu_custom_call" | custom-call | flops 1 | bytes 1 | tf_op jit(solution)/shard_map/dense/pallas_call | solution.py:320
  15.4 0.5 collective-permute-done.1.high_ref
  15.9 1.9 %collective-permute-start.2 = (bf16[1,64,256]{2,1,0:T(8,128)(2,1)S(1)}, bf16[1,64,256]{2,1,0:T(8,128)(2,1)S(1)}, u32[]{:S(2)}, u32[]{:S(2)}) collective-permute-start(bf16[1,64,256]{2,1,0:T(8,128)(2,1)S(1)} %get-tuple-element.41), channel_id=1, source_target_pairs={{0,3},{1,2},{2,1},{3,0},{4,7},{5,6},{6,5},{7,4},{8,11},{9,10},{10,... | collective-permute-start | bytes 98312 | tf_op jit(solution)/shard_map/ppermute | solution.py:315
  17.8 0.6 collective-permute-start.3
  18.4 1.1 %collective-permute-start.4 = (bf16[1,64,256]{2,1,0:T(8,128)(2,1)S(1)}, bf16[1,64,256]{2,1,0:T(8,128)(2,1)S(1)}, u32[]{:S(2)}, u32[]{:S(2)}) collective-permute-start(bf16[1,64,256]{2,1,0:T(8,128)(2,1)S(1)} %get-tuple-element.43), channel_id=1, source_target_pairs={{0,1},{1,0},{2,3},{3,2},{4,5},{5,4},{6,7},{7,6},{8,9},{9,8},{10,11... | collective-permute-start | bytes 98312 | tf_op jit(solution)/shard_map/ppermute | solution.py:315
  19.6 0.5 weights.1
  20.2 1.9 %collective-permute-done.2.refs_1_ = bf16[1,64,256]{2,1,0:T(8,128)(2,1)S(1)} collective-permute-done((bf16[1,64,256]{2,1,0:T(8,128)(2,1)S(1)}, bf16[1,64,256]{2,1,0:T(8,128)(2,1)S(1)}, u32[]{:S(2)}, u32[]{:S(2)}) %collective-permute-start.2) | collective-permute-done | bytes 32800 | tf_op jit(solution)/shard_map/ppermute | solution.py:315
  22.0 1.3 %collective-permute-start.11 = (bf16[4,64,256]{2,1,0:T(8,128)(2,1)S(1)}, bf16[4,64,256]{2,1,0:T(8,128)(2,1)S(1)}, u32[]{:S(2)}, u32[]{:S(2)}) collective-permute-start(bf16[4,64,256]{2,1,0:T(8,128)(2,1)S(1)} %get-tuple-element.56), channel_id=1, source_target_pairs={{0,3},{1,2},{2,1},{3,0},{4,7},{5,6},{6,5},{7,4},{8,11},{9,10},{10,... | collective-permute-start | bytes 393224 | tf_op jit(solution)/shard_map/ppermute | solution.py:315
  23.3 0.8 %collective-permute-start.12 = (bf16[4,64,256]{2,1,0:T(8,128)(2,1)S(1)}, bf16[4,64,256]{2,1,0:T(8,128)(2,1)S(1)}, u32[]{:S(2)}, u32[]{:S(2)}) collective-permute-start(bf16[4,64,256]{2,1,0:T(8,128)(2,1)S(1)} %get-tuple-element.57), channel_id=1, source_target_pairs={{0,2},{1,3},{2,0},{3,1},{4,6},{5,7},{6,4},{7,5},{8,10},{9,11},{10,... | collective-permute-start | bytes 393224 | tf_op jit(solution)/shard_map/ppermute | solution.py:315
  24.1 2.6 %collective-permute-start.13 = (bf16[4,64,256]{2,1,0:T(8,128)(2,1)S(1)}, bf16[4,64,256]{2,1,0:T(8,128)(2,1)S(1)}, u32[]{:S(2)}, u32[]{:S(2)}) collective-permute-start(bf16[4,64,256]{2,1,0:T(8,128)(2,1)S(1)} %get-tuple-element.58), channel_id=1, source_target_pairs={{0,1},{1,0},{2,3},{3,2},{4,5},{5,4},{6,7},{7,6},{8,9},{9,8},{10,11... | collective-permute-start | bytes 393224 | tf_op jit(solution)/shard_map/ppermute | solution.py:315
  26.7 6.5 %mix.2 = (bf16[4,64,256]{2,1,0:T(8,128)(2,1)S(1)}, bf16[4,64,256]{2,1,0:T(8,128)(2,1)S(1)}, bf16[4,64,256]{2,1,0:T(8,128)(2,1)S(1)}, bf16[4,64,256]{2,1,0:T(8,128)(2,1)S(1)}) custom-call(bf16[1,64,256]{2,1,0:T(8,128)(2,1)S(1)} %get-tuple-element.40.refs_0_, bf16[1,64,256]{2,1,0:T(8,128)(2,1)S(1)} %collective-permute-done.2.refs_1_, ...), custom_call_target="tpu_custom_call" | custom-call | flops 10000000000 | bytes 16777216 | tf_op jit(solution)/shard_map/mix/pallas_call | solution.py:387
  33.7 3.1 %collective-permute-start.8 = (bf16[4,64,256]{2,1,0:T(8,128)(2,1)S(1)}, bf16[4,64,256]{2,1,0:T(8,128)(2,1)S(1)}, u32[]{:S(2)}, u32[]{:S(2)}) collective-permute-start(bf16[4,64,256]{2,1,0:T(8,128)(2,1)S(1)} %get-tuple-element.51.refs_11_), channel_id=1, source_target_pairs={{0,3},{1,2},{2,1},{3,0},{4,7},{5,6},{6,5},{7,4},{8,11},{9,10},{10,... | collective-permute-start | bytes 393224 | tf_op jit(solution)/shard_map/ppermute | solution.py:315
  36.8 6.5 %mix.3 = (bf16[4,64,256]{2,1,0:T(8,128)(2,1)S(1)}, bf16[4,64,256]{2,1,0:T(8,128)(2,1)S(1)}, bf16[4,64,256]{2,1,0:T(8,128)(2,1)S(1)}, bf16[4,64,256]{2,1,0:T(8,128)(2,1)S(1)}) custom-call(bf16[5,64,256]{2,1,0:T(8,128)(2,1)S(1)} %get-tuple-element.44.refs_4_.refs_0_, bf16[5,64,256]{2,1,0:T(8,128)(2,1)S(1)} %collective-permute-done.5.refs_5_.refs_1_, ...), custom_call_target="tpu_custom_call" | custom-call | flops 10000000000 | bytes 16777216 | tf_op jit(solution)/shard_map/mix/pallas_call | solution.py:387
  43.3 3.3 %collective-permute-start.14 = (bf16[4,64,256]{2,1,0:T(8,128)(2,1)S(1)}, bf16[4,64,256]{2,1,0:T(8,128)(2,1)S(1)}, u32[]{:S(2)}, u32[]{:S(2)}) collective-permute-start(bf16[4,64,256]{2,1,0:T(8,128)(2,1)S(1)} %get-tuple-element.60), channel_id=1, source_target_pairs={{0,3},{1,2},{2,1},{3,0},{4,7},{5,6},{6,5},{7,4},{8,11},{9,10},{10,... | collective-permute-start | bytes 393224 | tf_op jit(solution)/shard_map/ppermute | solution.py:315
  47.1 6.8 %collective-permute-start.17 = (f32[64,256]{1,0:T(8,128)S(1)}, f32[64,256]{1,0:T(8,128)S(1)}, u32[]{:S(2)}, u32[]{:S(2)}) collective-permute-start(f32[64,256]{1,0:T(8,128)S(1)} %get-tuple-element.63), channel_id=1, source_target_pairs={{0,4},{4,8},{8,12},{12,16},{16,20},{20,24},{24,28},{1,5},{5,9},{9,... | collective-permute-start | bytes 196616 | tf_op jit(solution)/shard_map/ppermute | solution.py:421
  54.0 1.9 %collective-permute-start.18 = (f32[64,256]{1,0:T(8,128)S(1)}, f32[64,256]{1,0:T(8,128)S(1)}, u32[]{:S(2)}, u32[]{:S(2)}) collective-permute-start(f32[64,256]{1,0:T(8,128)S(1)} %get-tuple-element.64), channel_id=1, source_target_pairs={{4,0},{8,4},{12,8},{16,12},{20,16},{24,20},{28,24},{5,1},{9,5},{13... | collective-permute-start | bytes 196616 | tf_op jit(solution)/shard_map/ppermute | solution.py:422
  55.9 4.5 %collective-permute-done.18.refs_11_ = f32[64,256]{1,0:T(8,128)S(1)} collective-permute-done((f32[64,256]{1,0:T(8,128)S(1)}, f32[64,256]{1,0:T(8,128)S(1)}, u32[]{:S(2)}, u32[]{:S(2)}) %collective-permute-start.18) | collective-permute-done | bytes 65568 | tf_op jit(solution)/shard_map/ppermute | solution.py:422
  60.5 4.6 %post.1 = (f32[64,32,256]{2,1,0:T(8,128)}, f32[64,32,256]{2,1,0:T(8,128)}) custom-call(s32[1]{0:T(128)} %bitcast.z_ref, bf16[4,64,256]{2,1,0:T(8,128)(2,1)S(1)} %get-tuple-element.50.refs_0_, bf16[4,64,256]{2,1,0:T(8,128)(2,1)S(1)} %collective-permute-done.8.refs_1_, bf16[4,64,256]{2,1,0:T(8,128)(2,1)S(1)} %collective-permute-done.9.refs_2_, ...), custom_call_target="tpu_custom_call" | custom-call | tf_op jit(solution)/shard_map/post/pallas_call | solution.py:432
  (41 shorter events, 1.4 us)
Async XLA Ops:
  2.2 2.9 %copy-start.4 = (f32[32,256]{1,0:T(8,128)S(1)}, f32[32,256]{1,0:T(8,128)}, u32[]{:S(2)}) copy-start(f32[32,256]{1,0:T(8,128)} %mean_ref.3) | copy-start | bytes 98308
  2.2 10.2 %copy-start.6 = (f32[5376]{0:T(1024)S(1)}, f32[5376]{0:T(1024)}, u32[]{:S(2)}) copy-start(f32[5376]{0:T(1024)} %param.11) | copy-start | bytes 64516
  2.2 10.3 %copy-start.5 = (s32[5376,3]{0,1:T(4,128)S(1)}, s32[5376,3]{0,1:T(4,128)}, u32[]{:S(2)}) copy-start(s32[5376,3]{0,1:T(4,128)} %param.10) | copy-start | bytes 193540
  2.7 16.8 %copy-start.3 = (f32[64,32,256]{2,1,0:T(8,128)S(1)}, f32[64,32,256]{2,1,0:T(8,128)}, u32[]{:S(2)}) copy-start(f32[64,32,256]{2,1,0:T(8,128)} %refs_8_.1) | copy-start | bytes 6291460
  2.7 15.7 %collective-permute-start.6 = (bf16[5,64,256]{2,1,0:T(8,128)(2,1)S(1)}, bf16[5,64,256]{2,1,0:T(8,128)(2,1)S(1)}, u32[]{:S(2)}, u32[]{:S(2)}) collective-permute-start(bf16[5,64,256]{2,1,0:T(8,128)(2,1)S(1)} %get-tuple-element.46), channel_id=1, source_target_pairs={{0,2},{1,3},{2,0},{3,1},{4,6},{5,7},{6,4},{7,5},{8,10},{9,11},{10,... | collective-permute-start | bytes 491528 | tf_op jit(solution)/shard_map/ppermute | solution.py:315
  5.1 10.2 %collective-permute-start = (f32[88,256]{1,0:T(8,128)S(1)}, f32[88,256]{1,0:T(8,128)S(1)}, u32[]{:S(2)}, u32[]{:S(2)}) collective-permute-start(f32[88,256]{1,0:T(8,128)S(1)} %get-tuple-element.35), channel_id=1, source_target_pairs={{0,4},{4,8},{8,12},{12,16},{16,20},{20,24},{24,28},{1,5},{5,9},{9,... | collective-permute-start | bytes 270344 | tf_op jit(solution)/shard_map/ppermute | solution.py:344
  9.1 6.7 %collective-permute-start.1 = (f32[88,256]{1,0:T(8,128)S(1)}, f32[88,256]{1,0:T(8,128)S(1)}, u32[]{:S(2)}, u32[]{:S(2)}) collective-permute-start(f32[88,256]{1,0:T(8,128)S(1)} %get-tuple-element.36), channel_id=1, source_target_pairs={{4,0},{8,4},{12,8},{16,12},{20,16},{24,20},{28,24},{5,1},{9,5},{13... | collective-permute-start | bytes 270344 | tf_op jit(solution)/shard_map/ppermute | solution.py:345
  11.0 15.6 %collective-permute-start.5 = (bf16[5,64,256]{2,1,0:T(8,128)(2,1)S(1)}, bf16[5,64,256]{2,1,0:T(8,128)(2,1)S(1)}, u32[]{:S(2)}, u32[]{:S(2)}) collective-permute-start(bf16[5,64,256]{2,1,0:T(8,128)(2,1)S(1)} %get-tuple-element.45), channel_id=1, source_target_pairs={{0,3},{1,2},{2,1},{3,0},{4,7},{5,6},{6,5},{7,4},{8,11},{9,10},{10,... | collective-permute-start | bytes 491528 | tf_op jit(solution)/shard_map/ppermute | solution.py:315
  12.4 14.3 %collective-permute-start.7 = (bf16[5,64,256]{2,1,0:T(8,128)(2,1)S(1)}, bf16[5,64,256]{2,1,0:T(8,128)(2,1)S(1)}, u32[]{:S(2)}, u32[]{:S(2)}) collective-permute-start(bf16[5,64,256]{2,1,0:T(8,128)(2,1)S(1)} %get-tuple-element.47), channel_id=1, source_target_pairs={{0,1},{1,0},{2,3},{3,2},{4,5},{5,4},{6,7},{7,6},{8,9},{9,8},{10,11... | collective-permute-start | bytes 491528 | tf_op jit(solution)/shard_map/ppermute | solution.py:315
  15.9 6.1 %collective-permute-start.2 = (bf16[1,64,256]{2,1,0:T(8,128)(2,1)S(1)}, bf16[1,64,256]{2,1,0:T(8,128)(2,1)S(1)}, u32[]{:S(2)}, u32[]{:S(2)}) collective-permute-start(bf16[1,64,256]{2,1,0:T(8,128)(2,1)S(1)} %get-tuple-element.41), channel_id=1, source_target_pairs={{0,3},{1,2},{2,1},{3,0},{4,7},{5,6},{6,5},{7,4},{8,11},{9,10},{10,... | collective-permute-start | bytes 98312 | tf_op jit(solution)/shard_map/ppermute | solution.py:315
  17.8 5.5 %collective-permute-start.3 = (bf16[1,64,256]{2,1,0:T(8,128)(2,1)S(1)}, bf16[1,64,256]{2,1,0:T(8,128)(2,1)S(1)}, u32[]{:S(2)}, u32[]{:S(2)}) collective-permute-start(bf16[1,64,256]{2,1,0:T(8,128)(2,1)S(1)} %get-tuple-element.42), channel_id=1, source_target_pairs={{0,2},{1,3},{2,0},{3,1},{4,6},{5,7},{6,4},{7,5},{8,10},{9,11},{10,... | collective-permute-start | bytes 98312 | tf_op jit(solution)/shard_map/ppermute | solution.py:315
  18.4 5.6 %collective-permute-start.4 = (bf16[1,64,256]{2,1,0:T(8,128)(2,1)S(1)}, bf16[1,64,256]{2,1,0:T(8,128)(2,1)S(1)}, u32[]{:S(2)}, u32[]{:S(2)}) collective-permute-start(bf16[1,64,256]{2,1,0:T(8,128)(2,1)S(1)} %get-tuple-element.43), channel_id=1, source_target_pairs={{0,1},{1,0},{2,3},{3,2},{4,5},{5,4},{6,7},{7,6},{8,9},{9,8},{10,11... | collective-permute-start | bytes 98312 | tf_op jit(solution)/shard_map/ppermute | solution.py:315
  22.0 11.7 %collective-permute-start.11 = (bf16[4,64,256]{2,1,0:T(8,128)(2,1)S(1)}, bf16[4,64,256]{2,1,0:T(8,128)(2,1)S(1)}, u32[]{:S(2)}, u32[]{:S(2)}) collective-permute-start(bf16[4,64,256]{2,1,0:T(8,128)(2,1)S(1)} %get-tuple-element.56), channel_id=1, source_target_pairs={{0,3},{1,2},{2,1},{3,0},{4,7},{5,6},{6,5},{7,4},{8,11},{9,10},{10,... | collective-permute-start | bytes 393224 | tf_op jit(solution)/shard_map/ppermute | solution.py:315
  23.3 13.5 %collective-permute-start.12 = (bf16[4,64,256]{2,1,0:T(8,128)(2,1)S(1)}, bf16[4,64,256]{2,1,0:T(8,128)(2,1)S(1)}, u32[]{:S(2)}, u32[]{:S(2)}) collective-permute-start(bf16[4,64,256]{2,1,0:T(8,128)(2,1)S(1)} %get-tuple-element.57), channel_id=1, source_target_pairs={{0,2},{1,3},{2,0},{3,1},{4,6},{5,7},{6,4},{7,5},{8,10},{9,11},{10,... | collective-permute-start | bytes 393224 | tf_op jit(solution)/shard_map/ppermute | solution.py:315
  24.1 12.7 %collective-permute-start.13 = (bf16[4,64,256]{2,1,0:T(8,128)(2,1)S(1)}, bf16[4,64,256]{2,1,0:T(8,128)(2,1)S(1)}, u32[]{:S(2)}, u32[]{:S(2)}) collective-permute-start(bf16[4,64,256]{2,1,0:T(8,128)(2,1)S(1)} %get-tuple-element.58), channel_id=1, source_target_pairs={{0,1},{1,0},{2,3},{3,2},{4,5},{5,4},{6,7},{7,6},{8,9},{9,8},{10,11... | collective-permute-start | bytes 393224 | tf_op jit(solution)/shard_map/ppermute | solution.py:315
  33.2 13.5 %collective-permute-start.9 = (bf16[4,64,256]{2,1,0:T(8,128)(2,1)S(1)}, bf16[4,64,256]{2,1,0:T(8,128)(2,1)S(1)}, u32[]{:S(2)}, u32[]{:S(2)}) collective-permute-start(bf16[4,64,256]{2,1,0:T(8,128)(2,1)S(1)} %get-tuple-element.52), channel_id=1, source_target_pairs={{0,2},{1,3},{2,0},{3,1},{4,6},{5,7},{6,4},{7,5},{8,10},{9,11},{10,... | collective-permute-start | bytes 393224 | tf_op jit(solution)/shard_map/ppermute | solution.py:315
  33.3 13.7 %collective-permute-start.10 = (bf16[4,64,256]{2,1,0:T(8,128)(2,1)S(1)}, bf16[4,64,256]{2,1,0:T(8,128)(2,1)S(1)}, u32[]{:S(2)}, u32[]{:S(2)}) collective-permute-start(bf16[4,64,256]{2,1,0:T(8,128)(2,1)S(1)} %get-tuple-element.53), channel_id=1, source_target_pairs={{0,1},{1,0},{2,3},{3,2},{4,5},{5,4},{6,7},{7,6},{8,9},{9,8},{10,11... | collective-permute-start | bytes 393224 | tf_op jit(solution)/shard_map/ppermute | solution.py:315
  33.7 13.4 %collective-permute-start.8 = (bf16[4,64,256]{2,1,0:T(8,128)(2,1)S(1)}, bf16[4,64,256]{2,1,0:T(8,128)(2,1)S(1)}, u32[]{:S(2)}, u32[]{:S(2)}) collective-permute-start(bf16[4,64,256]{2,1,0:T(8,128)(2,1)S(1)} %get-tuple-element.51.refs_11_), channel_id=1, source_target_pairs={{0,3},{1,2},{2,1},{3,0},{4,7},{5,6},{6,5},{7,4},{8,11},{9,10},{10,... | collective-permute-start | bytes 393224 | tf_op jit(solution)/shard_map/ppermute | solution.py:315
  36.8 23.7 %copy-start.1 = (f32[64,32,256]{2,1,0:T(8,128)S(1)}, f32[64,32,256]{2,1,0:T(8,128)}, u32[]{:S(2)}) copy-start(f32[64,32,256]{2,1,0:T(8,128)} %refs_9_.1) | copy-start | bytes 6291460
  43.3 17.1 %collective-permute-start.14 = (bf16[4,64,256]{2,1,0:T(8,128)(2,1)S(1)}, bf16[4,64,256]{2,1,0:T(8,128)(2,1)S(1)}, u32[]{:S(2)}, u32[]{:S(2)}) collective-permute-start(bf16[4,64,256]{2,1,0:T(8,128)(2,1)S(1)} %get-tuple-element.60), channel_id=1, source_target_pairs={{0,3},{1,2},{2,1},{3,0},{4,7},{5,6},{6,5},{7,4},{8,11},{9,10},{10,... | collective-permute-start | bytes 393224 | tf_op jit(solution)/shard_map/ppermute | solution.py:315
  46.7 13.8 %collective-permute-start.15 = (bf16[4,64,256]{2,1,0:T(8,128)(2,1)S(1)}, bf16[4,64,256]{2,1,0:T(8,128)(2,1)S(1)}, u32[]{:S(2)}, u32[]{:S(2)}) collective-permute-start(bf16[4,64,256]{2,1,0:T(8,128)(2,1)S(1)} %get-tuple-element.61), channel_id=1, source_target_pairs={{0,2},{1,3},{2,0},{3,1},{4,6},{5,7},{6,4},{7,5},{8,10},{9,11},{10,... | collective-permute-start | bytes 393224 | tf_op jit(solution)/shard_map/ppermute | solution.py:315
  46.7 13.8 %collective-permute-start.16 = (bf16[4,64,256]{2,1,0:T(8,128)(2,1)S(1)}, bf16[4,64,256]{2,1,0:T(8,128)(2,1)S(1)}, u32[]{:S(2)}, u32[]{:S(2)}) collective-permute-start(bf16[4,64,256]{2,1,0:T(8,128)(2,1)S(1)} %get-tuple-element.62), channel_id=1, source_target_pairs={{0,1},{1,0},{2,3},{3,2},{4,5},{5,4},{6,7},{7,6},{8,9},{9,8},{10,11... | collective-permute-start | bytes 393224 | tf_op jit(solution)/shard_map/ppermute | solution.py:315
  47.1 8.8 %collective-permute-start.17 = (f32[64,256]{1,0:T(8,128)S(1)}, f32[64,256]{1,0:T(8,128)S(1)}, u32[]{:S(2)}, u32[]{:S(2)}) collective-permute-start(f32[64,256]{1,0:T(8,128)S(1)} %get-tuple-element.63), channel_id=1, source_target_pairs={{0,4},{4,8},{8,12},{12,16},{16,20},{20,24},{24,28},{1,5},{5,9},{9,... | collective-permute-start | bytes 196616 | tf_op jit(solution)/shard_map/ppermute | solution.py:421
  54.0 6.5 %collective-permute-start.18 = (f32[64,256]{1,0:T(8,128)S(1)}, f32[64,256]{1,0:T(8,128)S(1)}, u32[]{:S(2)}, u32[]{:S(2)}) collective-permute-start(f32[64,256]{1,0:T(8,128)S(1)} %get-tuple-element.64), channel_id=1, source_target_pairs={{4,0},{8,4},{12,8},{16,12},{20,16},{24,20},{28,24},{5,1},{9,5},{13... | collective-permute-start | bytes 196616 | tf_op jit(solution)/shard_map/ppermute | solution.py:422
  (2 other events, 4.5 us)

commit v10 on v9

--- a/solution.py
+++ b/solution.py
@@ -380,8 +380,6 @@
         cost_estimate=SMALL,
         name="late",
     )(z_arg, turned, early[-2], inverse)
-    late = swap(late)
-
     def mix(arrays, window, skip, begin, rows_out, after=()):
         flat = [a for group in arrays for a in group]
         return pl.pallas_call(
@@ -406,6 +404,9 @@
     window = ((0, 0),) + tuple((1, k) for k in range(half + 1))
     mixed = mix([rims, early], window, 0, (0, 0), half)
     back_early = swap(mixed)
+    late = list(late)
+    late[1], _ = lax.optimization_barrier((late[1], mixed[0]))
+    late = swap(late)
     window = ((0, half - 1), (0, half)) + tuple((1, k) for k in range(slab - half))
     back_late = swap(mix([early, late], window, 0, (half, half), slab - half, mixed[-1:]))
 

time: 66 us -> 68.8 us (1.042); the launches traced: 65 us -> 68.6 us
  waiting for transfers between devices: 6.93 us -> 11.6 us
  starting transfers between devices: 34 us -> 32.9 us
    ppermute x15, waiting for transfers between devices: 1.89 us -> 4.82 us  [swap(): lax.ppermute(arrays[p], 'mode', [(i, i ^ p) for i in range(count)])]
    ppermute x1, waiting for transfers between devices: 0.49 us -> 2.21 us  [body(): high_rim = lax.ppermute(first_rim, 'dom', downward)]
    ppermute x1, starting transfers between devices: 6.83 us -> 5.91 us  [body(): low = lax.ppermute(top, 'dom', upward)]
  transfers between devices with their start and end apart: 19 -> 19, of which waited for: 3 -> 4; matrix products, arithmetic and copies ran while one was open for 0% -> 0% of each run, Pallas kernels for 25% -> 24%
where the time goes in v10:
time: 68.8 us; the launch traced here: 68.6 us
  starting transfers between devices  32.9 us (48%)
  Pallas kernels  21.6 us (31%)
  waiting for transfers between devices  11.6 us (17%)
  local copies, waits for them, and re-layouts  1.73 us (3%)
  between operations  0.85 us (1%)
    ppermute x15, starting transfers between devices, swap(): lax.ppermute(arrays[p], 'mode', [(i, i ^ p) for i in range(count)])  18.9 us
    pallas_call x2, Pallas kernels, mix(): pl.pallas_call(functools.partial(mix_kernel, count, groups, fields, windo...  13 us
    ppermute x1, starting transfers between devices, body(): low = lax.ppermute(top, 'dom', upward)  5.91 us
    ppermute x15, waiting for transfers between devices, swap(): lax.ppermute(arrays[p], 'mode', [(i, i ^ p) for i in range(count)])  4.82 us
    pallas_call x1, Pallas kernels, body(): pl.pallas_call(functools.partial(post_kernel, count, slab, half, rows, rh...  4.57 us
    ppermute x1, waiting for transfers between devices, body(): high = lax.ppermute(bottom, 'dom', downward)  4.54 us
    ppermute x1, starting transfers between devices, body(): low_rim = lax.ppermute(last_rim, 'dom', upward)  4.24 us
    pallas_call x1, Pallas kernels, body(): pl.pallas_call(functools.partial(dense_kernel, groups, fields, here), out...  2.84 us
  transfers between devices with their start and end apart: 19, of which 4 were waited for; matrix products, arithmetic and copies ran while one was open for 0% of the time, Pallas kernels for 24%

profile of v10, /device:TPU:3, one launch (start us, length us, event | category | flops | bytes accessed | tf_op | source)
XLA Modules:
  0.0 68.6 jit_solution(5736257526400508265)
XLA Ops:
  0.6 1.6 %copy-done = f32[64,32,256]{2,1,0:T(8,128)S(1)} copy-done((f32[64,32,256]{2,1,0:T(8,128)S(1)}, f32[64,32,256]{2,1,0:T(8,128)}, u32[]{:S(2)}) %copy-start) | copy-done | bytes 2097176
  2.7 2.4 %collective-permute-start.6 = (bf16[5,64,256]{2,1,0:T(8,128)(2,1)S(1)}, bf16[5,64,256]{2,1,0:T(8,128)(2,1)S(1)}, u32[]{:S(2)}, u32[]{:S(2)}) collective-permute-start(bf16[5,64,256]{2,1,0:T(8,128)(2,1)S(1)} %get-tuple-element.47), channel_id=1, source_target_pairs={{0,2},{1,3},{2,0},{3,1},{4,6},{5,7},{6,4},{7,5},{8,10},{9,11},{10,... | collective-permute-start | bytes 491528 | tf_op jit(solution)/shard_map/ppermute | solution.py:315
  5.1 1.1 %collective-permute-start.5 = (bf16[5,64,256]{2,1,0:T(8,128)(2,1)S(1)}, bf16[5,64,256]{2,1,0:T(8,128)(2,1)S(1)}, u32[]{:S(2)}, u32[]{:S(2)}) collective-permute-start(bf16[5,64,256]{2,1,0:T(8,128)(2,1)S(1)} %get-tuple-element.46), channel_id=1, source_target_pairs={{0,3},{1,2},{2,1},{3,0},{4,7},{5,6},{6,5},{7,4},{8,11},{9,10},{10,... | collective-permute-start | bytes 491528 | tf_op jit(solution)/shard_map/ppermute | solution.py:315
  6.4 4.2 %collective-permute-start = (f32[88,256]{1,0:T(8,128)S(1)}, f32[88,256]{1,0:T(8,128)S(1)}, u32[]{:S(2)}, u32[]{:S(2)}) collective-permute-start(f32[88,256]{1,0:T(8,128)S(1)} %get-tuple-element.36), channel_id=1, source_target_pairs={{0,4},{4,8},{8,12},{12,16},{16,20},{20,24},{24,28},{1,5},{5,9},{9,... | collective-permute-start | bytes 270344 | tf_op jit(solution)/shard_map/ppermute | solution.py:344
  10.7 1.9 %collective-permute-start.1 = (f32[88,256]{1,0:T(8,128)S(1)}, f32[88,256]{1,0:T(8,128)S(1)}, u32[]{:S(2)}, u32[]{:S(2)}) collective-permute-start(f32[88,256]{1,0:T(8,128)S(1)} %get-tuple-element.37), channel_id=1, source_target_pairs={{4,0},{8,4},{12,8},{16,12},{20,16},{24,20},{28,24},{5,1},{9,5},{13... | collective-permute-start | bytes 270344 | tf_op jit(solution)/shard_map/ppermute | solution.py:345
  12.6 2.8 %dense.1 = (bf16[4,256,1280]{2,1,0:T(8,128)(2,1)S(1)}, f32[256,128]{1,0:T(8,128)S(1)}) custom-call(s32[1]{0:T(128)} %bitcast.z_ref, s32[3,5376]{1,0:T(4,128)S(1)} %bitcast.6, f32[1,5376]{1,0:T(1,128)S(1)} %broadcast_in_dim.3.value_ref), custom_call_target="tpu_custom_call" | custom-call | flops 1 | bytes 1 | tf_op jit(solution)/shard_map/dense/pallas_call | solution.py:320
  15.5 2.2 %collective-permute-done.1.high_ref = f32[88,256]{1,0:T(8,128)S(1)} collective-permute-done((f32[88,256]{1,0:T(8,128)S(1)}, f32[88,256]{1,0:T(8,128)S(1)}, u32[]{:S(2)}, u32[]{:S(2)}) %collective-permute-start.1) | collective-permute-done | bytes 90144 | tf_op jit(solution)/shard_map/ppermute | solution.py:345
  17.8 2.6 %collective-permute-start.2 = (bf16[1,64,256]{2,1,0:T(8,128)(2,1)S(1)}, bf16[1,64,256]{2,1,0:T(8,128)(2,1)S(1)}, u32[]{:S(2)}, u32[]{:S(2)}) collective-permute-start(bf16[1,64,256]{2,1,0:T(8,128)(2,1)S(1)} %get-tuple-element.42), channel_id=1, source_target_pairs={{0,3},{1,2},{2,1},{3,0},{4,7},{5,6},{6,5},{7,4},{8,11},{9,10},{10,... | collective-permute-start | bytes 98312 | tf_op jit(solution)/shard_map/ppermute | solution.py:315
  20.4 1.0 %collective-permute-start.4 = (bf16[1,64,256]{2,1,0:T(8,128)(2,1)S(1)}, bf16[1,64,256]{2,1,0:T(8,128)(2,1)S(1)}, u32[]{:S(2)}, u32[]{:S(2)}) collective-permute-start(bf16[1,64,256]{2,1,0:T(8,128)(2,1)S(1)} %get-tuple-element.44), channel_id=1, source_target_pairs={{0,1},{1,0},{2,3},{3,2},{4,5},{5,4},{6,7},{7,6},{8,9},{9,8},{10,11... | collective-permute-start | bytes 98312 | tf_op jit(solution)/shard_map/ppermute | solution.py:315
  21.9 0.5 collective-permute-done.2.refs_1_
  22.4 2.6 %collective-permute-start.11 = (bf16[4,64,256]{2,1,0:T(8,128)(2,1)S(1)}, bf16[4,64,256]{2,1,0:T(8,128)(2,1)S(1)}, u32[]{:S(2)}, u32[]{:S(2)}) collective-permute-start(bf16[4,64,256]{2,1,0:T(8,128)(2,1)S(1)} %get-tuple-element.57), channel_id=1, source_target_pairs={{0,3},{1,2},{2,1},{3,0},{4,7},{5,6},{6,5},{7,4},{8,11},{9,10},{10,... | collective-permute-start | bytes 393224 | tf_op jit(solution)/shard_map/ppermute | solution.py:315
  25.0 6.5 %mix.2 = (bf16[4,64,256]{2,1,0:T(8,128)(2,1)S(1)}, bf16[4,64,256]{2,1,0:T(8,128)(2,1)S(1)}, bf16[4,64,256]{2,1,0:T(8,128)(2,1)S(1)}, bf16[4,64,256]{2,1,0:T(8,128)(2,1)S(1)}) custom-call(bf16[1,64,256]{2,1,0:T(8,128)(2,1)S(1)} %get-tuple-element.41.refs_0_, bf16[1,64,256]{2,1,0:T(8,128)(2,1)S(1)} %collective-permute-done.2.refs_1_, ...), custom_call_target="tpu_custom_call" | custom-call | flops 10000000000 | bytes 16777216 | tf_op jit(solution)/shard_map/mix/pallas_call | solution.py:385
  31.6 1.8 %collective-permute-start.13 = (bf16[4,64,256]{2,1,0:T(8,128)(2,1)S(1)}, bf16[4,64,256]{2,1,0:T(8,128)(2,1)S(1)}, u32[]{:S(2)}, u32[]{:S(2)}) collective-permute-start(bf16[4,64,256]{2,1,0:T(8,128)(2,1)S(1)} %get-tuple-element.60), channel_id=1, source_target_pairs={{0,1},{1,0},{2,3},{3,2},{4,5},{5,4},{6,7},{7,6},{8,9},{9,8},{10,11... | collective-permute-start | bytes 393224 | tf_op jit(solution)/shard_map/ppermute | solution.py:315
  33.4 0.7 %collective-permute-start.9 = (bf16[4,64,256]{2,1,0:T(8,128)(2,1)S(1)}, bf16[4,64,256]{2,1,0:T(8,128)(2,1)S(1)}, u32[]{:S(2)}, u32[]{:S(2)}) collective-permute-start(bf16[4,64,256]{2,1,0:T(8,128)(2,1)S(1)} %get-tuple-element.53), channel_id=1, source_target_pairs={{0,2},{1,3},{2,0},{3,1},{4,6},{5,7},{6,4},{7,5},{8,10},{9,11},{10,... | collective-permute-start | bytes 393224 | tf_op jit(solution)/shard_map/ppermute | solution.py:315
  34.2 1.4 %collective-permute-start.10 = (bf16[4,64,256]{2,1,0:T(8,128)(2,1)S(1)}, bf16[4,64,256]{2,1,0:T(8,128)(2,1)S(1)}, u32[]{:S(2)}, u32[]{:S(2)}) collective-permute-start(bf16[4,64,256]{2,1,0:T(8,128)(2,1)S(1)} %get-tuple-element.54), channel_id=1, source_target_pairs={{0,1},{1,0},{2,3},{3,2},{4,5},{5,4},{6,7},{7,6},{8,9},{9,8},{10,11... | collective-permute-start | bytes 393224 | tf_op jit(solution)/shard_map/ppermute | solution.py:315
  35.6 1.4 %collective-permute-start.8 = (bf16[4,64,256]{2,1,0:T(8,128)(2,1)S(1)}, bf16[4,64,256]{2,1,0:T(8,128)(2,1)S(1)}, u32[]{:S(2)}, u32[]{:S(2)}) collective-permute-start(bf16[4,64,256]{2,1,0:T(8,128)(2,1)S(1)} %get-tuple-element.52.refs_11_), channel_id=1, source_target_pairs={{0,3},{1,2},{2,1},{3,0},{4,7},{5,6},{6,5},{7,4},{8,11},{9,10},{10,... | collective-permute-start | bytes 393224 | tf_op jit(solution)/shard_map/ppermute | solution.py:315
  37.1 4.3 %collective-permute-done.13.refs_7_ = bf16[4,64,256]{2,1,0:T(8,128)(2,1)S(1)} collective-permute-done((bf16[4,64,256]{2,1,0:T(8,128)(2,1)S(1)}, bf16[4,64,256]{2,1,0:T(8,128)(2,1)S(1)}, u32[]{:S(2)}, u32[]{:S(2)}) %collective-permute-start.13) | collective-permute-done | bytes 131104 | tf_op jit(solution)/shard_map/ppermute | solution.py:315
  41.4 6.5 %mix.3 = (bf16[4,64,256]{2,1,0:T(8,128)(2,1)S(1)}, bf16[4,64,256]{2,1,0:T(8,128)(2,1)S(1)}, bf16[4,64,256]{2,1,0:T(8,128)(2,1)S(1)}, bf16[4,64,256]{2,1,0:T(8,128)(2,1)S(1)}) custom-call(bf16[5,64,256]{2,1,0:T(8,128)(2,1)S(1)} %get-tuple-element.45.refs_4_.refs_0_, bf16[5,64,256]{2,1,0:T(8,128)(2,1)S(1)} %collective-permute-done.5.refs_5_.refs_1_, ...), custom_call_target="tpu_custom_call" | custom-call | flops 10000000000 | bytes 16777216 | tf_op jit(solution)/shard_map/mix/pallas_call | solution.py:385
  47.9 0.9 %collective-permute-start.14 = (bf16[4,64,256]{2,1,0:T(8,128)(2,1)S(1)}, bf16[4,64,256]{2,1,0:T(8,128)(2,1)S(1)}, u32[]{:S(2)}, u32[]{:S(2)}) collective-permute-start(bf16[4,64,256]{2,1,0:T(8,128)(2,1)S(1)} %get-tuple-element.62), channel_id=1, source_target_pairs={{0,3},{1,2},{2,1},{3,0},{4,7},{5,6},{6,5},{7,4},{8,11},{9,10},{10,... | collective-permute-start | bytes 393224 | tf_op jit(solution)/shard_map/ppermute | solution.py:315
  48.8 2.7 %collective-permute-start.16 = (bf16[4,64,256]{2,1,0:T(8,128)(2,1)S(1)}, bf16[4,64,256]{2,1,0:T(8,128)(2,1)S(1)}, u32[]{:S(2)}, u32[]{:S(2)}) collective-permute-start(bf16[4,64,256]{2,1,0:T(8,128)(2,1)S(1)} %get-tuple-element.64), channel_id=1, source_target_pairs={{0,1},{1,0},{2,3},{3,2},{4,5},{5,4},{6,7},{7,6},{8,9},{9,8},{10,11... | collective-permute-start | bytes 393224 | tf_op jit(solution)/shard_map/ppermute | solution.py:315
  51.6 5.9 %collective-permute-start.17 = (f32[64,256]{1,0:T(8,128)S(1)}, f32[64,256]{1,0:T(8,128)S(1)}, u32[]{:S(2)}, u32[]{:S(2)}) collective-permute-start(f32[64,256]{1,0:T(8,128)S(1)} %get-tuple-element.65), channel_id=1, source_target_pairs={{0,4},{4,8},{8,12},{12,16},{16,20},{20,24},{24,28},{1,5},{5,9},{9,... | collective-permute-start | bytes 196616 | tf_op jit(solution)/shard_map/ppermute | solution.py:422
  57.5 1.9 %collective-permute-start.18 = (f32[64,256]{1,0:T(8,128)S(1)}, f32[64,256]{1,0:T(8,128)S(1)}, u32[]{:S(2)}, u32[]{:S(2)}) collective-permute-start(f32[64,256]{1,0:T(8,128)S(1)} %get-tuple-element.66), channel_id=1, source_target_pairs={{4,0},{8,4},{12,8},{16,12},{20,16},{24,20},{28,24},{5,1},{9,5},{13... | collective-permute-start | bytes 196616 | tf_op jit(solution)/shard_map/ppermute | solution.py:423
  59.5 4.5 %collective-permute-done.18.refs_11_ = f32[64,256]{1,0:T(8,128)S(1)} collective-permute-done((f32[64,256]{1,0:T(8,128)S(1)}, f32[64,256]{1,0:T(8,128)S(1)}, u32[]{:S(2)}, u32[]{:S(2)}) %collective-permute-start.18) | collective-permute-done | bytes 65568 | tf_op jit(solution)/shard_map/ppermute | solution.py:423
  64.0 4.6 %post.1 = (f32[64,32,256]{2,1,0:T(8,128)}, f32[64,32,256]{2,1,0:T(8,128)}) custom-call(s32[1]{0:T(128)} %bitcast.z_ref, bf16[4,64,256]{2,1,0:T(8,128)(2,1)S(1)} %get-tuple-element.51.refs_0_, bf16[4,64,256]{2,1,0:T(8,128)(2,1)S(1)} %collective-permute-done.8.refs_1_, bf16[4,64,256]{2,1,0:T(8,128)(2,1)S(1)} %collective-permute-done.9.refs_2_, ...), custom_call_target="tpu_custom_call" | custom-call | tf_op jit(solution)/shard_map/post/pallas_call | solution.py:433
  (41 shorter events, 1.5 us)
Async XLA Ops:
  2.2 4.2 %copy-start.4 = (f32[32,256]{1,0:T(8,128)S(1)}, f32[32,256]{1,0:T(8,128)}, u32[]{:S(2)}) copy-start(f32[32,256]{1,0:T(8,128)} %mean_ref.3) | copy-start | bytes 98308
  2.2 10.4 %copy-start.6 = (f32[5376]{0:T(1024)S(1)}, f32[5376]{0:T(1024)}, u32[]{:S(2)}) copy-start(f32[5376]{0:T(1024)} %param.11) | copy-start | bytes 64516
  2.2 10.4 %copy-start.5 = (s32[5376,3]{0,1:T(4,128)S(1)}, s32[5376,3]{0,1:T(4,128)}, u32[]{:S(2)}) copy-start(s32[5376,3]{0,1:T(4,128)} %param.10) | copy-start | bytes 193540
  2.7 17.7 %collective-permute-start.6 = (bf16[5,64,256]{2,1,0:T(8,128)(2,1)S(1)}, bf16[5,64,256]{2,1,0:T(8,128)(2,1)S(1)}, u32[]{:S(2)}, u32[]{:S(2)}) collective-permute-start(bf16[5,64,256]{2,1,0:T(8,128)(2,1)S(1)} %get-tuple-element.47), channel_id=1, source_target_pairs={{0,2},{1,3},{2,0},{3,1},{4,6},{5,7},{6,4},{7,5},{8,10},{9,11},{10,... | collective-permute-start | bytes 491528 | tf_op jit(solution)/shard_map/ppermute | solution.py:315
  5.1 19.9 %collective-permute-start.5 = (bf16[5,64,256]{2,1,0:T(8,128)(2,1)S(1)}, bf16[5,64,256]{2,1,0:T(8,128)(2,1)S(1)}, u32[]{:S(2)}, u32[]{:S(2)}) collective-permute-start(bf16[5,64,256]{2,1,0:T(8,128)(2,1)S(1)} %get-tuple-element.46), channel_id=1, source_target_pairs={{0,3},{1,2},{2,1},{3,0},{4,7},{5,6},{6,5},{7,4},{8,11},{9,10},{10,... | collective-permute-start | bytes 491528 | tf_op jit(solution)/shard_map/ppermute | solution.py:315
  6.2 18.8 %collective-permute-start.7 = (bf16[5,64,256]{2,1,0:T(8,128)(2,1)S(1)}, bf16[5,64,256]{2,1,0:T(8,128)(2,1)S(1)}, u32[]{:S(2)}, u32[]{:S(2)}) collective-permute-start(bf16[5,64,256]{2,1,0:T(8,128)(2,1)S(1)} %get-tuple-element.48), channel_id=1, source_target_pairs={{0,1},{1,0},{2,3},{3,2},{4,5},{5,4},{6,7},{7,6},{8,9},{9,8},{10,11... | collective-permute-start | bytes 491528 | tf_op jit(solution)/shard_map/ppermute | solution.py:315
  6.4 9.1 %collective-permute-start = (f32[88,256]{1,0:T(8,128)S(1)}, f32[88,256]{1,0:T(8,128)S(1)}, u32[]{:S(2)}, u32[]{:S(2)}) collective-permute-start(f32[88,256]{1,0:T(8,128)S(1)} %get-tuple-element.36), channel_id=1, source_target_pairs={{0,4},{4,8},{8,12},{12,16},{16,20},{20,24},{24,28},{1,5},{5,9},{9,... | collective-permute-start | bytes 270344 | tf_op jit(solution)/shard_map/ppermute | solution.py:344
  10.7 7.0 %collective-permute-start.1 = (f32[88,256]{1,0:T(8,128)S(1)}, f32[88,256]{1,0:T(8,128)S(1)}, u32[]{:S(2)}, u32[]{:S(2)}) collective-permute-start(f32[88,256]{1,0:T(8,128)S(1)} %get-tuple-element.37), channel_id=1, source_target_pairs={{4,0},{8,4},{12,8},{16,12},{20,16},{24,20},{28,24},{5,1},{9,5},{13... | collective-permute-start | bytes 270344 | tf_op jit(solution)/shard_map/ppermute | solution.py:345
  17.8 4.6 %collective-permute-start.2 = (bf16[1,64,256]{2,1,0:T(8,128)(2,1)S(1)}, bf16[1,64,256]{2,1,0:T(8,128)(2,1)S(1)}, u32[]{:S(2)}, u32[]{:S(2)}) collective-permute-start(bf16[1,64,256]{2,1,0:T(8,128)(2,1)S(1)} %get-tuple-element.42), channel_id=1, source_target_pairs={{0,3},{1,2},{2,1},{3,0},{4,7},{5,6},{6,5},{7,4},{8,11},{9,10},{10,... | collective-permute-start | bytes 98312 | tf_op jit(solution)/shard_map/ppermute | solution.py:315
  20.4 4.6 %collective-permute-start.3 = (bf16[1,64,256]{2,1,0:T(8,128)(2,1)S(1)}, bf16[1,64,256]{2,1,0:T(8,128)(2,1)S(1)}, u32[]{:S(2)}, u32[]{:S(2)}) collective-permute-start(bf16[1,64,256]{2,1,0:T(8,128)(2,1)S(1)} %get-tuple-element.43), channel_id=1, source_target_pairs={{0,2},{1,3},{2,0},{3,1},{4,6},{5,7},{6,4},{7,5},{8,10},{9,11},{10,... | collective-permute-start | bytes 98312 | tf_op jit(solution)/shard_map/ppermute | solution.py:315
  20.4 4.6 %collective-permute-start.4 = (bf16[1,64,256]{2,1,0:T(8,128)(2,1)S(1)}, bf16[1,64,256]{2,1,0:T(8,128)(2,1)S(1)}, u32[]{:S(2)}, u32[]{:S(2)}) collective-permute-start(bf16[1,64,256]{2,1,0:T(8,128)(2,1)S(1)} %get-tuple-element.44), channel_id=1, source_target_pairs={{0,1},{1,0},{2,3},{3,2},{4,5},{5,4},{6,7},{7,6},{8,9},{9,8},{10,11... | collective-permute-start | bytes 98312 | tf_op jit(solution)/shard_map/ppermute | solution.py:315
  22.4 13.2 %collective-permute-start.11 = (bf16[4,64,256]{2,1,0:T(8,128)(2,1)S(1)}, bf16[4,64,256]{2,1,0:T(8,128)(2,1)S(1)}, u32[]{:S(2)}, u32[]{:S(2)}) collective-permute-start(bf16[4,64,256]{2,1,0:T(8,128)(2,1)S(1)} %get-tuple-element.57), channel_id=1, source_target_pairs={{0,3},{1,2},{2,1},{3,0},{4,7},{5,6},{6,5},{7,4},{8,11},{9,10},{10,... | collective-permute-start | bytes 393224 | tf_op jit(solution)/shard_map/ppermute | solution.py:315
  25.0 12.1 %collective-permute-start.12 = (bf16[4,64,256]{2,1,0:T(8,128)(2,1)S(1)}, bf16[4,64,256]{2,1,0:T(8,128)(2,1)S(1)}, u32[]{:S(2)}, u32[]{:S(2)}) collective-permute-start(bf16[4,64,256]{2,1,0:T(8,128)(2,1)S(1)} %get-tuple-element.58), channel_id=1, source_target_pairs={{0,2},{1,3},{2,0},{3,1},{4,6},{5,7},{6,4},{7,5},{8,10},{9,11},{10,... | collective-permute-start | bytes 393224 | tf_op jit(solution)/shard_map/ppermute | solution.py:315
  25.0 8.3 %copy-start.3 = (f32[64,32,256]{2,1,0:T(8,128)S(1)}, f32[64,32,256]{2,1,0:T(8,128)}, u32[]{:S(2)}) copy-start(f32[64,32,256]{2,1,0:T(8,128)} %refs_8_.1) | copy-start | bytes 6291460
  31.6 9.8 %collective-permute-start.13 = (bf16[4,64,256]{2,1,0:T(8,128)(2,1)S(1)}, bf16[4,64,256]{2,1,0:T(8,128)(2,1)S(1)}, u32[]{:S(2)}, u32[]{:S(2)}) collective-permute-start(bf16[4,64,256]{2,1,0:T(8,128)(2,1)S(1)} %get-tuple-element.60), channel_id=1, source_target_pairs={{0,1},{1,0},{2,3},{3,2},{4,5},{5,4},{6,7},{7,6},{8,9},{9,8},{10,11... | collective-permute-start | bytes 393224 | tf_op jit(solution)/shard_map/ppermute | solution.py:315
  33.4 15.4 %collective-permute-start.9 = (bf16[4,64,256]{2,1,0:T(8,128)(2,1)S(1)}, bf16[4,64,256]{2,1,0:T(8,128)(2,1)S(1)}, u32[]{:S(2)}, u32[]{:S(2)}) collective-permute-start(bf16[4,64,256]{2,1,0:T(8,128)(2,1)S(1)} %get-tuple-element.53), channel_id=1, source_target_pairs={{0,2},{1,3},{2,0},{3,1},{4,6},{5,7},{6,4},{7,5},{8,10},{9,11},{10,... | collective-permute-start | bytes 393224 | tf_op jit(solution)/shard_map/ppermute | solution.py:315
  34.2 17.4 %collective-permute-start.10 = (bf16[4,64,256]{2,1,0:T(8,128)(2,1)S(1)}, bf16[4,64,256]{2,1,0:T(8,128)(2,1)S(1)}, u32[]{:S(2)}, u32[]{:S(2)}) collective-permute-start(bf16[4,64,256]{2,1,0:T(8,128)(2,1)S(1)} %get-tuple-element.54), channel_id=1, source_target_pairs={{0,1},{1,0},{2,3},{3,2},{4,5},{5,4},{6,7},{7,6},{8,9},{9,8},{10,11... | collective-permute-start | bytes 393224 | tf_op jit(solution)/shard_map/ppermute | solution.py:315
  35.6 15.9 %collective-permute-start.8 = (bf16[4,64,256]{2,1,0:T(8,128)(2,1)S(1)}, bf16[4,64,256]{2,1,0:T(8,128)(2,1)S(1)}, u32[]{:S(2)}, u32[]{:S(2)}) collective-permute-start(bf16[4,64,256]{2,1,0:T(8,128)(2,1)S(1)} %get-tuple-element.52.refs_11_), channel_id=1, source_target_pairs={{0,3},{1,2},{2,1},{3,0},{4,7},{5,6},{6,5},{7,4},{8,11},{9,10},{10,... | collective-permute-start | bytes 393224 | tf_op jit(solution)/shard_map/ppermute | solution.py:315
  41.4 22.7 %copy-start.1 = (f32[64,32,256]{2,1,0:T(8,128)S(1)}, f32[64,32,256]{2,1,0:T(8,128)}, u32[]{:S(2)}) copy-start(f32[64,32,256]{2,1,0:T(8,128)} %refs_9_.1) | copy-start | bytes 6291460
  47.9 16.1 %collective-permute-start.14 = (bf16[4,64,256]{2,1,0:T(8,128)(2,1)S(1)}, bf16[4,64,256]{2,1,0:T(8,128)(2,1)S(1)}, u32[]{:S(2)}, u32[]{:S(2)}) collective-permute-start(bf16[4,64,256]{2,1,0:T(8,128)(2,1)S(1)} %get-tuple-element.62), channel_id=1, source_target_pairs={{0,3},{1,2},{2,1},{3,0},{4,7},{5,6},{6,5},{7,4},{8,11},{9,10},{10,... | collective-permute-start | bytes 393224 | tf_op jit(solution)/shard_map/ppermute | solution.py:315
  48.8 15.2 %collective-permute-start.15 = (bf16[4,64,256]{2,1,0:T(8,128)(2,1)S(1)}, bf16[4,64,256]{2,1,0:T(8,128)(2,1)S(1)}, u32[]{:S(2)}, u32[]{:S(2)}) collective-permute-start(bf16[4,64,256]{2,1,0:T(8,128)(2,1)S(1)} %get-tuple-element.63), channel_id=1, source_target_pairs={{0,2},{1,3},{2,0},{3,1},{4,6},{5,7},{6,4},{7,5},{8,10},{9,11},{10,... | collective-permute-start | bytes 393224 | tf_op jit(solution)/shard_map/ppermute | solution.py:315
  48.8 15.2 %collective-permute-start.16 = (bf16[4,64,256]{2,1,0:T(8,128)(2,1)S(1)}, bf16[4,64,256]{2,1,0:T(8,128)(2,1)S(1)}, u32[]{:S(2)}, u32[]{:S(2)}) collective-permute-start(bf16[4,64,256]{2,1,0:T(8,128)(2,1)S(1)} %get-tuple-element.64), channel_id=1, source_target_pairs={{0,1},{1,0},{2,3},{3,2},{4,5},{5,4},{6,7},{7,6},{8,9},{9,8},{10,11... | collective-permute-start | bytes 393224 | tf_op jit(solution)/shard_map/ppermute | solution.py:315
  51.6 7.8 %collective-permute-start.17 = (f32[64,256]{1,0:T(8,128)S(1)}, f32[64,256]{1,0:T(8,128)S(1)}, u32[]{:S(2)}, u32[]{:S(2)}) collective-permute-start(f32[64,256]{1,0:T(8,128)S(1)} %get-tuple-element.65), channel_id=1, source_target_pairs={{0,4},{4,8},{8,12},{12,16},{16,20},{20,24},{24,28},{1,5},{5,9},{9,... | collective-permute-start | bytes 196616 | tf_op jit(solution)/shard_map/ppermute | solution.py:422
  57.5 6.5 %collective-permute-start.18 = (f32[64,256]{1,0:T(8,128)S(1)}, f32[64,256]{1,0:T(8,128)S(1)}, u32[]{:S(2)}, u32[]{:S(2)}) collective-permute-start(f32[64,256]{1,0:T(8,128)S(1)} %get-tuple-element.66), channel_id=1, source_target_pairs={{4,0},{8,4},{12,8},{16,12},{20,16},{24,20},{28,24},{5,1},{9,5},{13... | collective-permute-start | bytes 196616 | tf_op jit(solution)/shard_map/ppermute | solution.py:423
  (2 other events, 5.8 us)

commit v11 on v9

--- a/solution.py
+++ b/solution.py
@@ -263,8 +263,8 @@
         place = jnp.bitwise_xor(z, (count - k) % count)
         for rho in range(slab):
             part = early[k][rho] if rho < half else late[k][rho - half]
-            image[row_of(place, rho, slab, count, rows)] = part.astype(jnp.float32)
-    residual[...] = source[...] - jnp.swapaxes(image[...], 0, 1)
+            image[row_of(place, rho, slab, count, rows)] = part
+    residual[...] = source[...] - jnp.swapaxes(image[...], 0, 1).astype(jnp.float32)
     place = lax.broadcasted_iota(jnp.int32, (rows, cells), 0)
     inv = inverse[...]
     for m in range(modes):
@@ -424,7 +424,7 @@
     sigma = cheb_center / cheb_radius
     rho_zero = 1.0 / sigma
     rho_one = 1.0 / (2.0 * sigma - rho_zero)
-    block = min(16, here)
+    block = min(32, here)
     row_spec = pl.BlockSpec((block, cells), lambda i: (i, 0))
     early_spec = pl.BlockSpec((half, block, cells), lambda i: (0, i, 0))
     late_spec = pl.BlockSpec((slab - half, block, cells), lambda i: (0, i, 0))
@@ -442,7 +442,7 @@
             pl.BlockSpec((rows, cells), lambda i: (0, 0)),
         ],
         out_specs=[flat_spec, flat_spec],
-        scratch_shapes=[pltpu.VMEM((rows, block, cells), jnp.float32)],
+        scratch_shapes=[pltpu.VMEM((rows, block, cells), bf16)],
         compiler_params=params,
         name="post",
     )(

time: 66 us -> 65.7 us (level)
  transfers between devices with their start and end apart: 19 -> 19, of which waited for: 3 -> 3; matrix products, arithmetic and copies ran while one was open for 0% -> 0% of each run, Pallas kernels for 25% -> 26%
where the time goes in v11:
time: 65.7 us; the launch traced here: 64.8 us
  starting transfers between devices  34 us (52%)
  Pallas kernels  21.3 us (32%)
  waiting for transfers between devices  6.94 us (11%)
  local copies, waits for them, and re-layouts  1.73 us (3%)
  between operations  0.82 us (1%)
    ppermute x15, starting transfers between devices, swap(): lax.ppermute(arrays[p], 'mode', [(i, i ^ p) for i in range(count)])  19.4 us
    pallas_call x2, Pallas kernels, mix(): pl.pallas_call(functools.partial(mix_kernel, count, groups, fields, windo...  13 us
    ppermute x1, starting transfers between devices, body(): low = lax.ppermute(top, 'dom', upward)  6.84 us
    ppermute x1, waiting for transfers between devices, body(): high = lax.ppermute(bottom, 'dom', downward)  4.54 us
    pallas_call x1, Pallas kernels, body(): pl.pallas_call(functools.partial(post_kernel, count, slab, half, rows, rh...  4.34 us
    ppermute x1, starting transfers between devices, body(): low_rim = lax.ppermute(last_rim, 'dom', upward)  3.96 us
    pallas_call x1, Pallas kernels, body(): pl.pallas_call(functools.partial(dense_kernel, groups, fields, here), out...  2.84 us
    ppermute x1, starting transfers between devices, body(): high_rim = lax.ppermute(first_rim, 'dom', downward)  1.92 us
  transfers between devices with their start and end apart: 19, of which 3 were waited for; matrix products, arithmetic and copies ran while one was open for 0% of the time, Pallas kernels for 26%

profile of v11, /device:TPU:3, one launch (start us, length us, event | category | flops | bytes accessed | tf_op | source)
XLA Modules:
  0.0 64.8 jit_solution(1994223207771507984)
XLA Ops:
  0.6 1.6 %copy-done = f32[64,32,256]{2,1,0:T(8,128)S(1)} copy-done((f32[64,32,256]{2,1,0:T(8,128)S(1)}, f32[64,32,256]{2,1,0:T(8,128)}, u32[]{:S(2)}) %copy-start) | copy-done | bytes 2097176
  2.2 0.5 turn.1
  2.7 2.4 %collective-permute-start.6 = (bf16[5,64,256]{2,1,0:T(8,128)(2,1)S(1)}, bf16[5,64,256]{2,1,0:T(8,128)(2,1)S(1)}, u32[]{:S(2)}, u32[]{:S(2)}) collective-permute-start(bf16[5,64,256]{2,1,0:T(8,128)(2,1)S(1)} %get-tuple-element.46), channel_id=1, source_target_pairs={{0,2},{1,3},{2,0},{3,1},{4,6},{5,7},{6,4},{7,5},{8,10},{9,11},{10,... | collective-permute-start | bytes 491528 | tf_op jit(solution)/shard_map/ppermute | solution.py:315
  5.1 4.0 %collective-permute-start = (f32[88,256]{1,0:T(8,128)S(1)}, f32[88,256]{1,0:T(8,128)S(1)}, u32[]{:S(2)}, u32[]{:S(2)}) collective-permute-start(f32[88,256]{1,0:T(8,128)S(1)} %get-tuple-element.35), channel_id=1, source_target_pairs={{0,4},{4,8},{8,12},{12,16},{16,20},{20,24},{24,28},{1,5},{5,9},{9,... | collective-permute-start | bytes 270344 | tf_op jit(solution)/shard_map/ppermute | solution.py:344
  9.1 1.9 %collective-permute-start.1 = (f32[88,256]{1,0:T(8,128)S(1)}, f32[88,256]{1,0:T(8,128)S(1)}, u32[]{:S(2)}, u32[]{:S(2)}) collective-permute-start(f32[88,256]{1,0:T(8,128)S(1)} %get-tuple-element.36), channel_id=1, source_target_pairs={{4,0},{8,4},{12,8},{16,12},{20,16},{24,20},{28,24},{5,1},{9,5},{13... | collective-permute-start | bytes 270344 | tf_op jit(solution)/shard_map/ppermute | solution.py:345
  11.0 1.3 %collective-permute-start.5 = (bf16[5,64,256]{2,1,0:T(8,128)(2,1)S(1)}, bf16[5,64,256]{2,1,0:T(8,128)(2,1)S(1)}, u32[]{:S(2)}, u32[]{:S(2)}) collective-permute-start(bf16[5,64,256]{2,1,0:T(8,128)(2,1)S(1)} %get-tuple-element.45), channel_id=1, source_target_pairs={{0,3},{1,2},{2,1},{3,0},{4,7},{5,6},{6,5},{7,4},{8,11},{9,10},{10,... | collective-permute-start | bytes 491528 | tf_op jit(solution)/shard_map/ppermute | solution.py:315
  12.5 2.8 %dense.1 = (bf16[4,256,1280]{2,1,0:T(8,128)(2,1)S(1)}, f32[256,128]{1,0:T(8,128)S(1)}) custom-call(s32[1]{0:T(128)} %bitcast.z_ref, s32[3,5376]{1,0:T(4,128)S(1)} %bitcast.6, f32[1,5376]{1,0:T(1,128)S(1)} %broadcast_in_dim.3.value_ref), custom_call_target="tpu_custom_call" | custom-call | flops 1 | bytes 1 | tf_op jit(solution)/shard_map/dense/pallas_call | solution.py:320
  15.4 0.5 collective-permute-done.1.high_ref
  15.9 1.9 %collective-permute-start.2 = (bf16[1,64,256]{2,1,0:T(8,128)(2,1)S(1)}, bf16[1,64,256]{2,1,0:T(8,128)(2,1)S(1)}, u32[]{:S(2)}, u32[]{:S(2)}) collective-permute-start(bf16[1,64,256]{2,1,0:T(8,128)(2,1)S(1)} %get-tuple-element.41), channel_id=1, source_target_pairs={{0,3},{1,2},{2,1},{3,0},{4,7},{5,6},{6,5},{7,4},{8,11},{9,10},{10,... | collective-permute-start | bytes 98312 | tf_op jit(solution)/shard_map/ppermute | solution.py:315
  17.8 0.6 %collective-permute-start.3 = (bf16[1,64,256]{2,1,0:T(8,128)(2,1)S(1)}, bf16[1,64,256]{2,1,0:T(8,128)(2,1)S(1)}, u32[]{:S(2)}, u32[]{:S(2)}) collective-permute-start(bf16[1,64,256]{2,1,0:T(8,128)(2,1)S(1)} %get-tuple-element.42), channel_id=1, source_target_pairs={{0,2},{1,3},{2,0},{3,1},{4,6},{5,7},{6,4},{7,5},{8,10},{9,11},{10,... | collective-permute-start | bytes 98312 | tf_op jit(solution)/shard_map/ppermute | solution.py:315
  18.4 1.1 %collective-permute-start.4 = (bf16[1,64,256]{2,1,0:T(8,128)(2,1)S(1)}, bf16[1,64,256]{2,1,0:T(8,128)(2,1)S(1)}, u32[]{:S(2)}, u32[]{:S(2)}) collective-permute-start(bf16[1,64,256]{2,1,0:T(8,128)(2,1)S(1)} %get-tuple-element.43), channel_id=1, source_target_pairs={{0,1},{1,0},{2,3},{3,2},{4,5},{5,4},{6,7},{7,6},{8,9},{9,8},{10,11... | collective-permute-start | bytes 98312 | tf_op jit(solution)/shard_map/ppermute | solution.py:315
  19.6 0.5 weights.1
  20.2 1.9 %collective-permute-done.2.refs_1_ = bf16[1,64,256]{2,1,0:T(8,128)(2,1)S(1)} collective-permute-done((bf16[1,64,256]{2,1,0:T(8,128)(2,1)S(1)}, bf16[1,64,256]{2,1,0:T(8,128)(2,1)S(1)}, u32[]{:S(2)}, u32[]{:S(2)}) %collective-permute-start.2) | collective-permute-done | bytes 32800 | tf_op jit(solution)/shard_map/ppermute | solution.py:315
  22.0 1.3 %collective-permute-start.11 = (bf16[4,64,256]{2,1,0:T(8,128)(2,1)S(1)}, bf16[4,64,256]{2,1,0:T(8,128)(2,1)S(1)}, u32[]{:S(2)}, u32[]{:S(2)}) collective-permute-start(bf16[4,64,256]{2,1,0:T(8,128)(2,1)S(1)} %get-tuple-element.56), channel_id=1, source_target_pairs={{0,3},{1,2},{2,1},{3,0},{4,7},{5,6},{6,5},{7,4},{8,11},{9,10},{10,... | collective-permute-start | bytes 393224 | tf_op jit(solution)/shard_map/ppermute | solution.py:315
  23.3 0.8 %collective-permute-start.12 = (bf16[4,64,256]{2,1,0:T(8,128)(2,1)S(1)}, bf16[4,64,256]{2,1,0:T(8,128)(2,1)S(1)}, u32[]{:S(2)}, u32[]{:S(2)}) collective-permute-start(bf16[4,64,256]{2,1,0:T(8,128)(2,1)S(1)} %get-tuple-element.57), channel_id=1, source_target_pairs={{0,2},{1,3},{2,0},{3,1},{4,6},{5,7},{6,4},{7,5},{8,10},{9,11},{10,... | collective-permute-start | bytes 393224 | tf_op jit(solution)/shard_map/ppermute | solution.py:315
  24.1 2.6 %collective-permute-start.13 = (bf16[4,64,256]{2,1,0:T(8,128)(2,1)S(1)}, bf16[4,64,256]{2,1,0:T(8,128)(2,1)S(1)}, u32[]{:S(2)}, u32[]{:S(2)}) collective-permute-start(bf16[4,64,256]{2,1,0:T(8,128)(2,1)S(1)} %get-tuple-element.58), channel_id=1, source_target_pairs={{0,1},{1,0},{2,3},{3,2},{4,5},{5,4},{6,7},{7,6},{8,9},{9,8},{10,11... | collective-permute-start | bytes 393224 | tf_op jit(solution)/shard_map/ppermute | solution.py:315
  26.7 6.5 %mix.2 = (bf16[4,64,256]{2,1,0:T(8,128)(2,1)S(1)}, bf16[4,64,256]{2,1,0:T(8,128)(2,1)S(1)}, bf16[4,64,256]{2,1,0:T(8,128)(2,1)S(1)}, bf16[4,64,256]{2,1,0:T(8,128)(2,1)S(1)}) custom-call(bf16[1,64,256]{2,1,0:T(8,128)(2,1)S(1)} %get-tuple-element.40.refs_0_, bf16[1,64,256]{2,1,0:T(8,128)(2,1)S(1)} %collective-permute-done.2.refs_1_, ...), custom_call_target="tpu_custom_call" | custom-call | flops 10000000000 | bytes 16777216 | tf_op jit(solution)/shard_map/mix/pallas_call | solution.py:387
  33.7 3.1 %collective-permute-start.8 = (bf16[4,64,256]{2,1,0:T(8,128)(2,1)S(1)}, bf16[4,64,256]{2,1,0:T(8,128)(2,1)S(1)}, u32[]{:S(2)}, u32[]{:S(2)}) collective-permute-start(bf16[4,64,256]{2,1,0:T(8,128)(2,1)S(1)} %get-tuple-element.51.refs_11_), channel_id=1, source_target_pairs={{0,3},{1,2},{2,1},{3,0},{4,7},{5,6},{6,5},{7,4},{8,11},{9,10},{10,... | collective-permute-start | bytes 393224 | tf_op jit(solution)/shard_map/ppermute | solution.py:315
  36.8 6.5 %mix.3 = (bf16[4,64,256]{2,1,0:T(8,128)(2,1)S(1)}, bf16[4,64,256]{2,1,0:T(8,128)(2,1)S(1)}, bf16[4,64,256]{2,1,0:T(8,128)(2,1)S(1)}, bf16[4,64,256]{2,1,0:T(8,128)(2,1)S(1)}) custom-call(bf16[5,64,256]{2,1,0:T(8,128)(2,1)S(1)} %get-tuple-element.44.refs_4_.refs_0_, bf16[5,64,256]{2,1,0:T(8,128)(2,1)S(1)} %collective-permute-done.5.refs_5_.refs_1_, ...), custom_call_target="tpu_custom_call" | custom-call | flops 10000000000 | bytes 16777216 | tf_op jit(solution)/shard_map/mix/pallas_call | solution.py:387
  43.3 3.3 %collective-permute-start.14 = (bf16[4,64,256]{2,1,0:T(8,128)(2,1)S(1)}, bf16[4,64,256]{2,1,0:T(8,128)(2,1)S(1)}, u32[]{:S(2)}, u32[]{:S(2)}) collective-permute-start(bf16[4,64,256]{2,1,0:T(8,128)(2,1)S(1)} %get-tuple-element.60), channel_id=1, source_target_pairs={{0,3},{1,2},{2,1},{3,0},{4,7},{5,6},{6,5},{7,4},{8,11},{9,10},{10,... | collective-permute-start | bytes 393224 | tf_op jit(solution)/shard_map/ppermute | solution.py:315
  47.1 6.8 %collective-permute-start.17 = (f32[64,256]{1,0:T(8,128)S(1)}, f32[64,256]{1,0:T(8,128)S(1)}, u32[]{:S(2)}, u32[]{:S(2)}) collective-permute-start(f32[64,256]{1,0:T(8,128)S(1)} %get-tuple-element.63), channel_id=1, source_target_pairs={{0,4},{4,8},{8,12},{12,16},{16,20},{20,24},{24,28},{1,5},{5,9},{9,... | collective-permute-start | bytes 196616 | tf_op jit(solution)/shard_map/ppermute | solution.py:421
  54.0 1.9 %collective-permute-start.18 = (f32[64,256]{1,0:T(8,128)S(1)}, f32[64,256]{1,0:T(8,128)S(1)}, u32[]{:S(2)}, u32[]{:S(2)}) collective-permute-start(f32[64,256]{1,0:T(8,128)S(1)} %get-tuple-element.64), channel_id=1, source_target_pairs={{4,0},{8,4},{12,8},{16,12},{20,16},{24,20},{28,24},{5,1},{9,5},{13... | collective-permute-start | bytes 196616 | tf_op jit(solution)/shard_map/ppermute | solution.py:422
  55.9 4.5 %collective-permute-done.18.refs_11_ = f32[64,256]{1,0:T(8,128)S(1)} collective-permute-done((f32[64,256]{1,0:T(8,128)S(1)}, f32[64,256]{1,0:T(8,128)S(1)}, u32[]{:S(2)}, u32[]{:S(2)}) %collective-permute-start.18) | collective-permute-done | bytes 65568 | tf_op jit(solution)/shard_map/ppermute | solution.py:422
  60.5 4.3 %post.1 = (f32[64,32,256]{2,1,0:T(8,128)}, f32[64,32,256]{2,1,0:T(8,128)}) custom-call(s32[1]{0:T(128)} %bitcast.z_ref, bf16[4,64,256]{2,1,0:T(8,128)(2,1)S(1)} %get-tuple-element.50.refs_0_, bf16[4,64,256]{2,1,0:T(8,128)(2,1)S(1)} %collective-permute-done.8.refs_1_, bf16[4,64,256]{2,1,0:T(8,128)(2,1)S(1)} %collective-permute-done.9.refs_2_, ...), custom_call_target="tpu_custom_call" | custom-call | tf_op jit(solution)/shard_map/post/pallas_call | solution.py:432
  (41 shorter events, 1.4 us)
Async XLA Ops:
  2.2 2.9 %copy-start.4 = (f32[32,256]{1,0:T(8,128)S(1)}, f32[32,256]{1,0:T(8,128)}, u32[]{:S(2)}) copy-start(f32[32,256]{1,0:T(8,128)} %mean_ref.3) | copy-start | bytes 98308
  2.2 10.2 %copy-start.6 = (f32[5376]{0:T(1024)S(1)}, f32[5376]{0:T(1024)}, u32[]{:S(2)}) copy-start(f32[5376]{0:T(1024)} %param.11) | copy-start | bytes 64516
  2.2 10.3 %copy-start.5 = (s32[5376,3]{0,1:T(4,128)S(1)}, s32[5376,3]{0,1:T(4,128)}, u32[]{:S(2)}) copy-start(s32[5376,3]{0,1:T(4,128)} %param.10) | copy-start | bytes 193540
  2.7 16.8 %copy-start.3 = (f32[64,32,256]{2,1,0:T(8,128)S(1)}, f32[64,32,256]{2,1,0:T(8,128)}, u32[]{:S(2)}) copy-start(f32[64,32,256]{2,1,0:T(8,128)} %refs_8_.1) | copy-start | bytes 6291460
  2.7 15.7 %collective-permute-start.6 = (bf16[5,64,256]{2,1,0:T(8,128)(2,1)S(1)}, bf16[5,64,256]{2,1,0:T(8,128)(2,1)S(1)}, u32[]{:S(2)}, u32[]{:S(2)}) collective-permute-start(bf16[5,64,256]{2,1,0:T(8,128)(2,1)S(1)} %get-tuple-element.46), channel_id=1, source_target_pairs={{0,2},{1,3},{2,0},{3,1},{4,6},{5,7},{6,4},{7,5},{8,10},{9,11},{10,... | collective-permute-start | bytes 491528 | tf_op jit(solution)/shard_map/ppermute | solution.py:315
  5.1 10.2 %collective-permute-start = (f32[88,256]{1,0:T(8,128)S(1)}, f32[88,256]{1,0:T(8,128)S(1)}, u32[]{:S(2)}, u32[]{:S(2)}) collective-permute-start(f32[88,256]{1,0:T(8,128)S(1)} %get-tuple-element.35), channel_id=1, source_target_pairs={{0,4},{4,8},{8,12},{12,16},{16,20},{20,24},{24,28},{1,5},{5,9},{9,... | collective-permute-start | bytes 270344 | tf_op jit(solution)/shard_map/ppermute | solution.py:344
  9.1 6.7 %collective-permute-start.1 = (f32[88,256]{1,0:T(8,128)S(1)}, f32[88,256]{1,0:T(8,128)S(1)}, u32[]{:S(2)}, u32[]{:S(2)}) collective-permute-start(f32[88,256]{1,0:T(8,128)S(1)} %get-tuple-element.36), channel_id=1, source_target_pairs={{4,0},{8,4},{12,8},{16,12},{20,16},{24,20},{28,24},{5,1},{9,5},{13... | collective-permute-start | bytes 270344 | tf_op jit(solution)/shard_map/ppermute | solution.py:345
  11.0 15.6 %collective-permute-start.5 = (bf16[5,64,256]{2,1,0:T(8,128)(2,1)S(1)}, bf16[5,64,256]{2,1,0:T(8,128)(2,1)S(1)}, u32[]{:S(2)}, u32[]{:S(2)}) collective-permute-start(bf16[5,64,256]{2,1,0:T(8,128)(2,1)S(1)} %get-tuple-element.45), channel_id=1, source_target_pairs={{0,3},{1,2},{2,1},{3,0},{4,7},{5,6},{6,5},{7,4},{8,11},{9,10},{10,... | collective-permute-start | bytes 491528 | tf_op jit(solution)/shard_map/ppermute | solution.py:315
  12.4 14.3 %collective-permute-start.7 = (bf16[5,64,256]{2,1,0:T(8,128)(2,1)S(1)}, bf16[5,64,256]{2,1,0:T(8,128)(2,1)S(1)}, u32[]{:S(2)}, u32[]{:S(2)}) collective-permute-start(bf16[5,64,256]{2,1,0:T(8,128)(2,1)S(1)} %get-tuple-element.47), channel_id=1, source_target_pairs={{0,1},{1,0},{2,3},{3,2},{4,5},{5,4},{6,7},{7,6},{8,9},{9,8},{10,11... | collective-permute-start | bytes 491528 | tf_op jit(solution)/shard_map/ppermute | solution.py:315
  15.9 6.1 %collective-permute-start.2 = (bf16[1,64,256]{2,1,0:T(8,128)(2,1)S(1)}, bf16[1,64,256]{2,1,0:T(8,128)(2,1)S(1)}, u32[]{:S(2)}, u32[]{:S(2)}) collective-permute-start(bf16[1,64,256]{2,1,0:T(8,128)(2,1)S(1)} %get-tuple-element.41), channel_id=1, source_target_pairs={{0,3},{1,2},{2,1},{3,0},{4,7},{5,6},{6,5},{7,4},{8,11},{9,10},{10,... | collective-permute-start | bytes 98312 | tf_op jit(solution)/shard_map/ppermute | solution.py:315
  17.8 5.5 %collective-permute-start.3 = (bf16[1,64,256]{2,1,0:T(8,128)(2,1)S(1)}, bf16[1,64,256]{2,1,0:T(8,128)(2,1)S(1)}, u32[]{:S(2)}, u32[]{:S(2)}) collective-permute-start(bf16[1,64,256]{2,1,0:T(8,128)(2,1)S(1)} %get-tuple-element.42), channel_id=1, source_target_pairs={{0,2},{1,3},{2,0},{3,1},{4,6},{5,7},{6,4},{7,5},{8,10},{9,11},{10,... | collective-permute-start | bytes 98312 | tf_op jit(solution)/shard_map/ppermute | solution.py:315
  18.4 5.6 %collective-permute-start.4 = (bf16[1,64,256]{2,1,0:T(8,128)(2,1)S(1)}, bf16[1,64,256]{2,1,0:T(8,128)(2,1)S(1)}, u32[]{:S(2)}, u32[]{:S(2)}) collective-permute-start(bf16[1,64,256]{2,1,0:T(8,128)(2,1)S(1)} %get-tuple-element.43), channel_id=1, source_target_pairs={{0,1},{1,0},{2,3},{3,2},{4,5},{5,4},{6,7},{7,6},{8,9},{9,8},{10,11... | collective-permute-start | bytes 98312 | tf_op jit(solution)/shard_map/ppermute | solution.py:315
  22.0 11.7 %collective-permute-start.11 = (bf16[4,64,256]{2,1,0:T(8,128)(2,1)S(1)}, bf16[4,64,256]{2,1,0:T(8,128)(2,1)S(1)}, u32[]{:S(2)}, u32[]{:S(2)}) collective-permute-start(bf16[4,64,256]{2,1,0:T(8,128)(2,1)S(1)} %get-tuple-element.56), channel_id=1, source_target_pairs={{0,3},{1,2},{2,1},{3,0},{4,7},{5,6},{6,5},{7,4},{8,11},{9,10},{10,... | collective-permute-start | bytes 393224 | tf_op jit(solution)/shard_map/ppermute | solution.py:315
  23.3 13.5 %collective-permute-start.12 = (bf16[4,64,256]{2,1,0:T(8,128)(2,1)S(1)}, bf16[4,64,256]{2,1,0:T(8,128)(2,1)S(1)}, u32[]{:S(2)}, u32[]{:S(2)}) collective-permute-start(bf16[4,64,256]{2,1,0:T(8,128)(2,1)S(1)} %get-tuple-element.57), channel_id=1, source_target_pairs={{0,2},{1,3},{2,0},{3,1},{4,6},{5,7},{6,4},{7,5},{8,10},{9,11},{10,... | collective-permute-start | bytes 393224 | tf_op jit(solution)/shard_map/ppermute | solution.py:315
  24.1 12.7 %collective-permute-start.13 = (bf16[4,64,256]{2,1,0:T(8,128)(2,1)S(1)}, bf16[4,64,256]{2,1,0:T(8,128)(2,1)S(1)}, u32[]{:S(2)}, u32[]{:S(2)}) collective-permute-start(bf16[4,64,256]{2,1,0:T(8,128)(2,1)S(1)} %get-tuple-element.58), channel_id=1, source_target_pairs={{0,1},{1,0},{2,3},{3,2},{4,5},{5,4},{6,7},{7,6},{8,9},{9,8},{10,11... | collective-permute-start | bytes 393224 | tf_op jit(solution)/shard_map/ppermute | solution.py:315
  33.2 13.5 %collective-permute-start.9 = (bf16[4,64,256]{2,1,0:T(8,128)(2,1)S(1)}, bf16[4,64,256]{2,1,0:T(8,128)(2,1)S(1)}, u32[]{:S(2)}, u32[]{:S(2)}) collective-permute-start(bf16[4,64,256]{2,1,0:T(8,128)(2,1)S(1)} %get-tuple-element.52), channel_id=1, source_target_pairs={{0,2},{1,3},{2,0},{3,1},{4,6},{5,7},{6,4},{7,5},{8,10},{9,11},{10,... | collective-permute-start | bytes 393224 | tf_op jit(solution)/shard_map/ppermute | solution.py:315
  33.3 13.7 %collective-permute-start.10 = (bf16[4,64,256]{2,1,0:T(8,128)(2,1)S(1)}, bf16[4,64,256]{2,1,0:T(8,128)(2,1)S(1)}, u32[]{:S(2)}, u32[]{:S(2)}) collective-permute-start(bf16[4,64,256]{2,1,0:T(8,128)(2,1)S(1)} %get-tuple-element.53), channel_id=1, source_target_pairs={{0,1},{1,0},{2,3},{3,2},{4,5},{5,4},{6,7},{7,6},{8,9},{9,8},{10,11... | collective-permute-start | bytes 393224 | tf_op jit(solution)/shard_map/ppermute | solution.py:315
  33.7 13.4 %collective-permute-start.8 = (bf16[4,64,256]{2,1,0:T(8,128)(2,1)S(1)}, bf16[4,64,256]{2,1,0:T(8,128)(2,1)S(1)}, u32[]{:S(2)}, u32[]{:S(2)}) collective-permute-start(bf16[4,64,256]{2,1,0:T(8,128)(2,1)S(1)} %get-tuple-element.51.refs_11_), channel_id=1, source_target_pairs={{0,3},{1,2},{2,1},{3,0},{4,7},{5,6},{6,5},{7,4},{8,11},{9,10},{10,... | collective-permute-start | bytes 393224 | tf_op jit(solution)/shard_map/ppermute | solution.py:315
  36.8 23.7 %copy-start.1 = (f32[64,32,256]{2,1,0:T(8,128)S(1)}, f32[64,32,256]{2,1,0:T(8,128)}, u32[]{:S(2)}) copy-start(f32[64,32,256]{2,1,0:T(8,128)} %refs_9_.1) | copy-start | bytes 6291460
  43.3 17.1 %collective-permute-start.14 = (bf16[4,64,256]{2,1,0:T(8,128)(2,1)S(1)}, bf16[4,64,256]{2,1,0:T(8,128)(2,1)S(1)}, u32[]{:S(2)}, u32[]{:S(2)}) collective-permute-start(bf16[4,64,256]{2,1,0:T(8,128)(2,1)S(1)} %get-tuple-element.60), channel_id=1, source_target_pairs={{0,3},{1,2},{2,1},{3,0},{4,7},{5,6},{6,5},{7,4},{8,11},{9,10},{10,... | collective-permute-start | bytes 393224 | tf_op jit(solution)/shard_map/ppermute | solution.py:315
  46.7 13.8 %collective-permute-start.15 = (bf16[4,64,256]{2,1,0:T(8,128)(2,1)S(1)}, bf16[4,64,256]{2,1,0:T(8,128)(2,1)S(1)}, u32[]{:S(2)}, u32[]{:S(2)}) collective-permute-start(bf16[4,64,256]{2,1,0:T(8,128)(2,1)S(1)} %get-tuple-element.61), channel_id=1, source_target_pairs={{0,2},{1,3},{2,0},{3,1},{4,6},{5,7},{6,4},{7,5},{8,10},{9,11},{10,... | collective-permute-start | bytes 393224 | tf_op jit(solution)/shard_map/ppermute | solution.py:315
  46.7 13.8 %collective-permute-start.16 = (bf16[4,64,256]{2,1,0:T(8,128)(2,1)S(1)}, bf16[4,64,256]{2,1,0:T(8,128)(2,1)S(1)}, u32[]{:S(2)}, u32[]{:S(2)}) collective-permute-start(bf16[4,64,256]{2,1,0:T(8,128)(2,1)S(1)} %get-tuple-element.62), channel_id=1, source_target_pairs={{0,1},{1,0},{2,3},{3,2},{4,5},{5,4},{6,7},{7,6},{8,9},{9,8},{10,11... | collective-permute-start | bytes 393224 | tf_op jit(solution)/shard_map/ppermute | solution.py:315
  47.1 8.8 %collective-permute-start.17 = (f32[64,256]{1,0:T(8,128)S(1)}, f32[64,256]{1,0:T(8,128)S(1)}, u32[]{:S(2)}, u32[]{:S(2)}) collective-permute-start(f32[64,256]{1,0:T(8,128)S(1)} %get-tuple-element.63), channel_id=1, source_target_pairs={{0,4},{4,8},{8,12},{12,16},{16,20},{20,24},{24,28},{1,5},{5,9},{9,... | collective-permute-start | bytes 196616 | tf_op jit(solution)/shard_map/ppermute | solution.py:421
  54.0 6.5 %collective-permute-start.18 = (f32[64,256]{1,0:T(8,128)S(1)}, f32[64,256]{1,0:T(8,128)S(1)}, u32[]{:S(2)}, u32[]{:S(2)}) collective-permute-start(f32[64,256]{1,0:T(8,128)S(1)} %get-tuple-element.64), channel_id=1, source_target_pairs={{4,0},{8,4},{12,8},{16,12},{20,16},{24,20},{28,24},{5,1},{9,5},{13... | collective-permute-start | bytes 196616 | tf_op jit(solution)/shard_map/ppermute | solution.py:422
  (2 other events, 4.5 us)

commit v12 on v11

--- a/solution.py
+++ b/solution.py
@@ -379,7 +379,7 @@
         compiler_params=params,
         cost_estimate=SMALL,
         name="late",
-    )(z_arg, turned, early[-2], inverse)
+    )(z_arg, turned, own, inverse)
     late = swap(late)
 
     def mix(arrays, window, skip, begin, rows_out, after=()):

time: 65.7 us -> 75.9 us (1.16)
  waiting for transfers between devices: 6.94 us -> 18.8 us
  starting transfers between devices: 34 us -> 31.5 us
    ppermute x15, waiting for transfers between devices: 1.9 us -> 16.1 us  [swap(): lax.ppermute(arrays[p], 'mode', [(i, i ^ p) for i in range(count)])]
    ppermute x1, waiting for transfers between devices: 4.54 us -> 0.71 us  [body(): high = lax.ppermute(bottom, 'dom', downward)]
    ppermute x1, waiting for transfers between devices: 0.49 us -> 1.92 us  [body(): high_rim = lax.ppermute(first_rim, 'dom', downward)]
    ppermute x15, starting transfers between devices: 19.4 us -> 18.1 us  [swap(): lax.ppermute(arrays[p], 'mode', [(i, i ^ p) for i in range(count)])]
    ppermute x1, starting transfers between devices: 6.84 us -> 5.96 us  [body(): low = lax.ppermute(top, 'dom', upward)]
  transfers between devices with their start and end apart: 19 -> 19, of which waited for: 3 -> 4; matrix products, arithmetic and copies ran while one was open for 0% -> 0% of each run, Pallas kernels for 26% -> 22%
where the time goes in v12:
time: 75.9 us; the launch traced here: 74.8 us
  starting transfers between devices  31.5 us (42%)
  Pallas kernels  21.3 us (28%)
  waiting for transfers between devices  18.8 us (25%)
  local copies, waits for them, and re-layouts  2.32 us (3%)
  between operations  0.83 us (1%)
    ppermute x15, starting transfers between devices, swap(): lax.ppermute(arrays[p], 'mode', [(i, i ^ p) for i in range(count)])  18.1 us
    ppermute x15, waiting for transfers between devices, swap(): lax.ppermute(arrays[p], 'mode', [(i, i ^ p) for i in range(count)])  16.1 us
    pallas_call x2, Pallas kernels, mix(): pl.pallas_call(functools.partial(mix_kernel, count, groups, fields, windo...  13 us
    ppermute x1, starting transfers between devices, body(): low = lax.ppermute(top, 'dom', upward)  5.96 us
    pallas_call x1, Pallas kernels, body(): pl.pallas_call(functools.partial(post_kernel, count, slab, half, rows, rh...  4.31 us
    ppermute x1, starting transfers between devices, body(): low_rim = lax.ppermute(last_rim, 'dom', upward)  3.68 us
    pallas_call x1, Pallas kernels, body(): pl.pallas_call(functools.partial(dense_kernel, groups, fields, here), out...  2.84 us
    unnamed x14, local copies, waits for them, and re-layouts  2.2 us
  transfers between devices with their start and end apart: 19, of which 4 were waited for; matrix products, arithmetic and copies ran while one was open for 0% of the time, Pallas kernels for 22%

profile of v12, /device:TPU:3, one launch (start us, length us, event | category | flops | bytes accessed | tf_op | source)
XLA Modules:
  0.0 74.8 jit_solution(2750001720376245577)
XLA Ops:
  0.6 1.6 %copy-done = f32[64,32,256]{2,1,0:T(8,128)S(1)} copy-done((f32[64,32,256]{2,1,0:T(8,128)S(1)}, f32[64,32,256]{2,1,0:T(8,128)}, u32[]{:S(2)}) %copy-start) | copy-done | bytes 2097176
  2.2 0.5 turn.1
  2.7 0.6 copy-done.2
  3.4 3.7 %collective-permute-start = (f32[88,256]{1,0:T(8,128)S(1)}, f32[88,256]{1,0:T(8,128)S(1)}, u32[]{:S(2)}, u32[]{:S(2)}) collective-permute-start(f32[88,256]{1,0:T(8,128)S(1)} %get-tuple-element.35), channel_id=1, source_target_pairs={{0,4},{4,8},{8,12},{12,16},{16,20},{20,24},{24,28},{1,5},{5,9},{9,... | collective-permute-start | bytes 270344 | tf_op jit(solution)/shard_map/ppermute | solution.py:344
  7.0 1.9 %collective-permute-start.1 = (f32[88,256]{1,0:T(8,128)S(1)}, f32[88,256]{1,0:T(8,128)S(1)}, u32[]{:S(2)}, u32[]{:S(2)}) collective-permute-start(f32[88,256]{1,0:T(8,128)S(1)} %get-tuple-element.36), channel_id=1, source_target_pairs={{4,0},{8,4},{12,8},{16,12},{20,16},{24,20},{28,24},{5,1},{9,5},{13... | collective-permute-start | bytes 270344 | tf_op jit(solution)/shard_map/ppermute | solution.py:345
  9.0 2.8 %dense.1 = (bf16[4,256,1280]{2,1,0:T(8,128)(2,1)S(1)}, f32[256,128]{1,0:T(8,128)S(1)}) custom-call(s32[1]{0:T(128)} %bitcast.z_ref, s32[3,5376]{1,0:T(4,128)S(1)} %bitcast.6, f32[1,5376]{1,0:T(1,128)S(1)} %broadcast_in_dim.3.value_ref), custom_call_target="tpu_custom_call" | custom-call | flops 1 | bytes 1 | tf_op jit(solution)/shard_map/dense/pallas_call | solution.py:320
  11.9 1.9 %collective-permute-done.1.high_ref = f32[88,256]{1,0:T(8,128)S(1)} collective-permute-done((f32[88,256]{1,0:T(8,128)S(1)}, f32[88,256]{1,0:T(8,128)S(1)}, u32[]{:S(2)}, u32[]{:S(2)}) %collective-permute-start.1) | collective-permute-done | bytes 90144 | tf_op jit(solution)/shard_map/ppermute | solution.py:345
  13.8 3.4 %collective-permute-start.2 = (bf16[1,64,256]{2,1,0:T(8,128)(2,1)S(1)}, bf16[1,64,256]{2,1,0:T(8,128)(2,1)S(1)}, u32[]{:S(2)}, u32[]{:S(2)}) collective-permute-start(bf16[1,64,256]{2,1,0:T(8,128)(2,1)S(1)} %get-tuple-element.41), channel_id=1, source_target_pairs={{0,3},{1,2},{2,1},{3,0},{4,7},{5,6},{6,5},{7,4},{8,11},{9,10},{10,... | collective-permute-start | bytes 98312 | tf_op jit(solution)/shard_map/ppermute | solution.py:315
  17.7 3.1 %collective-permute-start.7 = (bf16[5,64,256]{2,1,0:T(8,128)(2,1)S(1)}, bf16[5,64,256]{2,1,0:T(8,128)(2,1)S(1)}, u32[]{:S(2)}, u32[]{:S(2)}) collective-permute-start(bf16[5,64,256]{2,1,0:T(8,128)(2,1)S(1)} %get-tuple-element.47), channel_id=1, source_target_pairs={{0,1},{1,0},{2,3},{3,2},{4,5},{5,4},{6,7},{7,6},{8,9},{9,8},{10,11... | collective-permute-start | bytes 491528 | tf_op jit(solution)/shard_map/ppermute | solution.py:315
  21.8 12.3 %collective-permute-done.3.refs_2_ = bf16[1,64,256]{2,1,0:T(8,128)(2,1)S(1)} collective-permute-done((bf16[1,64,256]{2,1,0:T(8,128)(2,1)S(1)}, bf16[1,64,256]{2,1,0:T(8,128)(2,1)S(1)}, u32[]{:S(2)}, u32[]{:S(2)}) %collective-permute-start.3) | collective-permute-done | bytes 32800 | tf_op jit(solution)/shard_map/ppermute | solution.py:315
  34.0 1.6 %collective-permute-start.11 = (bf16[4,64,256]{2,1,0:T(8,128)(2,1)S(1)}, bf16[4,64,256]{2,1,0:T(8,128)(2,1)S(1)}, u32[]{:S(2)}, u32[]{:S(2)}) collective-permute-start(bf16[4,64,256]{2,1,0:T(8,128)(2,1)S(1)} %get-tuple-element.56), channel_id=1, source_target_pairs={{0,3},{1,2},{2,1},{3,0},{4,7},{5,6},{6,5},{7,4},{8,11},{9,10},{10,... | collective-permute-start | bytes 393224 | tf_op jit(solution)/shard_map/ppermute | solution.py:315
  35.7 1.9 %collective-permute-start.13 = (bf16[4,64,256]{2,1,0:T(8,128)(2,1)S(1)}, bf16[4,64,256]{2,1,0:T(8,128)(2,1)S(1)}, u32[]{:S(2)}, u32[]{:S(2)}) collective-permute-start(bf16[4,64,256]{2,1,0:T(8,128)(2,1)S(1)} %get-tuple-element.58), channel_id=1, source_target_pairs={{0,1},{1,0},{2,3},{3,2},{4,5},{5,4},{6,7},{7,6},{8,9},{9,8},{10,11... | collective-permute-start | bytes 393224 | tf_op jit(solution)/shard_map/ppermute | solution.py:315
  37.6 6.5 %mix.2 = (bf16[4,64,256]{2,1,0:T(8,128)(2,1)S(1)}, bf16[4,64,256]{2,1,0:T(8,128)(2,1)S(1)}, bf16[4,64,256]{2,1,0:T(8,128)(2,1)S(1)}, bf16[4,64,256]{2,1,0:T(8,128)(2,1)S(1)}) custom-call(bf16[1,64,256]{2,1,0:T(8,128)(2,1)S(1)} %get-tuple-element.40.refs_0_, bf16[1,64,256]{2,1,0:T(8,128)(2,1)S(1)} %collective-permute-done.2.refs_1_, ...), custom_call_target="tpu_custom_call" | custom-call | flops 10000000000 | bytes 16777216 | tf_op jit(solution)/shard_map/mix/pallas_call | solution.py:387
  44.1 0.5 collective-permute-start.9
  44.7 1.4 %collective-permute-start.10 = (bf16[4,64,256]{2,1,0:T(8,128)(2,1)S(1)}, bf16[4,64,256]{2,1,0:T(8,128)(2,1)S(1)}, u32[]{:S(2)}, u32[]{:S(2)}) collective-permute-start(bf16[4,64,256]{2,1,0:T(8,128)(2,1)S(1)} %get-tuple-element.53), channel_id=1, source_target_pairs={{0,1},{1,0},{2,3},{3,2},{4,5},{5,4},{6,7},{7,6},{8,9},{9,8},{10,11... | collective-permute-start | bytes 393224 | tf_op jit(solution)/shard_map/ppermute | solution.py:315
  46.1 1.6 %collective-permute-start.8 = (bf16[4,64,256]{2,1,0:T(8,128)(2,1)S(1)}, bf16[4,64,256]{2,1,0:T(8,128)(2,1)S(1)}, u32[]{:S(2)}, u32[]{:S(2)}) collective-permute-start(bf16[4,64,256]{2,1,0:T(8,128)(2,1)S(1)} %get-tuple-element.51.refs_11_), channel_id=1, source_target_pairs={{0,3},{1,2},{2,1},{3,0},{4,7},{5,6},{6,5},{7,4},{8,11},{9,10},{10,... | collective-permute-start | bytes 393224 | tf_op jit(solution)/shard_map/ppermute | solution.py:315
  47.8 6.5 %mix.3 = (bf16[4,64,256]{2,1,0:T(8,128)(2,1)S(1)}, bf16[4,64,256]{2,1,0:T(8,128)(2,1)S(1)}, bf16[4,64,256]{2,1,0:T(8,128)(2,1)S(1)}, bf16[4,64,256]{2,1,0:T(8,128)(2,1)S(1)}) custom-call(bf16[5,64,256]{2,1,0:T(8,128)(2,1)S(1)} %get-tuple-element.44.refs_4_.refs_0_, bf16[5,64,256]{2,1,0:T(8,128)(2,1)S(1)} %collective-permute-done.5.refs_5_.refs_1_, ...), custom_call_target="tpu_custom_call" | custom-call | flops 10000000000 | bytes 16777216 | tf_op jit(solution)/shard_map/mix/pallas_call | solution.py:387
  54.3 1.7 %collective-permute-start.14 = (bf16[4,64,256]{2,1,0:T(8,128)(2,1)S(1)}, bf16[4,64,256]{2,1,0:T(8,128)(2,1)S(1)}, u32[]{:S(2)}, u32[]{:S(2)}) collective-permute-start(bf16[4,64,256]{2,1,0:T(8,128)(2,1)S(1)} %get-tuple-element.60), channel_id=1, source_target_pairs={{0,3},{1,2},{2,1},{3,0},{4,7},{5,6},{6,5},{7,4},{8,11},{9,10},{10,... | collective-permute-start | bytes 393224 | tf_op jit(solution)/shard_map/ppermute | solution.py:315
  56.0 1.9 %collective-permute-start.16 = (bf16[4,64,256]{2,1,0:T(8,128)(2,1)S(1)}, bf16[4,64,256]{2,1,0:T(8,128)(2,1)S(1)}, u32[]{:S(2)}, u32[]{:S(2)}) collective-permute-start(bf16[4,64,256]{2,1,0:T(8,128)(2,1)S(1)} %get-tuple-element.62), channel_id=1, source_target_pairs={{0,1},{1,0},{2,3},{3,2},{4,5},{5,4},{6,7},{7,6},{8,9},{9,8},{10,11... | collective-permute-start | bytes 393224 | tf_op jit(solution)/shard_map/ppermute | solution.py:315
  58.0 6.0 %collective-permute-start.17 = (f32[64,256]{1,0:T(8,128)S(1)}, f32[64,256]{1,0:T(8,128)S(1)}, u32[]{:S(2)}, u32[]{:S(2)}) collective-permute-start(f32[64,256]{1,0:T(8,128)S(1)} %get-tuple-element.63), channel_id=1, source_target_pairs={{0,4},{4,8},{8,12},{12,16},{16,20},{20,24},{24,28},{1,5},{5,9},{9,... | collective-permute-start | bytes 196616 | tf_op jit(solution)/shard_map/ppermute | solution.py:421
  64.0 1.9 %collective-permute-start.18 = (f32[64,256]{1,0:T(8,128)S(1)}, f32[64,256]{1,0:T(8,128)S(1)}, u32[]{:S(2)}, u32[]{:S(2)}) collective-permute-start(f32[64,256]{1,0:T(8,128)S(1)} %get-tuple-element.64), channel_id=1, source_target_pairs={{4,0},{8,4},{12,8},{16,12},{20,16},{24,20},{28,24},{5,1},{9,5},{13... | collective-permute-start | bytes 196616 | tf_op jit(solution)/shard_map/ppermute | solution.py:422
  65.9 3.8 %collective-permute-done.15.refs_6_ = bf16[4,64,256]{2,1,0:T(8,128)(2,1)S(1)} collective-permute-done((bf16[4,64,256]{2,1,0:T(8,128)(2,1)S(1)}, bf16[4,64,256]{2,1,0:T(8,128)(2,1)S(1)}, u32[]{:S(2)}, u32[]{:S(2)}) %collective-permute-start.15) | collective-permute-done | bytes 131104 | tf_op jit(solution)/shard_map/ppermute | solution.py:315
  69.7 0.7 collective-permute-done.18.refs_11_
  70.5 4.3 %post.1 = (f32[64,32,256]{2,1,0:T(8,128)}, f32[64,32,256]{2,1,0:T(8,128)}) custom-call(s32[1]{0:T(128)} %bitcast.z_ref, bf16[4,64,256]{2,1,0:T(8,128)(2,1)S(1)} %get-tuple-element.50.refs_0_, bf16[4,64,256]{2,1,0:T(8,128)(2,1)S(1)} %collective-permute-done.8.refs_1_, bf16[4,64,256]{2,1,0:T(8,128)(2,1)S(1)} %collective-permute-done.9.refs_2_, ...), custom_call_target="tpu_custom_call" | custom-call | tf_op jit(solution)/shard_map/post/pallas_call | solution.py:432
  (41 shorter events, 1.6 us)
Async XLA Ops:
  0.6 1.6 %copy-start = (f32[64,32,256]{2,1,0:T(8,128)S(1)}, f32[64,32,256]{2,1,0:T(8,128)}, u32[]{:S(2)}) copy-start(f32[64,32,256]{2,1,0:T(8,128)} %refs_9_.1) | copy-start | bytes 6291460
  2.2 6.7 %copy-start.6 = (f32[5376]{0:T(1024)S(1)}, f32[5376]{0:T(1024)}, u32[]{:S(2)}) copy-start(f32[5376]{0:T(1024)} %param.11) | copy-start | bytes 64516
  2.2 6.8 %copy-start.5 = (s32[5376,3]{0,1:T(4,128)S(1)}, s32[5376,3]{0,1:T(4,128)}, u32[]{:S(2)}) copy-start(s32[5376,3]{0,1:T(4,128)} %param.10) | copy-start | bytes 193540
  2.7 18.4 %copy-start.3 = (f32[64,32,256]{2,1,0:T(8,128)S(1)}, f32[64,32,256]{2,1,0:T(8,128)}, u32[]{:S(2)}) copy-start(f32[64,32,256]{2,1,0:T(8,128)} %refs_8_.1) | copy-start | bytes 6291460
  3.4 8.5 %collective-permute-start = (f32[88,256]{1,0:T(8,128)S(1)}, f32[88,256]{1,0:T(8,128)S(1)}, u32[]{:S(2)}, u32[]{:S(2)}) collective-permute-start(f32[88,256]{1,0:T(8,128)S(1)} %get-tuple-element.35), channel_id=1, source_target_pairs={{0,4},{4,8},{8,12},{12,16},{16,20},{20,24},{24,28},{1,5},{5,9},{9,... | collective-permute-start | bytes 270344 | tf_op jit(solution)/shard_map/ppermute | solution.py:344
  7.0 6.7 %collective-permute-start.1 = (f32[88,256]{1,0:T(8,128)S(1)}, f32[88,256]{1,0:T(8,128)S(1)}, u32[]{:S(2)}, u32[]{:S(2)}) collective-permute-start(f32[88,256]{1,0:T(8,128)S(1)} %get-tuple-element.36), channel_id=1, source_target_pairs={{4,0},{8,4},{12,8},{16,12},{20,16},{24,20},{28,24},{5,1},{9,5},{13... | collective-permute-start | bytes 270344 | tf_op jit(solution)/shard_map/ppermute | solution.py:345
  13.8 7.0 %collective-permute-start.2 = (bf16[1,64,256]{2,1,0:T(8,128)(2,1)S(1)}, bf16[1,64,256]{2,1,0:T(8,128)(2,1)S(1)}, u32[]{:S(2)}, u32[]{:S(2)}) collective-permute-start(bf16[1,64,256]{2,1,0:T(8,128)(2,1)S(1)} %get-tuple-element.41), channel_id=1, source_target_pairs={{0,3},{1,2},{2,1},{3,0},{4,7},{5,6},{6,5},{7,4},{8,11},{9,10},{10,... | collective-permute-start | bytes 98312 | tf_op jit(solution)/shard_map/ppermute | solution.py:315
  17.2 18.5 %collective-permute-start.5 = (bf16[5,64,256]{2,1,0:T(8,128)(2,1)S(1)}, bf16[5,64,256]{2,1,0:T(8,128)(2,1)S(1)}, u32[]{:S(2)}, u32[]{:S(2)}) collective-permute-start(bf16[5,64,256]{2,1,0:T(8,128)(2,1)S(1)} %get-tuple-element.45), channel_id=1, source_target_pairs={{0,3},{1,2},{2,1},{3,0},{4,7},{5,6},{6,5},{7,4},{8,11},{9,10},{10,... | collective-permute-start | bytes 491528 | tf_op jit(solution)/shard_map/ppermute | solution.py:315
  17.3 20.3 %collective-permute-start.6 = (bf16[5,64,256]{2,1,0:T(8,128)(2,1)S(1)}, bf16[5,64,256]{2,1,0:T(8,128)(2,1)S(1)}, u32[]{:S(2)}, u32[]{:S(2)}) collective-permute-start(bf16[5,64,256]{2,1,0:T(8,128)(2,1)S(1)} %get-tuple-element.46), channel_id=1, source_target_pairs={{0,2},{1,3},{2,0},{3,1},{4,6},{5,7},{6,4},{7,5},{8,10},{9,11},{10,... | collective-permute-start | bytes 491528 | tf_op jit(solution)/shard_map/ppermute | solution.py:315
  17.7 19.9 %collective-permute-start.7 = (bf16[5,64,256]{2,1,0:T(8,128)(2,1)S(1)}, bf16[5,64,256]{2,1,0:T(8,128)(2,1)S(1)}, u32[]{:S(2)}, u32[]{:S(2)}) collective-permute-start(bf16[5,64,256]{2,1,0:T(8,128)(2,1)S(1)} %get-tuple-element.47), channel_id=1, source_target_pairs={{0,1},{1,0},{2,3},{3,2},{4,5},{5,4},{6,7},{7,6},{8,9},{9,8},{10,11... | collective-permute-start | bytes 491528 | tf_op jit(solution)/shard_map/ppermute | solution.py:315
  20.8 13.3 %collective-permute-start.3 = (bf16[1,64,256]{2,1,0:T(8,128)(2,1)S(1)}, bf16[1,64,256]{2,1,0:T(8,128)(2,1)S(1)}, u32[]{:S(2)}, u32[]{:S(2)}) collective-permute-start(bf16[1,64,256]{2,1,0:T(8,128)(2,1)S(1)} %get-tuple-element.42), channel_id=1, source_target_pairs={{0,2},{1,3},{2,0},{3,1},{4,6},{5,7},{6,4},{7,5},{8,10},{9,11},{10,... | collective-permute-start | bytes 98312 | tf_op jit(solution)/shard_map/ppermute | solution.py:315
  20.8 14.9 %collective-permute-start.4 = (bf16[1,64,256]{2,1,0:T(8,128)(2,1)S(1)}, bf16[1,64,256]{2,1,0:T(8,128)(2,1)S(1)}, u32[]{:S(2)}, u32[]{:S(2)}) collective-permute-start(bf16[1,64,256]{2,1,0:T(8,128)(2,1)S(1)} %get-tuple-element.43), channel_id=1, source_target_pairs={{0,1},{1,0},{2,3},{3,2},{4,5},{5,4},{6,7},{7,6},{8,9},{9,8},{10,11... | collective-permute-start | bytes 98312 | tf_op jit(solution)/shard_map/ppermute | solution.py:315
  34.0 12.1 %collective-permute-start.11 = (bf16[4,64,256]{2,1,0:T(8,128)(2,1)S(1)}, bf16[4,64,256]{2,1,0:T(8,128)(2,1)S(1)}, u32[]{:S(2)}, u32[]{:S(2)}) collective-permute-start(bf16[4,64,256]{2,1,0:T(8,128)(2,1)S(1)} %get-tuple-element.56), channel_id=1, source_target_pairs={{0,3},{1,2},{2,1},{3,0},{4,7},{5,6},{6,5},{7,4},{8,11},{9,10},{10,... | collective-permute-start | bytes 393224 | tf_op jit(solution)/shard_map/ppermute | solution.py:315
  35.7 12.1 %collective-permute-start.12 = (bf16[4,64,256]{2,1,0:T(8,128)(2,1)S(1)}, bf16[4,64,256]{2,1,0:T(8,128)(2,1)S(1)}, u32[]{:S(2)}, u32[]{:S(2)}) collective-permute-start(bf16[4,64,256]{2,1,0:T(8,128)(2,1)S(1)} %get-tuple-element.57), channel_id=1, source_target_pairs={{0,2},{1,3},{2,0},{3,1},{4,6},{5,7},{6,4},{7,5},{8,10},{9,11},{10,... | collective-permute-start | bytes 393224 | tf_op jit(solution)/shard_map/ppermute | solution.py:315
  35.7 12.1 %collective-permute-start.13 = (bf16[4,64,256]{2,1,0:T(8,128)(2,1)S(1)}, bf16[4,64,256]{2,1,0:T(8,128)(2,1)S(1)}, u32[]{:S(2)}, u32[]{:S(2)}) collective-permute-start(bf16[4,64,256]{2,1,0:T(8,128)(2,1)S(1)} %get-tuple-element.58), channel_id=1, source_target_pairs={{0,1},{1,0},{2,3},{3,2},{4,5},{5,4},{6,7},{7,6},{8,9},{9,8},{10,11... | collective-permute-start | bytes 393224 | tf_op jit(solution)/shard_map/ppermute | solution.py:315
  44.1 11.9 %collective-permute-start.9 = (bf16[4,64,256]{2,1,0:T(8,128)(2,1)S(1)}, bf16[4,64,256]{2,1,0:T(8,128)(2,1)S(1)}, u32[]{:S(2)}, u32[]{:S(2)}) collective-permute-start(bf16[4,64,256]{2,1,0:T(8,128)(2,1)S(1)} %get-tuple-element.52), channel_id=1, source_target_pairs={{0,2},{1,3},{2,0},{3,1},{4,6},{5,7},{6,4},{7,5},{8,10},{9,11},{10,... | collective-permute-start | bytes 393224 | tf_op jit(solution)/shard_map/ppermute | solution.py:315
  44.7 13.2 %collective-permute-start.10 = (bf16[4,64,256]{2,1,0:T(8,128)(2,1)S(1)}, bf16[4,64,256]{2,1,0:T(8,128)(2,1)S(1)}, u32[]{:S(2)}, u32[]{:S(2)}) collective-permute-start(bf16[4,64,256]{2,1,0:T(8,128)(2,1)S(1)} %get-tuple-element.53), channel_id=1, source_target_pairs={{0,1},{1,0},{2,3},{3,2},{4,5},{5,4},{6,7},{7,6},{8,9},{9,8},{10,11... | collective-permute-start | bytes 393224 | tf_op jit(solution)/shard_map/ppermute | solution.py:315
  46.1 11.8 %collective-permute-start.8 = (bf16[4,64,256]{2,1,0:T(8,128)(2,1)S(1)}, bf16[4,64,256]{2,1,0:T(8,128)(2,1)S(1)}, u32[]{:S(2)}, u32[]{:S(2)}) collective-permute-start(bf16[4,64,256]{2,1,0:T(8,128)(2,1)S(1)} %get-tuple-element.51.refs_11_), channel_id=1, source_target_pairs={{0,3},{1,2},{2,1},{3,0},{4,7},{5,6},{6,5},{7,4},{8,11},{9,10},{10,... | collective-permute-start | bytes 393224 | tf_op jit(solution)/shard_map/ppermute | solution.py:315
  47.8 22.7 %copy-start.1 = (f32[64,32,256]{2,1,0:T(8,128)S(1)}, f32[64,32,256]{2,1,0:T(8,128)}, u32[]{:S(2)}) copy-start(f32[64,32,256]{2,1,0:T(8,128)} %refs_9_.1) | copy-start | bytes 6291460
  54.3 11.6 %collective-permute-start.14 = (bf16[4,64,256]{2,1,0:T(8,128)(2,1)S(1)}, bf16[4,64,256]{2,1,0:T(8,128)(2,1)S(1)}, u32[]{:S(2)}, u32[]{:S(2)}) collective-permute-start(bf16[4,64,256]{2,1,0:T(8,128)(2,1)S(1)} %get-tuple-element.60), channel_id=1, source_target_pairs={{0,3},{1,2},{2,1},{3,0},{4,7},{5,6},{6,5},{7,4},{8,11},{9,10},{10,... | collective-permute-start | bytes 393224 | tf_op jit(solution)/shard_map/ppermute | solution.py:315
  56.0 13.7 %collective-permute-start.15 = (bf16[4,64,256]{2,1,0:T(8,128)(2,1)S(1)}, bf16[4,64,256]{2,1,0:T(8,128)(2,1)S(1)}, u32[]{:S(2)}, u32[]{:S(2)}) collective-permute-start(bf16[4,64,256]{2,1,0:T(8,128)(2,1)S(1)} %get-tuple-element.61), channel_id=1, source_target_pairs={{0,2},{1,3},{2,0},{3,1},{4,6},{5,7},{6,4},{7,5},{8,10},{9,11},{10,... | collective-permute-start | bytes 393224 | tf_op jit(solution)/shard_map/ppermute | solution.py:315
  56.0 13.7 %collective-permute-start.16 = (bf16[4,64,256]{2,1,0:T(8,128)(2,1)S(1)}, bf16[4,64,256]{2,1,0:T(8,128)(2,1)S(1)}, u32[]{:S(2)}, u32[]{:S(2)}) collective-permute-start(bf16[4,64,256]{2,1,0:T(8,128)(2,1)S(1)} %get-tuple-element.62), channel_id=1, source_target_pairs={{0,1},{1,0},{2,3},{3,2},{4,5},{5,4},{6,7},{7,6},{8,9},{9,8},{10,11... | collective-permute-start | bytes 393224 | tf_op jit(solution)/shard_map/ppermute | solution.py:315
  58.0 11.7 %collective-permute-start.17 = (f32[64,256]{1,0:T(8,128)S(1)}, f32[64,256]{1,0:T(8,128)S(1)}, u32[]{:S(2)}, u32[]{:S(2)}) collective-permute-start(f32[64,256]{1,0:T(8,128)S(1)} %get-tuple-element.63), channel_id=1, source_target_pairs={{0,4},{4,8},{8,12},{12,16},{16,20},{20,24},{24,28},{1,5},{5,9},{9,... | collective-permute-start | bytes 196616 | tf_op jit(solution)/shard_map/ppermute | solution.py:421
  64.0 6.5 %collective-permute-start.18 = (f32[64,256]{1,0:T(8,128)S(1)}, f32[64,256]{1,0:T(8,128)S(1)}, u32[]{:S(2)}, u32[]{:S(2)}) collective-permute-start(f32[64,256]{1,0:T(8,128)S(1)} %get-tuple-element.64), channel_id=1, source_target_pairs={{4,0},{8,4},{12,8},{16,12},{20,16},{24,20},{28,24},{5,1},{9,5},{13... | collective-permute-start | bytes 196616 | tf_op jit(solution)/shard_map/ppermute | solution.py:422
  (2 other events, 2.2 us)
